TPU v7x, 32 devices: a whole 2x2x4 slice. The times are simulated.
32 devices in a mesh: section: 2 (over core), seq: 16 (over z, y, x).
Axes of the slice: x: 2, y: 2, z: 4, core: 2. Of those that a mesh axis runs over, the one named last changes fastest.
Arguments:
- down_input: bfloat16 [64, 6144], P(None, 'seq'), may hold values from -6 to 6
- up_input: bfloat16 [64, 6144], P(None, 'seq'), may hold values from -6 to 6
- down_cot: bfloat16 [64, 6144], P(None, 'seq'), may hold values from -6 to 6
- up_cot: bfloat16 [64, 6144], P(None, 'seq'), may hold values from -6 to 6
- section_weights: bfloat16 [2, 2, 6144, 6144], P('section', None, 'seq'), as said below
- section_gains: float32 [2, 2, 6144], P('section', None, 'seq'), as said below
Outputs:
- down_outputs: bfloat16 [2, 64, 6144], P('section', None, 'seq')
- up_outputs: bfloat16 [2, 64, 6144], P('section', None, 'seq')
- grad_first: float32 [2, 6144, 3072], P('section', 'seq')
- grad_second: float32 [2, 6144, 3072], P('section', 'seq')
- gain_grads: float32 [2, 6144], P('section', 'seq')
Inputs may be any that keep to these rules, and one draw needn't show every extreme that they name: For every i, section_weights[i, 1] equals section_weights[1 - i, 0]. For every i, section_gains[i, 1] equals section_gains[1 - i, 0]; all entries lie in 0.3 to 3.
All inputs are finite; a program needn't handle non-finite values.
Results may differ from a plain program's by a relative error of at most 0.024.
Values may be sent and summed in bfloat16 or wider, within the bound.
No kernel may reach another device: no remote copies, remote signals or barrier semaphores. Data moves between devices by JAX's collectives and lax.ppermute only.
A program may use at most 128 MiB of HBM per device.

v0:
```python
import jax
import jax.numpy as jnp
from jax import lax
from jax.sharding import PartitionSpec as P

EPS = 1e-05


def passed_along(block, axis, distance):
    devices = range(lax.axis_size(axis))
    route = [(i - distance, i) for i in devices if i - distance in devices]
    return lax.ppermute(block, axis, route)


def from_partner(shard, axis, stride):
    return lax.ppermute(shard, axis, [(i, i ^ 1 << stride) for i in range(lax.axis_size(axis))])


def gelu_exact(values):
    return jax.nn.gelu(values, approximate=False)


def rounded(values):
    return lax.optimization_barrier(values.astype(jnp.bfloat16)).astype(jnp.float32)


def norm_from_sums(first_sum, second_sum, model_width):
    row_mean = (first_sum / model_width)[:, None]
    row_var = (second_sum / model_width)[:, None] - row_mean * row_mean
    row_scale = lax.rsqrt(row_var + EPS)
    return (row_mean, row_scale)


def keep_live(live_flag, record, previous):
    return jax.tree.map(lambda fresh, older: jnp.where(live_flag, fresh, older), record, previous)


def project_rows(normed, weight):
    return lax.dot_general(
        normed, weight, (((1,), (1,)), ((), ())), preferred_element_type=jnp.float32
    )


def back_rows(weight_cols, grad_hidden):
    return lax.dot_general(
        weight_cols, grad_hidden, (((0,), (1,)), ((), ())), preferred_element_type=jnp.float32
    )


def per_device(down_input, up_input, down_cot, up_cot, section_weights, section_gains):
    sections = lax.axis_size("section")
    position = lax.axis_index("section")
    weight_down = section_weights[0, 0]
    weight_up = section_weights[0, 1]
    gain_pair = section_gains[0]
    model_width = weight_down.shape[1]
    tokens = down_input.shape[0]
    half_cols = model_width // 2
    state_down = down_input
    state_up = up_input
    saved_down = None
    saved_up = None
    for section_step in range(sections):
        wide_down = state_down.astype(jnp.float32)
        wide_up = state_up.astype(jnp.float32)
        totals = lax.psum(
            (
                jnp.sum(wide_down, axis=1),
                jnp.sum(wide_down * wide_down, axis=1),
                jnp.sum(wide_up, axis=1),
                jnp.sum(wide_up * wide_up, axis=1),
            ),
            "seq",
        )
        mean_down, scale_down = norm_from_sums(totals[0], totals[1], model_width)
        mean_up, scale_up = norm_from_sums(totals[2], totals[3], model_width)
        local_down = ((wide_down - mean_down) * scale_down * gain_pair[0][None, :]).astype(
            jnp.bfloat16
        )
        local_up = ((wide_up - mean_up) * scale_up * gain_pair[1][None, :]).astype(jnp.bfloat16)
        normed_down, normed_up = (
            lax.all_gather(local_down, "seq", axis=1, tiled=True),
            lax.all_gather(local_up, "seq", axis=1, tiled=True),
        )
        hidden_down = project_rows(normed_down, weight_down)
        hidden_up = project_rows(normed_up, weight_up)
        output_down = (wide_down + gelu_exact(hidden_down)).astype(jnp.bfloat16)
        output_up = (wide_up + gelu_exact(hidden_up)).astype(jnp.bfloat16)
        record_down = (state_down, mean_down, scale_down, normed_down, hidden_down, output_down)
        record_up = (state_up, mean_up, scale_up, normed_up, hidden_up, output_up)
        if section_step == 0:
            saved_down = record_down
            saved_up = record_up
        else:
            saved_down = keep_live(position == section_step, record_down, saved_down)
            saved_up = keep_live(position == sections - 1 - section_step, record_up, saved_up)
        if section_step + 1 < sections:
            state_down = passed_along(output_down, "section", 1)
            state_up = passed_along(output_up, "section", -1)
    input_down, mean_down, scale_down, normed_down, hidden_down, output_down = saved_down
    input_up, mean_up, scale_up, normed_up, hidden_up, output_up = saved_up
    hat_down = (input_down.astype(jnp.float32) - mean_down) * scale_down
    hat_up = (input_up.astype(jnp.float32) - mean_up) * scale_up
    unused_down, pullback_down = jax.vjp(gelu_exact, hidden_down)
    unused_up, pullback_up = jax.vjp(gelu_exact, hidden_up)
    grad_down = down_cot
    grad_up = up_cot
    kept_down = None
    kept_up = None
    for section_step in range(sections):
        wide_grad_down = grad_down.astype(jnp.float32)
        wide_grad_up = grad_up.astype(jnp.float32)
        hidden_grad_down = pullback_down(wide_grad_down)[0].astype(jnp.bfloat16)
        hidden_grad_up = pullback_up(wide_grad_up)[0].astype(jnp.bfloat16)
        part_down = back_rows(weight_down, hidden_grad_down)
        part_up = back_rows(weight_up, hidden_grad_up)
        grad_rows = lax.psum_scatter(
            jnp.concatenate([part_down, part_up], axis=1).astype(jnp.bfloat16),
            "seq",
            scatter_dimension=0,
            tiled=True,
        ).astype(jnp.float32)
        normed_grad_down = grad_rows[:, :tokens].T
        normed_grad_up = grad_rows[:, tokens:].T
        gained_down = normed_grad_down * gain_pair[0][None, :]
        gained_up = normed_grad_up * gain_pair[1][None, :]
        sums = lax.psum(
            (
                jnp.sum(gained_down, axis=1),
                jnp.sum(gained_down * hat_down, axis=1),
                jnp.sum(gained_up, axis=1),
                jnp.sum(gained_up * hat_up, axis=1),
            ),
            "seq",
        )
        back_down = (
            wide_grad_down
            + scale_down
            * (
                gained_down
                - (sums[0] / model_width)[:, None]
                - hat_down * (sums[1] / model_width)[:, None]
            )
        ).astype(jnp.bfloat16)
        back_up = (
            wide_grad_up
            + scale_up
            * (
                gained_up
                - (sums[2] / model_width)[:, None]
                - hat_up * (sums[3] / model_width)[:, None]
            )
        ).astype(jnp.bfloat16)
        record_down = (hidden_grad_down, jnp.sum(normed_grad_down * hat_down, axis=0))
        record_up = (hidden_grad_up, jnp.sum(normed_grad_up * hat_up, axis=0))
        if section_step == 0:
            kept_down = record_down
            kept_up = record_up
        else:
            kept_down = keep_live(position == sections - 1 - section_step, record_down, kept_down)
            kept_up = keep_live(position == section_step, record_up, kept_up)
        if section_step + 1 < sections:
            grad_down = passed_along(back_down, "section", -1)
            grad_up = passed_along(back_up, "section", 1)
    final_grad_down, gain_grad_down = kept_down
    final_grad_up, gain_grad_up = kept_up
    own_first = jnp.dot(
        final_grad_down.T, normed_down[:, :half_cols], preferred_element_type=jnp.float32
    )
    own_second = jnp.dot(
        final_grad_up.T, normed_up[:, half_cols:], preferred_element_type=jnp.float32
    )
    outgoing = (
        jnp.stack([normed_up[:, :half_cols], normed_down[:, half_cols:]]),
        jnp.stack([final_grad_up, final_grad_down]),
        gain_grad_up.astype(jnp.bfloat16),
    )
    bit_count = sections.bit_length() - 1
    bit_order = list(range(bit_count))
    for bit_number in bit_order:
        outgoing = from_partner((outgoing[0], outgoing[1], outgoing[2]), "section", bit_number)
    mirror_rows, mirror_grads, mirror_gain = outgoing
    mirror_first = jnp.dot(mirror_grads[0].T, mirror_rows[0], preferred_element_type=jnp.float32)
    mirror_second = jnp.dot(mirror_grads[1].T, mirror_rows[1], preferred_element_type=jnp.float32)
    grad_first = rounded(own_first) + rounded(mirror_first)
    grad_second = rounded(own_second) + rounded(mirror_second)
    gain_grads = rounded(gain_grad_down) + mirror_gain.astype(jnp.float32)
    return (
        output_down[None],
        output_up[None],
        grad_first[None],
        grad_second[None],
        gain_grads[None],
    )


def solution(mesh):
    in_specs = (
        P(None, "seq"),
        P(None, "seq"),
        P(None, "seq"),
        P(None, "seq"),
        P("section", None, "seq", None),
        P("section", None, "seq"),
    )
    out_specs = (
        P("section", None, "seq"),
        P("section", None, "seq"),
        P("section", "seq", None),
        P("section", "seq", None),
        P("section", "seq"),
    )
    return jax.shard_map(
        per_device, mesh=mesh, in_specs=in_specs, out_specs=out_specs, check_vma=False
    )
```

profile of v0, /device:TPU:0, one launch (start us, length us, event | category | flops | bytes accessed | tf_op | source)
XLA Modules:
  0.0 597.1 jit_solution(5143511365724000826)
XLA Ops:
  9.9 43.5 %all-reduce.2 = (f32[64]{0:T(128)S(1)}, f32[64]{0:T(128)S(1)}, f32[64]{0:T(128)S(1)}, f32[64]{0:T(128)S(1)}) all-reduce(f32[64]{0:T(128)S(1)} %get-tuple-element.23, f32[64]{0:T(128)S(1)} %get-tuple-element.22, f32[64]{0:T(128)S(1)} %get-tuple-element.19, f32[64]{0:T(128)S(1)} %get-tuple-element.18), channel_id=1, replica_groups=mesh['section'=2,'seq'=16] {'seq'}, use_global_device_ids=true, to_apply=%region_3.0 | all-reduce | flops 256 | bytes 2048 | tf_op jit(solution)/shard_map/psum | solution.py:66
  54.3 40.5 %all_gather.12 = bf16[64,6144]{1,0:T(8,128)(2,1)S(1)} all-gather(bf16[64,384]{1,0:T(8,128)(2,1)S(1)} %fusion.68), channel_id=1, replica_groups=mesh['section'=2,'seq'=16] {'seq'}, dimensions={1}, use_global_device_ids=true | all-gather | bytes 835584 | tf_op jit(solution)/shard_map/all_gather | solution.py:82
  94.8 4.1 fusion.70
  98.9 1.3 collective-permute-start
  100.3 43.2 %all_gather.14 = bf16[64,6144]{1,0:T(8,128)(2,1)S(1)} all-gather(bf16[64,384]{1,0:T(8,128)(2,1)S(1)} %fusion.78), channel_id=1, replica_groups=mesh['section'=2,'seq'=16] {'seq'}, dimensions={1}, use_global_device_ids=true | all-gather | bytes 835584 | tf_op jit(solution)/shard_map/all_gather | solution.py:83
  143.6 1.8 fusion.80
  145.4 1.3 collective-permute-start.1
  146.8 1.7 collective-permute-done.1
  148.6 36.6 %all-reduce.1 = (f32[64]{0:T(128)S(1)}, f32[64]{0:T(128)S(1)}, f32[64]{0:T(128)S(1)}, f32[64]{0:T(128)S(1)}) all-reduce(f32[64]{0:T(128)S(1)} %get-tuple-element.21, f32[64]{0:T(128)S(1)} %get-tuple-element.20, f32[64]{0:T(128)S(1)} %get-tuple-element.17, f32[64]{0:T(128)S(1)} %get-tuple-element.16), channel_id=1, replica_groups=mesh['section'=2,'seq'=16] {'seq'}, use_global_device_ids=true, to_apply=%region_7.0 | all-reduce | flops 256 | bytes 2048 | tf_op jit(solution)/shard_map/psum | solution.py:66
  185.9 42.6 %all_gather.13 = bf16[64,6144]{1,0:T(8,128)(2,1)S(1)} all-gather(bf16[64,384]{1,0:T(8,128)(2,1)S(1)} %fusion.73), channel_id=1, replica_groups=mesh['section'=2,'seq'=16] {'seq'}, dimensions={1}, use_global_device_ids=true | all-gather | bytes 835584 | tf_op jit(solution)/shard_map/all_gather | solution.py:82
  228.6 41.3 %all_gather.15 = bf16[64,6144]{1,0:T(8,128)(2,1)S(1)} all-gather(bf16[64,384]{1,0:T(8,128)(2,1)S(1)} %fusion.83), channel_id=1, replica_groups=mesh['section'=2,'seq'=16] {'seq'}, dimensions={1}, use_global_device_ids=true | all-gather | bytes 835584 | tf_op jit(solution)/shard_map/all_gather | solution.py:83
  269.9 5.1 fusion.62
  275.1 3.3 fusion.1
  278.4 4.9 fusion.53
  284.4 1.6 copy.11
  288.4 118.8 %reduce-scatter.7.cloned.1.call-done = bf16[384,128]{1,0:T(8,128)(2,1)} async-done(((bf16[6144,128]{1,0:T(8,128)(2,1)}), bf16[384,128]{1,0:T(8,128)(2,1)}) %reduce-scatter.7.cloned.1.call-update) | async-done | bytes 98320
  408.3 1.4 multiply_reduce_fusion.1
  409.7 39.7 %all-reduce = (f32[64]{0:T(128)S(1)}, f32[64]{0:T(128)S(1)}, f32[64]{0:T(128)S(1)}, f32[64]{0:T(128)S(1)}) all-reduce(f32[64]{0:T(128)S(1)} %get-tuple-element.6, f32[64]{0:T(128)S(1)} %get-tuple-element.10, f32[64]{0:T(128)S(1)} %get-tuple-element.12, f32[64]{0:T(128)S(1)} %get-tuple-element.11), channel_id=1, replica_groups=mesh['section'=2,'seq'=16] {'seq'}, use_global_device_ids=true, to_apply=%region_20.21 | all-reduce | flops 256 | bytes 2048 | tf_op jit(solution)/shard_map/psum | solution.py:127
  450.4 1.3 collective-permute-start.2
  451.7 1.8 select_bitcast_fusion.1
  453.5 3.2 collective-permute-start.3
  457.7 3.3 fusion.2
  461.7 3.3 fusion.3
  465.1 1.6 copy.13
  466.7 1.8 select_bitcast_fusion
  471.0 1.8 convolution_convert_fusion.4
  472.8 1.8 convolution_convert_fusion.6
  474.6 3.0 add_bitcast_fusion
  477.6 3.0 add_bitcast_fusion.1
  480.7 106.6 %reduce-scatter.9.cloned.1.call-done = bf16[384,128]{1,0:T(8,128)(2,1)} async-done(((bf16[6144,128]{1,0:T(8,128)(2,1)}), bf16[384,128]{1,0:T(8,128)(2,1)}) %reduce-scatter.9.cloned.1.call-update) | async-done | bytes 98320
  587.3 1.0 copy.14
  588.6 1.1 collective-permute-done.6
  (93 shorter events, 15.4 us)
Async XLA Ops:
  7.2 400.1 %reduce-scatter.7.cloned.1.call-start = ((), (), s32[]{:S(2)}) async-start(), calls=%async_computation.2 | async-start | bytes 1671168
  8.1 92.1 %copy-start.7 = (bf16[64,384]{1,0:T(8,128)(2,1)S(1)}, bf16[64,384]{1,0:T(8,128)(2,1)}, u32[]{:S(2)}) copy-start(bf16[64,384]{1,0:T(8,128)(2,1)} %param.7) | copy-start | bytes 147460
  54.3 89.3 %copy-start = (bf16[1,2,384,6144]{3,2,1,0:T(8,128)(2,1)S(1)}, bf16[1,2,384,6144]{3,2,1,0:T(8,128)(2,1)}, u32[]{:S(2)}) copy-start(bf16[1,2,384,6144]{3,2,1,0:T(8,128)(2,1)} %param.10) | copy-start | bytes 28311556
  98.9 49.7 %copy-start.11 = (bf16[64,384]{1,0:T(8,128)(2,1)}, bf16[64,384]{1,0:T(8,128)(2,1)S(1)}, u32[]{:S(2)}) copy-start(bf16[64,384]{1,0:T(8,128)(2,1)S(1)} %get-tuple-element.68) | copy-start | bytes 147460
  98.9 47.8 %collective-permute-start = (bf16[64,384]{1,0:T(8,128)(2,1)S(1)}, bf16[64,384]{1,0:T(8,128)(2,1)S(1)}, u32[]{:S(2)}, u32[]{:S(2)}) collective-permute-start(bf16[64,384]{1,0:T(8,128)(2,1)S(1)} %get-tuple-element.68), channel_id=1, source_target_pairs={{0,16},{1,17},{2,18},{3,19},{4,20},{5,21},{6,22},{7,23},{8,24},{9,... | collective-permute-start | bytes 147464 | tf_op jit(solution)/shard_map/ppermute | solution.py:12
  143.6 1.8 copy-start.1
  143.6 126.4 %copy-start.13 = (bf16[64,384]{1,0:T(8,128)(2,1)S(1)}, bf16[64,384]{1,0:T(8,128)(2,1)}, u32[]{:S(2)}) copy-start(bf16[64,384]{1,0:T(8,128)(2,1)} %param.9) | copy-start | bytes 147460
  145.3 129.7 %copy-start.10 = (bf16[64,384]{1,0:T(8,128)(2,1)}, bf16[64,384]{1,0:T(8,128)(2,1)S(1)}, u32[]{:S(2)}) copy-start(bf16[64,384]{1,0:T(8,128)(2,1)S(1)} %get-tuple-element.70) | copy-start | bytes 147460
  145.4 3.1 collective-permute-start.1
  228.5 49.9 %copy-start.3 = (bf16[64,6144]{1,0:T(8,128)(2,1)}, bf16[64,6144]{1,0:T(8,128)(2,1)S(1)}, u32[]{:S(2)}) copy-start(bf16[64,6144]{1,0:T(8,128)(2,1)S(1)} %all_gather.13) | copy-start | bytes 2359300
  269.9 8.4 %copy-start.4 = (bf16[64,6144]{1,0:T(8,128)(2,1)}, bf16[64,6144]{1,0:T(8,128)(2,1)S(1)}, u32[]{:S(2)}) copy-start(bf16[64,6144]{1,0:T(8,128)(2,1)S(1)} %all_gather.15) | copy-start | bytes 2359300
  269.9 13.4 %slice-start = ((s8[9437184]{0:T(1024)(128)(4,1)}), s8[4194304]{0:T(1024)(128)(4,1)S(1)}, s32[]{:S(2)}) async-start(s8[9437184]{0:T(1024)(128)(4,1)} %bitcast.108), calls=%async_computation.4 | async-start | bytes 8388608
  269.9 13.4 %slice-start.1 = ((s8[9437184]{0:T(1024)(128)(4,1)}), s8[4194304]{0:T(1024)(128)(4,1)S(1)}, s32[]{:S(2)}) async-start(s8[9437184]{0:T(1024)(128)(4,1)} %bitcast.108), calls=%async_computation.5 | async-start | bytes 8388608
  275.1 3.3 copy-start.12
  278.4 4.9 slice-start.2
  286.0 1.1 copy-start.2
  286.0 1.4 copy-start.5
  286.0 122.3 %copy-start.6 = (bf16[64,384]{1,0:T(8,128)(2,1)S(1)}, bf16[64,384]{1,0:T(8,128)(2,1)}, u32[]{:S(2)}) copy-start(bf16[64,384]{1,0:T(8,128)(2,1)} %param.6) | copy-start | bytes 147460
  286.0 301.3 %reduce-scatter.9.cloned.1.call-start = ((), (), s32[]{:S(2)}) async-start(), calls=%async_computation.3 | async-start | bytes 1671168
  287.5 173.5 %copy-start.8 = (f32[64,384]{1,0:T(8,128)S(1)}, f32[64,384]{1,0:T(8,128)}, u32[]{:S(2)}) copy-start(f32[64,384]{1,0:T(8,128)} %get-tuple-element.52) | copy-start | bytes 294916
  287.5 173.5 %copy-start.9 = (f32[64,384]{1,0:T(8,128)S(1)}, f32[64,384]{1,0:T(8,128)}, u32[]{:S(2)}) copy-start(f32[64,384]{1,0:T(8,128)} %get-tuple-element.53) | copy-start | bytes 294916
  288.4 182.5 %collective-permute-start.5 = (bf16[2,64,3072]{2,1,0:T(8,128)(2,1)}, bf16[2,64,3072]{2,1,0:T(8,128)(2,1)}, u32[]{:S(2)}, u32[]{:S(2)}) collective-permute-start(bf16[2,64,3072]{2,1,0:T(8,128)(2,1)} %pad_maximum_fusion.2), channel_id=1, source_target_pairs={{0,16},{16,0},{1,17},{17,1},{2,18},{18,2},{3,19},{19,3},{4,20},{20... | collective-permute-start | bytes 2359304 | tf_op jit(solution)/shard_map/ppermute | solution.py:16
  450.4 6.3 %collective-permute-start.2 = (bf16[64,384]{1,0:T(8,128)(2,1)S(1)}, bf16[64,384]{1,0:T(8,128)(2,1)S(1)}, u32[]{:S(2)}, u32[]{:S(2)}) collective-permute-start(bf16[64,384]{1,0:T(8,128)(2,1)S(1)} %get-tuple-element.55), channel_id=1, source_target_pairs={{16,0},{17,1},{18,2},{19,3},{20,4},{21,5},{22,6},{23,7},{24,8},{25... | collective-permute-start | bytes 147464 | tf_op jit(solution)/shard_map/ppermute | solution.py:12
  453.5 7.5 %collective-permute-start.3 = (bf16[64,384]{1,0:T(8,128)(2,1)S(1)}, bf16[64,384]{1,0:T(8,128)(2,1)S(1)}, u32[]{:S(2)}, u32[]{:S(2)}) collective-permute-start(bf16[64,384]{1,0:T(8,128)(2,1)S(1)} %get-tuple-element.54), channel_id=1, source_target_pairs={{0,16},{1,17},{2,18},{3,19},{4,20},{5,21},{6,22},{7,23},{8,24},{9,... | collective-permute-start | bytes 147464 | tf_op jit(solution)/shard_map/ppermute | solution.py:12
  469.3 1.7 collective-permute-start.4
  477.6 110.7 %copy-start.14 = (f32[64]{0:T(128)S(1)}, f32[64]{0:T(128)}, u32[]{:S(2)}) copy-start(f32[64]{0:T(128)} %get-tuple-element.74) | copy-start | bytes 772
  477.6 110.7 %copy-start.15 = (f32[64]{0:T(128)S(1)}, f32[64]{0:T(128)}, u32[]{:S(2)}) copy-start(f32[64]{0:T(128)} %get-tuple-element.77) | copy-start | bytes 772
  477.6 110.8 %copy-start.17 = (bf16[384]{0:T(512)(128)(2,1)S(1)}, bf16[384]{0:T(512)(128)(2,1)}, u32[]{:S(2)}) copy-start(bf16[384]{0:T(512)(128)(2,1)} %get-tuple-element.13) | copy-start | bytes 2308
  477.6 110.9 %copy-start.16 = (bf16[384]{0:T(512)(128)(2,1)S(1)}, bf16[384]{0:T(512)(128)(2,1)}, u32[]{:S(2)}) copy-start(bf16[384]{0:T(512)(128)(2,1)} %get-tuple-element.5) | copy-start | bytes 2308
  588.5 1.2 collective-permute-start.6
Sparse Core Ops, SparseCore 0:
  286.1 121.0 reduce-scatter.6
  466.8 120.4 reduce-scatter.8
where the time goes:
time: 598 us; the launch traced here: 597 us
  blocking collectives  287 us (48%)
  waiting for transfers between devices  228 us (38%)
  matrix products  31.9 us (5%)
  other arithmetic  19.9 us (3%)
  between operations  14.6 us (2%)
  local copies, waits for them, and re-layouts  7.82 us (1%)
  starting transfers between devices  7.27 us (1%)
    unnamed x4, waiting for transfers between devices  225 us
    all_gather x2, blocking collectives, per_device(): lax.all_gather(local_up, 'seq', axis=1, tiled=True)  84.6 us
    all_gather x2, blocking collectives, per_device(): lax.all_gather(local_down, 'seq', axis=1, tiled=True)  83.1 us
    psum x2, blocking collectives, per_device(): lax.psum((jnp.sum(wide_down, axis=1), jnp.sum(wide_down * wide_down, axis...  80.1 us
    psum x1, blocking collectives, per_device(): lax.psum((jnp.sum(gained_down, axis=1), jnp.sum(gained_down * hat_down, a...  39.7 us
    dot_general x4, matrix products, project_rows(): lax.dot_general(normed, weight, (((1,), (1,)), ((), ())), preferred_eleme...  15.9 us
  transfers between devices with their start and end apart: 9, of which 4 were waited for; matrix products, arithmetic and copies ran while one was open for 5% of the time, Pallas kernels for 0%

commit v1 on v0

v1 whole, which is shorter than its diff:
```python
import functools
import math

import jax
import jax.numpy as jnp
from jax import lax
from jax.experimental import pallas as pl
from jax.experimental.pallas import tpu as pltpu
from jax.sharding import PartitionSpec as P

EPS = 1e-05
F32 = jnp.float32
BF16 = jnp.bfloat16
LANES = 128
PAD_ROWS = 16
SQRT_HALF = math.sqrt(0.5)
INV_SQRT_2PI = 1.0 / math.sqrt(2.0 * math.pi)
VMEM_LIMIT = 48 * 1024 * 1024

ANY = pl.BlockSpec(memory_space=pl.ANY)
VMEM = pl.BlockSpec(memory_space=pltpu.VMEM)
SMEM = pl.BlockSpec(memory_space=pltpu.SMEM)


def from_xor(value, distance):
    size = lax.axis_size("seq")
    return lax.ppermute(value, "seq", [(i, i ^ distance) for i in range(size)])


def swapped(value):
    size = lax.axis_size("section")
    return lax.ppermute(value, "section", [(i, size - 1 - i) for i in range(size)])


def bit_groups(low, count):
    bits = [1 << b for b in range(low, count)][::-1]
    groups = []
    while bits:
        pair, bits = bits[:2], bits[2:]
        groups.append(tuple(pair) if len(pair) == 1 else (pair[0], pair[1], pair[0] ^ pair[1]))
    return groups


def offsets_of(groups):
    offsets = [0]
    for group in groups:
        offsets = [o ^ d for d in (0,) + group for o in offsets]
    return offsets


def gather_xor(block, groups):
    held = block[None]
    for group in groups:
        held = jnp.concatenate([held] + [from_xor(held, d) for d in group], axis=0)
    return held


def reduce_round(held, group):
    sent = [from_xor(held[n + 1], d) for n, d in enumerate(group)]
    return [held[0]] + sent


def gelu_and_slope(z):
    cdf = 0.5 * (1.0 + lax.erf(z * SQRT_HALF))
    slope = cdf + z * (jnp.exp(-0.5 * z * z) * INV_SQRT_2PI)
    return z * cdf, slope


def column_to_row(column):
    tokens = column.shape[0]
    rows = lax.broadcasted_iota(jnp.int32, (tokens, LANES), 0)
    lanes = lax.broadcasted_iota(jnp.int32, (tokens, LANES), 1)
    return jnp.sum(jnp.where(rows == lanes, column, 0.0), axis=0, keepdims=True)


def row_to_column(row, tokens):
    rows = lax.broadcasted_iota(jnp.int32, (tokens, LANES), 0)
    lanes = lax.broadcasted_iota(jnp.int32, (tokens, LANES), 1)
    return jnp.sum(jnp.where(rows == lanes, row, 0.0), axis=1, keepdims=True)


def two_terms(value):
    high = value.astype(BF16)
    return high, (value - high.astype(F32)).astype(BF16)


def three_terms(value):
    high, rest = value.astype(BF16), None
    rest = value - high.astype(F32)
    middle = rest.astype(BF16)
    return high, middle, (rest - middle.astype(F32)).astype(BF16)


def sums_block(first_sum, second_sum):
    row = lax.broadcasted_iota(jnp.int32, (PAD_ROWS, LANES), 0)
    block = jnp.zeros((PAD_ROWS, LANES), F32)
    n = 0
    for column in (first_sum, second_sum):
        for term in two_terms(column_to_row(column)):
            block = jnp.where(row == n, term.astype(F32), block)
            n += 1
    return block.astype(BF16)


def split_packed(total, tokens, width):
    chunks = width // LANES
    du = jnp.concatenate([total[c * tokens : (c + 1) * tokens] for c in range(chunks)], axis=1)
    tail = total[chunks * tokens : chunks * tokens + PAD_ROWS]
    first = row_to_column(tail[0:1] + tail[1:2], tokens)
    second = row_to_column(tail[2:3] + tail[3:4], tokens)
    return du, first, second


def input_gradient(du, first_sum, second_sum, dy, block, mean, scale, gain, model_width):
    hat = (block.astype(F32) - mean) * scale
    gained = du * gain
    dx = dy.astype(F32) + scale * (
        gained - first_sum / model_width - hat * (second_sum / model_width)
    )
    return dx.astype(BF16), jnp.sum(du * hat, axis=0, keepdims=True)


def weight_copies(weights, index, held, sems, chunks):
    width = held.shape[1] // chunks
    return [
        pltpu.make_async_copy(
            weights.at[0, index, :, pl.ds(c * width, width)],
            held.at[:, pl.ds(c * width, width)],
            sems.at[c],
        )
        for c in range(chunks)
    ]


def section_kernel(offsets, dims, forward, unpack, backward, send_order, *refs):
    tokens, block, model_width, chunks = dims
    refs = list(refs)
    take = refs.pop
    scalars = take(0)
    weights = take(0)
    pieces = take(0) if forward else None
    own = take(0) if forward else None
    gains = None if unpack else take(0)
    dy_ref = take(0) if backward else None
    z_ref = None if forward else take(0)
    if forward:
        u_out, stat_out, z_out, y_out = take(0), take(0), take(0), take(0)
    if unpack:
        gains = take(0)
    if backward:
        dz_out, sent_out = take(0), take(0)
    held, sems = refs
    me, windex = scalars[0], scalars[1]
    copies = weight_copies(weights, windex, held, sems, chunks)
    for copy in copies:
        copy.start()
    wide = block
    per = model_width // chunks
    if forward:
        total = jnp.zeros((tokens, LANES), F32)
        squares = jnp.zeros((tokens, LANES), F32)
        for e in range(len(offsets)):
            for c in range(wide // LANES):
                part = pieces[e, 0:tokens, c * LANES : (c + 1) * LANES].astype(F32)
                total = total + part
                squares = squares + part * part
        mean = jnp.sum(total, axis=1, keepdims=True) / model_width
        var = jnp.sum(squares, axis=1, keepdims=True) / model_width - mean * mean
        scale = lax.rsqrt(var + EPS)
        lane = lax.broadcasted_iota(jnp.int32, (tokens, LANES), 1)
        stat_out[...] = jnp.where(lane == 0, mean, scale)
        for e, offset in enumerate(offsets):
            column = pl.multiple_of((me ^ offset) * wide, LANES)
            if unpack:
                terms = pieces[e, tokens : tokens + PAD_ROWS, :].astype(F32)
                gains[0:1, pl.ds(column, wide)] = terms[0:1] + terms[1:2] + terms[2:3]
                gains[1:2, pl.ds(column, wide)] = terms[3:4] + terms[4:5] + terms[5:6]
            gain = gains[pl.ds(windex, 1), pl.ds(column, wide)]
            hat = (pieces[e, 0:tokens, :].astype(F32) - mean) * scale
            u_out[:, pl.ds(column, wide)] = (hat * gain).astype(BF16)
        z = None
        for c, copy in enumerate(copies):
            copy.wait()
            part = lax.dot_general(
                u_out[:, c * per : (c + 1) * per],
                held[:, c * per : (c + 1) * per],
                (((1,), (1,)), ((), ())),
                preferred_element_type=F32,
            )
            z = part if z is None else z + part
        gelu, slope = gelu_and_slope(z)
        z_out[...] = z
        y_out[...] = (own[...].astype(F32) + gelu).astype(BF16)
    if backward:
        if not forward:
            for copy in copies:
                copy.wait()
            z = z_ref[...]
            gelu, slope = gelu_and_slope(z)
        dz = (dy_ref[...].astype(F32) * slope).astype(BF16)
        dz_out[...] = dz
        second = jnp.sum(dz.astype(F32) * z, axis=1, keepdims=True)
        first = jnp.zeros((tokens, LANES), F32)
        for n, offset in enumerate(send_order):
            column = pl.multiple_of((me ^ offset) * wide, LANES)
            part = jnp.dot(dz, held[:, pl.ds(column, wide)], preferred_element_type=F32)
            gained = part * gains[pl.ds(windex, 1), pl.ds(column, wide)]
            for c in range(wide // LANES):
                first = first + gained[:, c * LANES : (c + 1) * LANES]
                sent_out[n, c * tokens : (c + 1) * tokens, :] = part[
                    :, c * LANES : (c + 1) * LANES
                ].astype(BF16)
        tail = sums_block(jnp.sum(first, axis=1, keepdims=True), second)
        rows = tokens * (wide // LANES)
        for n in range(len(send_order)):
            sent_out[n, rows : rows + PAD_ROWS, :] = tail


def section_call(scalars, weights, pieces, own, gains, dy, z, offsets, send_order, wide, unpack):
    forward, backward = pieces is not None, dy is not None
    rows, model_width = weights.shape[2:]
    tokens = (own if forward else dy).shape[0]
    chunks = 4
    operands, specs = [scalars, weights], [SMEM, ANY]
    for value in (pieces, own, gains, dy, z):
        if value is not None:
            operands.append(value)
            specs.append(VMEM)
    outs = []
    if forward:
        outs += [
            jax.ShapeDtypeStruct((tokens, model_width), BF16),
            jax.ShapeDtypeStruct((tokens, LANES), F32),
            jax.ShapeDtypeStruct((tokens, rows), F32),
            jax.ShapeDtypeStruct((tokens, rows), BF16),
        ]
    if unpack:
        outs.append(jax.ShapeDtypeStruct((2, model_width), F32))
    if backward:
        outs += [
            jax.ShapeDtypeStruct((tokens, rows), BF16),
            jax.ShapeDtypeStruct(
                (len(send_order), tokens * (wide // LANES) + PAD_ROWS, LANES), BF16
            ),
        ]
    flops = 2 * tokens * rows * model_width * (int(forward) + int(backward))
    return pl.pallas_call(
        functools.partial(
            section_kernel,
            offsets,
            (tokens, wide, model_width, chunks),
            forward,
            unpack,
            backward,
            send_order,
        ),
        out_shape=outs,
        in_specs=specs,
        out_specs=[VMEM] * len(outs),
        scratch_shapes=[
            pltpu.VMEM((rows, model_width), BF16),
            pltpu.SemaphoreType.DMA((chunks,)),
        ],
        compiler_params=pltpu.CompilerParams(vmem_limit_bytes=VMEM_LIMIT),
        cost_estimate=pl.CostEstimate(
            flops=flops, bytes_accessed=2 * rows * model_width, transcendentals=tokens * rows
        ),
    )(*operands)


def last_kernel(offsets, places, dims, part_count, *refs):
    tokens, wide, model_width, chunks = dims
    scalars, weights, pieces, stat, z_ref, dy_ref = refs[:6]
    refs = refs[6:]
    if part_count:
        parts, (block_ref, next_stat, next_gain), refs = (
            refs[:part_count],
            refs[part_count : part_count + 3],
            refs[part_count + 3 :],
        )
        dz_out, gain_out, next_gain_out, held, sems = refs
    else:
        dz_out, gain_out, held, sems = refs
    me, windex = scalars[0], scalars[1]
    copies = weight_copies(weights, windex, held, sems, chunks)
    for copy in copies:
        copy.start()
    dy = dy_ref[...]
    if part_count:
        total = parts[0][...]
        for part in parts[1:]:
            total = total + part[...].astype(F32)
        du, first, second = split_packed(total, tokens, wide)
        dy, gain_grad = input_gradient(
            du,
            first,
            second,
            dy,
            block_ref[...],
            next_stat[:, 0:1],
            next_stat[:, 1:2],
            next_gain[...],
            model_width,
        )
        next_gain_out[...] = gain_grad
    slope = gelu_and_slope(z_ref[...])[1]
    dz = (dy.astype(F32) * slope).astype(BF16)
    dz_out[...] = dz
    mean, scale = stat[:, 0:1], stat[:, 1:2]
    for copy in copies:
        copy.wait()
    for e, offset in enumerate(offsets):
        column = pl.multiple_of((me ^ offset) * wide, LANES)
        part = jnp.dot(dz, held[:, pl.ds(column, wide)], preferred_element_type=F32)
        hat = (pieces[e, 0:tokens, :].astype(F32) - mean) * scale
        a, b = places[e]
        gain_out[a, b : b + 1, :] = jnp.sum(part * hat, axis=0, keepdims=True)


def last_call(scalars, weights, pieces, stat, z, dy, finish, offsets, send_order, wide, first_size):
    rows, model_width = weights.shape[2:]
    tokens = dy.shape[0]
    chunks = 4
    rest = len(offsets) // first_size
    places = [divmod(send_order.index(o), rest) for o in offsets]
    operands = [scalars, weights, pieces, stat, z, dy]
    outs = [
        jax.ShapeDtypeStruct((tokens, rows), BF16),
        jax.ShapeDtypeStruct((first_size, rest, wide), F32),
    ]
    part_count = 0
    if finish is not None:
        parts, others = finish
        part_count = len(parts)
        operands += list(parts) + list(others)
        outs.append(jax.ShapeDtypeStruct((1, rows), F32))
    return pl.pallas_call(
        functools.partial(
            last_kernel, offsets, places, (tokens, wide, model_width, chunks), part_count
        ),
        out_shape=outs,
        in_specs=[SMEM, ANY] + [VMEM] * (len(operands) - 2),
        out_specs=[VMEM] * len(outs),
        scratch_shapes=[
            pltpu.VMEM((rows, model_width), BF16),
            pltpu.SemaphoreType.DMA((chunks,)),
        ],
        compiler_params=pltpu.CompilerParams(vmem_limit_bytes=VMEM_LIMIT),
        cost_estimate=pl.CostEstimate(
            flops=2 * tokens * rows * model_width,
            bytes_accessed=2 * rows * model_width,
            transcendentals=tokens * rows,
        ),
    )(*operands)


def weight_grad_kernel(dz_first, dz_second, u_first, u_second, first_out, second_out):
    contract = (((0,), (0,)), ((), ()))
    first_out[...] = lax.dot_general(
        dz_first[...], u_first[...], contract, preferred_element_type=F32
    )
    second_out[...] = lax.dot_general(
        dz_second[...], u_second[...], contract, preferred_element_type=F32
    )


def weight_grad_call(dz_first, dz_second, u_first, u_second):
    depth, rows = dz_first.shape
    columns = u_first.shape[1]
    tile = columns // 6
    whole = pl.BlockSpec((depth, rows), lambda i: (0, 0))
    narrow = pl.BlockSpec((depth, tile), lambda i: (0, i))
    out = pl.BlockSpec((rows, tile), lambda i: (0, i))
    return pl.pallas_call(
        weight_grad_kernel,
        grid=(6,),
        out_shape=[jax.ShapeDtypeStruct((rows, columns), F32)] * 2,
        in_specs=[whole, whole, narrow, narrow],
        out_specs=[out, out],
        compiler_params=pltpu.CompilerParams(vmem_limit_bytes=VMEM_LIMIT),
        cost_estimate=pl.CostEstimate(
            flops=4 * depth * rows * columns, bytes_accessed=8 * rows * columns, transcendentals=0
        ),
    )(dz_first, dz_second, u_first, u_second)


def keep_live(live, record, previous):
    if previous is None or live is None:
        return record
    return jax.tree.map(lambda fresh, older: jnp.where(live, fresh, older), record, previous)


def per_device(down_input, up_input, down_cot, up_cot, section_weights, section_gains):
    sections = lax.axis_size("section")
    middle = sections // 2
    position = lax.axis_index("section")
    seq_size = lax.axis_size("seq")
    seq_index = lax.axis_index("seq")
    lower = position < middle
    tokens, block = down_input.shape
    model_width = section_weights.shape[3]
    half = model_width // 2
    merged = 0
    while (block << merged) % LANES:
        merged += 1
    wide = block << merged
    bit_count = seq_size.bit_length() - 1
    groups = bit_groups(merged, bit_count)
    back_groups = groups[::-1]
    offsets = [o >> merged for o in offsets_of(groups)]
    send_order = [0]
    for group in groups:
        send_order = [o ^ (d >> merged) for d in (0,) + group for o in send_order]
    me = (seq_index >> merged).astype(jnp.int32)
    first_index = jnp.where(lower, 0, 1).astype(jnp.int32)
    turn = jnp.minimum(position, sections - 1 - position)

    def index_at(step):
        return first_index if step < middle else 1 - first_index

    def scalars_at(step):
        return jnp.stack([me, index_at(step)]).astype(jnp.int32)

    def live_at(step):
        if sections == 2:
            return None
        return turn == min(step, sections - 1 - step)

    def joined_halves(value, axis):
        for bit in range(merged):
            other = from_xor(value, 1 << bit)
            upper = (seq_index >> bit) & 1
            value = jnp.where(
                upper == 1,
                jnp.concatenate([other, value], axis=axis),
                jnp.concatenate([value, other], axis=axis),
            )
        return value

    def own_part(value, width, bit):
        start = ((seq_index >> bit) & 1) * width
        return (
            lax.dynamic_slice_in_dim(value, start, width, axis=1),
            lax.dynamic_slice_in_dim(value, width - start, width, axis=1),
        )

    def gathered(value):
        return gather_xor(joined_halves(value, 1), groups)

    def moved(value, step, later):
        low = min(step, sections - 1 - step)
        new = min(later, sections - 1 - later)
        if low == new:
            return value
        route = [(low, new), (sections - 1 - low, sections - 1 - new)]
        return lax.ppermute(value, "section", route)

    def reduced(sent):
        parts = None
        for n, group in enumerate(back_groups):
            sent = sent.reshape((len(group) + 1, -1) + sent.shape[1:])
            parts = reduce_round(sent, group)
            if n + 1 < len(back_groups):
                total = functools.reduce(jnp.add, [p.astype(F32) for p in parts])
                sent = total.astype(BF16)
                kept = total[0]
        parts = [kept if len(back_groups) > 1 else parts[0][0].astype(F32)] + [
            p[0] for p in parts[1:]
        ]
        return parts

    def finished(parts):
        total = functools.reduce(jnp.add, [p.astype(F32) for p in parts])
        du, first, second = split_packed(total, tokens, wide)
        for bit in reversed(range(merged)):
            width = du.shape[1] // 2
            mine, theirs = own_part(du, width, bit)
            tail = jnp.concatenate(two_terms(first) + two_terms(second), axis=1)
            message = jnp.concatenate([theirs.astype(BF16), tail], axis=1)
            message = from_xor(message, 1 << bit).astype(F32)
            du = mine + message[:, :width]
            first = first + message[:, width : width + 1] + message[:, width + 1 : width + 2]
            second = second + message[:, width + 2 : width + 3] + message[:, width + 3 :]
        return du, first, second

    own_gains = section_gains[0]
    state = jnp.where(lower, down_input, up_input)
    grad = jnp.where(lower, down_cot, up_cot)
    gain_rows = jnp.stack(three_terms(own_gains[0]) + three_terms(own_gains[1]))
    gain_rows = jnp.pad(gain_rows, ((0, PAD_ROWS - gain_rows.shape[0]), (0, 0)))
    first_record = second_record = None
    gains = None
    for step in range(sections):
        last = step == sections - 1
        payload = jnp.concatenate([state, gain_rows], axis=0) if step == 0 else state
        pieces = gathered(payload)
        result = section_call(
            scalars_at(step),
            section_weights,
            pieces,
            state,
            gains,
            grad if last else None,
            None,
            offsets,
            send_order,
            wide,
            step == 0,
        )
        u, stat, z, y = result[:4]
        if step == 0:
            gains = result[4]
        record = (state, pieces[:, :tokens] if sections > 2 else pieces, u, stat, z, y)
        if step < middle:
            first_record = keep_live(live_at(step), record, first_record)
        else:
            second_record = keep_live(live_at(step), record, second_record)
        if last:
            dz, sent = result[-2:]
        else:
            state = moved(y, step, step + 1)
    u_a, y_a = first_record[2], first_record[5]
    u_b, y_b = second_record[2], second_record[5]
    y_other = swapped(y_b)
    down_out = jnp.where(lower, y_a, y_other)
    up_out = jnp.where(lower, y_other, y_a)
    u_first = jnp.where(lower, u_a[:, :half], u_b[:, :half])
    u_second = jnp.where(lower, u_b[:, half:], u_a[:, half:])
    other_first = swapped(jnp.where(lower, u_b[:, :half], u_a[:, :half]))
    other_second = swapped(jnp.where(lower, u_a[:, half:], u_b[:, half:]))
    u_first = jnp.concatenate([u_first, other_first], axis=0)
    u_second = jnp.concatenate([u_second, other_second], axis=0)

    dz_a = dz_b = gain_b = gain_a = None
    for step in reversed(range(1, sections)):
        source, _, _, stat, z, _ = second_record if step >= middle else first_record
        if step < sections - 1:
            dz, sent = section_call(
                scalars_at(step),
                section_weights,
                None,
                None,
                gains,
                grad,
                z,
                offsets,
                send_order,
                wide,
                False,
            )
        parts = reduced(sent)
        gain_row = lax.dynamic_slice_in_dim(own_gains, index_at(step), 1, axis=0)
        if step >= middle:
            dz_b = keep_live(live_at(step), dz, dz_b)
        else:
            dz_a = keep_live(live_at(step), dz, dz_a)
        finish = None
        if sections == 2 and not merged:
            finish = (parts, (source, stat, gain_row))
        else:
            du, first, second = finished(parts)
            new_grad, gain_grad = input_gradient(
                du,
                first,
                second,
                grad,
                source,
                stat[:, 0:1],
                stat[:, 1:2],
                gain_row,
                model_width,
            )
            if step >= middle:
                gain_b = keep_live(live_at(step), gain_grad, gain_b)
            else:
                gain_a = keep_live(live_at(step), gain_grad, gain_a)
            grad = moved(new_grad, step, step - 1)
    _, pieces, _, stat, z, _ = first_record
    first_size = len(back_groups[0]) + 1
    result = last_call(
        scalars_at(0),
        section_weights,
        pieces,
        stat,
        z,
        grad,
        finish,
        offsets,
        send_order,
        wide,
        first_size,
    )
    dz, gain_parts = result[:2]
    if finish is not None:
        gain_b = result[2]
    dz_a = keep_live(live_at(0), dz, dz_a)
    for n, group in enumerate(back_groups):
        if n:
            gain_parts = gain_parts.reshape((len(group) + 1, -1) + gain_parts.shape[1:])
        gain_parts = functools.reduce(jnp.add, reduce_round(gain_parts, group))
    gain = gain_parts.reshape(1, wide)
    for bit in reversed(range(merged)):
        mine, theirs = own_part(gain, gain.shape[1] // 2, bit)
        gain = mine + from_xor(theirs, 1 << bit)
    gain_a = keep_live(live_at(0), gain, gain_a)

    dz_a_other = swapped(dz_a)
    dz_b_other = swapped(dz_b)
    dz_first = jnp.where(
        lower,
        jnp.concatenate([dz_a, dz_a_other], axis=0),
        jnp.concatenate([dz_b, dz_b_other], axis=0),
    )
    dz_second = jnp.where(
        lower,
        jnp.concatenate([dz_b, dz_b_other], axis=0),
        jnp.concatenate([dz_a, dz_a_other], axis=0),
    )
    grad_first, grad_second = weight_grad_call(dz_first, dz_second, u_first, u_second)
    gain_other = swapped(jnp.where(lower, gain_b, gain_a))
    gain_total = jnp.where(lower, gain_a, gain_b) + gain_other
    return (
        down_out[None],
        up_out[None],
        grad_first[None],
        grad_second[None],
        gain_total,
    )


def solution(mesh):
    in_specs = (
        P(None, "seq"),
        P(None, "seq"),
        P(None, "seq"),
        P(None, "seq"),
        P("section", None, "seq", None),
        P("section", None, "seq"),
    )
    out_specs = (
        P("section", None, "seq"),
        P("section", None, "seq"),
        P("section", "seq", None),
        P("section", "seq", None),
        P("section", "seq"),
    )
    return jax.shard_map(
        per_device, mesh=mesh, in_specs=in_specs, out_specs=out_specs, check_vma=False
    )
```

time: 598 us -> 102 us (0.17)
  blocking collectives: 287 us -> 0 us
  waiting for transfers between devices: 228 us -> 42.3 us
  matrix products: 31.9 us -> 0 us
  starting transfers between devices: 7.27 us -> 33.7 us
  Pallas kernels: 0 us -> 19.1 us
  other arithmetic: 19.9 us -> 4.21 us
  between operations: 14.6 us -> 0.89 us
    unnamed x4 -> x0, waiting for transfers between devices: 225 us -> none
    all_gather x4 -> x0, blocking collectives: 168 us -> none  [the longest x2 84.6 us: per_device(): lax.all_gather(local_up, 'seq', axis=1, tiled=True)]
    psum x3 -> x0, blocking collectives: 120 us -> none  [the longest x2 80.1 us: per_device(): lax.psum((jnp.sum(wide_down, axis=1), jnp.sum(wide_down * wide_down, axis...]
    ppermute x7 -> x30, waiting for transfers between devices: 2.81 us -> 42.3 us  [the longest x24 41.1 us: from_xor(): return lax.ppermute(value, 'seq', [(i, i ^ distance) for i in range(size)])]
    dot_general x12 -> x0, matrix products: 31.9 us -> none  [the longest x4 15.9 us: project_rows(): lax.dot_general(normed, weight, (((1,), (1,)), ((), ())), preferred_eleme...]
    ppermute x7 -> x30, starting transfers between devices: 7.19 us -> 33.7 us  [the longest x24 33 us: from_xor(): return lax.ppermute(value, 'seq', [(i, i ^ distance) for i in range(size)])]
    pallas_call x0 -> x4, Pallas kernels: none -> 19.1 us  [the longest x2 10.4 us: section_call(): pl.pallas_call(functools.partial(section_kernel, offsets, (tokens, wide,...]
    broadcast_in_dim x4 -> x2, other arithmetic: 9.61 us -> 0.66 us  [the longest x1 0.65 us: per_device(): up_out[None]]
  transfers between devices with their start and end apart: 9 -> 30, of which waited for: 4 -> 19; matrix products, arithmetic and copies ran while one was open for 5% -> 3% of each run, Pallas kernels for 0% -> 4%
where the time goes in v1:
time: 102 us
  waiting for transfers between devices  42.3 us (41%)
  starting transfers between devices  33.7 us (33%)
  Pallas kernels  19.1 us (19%)
  other arithmetic  4.21 us (4%)
  local copies, waits for them, and re-layouts  1.92 us (2%)
    ppermute x24, waiting for transfers between devices, from_xor(): return lax.ppermute(value, 'seq', [(i, i ^ distance) for i in range(size)])  41.1 us
    ppermute x24, starting transfers between devices, from_xor(): return lax.ppermute(value, 'seq', [(i, i ^ distance) for i in range(size)])  33 us
    pallas_call x2, Pallas kernels, section_call(): pl.pallas_call(functools.partial(section_kernel, offsets, (tokens, wide,...  10.4 us
    pallas_call x1, Pallas kernels, weight_grad_call(): pl.pallas_call(weight_grad_kernel, grid=(6,), out_shape=[jax.ShapeDtypeSt...  4.83 us
    pallas_call x1, Pallas kernels, last_call(): pl.pallas_call(functools.partial(last_kernel, offsets, places, (tokens, w...  3.92 us
  transfers between devices with their start and end apart: 30, of which 19 were waited for; matrix products, arithmetic and copies ran while one was open for 3% of the time, Pallas kernels for 4%

profile of v1, /device:TPU:0, one launch (start us, length us, event | category | flops | bytes accessed | tf_op | source)
XLA Modules:
  0.0 102.1 jit_solution(7829538376194785469)
XLA Ops:
  2.2 0.8 broadcast_select_fusion.7.refs_3_
  3.0 5.1 %collective-permute-start.2 = (bf16[1,80,384]{2,1,0:T(8,128)(2,1)S(1)}, bf16[1,80,384]{2,1,0:T(8,128)(2,1)S(1)}, u32[]{:S(2)}, u32[]{:S(2)}) collective-permute-start(bf16[1,80,384]{2,1,0:T(8,128)(2,1)S(1)} %fusion.2), channel_id=1, source_target_pairs={{0,12},{1,13},{2,14},{3,15},{4,8},{5,9},{6,10},{7,11},{8,4},{9,5},... | collective-permute-start | bytes 184328 | tf_op jit(solution)/shard_map/ppermute | solution.py:27
  9.6 0.8 broadcast_select_fusion.6.refs_5_
  10.9 1.7 %collective-permute-done.1 = bf16[1,80,384]{2,1,0:T(8,128)(2,1)S(1)} collective-permute-done((bf16[1,80,384]{2,1,0:T(8,128)(2,1)S(1)}, bf16[1,80,384]{2,1,0:T(8,128)(2,1)S(1)}, u32[]{:S(2)}, u32[]{:S(2)}) %collective-permute-start.1) | collective-permute-done | bytes 61472 | tf_op jit(solution)/shard_map/ppermute | solution.py:27
  12.6 1.1 %collective-permute-done = bf16[1,80,384]{2,1,0:T(8,128)(2,1)S(1)} collective-permute-done((bf16[1,80,384]{2,1,0:T(8,128)(2,1)S(1)}, bf16[1,80,384]{2,1,0:T(8,128)(2,1)S(1)}, u32[]{:S(2)}, u32[]{:S(2)}) %collective-permute-start) | collective-permute-done | bytes 61472 | tf_op jit(solution)/shard_map/ppermute | solution.py:27
  13.7 2.5 %collective-permute-start.5 = (bf16[4,80,384]{2,1,0:T(8,128)(2,1)S(1)}, bf16[4,80,384]{2,1,0:T(8,128)(2,1)S(1)}, u32[]{:S(2)}, u32[]{:S(2)}) collective-permute-start(bf16[4,80,384]{2,1,0:T(8,128)(2,1)S(1)} %pad_maximum_fusion.2), channel_id=1, source_target_pairs={{0,3},{1,2},{2,1},{3,0},{4,7},{5,6},{6,5},{7,4},{8,11},{9,10},{10,... | collective-permute-start | bytes 737288 | tf_op jit(solution)/shard_map/ppermute | solution.py:27
  17.3 8.9 %collective-permute-done.3 = bf16[4,80,384]{2,1,0:T(8,128)(2,1)S(1)} collective-permute-done((bf16[4,80,384]{2,1,0:T(8,128)(2,1)S(1)}, bf16[4,80,384]{2,1,0:T(8,128)(2,1)S(1)}, u32[]{:S(2)}, u32[]{:S(2)}) %collective-permute-start.3) | collective-permute-done | bytes 245792 | tf_op jit(solution)/shard_map/ppermute | solution.py:27
  26.6 4.4 %shard_map.101 = (bf16[64,6144]{1,0:T(8,128)(2,1)S(1)}, f32[64,128]{1,0:T(8,128)S(1)}, f32[64,384]{1,0:T(8,128)S(1)}, bf16[64,384]{1,0:T(8,128)(2,1)S(1)}, f32[2,6144]{1,0:T(2,128)S(1)}) custom-call(s32[2]{0:T(128)S(1)} %pad_add_fusion.refs_0_, bf16[1,2,384,6144]{3,2,1,0:T(8,128)(2,1)} %refs_1_.5, ...), custom_call_target="tpu_custom_call" | custom-call | flops 301989888 | bytes 4718592 | tf_op jit(solution)/shard_map/pallas_call | solution.py:247
  31.0 1.8 %collective-permute-start.8 = (bf16[1,64,384]{2,1,0:T(8,128)(2,1)S(1)}, bf16[1,64,384]{2,1,0:T(8,128)(2,1)S(1)}, u32[]{:S(2)}, u32[]{:S(2)}) collective-permute-start(bf16[1,64,384]{2,1,0:T(8,128)(2,1)S(1)} %bitcast.56), channel_id=1, source_target_pairs={{0,12},{1,13},{2,14},{3,15},{4,8},{5,9},{6,10},{7,11},{8,4},{9,5},... | collective-permute-start | bytes 147464 | tf_op jit(solution)/shard_map/ppermute | solution.py:27
  33.4 2.0 %collective-permute-start.6 = (bf16[1,64,384]{2,1,0:T(8,128)(2,1)S(1)}, bf16[1,64,384]{2,1,0:T(8,128)(2,1)S(1)}, u32[]{:S(2)}, u32[]{:S(2)}) collective-permute-start(bf16[1,64,384]{2,1,0:T(8,128)(2,1)S(1)} %bitcast.58), channel_id=1, source_target_pairs={{0,8},{1,9},{2,10},{3,11},{4,12},{5,13},{6,14},{7,15},{8,0},{9,1},... | collective-permute-start | bytes 147464 | tf_op jit(solution)/shard_map/ppermute | solution.py:27
  35.5 1.8 %collective-permute-done.8 = bf16[1,64,384]{2,1,0:T(8,128)(2,1)S(1)} collective-permute-done((bf16[1,64,384]{2,1,0:T(8,128)(2,1)S(1)}, bf16[1,64,384]{2,1,0:T(8,128)(2,1)S(1)}, u32[]{:S(2)}, u32[]{:S(2)}) %collective-permute-start.8) | collective-permute-done | bytes 49184 | tf_op jit(solution)/shard_map/ppermute | solution.py:27
  37.6 0.9 collective-permute-done.6
  38.5 2.5 %collective-permute-start.11 = (bf16[4,64,384]{2,1,0:T(8,128)(2,1)S(1)}, bf16[4,64,384]{2,1,0:T(8,128)(2,1)S(1)}, u32[]{:S(2)}, u32[]{:S(2)}) collective-permute-start(bf16[4,64,384]{2,1,0:T(8,128)(2,1)S(1)} %pad_maximum_fusion.3), channel_id=1, source_target_pairs={{0,3},{1,2},{2,1},{3,0},{4,7},{5,6},{6,5},{7,4},{8,11},{9,10},{10,... | collective-permute-start | bytes 589832 | tf_op jit(solution)/shard_map/ppermute | solution.py:27
  42.1 7.4 %collective-permute-done.9 = bf16[4,64,384]{2,1,0:T(8,128)(2,1)S(1)} collective-permute-done((bf16[4,64,384]{2,1,0:T(8,128)(2,1)S(1)}, bf16[4,64,384]{2,1,0:T(8,128)(2,1)S(1)}, u32[]{:S(2)}, u32[]{:S(2)}) %collective-permute-start.9) | collective-permute-done | bytes 196640 | tf_op jit(solution)/shard_map/ppermute | solution.py:27
  49.9 6.0 %shard_map.102 = (bf16[64,6144]{1,0:T(8,128)(2,1)S(1)}, f32[64,128]{1,0:T(8,128)S(1)}, f32[64,384]{1,0:T(8,128)}, bf16[64,384]{1,0:T(8,128)(2,1)S(1)}, bf16[64,3...) custom-call(s32[2]{0:T(128)S(1)} %pad_add_fusion.1.refs_0_, bf16[1,2,384,6144]{3,2,1,0:T(8,128)(2,1)} %refs_1_.5, ...), custom_call_target="tpu_custom_call" | custom-call | flops 603979776 | bytes 4718592 | tf_op jit(solution)/shard_map/pallas_call | solution.py:247
  56.5 1.5 %collective-permute-start.13 = (bf16[4,208,128]{2,1,0:T(8,128)(2,1)S(1)}, bf16[4,208,128]{2,1,0:T(8,128)(2,1)S(1)}, u32[]{:S(2)}, u32[]{:S(2)}) collective-permute-start(bf16[4,208,128]{2,1,0:T(8,128)(2,1)S(1)} %get-tuple-element.43), channel_id=1, source_target_pairs={{0,2},{1,3},{2,0},{3,1},{4,6},{5,7},{6,4},{7,5},{8,10},{9,11},{10,... | collective-permute-start | bytes 638984 | tf_op jit(solution)/shard_map/ppermute | solution.py:27
  58.0 1.5 %collective-permute-start.15 = (bf16[4,208,128]{2,1,0:T(8,128)(2,1)S(1)}, bf16[4,208,128]{2,1,0:T(8,128)(2,1)S(1)}, u32[]{:S(2)}, u32[]{:S(2)}) collective-permute-start(bf16[4,208,128]{2,1,0:T(8,128)(2,1)S(1)} %get-tuple-element.44), channel_id=1, source_target_pairs={{0,3},{1,2},{2,1},{3,0},{4,7},{5,6},{6,5},{7,4},{8,11},{9,10},{10,... | collective-permute-start | bytes 638984 | tf_op jit(solution)/shard_map/ppermute | solution.py:27
  60.2 8.2 %collective-permute-done.13 = bf16[4,208,128]{2,1,0:T(8,128)(2,1)S(1)} collective-permute-done((bf16[4,208,128]{2,1,0:T(8,128)(2,1)S(1)}, bf16[4,208,128]{2,1,0:T(8,128)(2,1)S(1)}, u32[]{:S(2)}, u32[]{:S(2)}) %collective-permute-start.13) | collective-permute-done | bytes 213024 | tf_op jit(solution)/shard_map/ppermute | solution.py:27
  68.4 1.2 %collective-permute-done.14 = bf16[4,208,128]{2,1,0:T(8,128)(2,1)S(1)} collective-permute-done((bf16[4,208,128]{2,1,0:T(8,128)(2,1)S(1)}, bf16[4,208,128]{2,1,0:T(8,128)(2,1)S(1)}, u32[]{:S(2)}, u32[]{:S(2)}) %collective-permute-start.14) | collective-permute-done | bytes 213024 | tf_op jit(solution)/shard_map/ppermute | solution.py:27
  69.7 1.2 %collective-permute-start.18 = (bf16[1,208,128]{2,1,0:T(8,128)(2,1)S(1)}, bf16[1,208,128]{2,1,0:T(8,128)(2,1)S(1)}, u32[]{:S(2)}, u32[]{:S(2)}) collective-permute-start(bf16[1,208,128]{2,1,0:T(8,128)(2,1)S(1)} %get-tuple-element.46), channel_id=1, source_target_pairs={{0,12},{1,13},{2,14},{3,15},{4,8},{5,9},{6,10},{7,11},{8,4},{9,5},... | collective-permute-start | bytes 159752 | tf_op jit(solution)/shard_map/ppermute | solution.py:27
  71.4 2.8 %collective-permute-start.16 = (bf16[1,208,128]{2,1,0:T(8,128)(2,1)S(1)}, bf16[1,208,128]{2,1,0:T(8,128)(2,1)S(1)}, u32[]{:S(2)}, u32[]{:S(2)}) collective-permute-start(bf16[1,208,128]{2,1,0:T(8,128)(2,1)S(1)} %get-tuple-element.48), channel_id=1, source_target_pairs={{0,8},{1,9},{2,10},{3,11},{4,12},{5,13},{6,14},{7,15},{8,0},{9,1},... | collective-permute-start | bytes 159752 | tf_op jit(solution)/shard_map/ppermute | solution.py:27
  74.2 1.6 %collective-permute-done.18 = bf16[1,208,128]{2,1,0:T(8,128)(2,1)S(1)} collective-permute-done((bf16[1,208,128]{2,1,0:T(8,128)(2,1)S(1)}, bf16[1,208,128]{2,1,0:T(8,128)(2,1)S(1)}, u32[]{:S(2)}, u32[]{:S(2)}) %collective-permute-start.18) | collective-permute-done | bytes 53280 | tf_op jit(solution)/shard_map/ppermute | solution.py:27
  75.8 0.8 collective-permute-done.16
  76.6 3.9 %shard_map.103 = (bf16[64,384]{1,0:T(8,128)(2,1)S(1)}, f32[4,4,384]{2,1,0:T(4,128)S(1)}, f32[1,384]{1,0:T(1,128)S(1)}) custom-call(s32[2]{0:T(128)S(1)} %pad_add_fusion.refs_0_, bf16[1,2,384,6144]{3,2,1,0:T(8,128)(2,1)} %refs_1_.5, bf16[16,80,384]{2,1,0:T(8,128)(2,1)S(1)} %constant_dynamic-update-slice_fusion.refs_2_, ...), custom_call_target="tpu_custom_call" | custom-call | flops 301989888 | bytes 4718592 | tf_op jit(solution)/shard_map/pallas_call | solution.py:337
  80.5 1.5 %collective-permute-start.23 = (f32[4,384]{1,0:T(4,128)S(1)}, f32[4,384]{1,0:T(4,128)S(1)}, u32[]{:S(2)}, u32[]{:S(2)}) collective-permute-start(f32[4,384]{1,0:T(4,128)S(1)} %get-tuple-element.53), channel_id=1, source_target_pairs={{0,2},{1,3},{2,0},{3,1},{4,6},{5,7},{6,4},{7,5},{8,10},{9,11},{10,... | collective-permute-start | bytes 18440 | tf_op jit(solution)/shard_map/ppermute | solution.py:27
  82.1 1.5 %collective-permute-start.25 = (f32[4,384]{1,0:T(4,128)S(1)}, f32[4,384]{1,0:T(4,128)S(1)}, u32[]{:S(2)}, u32[]{:S(2)}) collective-permute-start(f32[4,384]{1,0:T(4,128)S(1)} %get-tuple-element.54), channel_id=1, source_target_pairs={{0,3},{1,2},{2,1},{3,0},{4,7},{5,6},{6,5},{7,4},{8,11},{9,10},{10,... | collective-permute-start | bytes 18440 | tf_op jit(solution)/shard_map/ppermute | solution.py:27
  84.7 1.8 %collective-permute-done.25 = f32[4,384]{1,0:T(4,128)S(1)} collective-permute-done((f32[4,384]{1,0:T(4,128)S(1)}, f32[4,384]{1,0:T(4,128)S(1)}, u32[]{:S(2)}, u32[]{:S(2)}) %collective-permute-start.25) | collective-permute-done | bytes 6176 | tf_op jit(solution)/shard_map/ppermute | solution.py:27
  87.3 2.6 %collective-permute-start.26 = (f32[1,384]{1,0:T(1,128)S(1)}, f32[1,384]{1,0:T(1,128)S(1)}, u32[]{:S(2)}, u32[]{:S(2)}) collective-permute-start(f32[1,384]{1,0:T(1,128)S(1)} %get-tuple-element.56), channel_id=1, source_target_pairs={{0,8},{1,9},{2,10},{3,11},{4,12},{5,13},{6,14},{7,15},{8,0},{9,1},... | collective-permute-start | bytes 4616 | tf_op jit(solution)/shard_map/ppermute | solution.py:27
  89.9 1.5 %collective-permute-start.28 = (f32[1,384]{1,0:T(1,128)S(1)}, f32[1,384]{1,0:T(1,128)S(1)}, u32[]{:S(2)}, u32[]{:S(2)}) collective-permute-start(f32[1,384]{1,0:T(1,128)S(1)} %get-tuple-element.57), channel_id=1, source_target_pairs={{0,12},{1,13},{2,14},{3,15},{4,8},{5,9},{6,10},{7,11},{8,4},{9,5},... | collective-permute-start | bytes 4616 | tf_op jit(solution)/shard_map/ppermute | solution.py:27
  91.8 3.5 %collective-permute-done.28 = f32[1,384]{1,0:T(1,128)S(1)} collective-permute-done((f32[1,384]{1,0:T(1,128)S(1)}, f32[1,384]{1,0:T(1,128)S(1)}, u32[]{:S(2)}, u32[]{:S(2)}) %collective-permute-start.28) | collective-permute-done | bytes 1568 | tf_op jit(solution)/shard_map/ppermute | solution.py:27
  95.4 1.1 %collective-permute-done.29 = f32[1,384]{1,0:T(1,128)S(1)} collective-permute-done((f32[1,384]{1,0:T(1,128)S(1)}, f32[1,384]{1,0:T(1,128)S(1)}, u32[]{:S(2)}, u32[]{:S(2)}) %collective-permute-start.29) | collective-permute-done | bytes 1568 | tf_op jit(solution)/shard_map/ppermute | solution.py:32
  97.3 4.8 %shard_map.104 = (f32[384,3072]{1,0:T(8,128)}, f32[384,3072]{1,0:T(8,128)}) custom-call(bf16[128,384]{1,0:T(8,128)(2,1)S(1)} %get-tuple-element.50.dz_first, bf16[128,384]{1,0:T(8,128)(2,1)S(1)} %get-tuple-element.49.dz_second, bf16[128,3072]{1,0:T(8,128)(2,1)S(1)} %pad_maximum_fusion.u_first, bf16[128,3072]{1,0:T(8,128)(2,1)S(1)} %pad_maximum_fusion.1.u_second), custom_call_target="tpu_custom_call" | custom-call | flops 603979776 | bytes 9437184 | tf_op jit(solution)/shard_map/pallas_call | solution.py:374
  (75 shorter events, 12.4 us)
Async XLA Ops:
  3.0 7.9 %collective-permute-start.2 = (bf16[1,80,384]{2,1,0:T(8,128)(2,1)S(1)}, bf16[1,80,384]{2,1,0:T(8,128)(2,1)S(1)}, u32[]{:S(2)}, u32[]{:S(2)}) collective-permute-start(bf16[1,80,384]{2,1,0:T(8,128)(2,1)S(1)} %fusion.2), channel_id=1, source_target_pairs={{0,12},{1,13},{2,14},{3,15},{4,8},{5,9},{6,10},{7,11},{8,4},{9,5},... | collective-permute-start | bytes 184328 | tf_op jit(solution)/shard_map/ppermute | solution.py:27
  8.1 4.5 %collective-permute-start.1 = (bf16[1,80,384]{2,1,0:T(8,128)(2,1)S(1)}, bf16[1,80,384]{2,1,0:T(8,128)(2,1)S(1)}, u32[]{:S(2)}, u32[]{:S(2)}) collective-permute-start(bf16[1,80,384]{2,1,0:T(8,128)(2,1)S(1)} %fusion.2), channel_id=1, source_target_pairs={{0,4},{1,5},{2,6},{3,7},{4,0},{5,1},{6,2},{7,3},{8,12},{9,13},{10,... | collective-permute-start | bytes 184328 | tf_op jit(solution)/shard_map/ppermute | solution.py:27
  8.1 5.5 %collective-permute-start = (bf16[1,80,384]{2,1,0:T(8,128)(2,1)S(1)}, bf16[1,80,384]{2,1,0:T(8,128)(2,1)S(1)}, u32[]{:S(2)}, u32[]{:S(2)}) collective-permute-start(bf16[1,80,384]{2,1,0:T(8,128)(2,1)S(1)} %fusion.2), channel_id=1, source_target_pairs={{0,8},{1,9},{2,10},{3,11},{4,12},{5,13},{6,14},{7,15},{8,0},{9,1},... | collective-permute-start | bytes 184328 | tf_op jit(solution)/shard_map/ppermute | solution.py:27
  13.7 12.9 %collective-permute-start.5 = (bf16[4,80,384]{2,1,0:T(8,128)(2,1)S(1)}, bf16[4,80,384]{2,1,0:T(8,128)(2,1)S(1)}, u32[]{:S(2)}, u32[]{:S(2)}) collective-permute-start(bf16[4,80,384]{2,1,0:T(8,128)(2,1)S(1)} %pad_maximum_fusion.2), channel_id=1, source_target_pairs={{0,3},{1,2},{2,1},{3,0},{4,7},{5,6},{6,5},{7,4},{8,11},{9,10},{10,... | collective-permute-start | bytes 737288 | tf_op jit(solution)/shard_map/ppermute | solution.py:27
  16.2 10.3 %collective-permute-start.4 = (bf16[4,80,384]{2,1,0:T(8,128)(2,1)S(1)}, bf16[4,80,384]{2,1,0:T(8,128)(2,1)S(1)}, u32[]{:S(2)}, u32[]{:S(2)}) collective-permute-start(bf16[4,80,384]{2,1,0:T(8,128)(2,1)S(1)} %pad_maximum_fusion.2), channel_id=1, source_target_pairs={{0,1},{1,0},{2,3},{3,2},{4,5},{5,4},{6,7},{7,6},{8,9},{9,8},{10,11... | collective-permute-start | bytes 737288 | tf_op jit(solution)/shard_map/ppermute | solution.py:27
  16.8 9.5 %collective-permute-start.3 = (bf16[4,80,384]{2,1,0:T(8,128)(2,1)S(1)}, bf16[4,80,384]{2,1,0:T(8,128)(2,1)S(1)}, u32[]{:S(2)}, u32[]{:S(2)}) collective-permute-start(bf16[4,80,384]{2,1,0:T(8,128)(2,1)S(1)} %pad_maximum_fusion.2), channel_id=1, source_target_pairs={{0,2},{1,3},{2,0},{3,1},{4,6},{5,7},{6,4},{7,5},{8,10},{9,11},{10,... | collective-permute-start | bytes 737288 | tf_op jit(solution)/shard_map/ppermute | solution.py:27
  31.0 6.2 %collective-permute-start.8 = (bf16[1,64,384]{2,1,0:T(8,128)(2,1)S(1)}, bf16[1,64,384]{2,1,0:T(8,128)(2,1)S(1)}, u32[]{:S(2)}, u32[]{:S(2)}) collective-permute-start(bf16[1,64,384]{2,1,0:T(8,128)(2,1)S(1)} %bitcast.56), channel_id=1, source_target_pairs={{0,12},{1,13},{2,14},{3,15},{4,8},{5,9},{6,10},{7,11},{8,4},{9,5},... | collective-permute-start | bytes 147464 | tf_op jit(solution)/shard_map/ppermute | solution.py:27
  32.8 4.8 %collective-permute-start.7 = (bf16[1,64,384]{2,1,0:T(8,128)(2,1)S(1)}, bf16[1,64,384]{2,1,0:T(8,128)(2,1)S(1)}, u32[]{:S(2)}, u32[]{:S(2)}) collective-permute-start(bf16[1,64,384]{2,1,0:T(8,128)(2,1)S(1)} %bitcast.57), channel_id=1, source_target_pairs={{0,4},{1,5},{2,6},{3,7},{4,0},{5,1},{6,2},{7,3},{8,12},{9,13},{10,... | collective-permute-start | bytes 147464 | tf_op jit(solution)/shard_map/ppermute | solution.py:27
  33.4 5.0 %collective-permute-start.6 = (bf16[1,64,384]{2,1,0:T(8,128)(2,1)S(1)}, bf16[1,64,384]{2,1,0:T(8,128)(2,1)S(1)}, u32[]{:S(2)}, u32[]{:S(2)}) collective-permute-start(bf16[1,64,384]{2,1,0:T(8,128)(2,1)S(1)} %bitcast.58), channel_id=1, source_target_pairs={{0,8},{1,9},{2,10},{3,11},{4,12},{5,13},{6,14},{7,15},{8,0},{9,1},... | collective-permute-start | bytes 147464 | tf_op jit(solution)/shard_map/ppermute | solution.py:27
  38.5 11.4 %collective-permute-start.11 = (bf16[4,64,384]{2,1,0:T(8,128)(2,1)S(1)}, bf16[4,64,384]{2,1,0:T(8,128)(2,1)S(1)}, u32[]{:S(2)}, u32[]{:S(2)}) collective-permute-start(bf16[4,64,384]{2,1,0:T(8,128)(2,1)S(1)} %pad_maximum_fusion.3), channel_id=1, source_target_pairs={{0,3},{1,2},{2,1},{3,0},{4,7},{5,6},{6,5},{7,4},{8,11},{9,10},{10,... | collective-permute-start | bytes 589832 | tf_op jit(solution)/shard_map/ppermute | solution.py:27
  40.9 8.8 %collective-permute-start.10 = (bf16[4,64,384]{2,1,0:T(8,128)(2,1)S(1)}, bf16[4,64,384]{2,1,0:T(8,128)(2,1)S(1)}, u32[]{:S(2)}, u32[]{:S(2)}) collective-permute-start(bf16[4,64,384]{2,1,0:T(8,128)(2,1)S(1)} %pad_maximum_fusion.3), channel_id=1, source_target_pairs={{0,1},{1,0},{2,3},{3,2},{4,5},{5,4},{6,7},{7,6},{8,9},{9,8},{10,11... | collective-permute-start | bytes 589832 | tf_op jit(solution)/shard_map/ppermute | solution.py:27
  41.5 8.0 %collective-permute-start.9 = (bf16[4,64,384]{2,1,0:T(8,128)(2,1)S(1)}, bf16[4,64,384]{2,1,0:T(8,128)(2,1)S(1)}, u32[]{:S(2)}, u32[]{:S(2)}) collective-permute-start(bf16[4,64,384]{2,1,0:T(8,128)(2,1)S(1)} %pad_maximum_fusion.3), channel_id=1, source_target_pairs={{0,2},{1,3},{2,0},{3,1},{4,6},{5,7},{6,4},{7,5},{8,10},{9,11},{10,... | collective-permute-start | bytes 589832 | tf_op jit(solution)/shard_map/ppermute | solution.py:27
  55.9 27.7 %collective-permute-start.12 = (bf16[64,384]{1,0:T(8,128)(2,1)S(1)}, bf16[64,384]{1,0:T(8,128)(2,1)S(1)}, u32[]{:S(2)}, u32[]{:S(2)}) collective-permute-start(bf16[64,384]{1,0:T(8,128)(2,1)S(1)} %get-tuple-element.22), channel_id=1, source_target_pairs={{0,16},{16,0},{1,17},{17,1},{2,18},{18,2},{3,19},{19,3},{4,20},{20... | collective-permute-start | bytes 147464 | tf_op jit(solution)/shard_map/ppermute | solution.py:32
  56.0 35.4 %collective-permute-start.20 = (bf16[64,384]{1,0:T(8,128)(2,1)S(1)}, bf16[64,384]{1,0:T(8,128)(2,1)S(1)}, u32[]{:S(2)}, u32[]{:S(2)}) collective-permute-start(bf16[64,384]{1,0:T(8,128)(2,1)S(1)} %get-tuple-element.28), channel_id=1, source_target_pairs={{0,16},{16,0},{1,17},{17,1},{2,18},{18,2},{3,19},{19,3},{4,20},{20... | collective-permute-start | bytes 147464 | tf_op jit(solution)/shard_map/ppermute | solution.py:32
  56.5 11.9 %collective-permute-start.13 = (bf16[4,208,128]{2,1,0:T(8,128)(2,1)S(1)}, bf16[4,208,128]{2,1,0:T(8,128)(2,1)S(1)}, u32[]{:S(2)}, u32[]{:S(2)}) collective-permute-start(bf16[4,208,128]{2,1,0:T(8,128)(2,1)S(1)} %get-tuple-element.43), channel_id=1, source_target_pairs={{0,2},{1,3},{2,0},{3,1},{4,6},{5,7},{6,4},{7,5},{8,10},{9,11},{10,... | collective-permute-start | bytes 638984 | tf_op jit(solution)/shard_map/ppermute | solution.py:27
  58.0 10.3 %collective-permute-start.15 = (bf16[4,208,128]{2,1,0:T(8,128)(2,1)S(1)}, bf16[4,208,128]{2,1,0:T(8,128)(2,1)S(1)}, u32[]{:S(2)}, u32[]{:S(2)}) collective-permute-start(bf16[4,208,128]{2,1,0:T(8,128)(2,1)S(1)} %get-tuple-element.44), channel_id=1, source_target_pairs={{0,3},{1,2},{2,1},{3,0},{4,7},{5,6},{6,5},{7,4},{8,11},{9,10},{10,... | collective-permute-start | bytes 638984 | tf_op jit(solution)/shard_map/ppermute | solution.py:27
  59.5 10.1 %collective-permute-start.14 = (bf16[4,208,128]{2,1,0:T(8,128)(2,1)S(1)}, bf16[4,208,128]{2,1,0:T(8,128)(2,1)S(1)}, u32[]{:S(2)}, u32[]{:S(2)}) collective-permute-start(bf16[4,208,128]{2,1,0:T(8,128)(2,1)S(1)} %get-tuple-element.45), channel_id=1, source_target_pairs={{0,1},{1,0},{2,3},{3,2},{4,5},{5,4},{6,7},{7,6},{8,9},{9,8},{10,11... | collective-permute-start | bytes 638984 | tf_op jit(solution)/shard_map/ppermute | solution.py:27
  69.7 6.0 %collective-permute-start.18 = (bf16[1,208,128]{2,1,0:T(8,128)(2,1)S(1)}, bf16[1,208,128]{2,1,0:T(8,128)(2,1)S(1)}, u32[]{:S(2)}, u32[]{:S(2)}) collective-permute-start(bf16[1,208,128]{2,1,0:T(8,128)(2,1)S(1)} %get-tuple-element.46), channel_id=1, source_target_pairs={{0,12},{1,13},{2,14},{3,15},{4,8},{5,9},{6,10},{7,11},{8,4},{9,5},... | collective-permute-start | bytes 159752 | tf_op jit(solution)/shard_map/ppermute | solution.py:27
  71.0 4.8 %collective-permute-start.17 = (bf16[1,208,128]{2,1,0:T(8,128)(2,1)S(1)}, bf16[1,208,128]{2,1,0:T(8,128)(2,1)S(1)}, u32[]{:S(2)}, u32[]{:S(2)}) collective-permute-start(bf16[1,208,128]{2,1,0:T(8,128)(2,1)S(1)} %get-tuple-element.47), channel_id=1, source_target_pairs={{0,4},{1,5},{2,6},{3,7},{4,0},{5,1},{6,2},{7,3},{8,12},{9,13},{10,... | collective-permute-start | bytes 159752 | tf_op jit(solution)/shard_map/ppermute | solution.py:27
  71.4 5.2 %collective-permute-start.16 = (bf16[1,208,128]{2,1,0:T(8,128)(2,1)S(1)}, bf16[1,208,128]{2,1,0:T(8,128)(2,1)S(1)}, u32[]{:S(2)}, u32[]{:S(2)}) collective-permute-start(bf16[1,208,128]{2,1,0:T(8,128)(2,1)S(1)} %get-tuple-element.48), channel_id=1, source_target_pairs={{0,8},{1,9},{2,10},{3,11},{4,12},{5,13},{6,14},{7,15},{8,0},{9,1},... | collective-permute-start | bytes 159752 | tf_op jit(solution)/shard_map/ppermute | solution.py:27
  75.8 21.4 %collective-permute-start.21 = (bf16[64,3072]{1,0:T(8,128)(2,1)S(1)}, bf16[64,3072]{1,0:T(8,128)(2,1)S(1)}, u32[]{:S(2)}, u32[]{:S(2)}) collective-permute-start(bf16[64,3072]{1,0:T(8,128)(2,1)S(1)} %get-tuple-element.40), channel_id=1, source_target_pairs={{0,16},{16,0},{1,17},{17,1},{2,18},{18,2},{3,19},{19,3},{4,20},{20... | collective-permute-start | bytes 1179656 | tf_op jit(solution)/shard_map/ppermute | solution.py:32
  80.5 4.2 %collective-permute-start.23 = (f32[4,384]{1,0:T(4,128)S(1)}, f32[4,384]{1,0:T(4,128)S(1)}, u32[]{:S(2)}, u32[]{:S(2)}) collective-permute-start(f32[4,384]{1,0:T(4,128)S(1)} %get-tuple-element.53), channel_id=1, source_target_pairs={{0,2},{1,3},{2,0},{3,1},{4,6},{5,7},{6,4},{7,5},{8,10},{9,11},{10,... | collective-permute-start | bytes 18440 | tf_op jit(solution)/shard_map/ppermute | solution.py:27
  82.1 4.5 %collective-permute-start.25 = (f32[4,384]{1,0:T(4,128)S(1)}, f32[4,384]{1,0:T(4,128)S(1)}, u32[]{:S(2)}, u32[]{:S(2)}) collective-permute-start(f32[4,384]{1,0:T(4,128)S(1)} %get-tuple-element.54), channel_id=1, source_target_pairs={{0,3},{1,2},{2,1},{3,0},{4,7},{5,6},{6,5},{7,4},{8,11},{9,10},{10,... | collective-permute-start | bytes 18440 | tf_op jit(solution)/shard_map/ppermute | solution.py:27
  83.6 3.6 %collective-permute-start.24 = (f32[4,384]{1,0:T(4,128)S(1)}, f32[4,384]{1,0:T(4,128)S(1)}, u32[]{:S(2)}, u32[]{:S(2)}) collective-permute-start(f32[4,384]{1,0:T(4,128)S(1)} %get-tuple-element.55), channel_id=1, source_target_pairs={{0,1},{1,0},{2,3},{3,2},{4,5},{5,4},{6,7},{7,6},{8,9},{9,8},{10,11... | collective-permute-start | bytes 18440 | tf_op jit(solution)/shard_map/ppermute | solution.py:27
  84.7 12.4 %collective-permute-start.22 = (bf16[64,3072]{1,0:T(8,128)(2,1)S(1)}, bf16[64,3072]{1,0:T(8,128)(2,1)S(1)}, u32[]{:S(2)}, u32[]{:S(2)}) collective-permute-start(bf16[64,3072]{1,0:T(8,128)(2,1)S(1)} %get-tuple-element.41), channel_id=1, source_target_pairs={{0,16},{16,0},{1,17},{17,1},{2,18},{18,2},{3,19},{19,3},{4,20},{20... | collective-permute-start | bytes 1179656 | tf_op jit(solution)/shard_map/ppermute | solution.py:32
  87.3 4.5 %collective-permute-start.26 = (f32[1,384]{1,0:T(1,128)S(1)}, f32[1,384]{1,0:T(1,128)S(1)}, u32[]{:S(2)}, u32[]{:S(2)}) collective-permute-start(f32[1,384]{1,0:T(1,128)S(1)} %get-tuple-element.56), channel_id=1, source_target_pairs={{0,8},{1,9},{2,10},{3,11},{4,12},{5,13},{6,14},{7,15},{8,0},{9,1},... | collective-permute-start | bytes 4616 | tf_op jit(solution)/shard_map/ppermute | solution.py:27
  89.9 5.4 %collective-permute-start.28 = (f32[1,384]{1,0:T(1,128)S(1)}, f32[1,384]{1,0:T(1,128)S(1)}, u32[]{:S(2)}, u32[]{:S(2)}) collective-permute-start(f32[1,384]{1,0:T(1,128)S(1)} %get-tuple-element.57), channel_id=1, source_target_pairs={{0,12},{1,13},{2,14},{3,15},{4,8},{5,9},{6,10},{7,11},{8,4},{9,5},... | collective-permute-start | bytes 4616 | tf_op jit(solution)/shard_map/ppermute | solution.py:27
  91.4 3.9 %collective-permute-start.27 = (f32[1,384]{1,0:T(1,128)S(1)}, f32[1,384]{1,0:T(1,128)S(1)}, u32[]{:S(2)}, u32[]{:S(2)}) collective-permute-start(f32[1,384]{1,0:T(1,128)S(1)} %get-tuple-element.58), channel_id=1, source_target_pairs={{0,4},{1,5},{2,6},{3,7},{4,0},{5,1},{6,2},{7,3},{8,12},{9,13},{10,... | collective-permute-start | bytes 4616 | tf_op jit(solution)/shard_map/ppermute | solution.py:27
  91.8 5.3 %collective-permute-start.19 = (bf16[64,384]{1,0:T(8,128)(2,1)S(1)}, bf16[64,384]{1,0:T(8,128)(2,1)S(1)}, u32[]{:S(2)}, u32[]{:S(2)}) collective-permute-start(bf16[64,384]{1,0:T(8,128)(2,1)S(1)} %get-tuple-element.27), channel_id=1, source_target_pairs={{0,16},{16,0},{1,17},{17,1},{2,18},{18,2},{3,19},{19,3},{4,20},{20... | collective-permute-start | bytes 147464 | tf_op jit(solution)/shard_map/ppermute | solution.py:32
  95.3 1.2 %collective-permute-start.29 = (f32[1,384]{1,0:T(1,128)S(1)}, f32[1,384]{1,0:T(1,128)S(1)}, u32[]{:S(2)}, u32[]{:S(2)}) collective-permute-start(f32[1,384]{1,0:T(1,128)S(1)} %get-tuple-element.35), channel_id=1, source_target_pairs={{0,16},{16,0},{1,17},{17,1},{2,18},{18,2},{3,19},{19,3},{4,20},{20... | collective-permute-start | bytes 4616 | tf_op jit(solution)/shard_map/ppermute | solution.py:32

commit v2 on v1

--- a/solution.py
+++ b/solution.py
@@ -12,12 +12,11 @@
 F32 = jnp.float32
 BF16 = jnp.bfloat16
 LANES = 128
-PAD_ROWS = 16
+PAD_ROWS = 8
 SQRT_HALF = math.sqrt(0.5)
 INV_SQRT_2PI = 1.0 / math.sqrt(2.0 * math.pi)
-VMEM_LIMIT = 48 * 1024 * 1024
-
-ANY = pl.BlockSpec(memory_space=pl.ANY)
+VMEM_LIMIT = 32 * 1024 * 1024
+
 VMEM = pl.BlockSpec(memory_space=pltpu.VMEM)
 SMEM = pl.BlockSpec(memory_space=pltpu.SMEM)
 
@@ -120,20 +119,8 @@
     return dx.astype(BF16), jnp.sum(du * hat, axis=0, keepdims=True)
 
 
-def weight_copies(weights, index, held, sems, chunks):
-    width = held.shape[1] // chunks
-    return [
-        pltpu.make_async_copy(
-            weights.at[0, index, :, pl.ds(c * width, width)],
-            held.at[:, pl.ds(c * width, width)],
-            sems.at[c],
-        )
-        for c in range(chunks)
-    ]
-
-
 def section_kernel(offsets, dims, forward, unpack, backward, send_order, *refs):
-    tokens, block, model_width, chunks = dims
+    tokens, block, model_width = dims
     refs = list(refs)
     take = refs.pop
     scalars = take(0)
@@ -149,13 +136,9 @@
         gains = take(0)
     if backward:
         dz_out, sent_out = take(0), take(0)
-    held, sems = refs
     me, windex = scalars[0], scalars[1]
-    copies = weight_copies(weights, windex, held, sems, chunks)
-    for copy in copies:
-        copy.start()
+    held = weights.at[0, windex]
     wide = block
-    per = model_width // chunks
     if forward:
         total = jnp.zeros((tokens, LANES), F32)
         squares = jnp.zeros((tokens, LANES), F32)
@@ -178,23 +161,14 @@
             gain = gains[pl.ds(windex, 1), pl.ds(column, wide)]
             hat = (pieces[e, 0:tokens, :].astype(F32) - mean) * scale
             u_out[:, pl.ds(column, wide)] = (hat * gain).astype(BF16)
-        z = None
-        for c, copy in enumerate(copies):
-            copy.wait()
-            part = lax.dot_general(
-                u_out[:, c * per : (c + 1) * per],
-                held[:, c * per : (c + 1) * per],
-                (((1,), (1,)), ((), ())),
-                preferred_element_type=F32,
-            )
-            z = part if z is None else z + part
+        z = lax.dot_general(
+            u_out[...], held[...], (((1,), (1,)), ((), ())), preferred_element_type=F32
+        )
         gelu, slope = gelu_and_slope(z)
         z_out[...] = z
         y_out[...] = (own[...].astype(F32) + gelu).astype(BF16)
     if backward:
         if not forward:
-            for copy in copies:
-                copy.wait()
             z = z_ref[...]
             gelu, slope = gelu_and_slope(z)
         dz = (dy_ref[...].astype(F32) * slope).astype(BF16)
@@ -220,8 +194,7 @@
     forward, backward = pieces is not None, dy is not None
     rows, model_width = weights.shape[2:]
     tokens = (own if forward else dy).shape[0]
-    chunks = 4
-    operands, specs = [scalars, weights], [SMEM, ANY]
+    operands, specs = [scalars, weights], [SMEM, VMEM]
     for value in (pieces, own, gains, dy, z):
         if value is not None:
             operands.append(value)
@@ -248,7 +221,7 @@
         functools.partial(
             section_kernel,
             offsets,
-            (tokens, wide, model_width, chunks),
+            (tokens, wide, model_width),
             forward,
             unpack,
             backward,
@@ -257,10 +230,6 @@
         out_shape=outs,
         in_specs=specs,
         out_specs=[VMEM] * len(outs),
-        scratch_shapes=[
-            pltpu.VMEM((rows, model_width), BF16),
-            pltpu.SemaphoreType.DMA((chunks,)),
-        ],
         compiler_params=pltpu.CompilerParams(vmem_limit_bytes=VMEM_LIMIT),
         cost_estimate=pl.CostEstimate(
             flops=flops, bytes_accessed=2 * rows * model_width, transcendentals=tokens * rows
@@ -269,7 +238,7 @@
 
 
 def last_kernel(offsets, places, dims, part_count, *refs):
-    tokens, wide, model_width, chunks = dims
+    tokens, wide, model_width = dims
     scalars, weights, pieces, stat, z_ref, dy_ref = refs[:6]
     refs = refs[6:]
     if part_count:
@@ -278,13 +247,11 @@
             refs[part_count : part_count + 3],
             refs[part_count + 3 :],
         )
-        dz_out, gain_out, next_gain_out, held, sems = refs
+        dz_out, gain_out, next_gain_out = refs
     else:
-        dz_out, gain_out, held, sems = refs
+        dz_out, gain_out = refs
     me, windex = scalars[0], scalars[1]
-    copies = weight_copies(weights, windex, held, sems, chunks)
-    for copy in copies:
-        copy.start()
+    held = weights.at[0, windex]
     dy = dy_ref[...]
     if part_count:
         total = parts[0][...]
@@ -307,8 +274,6 @@
     dz = (dy.astype(F32) * slope).astype(BF16)
     dz_out[...] = dz
     mean, scale = stat[:, 0:1], stat[:, 1:2]
-    for copy in copies:
-        copy.wait()
     for e, offset in enumerate(offsets):
         column = pl.multiple_of((me ^ offset) * wide, LANES)
         part = jnp.dot(dz, held[:, pl.ds(column, wide)], preferred_element_type=F32)
@@ -320,7 +285,6 @@
 def last_call(scalars, weights, pieces, stat, z, dy, finish, offsets, send_order, wide, first_size):
     rows, model_width = weights.shape[2:]
     tokens = dy.shape[0]
-    chunks = 4
     rest = len(offsets) // first_size
     places = [divmod(send_order.index(o), rest) for o in offsets]
     operands = [scalars, weights, pieces, stat, z, dy]
@@ -336,15 +300,11 @@
         outs.append(jax.ShapeDtypeStruct((1, rows), F32))
     return pl.pallas_call(
         functools.partial(
-            last_kernel, offsets, places, (tokens, wide, model_width, chunks), part_count
+            last_kernel, offsets, places, (tokens, wide, model_width), part_count
         ),
         out_shape=outs,
-        in_specs=[SMEM, ANY] + [VMEM] * (len(operands) - 2),
+        in_specs=[SMEM] + [VMEM] * (len(operands) - 1),
         out_specs=[VMEM] * len(outs),
-        scratch_shapes=[
-            pltpu.VMEM((rows, model_width), BF16),
-            pltpu.SemaphoreType.DMA((chunks,)),
-        ],
         compiler_params=pltpu.CompilerParams(vmem_limit_bytes=VMEM_LIMIT),
         cost_estimate=pl.CostEstimate(
             flops=2 * tokens * rows * model_width,
@@ -354,34 +314,77 @@
     )(*operands)
 
 
-def weight_grad_kernel(dz_first, dz_second, u_first, u_second, first_out, second_out):
-    contract = (((0,), (0,)), ((), ()))
-    first_out[...] = lax.dot_general(
-        dz_first[...], u_first[...], contract, preferred_element_type=F32
-    )
-    second_out[...] = lax.dot_general(
-        dz_second[...], u_second[...], contract, preferred_element_type=F32
-    )
-
-
-def weight_grad_call(dz_first, dz_second, u_first, u_second):
-    depth, rows = dz_first.shape
-    columns = u_first.shape[1]
-    tile = columns // 6
-    whole = pl.BlockSpec((depth, rows), lambda i: (0, 0))
-    narrow = pl.BlockSpec((depth, tile), lambda i: (0, i))
-    out = pl.BlockSpec((rows, tile), lambda i: (0, i))
+def weight_grad_kernel(take_early, tile, *refs):
+    scalars, early, early_other, late, late_other, u_own, u_other, _, out, order, depth = refs
+    tokens = early.shape[0]
+    step = pl.program_id(0)
+
+    @pl.when(step == 0)
+    def _():
+        pick = scalars[1] == (0 if take_early else 1)
+        depth[0:tokens] = jnp.where(pick, early[...], late[...])
+        depth[tokens:] = jnp.where(pick, early_other[...], late_other[...])
+        order[...] = jnp.zeros_like(order)
+
+    columns = pl.ds(pl.multiple_of(step * tile, LANES), tile)
+    both = jnp.concatenate([u_own[:, columns], u_other[:, columns]], axis=0)
+    out[...] = lax.dot_general(
+        depth[...], both, (((0,), (0,)), ((), ())), preferred_element_type=F32
+    )
+
+
+def weight_grad_call(scalars, first, dz_a, dz_a_other, dz_b, dz_b_other, u_own, u_other, after):
+    tokens, rows = dz_a.shape
+    columns = u_own.shape[1]
+    steps = 6
+    tile = columns // steps
     return pl.pallas_call(
-        weight_grad_kernel,
-        grid=(6,),
-        out_shape=[jax.ShapeDtypeStruct((rows, columns), F32)] * 2,
-        in_specs=[whole, whole, narrow, narrow],
-        out_specs=[out, out],
+        functools.partial(weight_grad_kernel, first, tile),
+        grid=(steps,),
+        out_shape=[
+            jax.ShapeDtypeStruct((rows, columns), F32),
+            jax.ShapeDtypeStruct((8, LANES), F32),
+        ],
+        in_specs=[SMEM] + [VMEM] * 7,
+        out_specs=[pl.BlockSpec((rows, tile), lambda i: (0, i)), VMEM],
+        scratch_shapes=[pltpu.VMEM((2 * tokens, rows), BF16)],
         compiler_params=pltpu.CompilerParams(vmem_limit_bytes=VMEM_LIMIT),
         cost_estimate=pl.CostEstimate(
-            flops=4 * depth * rows * columns, bytes_accessed=8 * rows * columns, transcendentals=0
+            flops=4 * tokens * rows * columns, bytes_accessed=4 * rows * columns, transcendentals=0
         ),
-    )(dz_first, dz_second, u_first, u_second)
+    )(scalars, dz_a, dz_a_other, dz_b, dz_b_other, u_own, u_other, after)
+
+
+def pack_kernel(scalars, down_input, up_input, down_cot, up_cot, gains, state, cot, payload):
+    lower = scalars[1] == 0
+    tokens = state.shape[0]
+    value = jnp.where(lower, down_input[...], up_input[...])
+    state[...] = value
+    payload[0:tokens] = value
+    cot[...] = jnp.where(lower, down_cot[...], up_cot[...])
+    row = lax.broadcasted_iota(jnp.int32, (PAD_ROWS, value.shape[1]), 0)
+    block = jnp.zeros((PAD_ROWS, value.shape[1]), F32)
+    n = 0
+    for section in range(2):
+        for term in three_terms(gains[section : section + 1, :]):
+            block = jnp.where(row == n, term.astype(F32), block)
+            n += 1
+    payload[tokens:] = block.astype(BF16)
+
+
+def pack_call(scalars, down_input, up_input, down_cot, up_cot, gains):
+    tokens, block = down_input.shape
+    return pl.pallas_call(
+        pack_kernel,
+        out_shape=[
+            jax.ShapeDtypeStruct((tokens, block), BF16),
+            jax.ShapeDtypeStruct((tokens, block), BF16),
+            jax.ShapeDtypeStruct((tokens + PAD_ROWS, block), BF16),
+        ],
+        in_specs=[SMEM] + [VMEM] * 5,
+        out_specs=[VMEM] * 3,
+        compiler_params=pltpu.CompilerParams(vmem_limit_bytes=VMEM_LIMIT),
+    )(scalars, down_input, up_input, down_cot, up_cot, gains)
 
 
 def keep_live(live, record, previous):
@@ -406,11 +409,9 @@
     wide = block << merged
     bit_count = seq_size.bit_length() - 1
     groups = bit_groups(merged, bit_count)
-    back_groups = groups[::-1]
+    back_groups = [group[::-1] for group in groups[::-1]]
     offsets = [o >> merged for o in offsets_of(groups)]
-    send_order = [0]
-    for group in groups:
-        send_order = [o ^ (d >> merged) for d in (0,) + group for o in send_order]
+    send_order = [o >> merged for o in offsets_of(back_groups[::-1])]
     me = (seq_index >> merged).astype(jnp.int32)
     first_index = jnp.where(lower, 0, 1).astype(jnp.int32)
     turn = jnp.minimum(position, sections - 1 - position)
@@ -484,16 +485,14 @@
         return du, first, second
 
     own_gains = section_gains[0]
-    state = jnp.where(lower, down_input, up_input)
-    grad = jnp.where(lower, down_cot, up_cot)
-    gain_rows = jnp.stack(three_terms(own_gains[0]) + three_terms(own_gains[1]))
-    gain_rows = jnp.pad(gain_rows, ((0, PAD_ROWS - gain_rows.shape[0]), (0, 0)))
+    state, grad, packed = pack_call(
+        scalars_at(0), down_input, up_input, down_cot, up_cot, own_gains
+    )
     first_record = second_record = None
     gains = None
     for step in range(sections):
         last = step == sections - 1
-        payload = jnp.concatenate([state, gain_rows], axis=0) if step == 0 else state
-        pieces = gathered(payload)
+        pieces = gathered(packed if step == 0 else state)
         result = section_call(
             scalars_at(step),
             section_weights,
@@ -528,9 +527,6 @@
     u_second = jnp.where(lower, u_b[:, half:], u_a[:, half:])
     other_first = swapped(jnp.where(lower, u_b[:, :half], u_a[:, :half]))
     other_second = swapped(jnp.where(lower, u_a[:, half:], u_b[:, half:]))
-    u_first = jnp.concatenate([u_first, other_first], axis=0)
-    u_second = jnp.concatenate([u_second, other_second], axis=0)
-
     dz_a = dz_b = gain_b = gain_a = None
     for step in reversed(range(1, sections)):
         source, _, _, stat, z, _ = second_record if step >= middle else first_record
@@ -594,29 +590,32 @@
     if finish is not None:
         gain_b = result[2]
     dz_a = keep_live(live_at(0), dz, dz_a)
+    dz_a_other = swapped(dz_a)
+    dz_b_other = swapped(dz_b)
+    dz_all = (dz_a, dz_a_other, dz_b, dz_b_other)
+    grads = []
+    token = jnp.zeros((8, LANES), F32)
+    halves = [(True, u_first, other_first), (False, u_second, other_second)]
     for n, group in enumerate(back_groups):
         if n:
             gain_parts = gain_parts.reshape((len(group) + 1, -1) + gain_parts.shape[1:])
-        gain_parts = functools.reduce(jnp.add, reduce_round(gain_parts, group))
+        parts = reduce_round(gain_parts, group)
+        if halves:
+            first, mine, theirs = halves.pop(0)
+            grad_half, token = weight_grad_call(
+                scalars_at(0), first, *dz_all, mine, theirs, token
+            )
+            grads.append(grad_half)
+            parts.append(token[0, 0])
+        gain_parts = functools.reduce(jnp.add, parts)
+    for first, mine, theirs in halves:
+        grads.append(weight_grad_call(scalars_at(0), first, *dz_all, mine, theirs, token)[0])
+    grad_first, grad_second = grads
     gain = gain_parts.reshape(1, wide)
     for bit in reversed(range(merged)):
         mine, theirs = own_part(gain, gain.shape[1] // 2, bit)
         gain = mine + from_xor(theirs, 1 << bit)
     gain_a = keep_live(live_at(0), gain, gain_a)
-
-    dz_a_other = swapped(dz_a)
-    dz_b_other = swapped(dz_b)
-    dz_first = jnp.where(
-        lower,
-        jnp.concatenate([dz_a, dz_a_other], axis=0),
-        jnp.concatenate([dz_b, dz_b_other], axis=0),
-    )
-    dz_second = jnp.where(
-        lower,
-        jnp.concatenate([dz_b, dz_b_other], axis=0),
-        jnp.concatenate([dz_a, dz_a_other], axis=0),
-    )
-    grad_first, grad_second = weight_grad_call(dz_first, dz_second, u_first, u_second)
     gain_other = swapped(jnp.where(lower, gain_b, gain_a))
     gain_total = jnp.where(lower, gain_a, gain_b) + gain_other
     return (

time: 102 us -> 101 us (level)
  local copies, waits for them, and re-layouts: 1.92 us -> 9.64 us
  waiting for transfers between devices: 42.3 us -> 35.3 us
  other arithmetic: 4.21 us -> 2.97 us
  Pallas kernels: 19.1 us -> 17.9 us
    unnamed x13 -> x26, local copies, waits for them, and re-layouts: 0.24 us -> 7.78 us
    ppermute x24, waiting for transfers between devices: 41.1 us -> 34.8 us  [from_xor(): return lax.ppermute(value, 'seq', [(i, i ^ distance) for i in range(size)])]
    pallas_call x1 -> x3, Pallas kernels: 4.83 us -> 9.32 us  [the longest x2 8.74 us: weight_grad_call(): pl.pallas_call(functools.partial(weight_grad_kernel, first, tile), grid=(...]
    pallas_call x2, Pallas kernels: 10.4 us -> 6.99 us  [section_call(): pl.pallas_call(functools.partial(section_kernel, offsets, (tokens, wide,...]
    pallas_call x1, Pallas kernels: 3.92 us -> 1.63 us  [last_call(): pl.pallas_call(functools.partial(last_kernel, offsets, places, (tokens, w...]
    select_n x4 -> x1, other arithmetic: 1.75 us -> 0.11 us  [per_device(): other_second = swapped(jnp.where(lower, u_a[:, half:], u_b[:, half:]))]
    slice x0 -> x2, local copies, waits for them, and re-layouts: none -> 1.02 us  [per_device(): parts.append(token[0, 0])]
  transfers between devices with their start and end apart: 30 -> 30, of which waited for: 19 -> 15; matrix products, arithmetic and copies ran while one was open for 3% -> 4% of each run, Pallas kernels for 4% -> 10%
where the time goes in v2:
time: 101 us
  waiting for transfers between devices  35.3 us (35%)
  starting transfers between devices  34.1 us (34%)
  Pallas kernels  17.9 us (18%)
  local copies, waits for them, and re-layouts  9.64 us (10%)
  other arithmetic  2.97 us (3%)
    ppermute x24, waiting for transfers between devices, from_xor(): return lax.ppermute(value, 'seq', [(i, i ^ distance) for i in range(size)])  34.8 us
    ppermute x24, starting transfers between devices, from_xor(): return lax.ppermute(value, 'seq', [(i, i ^ distance) for i in range(size)])  33.3 us
    pallas_call x2, Pallas kernels, weight_grad_call(): pl.pallas_call(functools.partial(weight_grad_kernel, first, tile), grid=(...  8.74 us
    unnamed x26, local copies, waits for them, and re-layouts  7.78 us
    pallas_call x2, Pallas kernels, section_call(): pl.pallas_call(functools.partial(section_kernel, offsets, (tokens, wide,...  6.99 us
  transfers between devices with their start and end apart: 30, of which 15 were waited for; matrix products, arithmetic and copies ran while one was open for 4% of the time, Pallas kernels for 10%

profile of v2, /device:TPU:0, one launch (start us, length us, event | category | flops | bytes accessed | tf_op | source)
XLA Modules:
  0.0 100.9 jit_solution(8546842105677659841)
XLA Ops:
  0.7 0.8 copy-done.2
  2.3 0.8 copy-done.4
  3.1 0.8 copy-done.5
  5.2 5.1 %collective-permute-start.2 = (bf16[1,72,384]{2,1,0:T(8,128)(2,1)S(1)}, bf16[1,72,384]{2,1,0:T(8,128)(2,1)S(1)}, u32[]{:S(2)}, u32[]{:S(2)}) collective-permute-start(bf16[1,72,384]{2,1,0:T(8,128)(2,1)S(1)} %bitcast.41), channel_id=1, source_target_pairs={{0,12},{1,13},{2,14},{3,15},{4,8},{5,9},{6,10},{7,11},{8,4},{9,5},... | collective-permute-start | bytes 165896 | tf_op jit(solution)/shard_map/ppermute | solution.py:26
  11.7 1.2 %collective-permute-done.2 = bf16[1,72,384]{2,1,0:T(8,128)(2,1)S(1)} collective-permute-done((bf16[1,72,384]{2,1,0:T(8,128)(2,1)S(1)}, bf16[1,72,384]{2,1,0:T(8,128)(2,1)S(1)}, u32[]{:S(2)}, u32[]{:S(2)}) %collective-permute-start.2) | collective-permute-done | bytes 55328 | tf_op jit(solution)/shard_map/ppermute | solution.py:26
  12.9 1.7 %collective-permute-done.1 = bf16[1,72,384]{2,1,0:T(8,128)(2,1)S(1)} collective-permute-done((bf16[1,72,384]{2,1,0:T(8,128)(2,1)S(1)}, bf16[1,72,384]{2,1,0:T(8,128)(2,1)S(1)}, u32[]{:S(2)}, u32[]{:S(2)}) %collective-permute-start.1) | collective-permute-done | bytes 55328 | tf_op jit(solution)/shard_map/ppermute | solution.py:26
  14.5 1.2 %collective-permute-done = bf16[1,72,384]{2,1,0:T(8,128)(2,1)S(1)} collective-permute-done((bf16[1,72,384]{2,1,0:T(8,128)(2,1)S(1)}, bf16[1,72,384]{2,1,0:T(8,128)(2,1)S(1)}, u32[]{:S(2)}, u32[]{:S(2)}) %collective-permute-start) | collective-permute-done | bytes 55328 | tf_op jit(solution)/shard_map/ppermute | solution.py:26
  15.8 2.5 %collective-permute-start.5 = (bf16[4,72,384]{2,1,0:T(8,128)(2,1)S(1)}, bf16[4,72,384]{2,1,0:T(8,128)(2,1)S(1)}, u32[]{:S(2)}, u32[]{:S(2)}) collective-permute-start(bf16[4,72,384]{2,1,0:T(8,128)(2,1)S(1)} %pad_maximum_fusion), channel_id=1, source_target_pairs={{0,3},{1,2},{2,1},{3,0},{4,7},{5,6},{6,5},{7,4},{8,11},{9,10},{10,... | collective-permute-start | bytes 663560 | tf_op jit(solution)/shard_map/ppermute | solution.py:26
  19.4 7.5 %collective-permute-done.3 = bf16[4,72,384]{2,1,0:T(8,128)(2,1)S(1)} collective-permute-done((bf16[4,72,384]{2,1,0:T(8,128)(2,1)S(1)}, bf16[4,72,384]{2,1,0:T(8,128)(2,1)S(1)}, u32[]{:S(2)}, u32[]{:S(2)}) %collective-permute-start.3) | collective-permute-done | bytes 221216 | tf_op jit(solution)/shard_map/ppermute | solution.py:26
  27.1 3.7 %copy-done = bf16[1,2,384,6144]{3,2,1,0:T(8,128)(2,1)S(1)} copy-done((bf16[1,2,384,6144]{3,2,1,0:T(8,128)(2,1)S(1)}, bf16[1,2,384,6144]{3,2,1,0:T(8,128)(2,1)}, u32[]{:S(2)}) %copy-start) | copy-done | bytes 9437208
  30.7 2.7 %shard_map.102 = (bf16[64,6144]{1,0:T(8,128)(2,1)S(1)}, f32[64,128]{1,0:T(8,128)S(1)}, f32[64,384]{1,0:T(8,128)S(1)}, bf16[64,384]{1,0:T(8,128)(2,1)S(1)}, f32[2,6144]{1,0:T(2,128)S(1)}) custom-call(s32[2]{0:T(128)S(1)} %pad_add_fusion.scalars.refs_0_, bf16[1,2,384,6144]{3,2,1,0:T(8,128)(2,1)S(1)} %copy-done, ...), custom_call_target="tpu_custom_call" | custom-call | flops 301989888 | bytes 4718592 | tf_op jit(solution)/shard_map/pallas_call | solution.py:220
  33.4 2.2 %collective-permute-start.8 = (bf16[1,64,384]{2,1,0:T(8,128)(2,1)S(1)}, bf16[1,64,384]{2,1,0:T(8,128)(2,1)S(1)}, u32[]{:S(2)}, u32[]{:S(2)}) collective-permute-start(bf16[1,64,384]{2,1,0:T(8,128)(2,1)S(1)} %bitcast.37), channel_id=1, source_target_pairs={{0,12},{1,13},{2,14},{3,15},{4,8},{5,9},{6,10},{7,11},{8,4},{9,5},... | collective-permute-start | bytes 147464 | tf_op jit(solution)/shard_map/ppermute | solution.py:26
  36.2 1.7 %collective-permute-start.6 = (bf16[1,64,384]{2,1,0:T(8,128)(2,1)S(1)}, bf16[1,64,384]{2,1,0:T(8,128)(2,1)S(1)}, u32[]{:S(2)}, u32[]{:S(2)}) collective-permute-start(bf16[1,64,384]{2,1,0:T(8,128)(2,1)S(1)} %bitcast.39), channel_id=1, source_target_pairs={{0,8},{1,9},{2,10},{3,11},{4,12},{5,13},{6,14},{7,15},{8,0},{9,1},... | collective-permute-start | bytes 147464 | tf_op jit(solution)/shard_map/ppermute | solution.py:26
  37.9 2.0 %collective-permute-done.8 = bf16[1,64,384]{2,1,0:T(8,128)(2,1)S(1)} collective-permute-done((bf16[1,64,384]{2,1,0:T(8,128)(2,1)S(1)}, bf16[1,64,384]{2,1,0:T(8,128)(2,1)S(1)}, u32[]{:S(2)}, u32[]{:S(2)}) %collective-permute-start.8) | collective-permute-done | bytes 49184 | tf_op jit(solution)/shard_map/ppermute | solution.py:26
  40.2 0.9 collective-permute-done.6
  41.2 2.5 %collective-permute-start.11 = (bf16[4,64,384]{2,1,0:T(8,128)(2,1)S(1)}, bf16[4,64,384]{2,1,0:T(8,128)(2,1)S(1)}, u32[]{:S(2)}, u32[]{:S(2)}) collective-permute-start(bf16[4,64,384]{2,1,0:T(8,128)(2,1)S(1)} %pad_maximum_fusion.1), channel_id=1, source_target_pairs={{0,3},{1,2},{2,1},{3,0},{4,7},{5,6},{6,5},{7,4},{8,11},{9,10},{10,... | collective-permute-start | bytes 589832 | tf_op jit(solution)/shard_map/ppermute | solution.py:26
  44.8 7.1 %collective-permute-done.9 = bf16[4,64,384]{2,1,0:T(8,128)(2,1)S(1)} collective-permute-done((bf16[4,64,384]{2,1,0:T(8,128)(2,1)S(1)}, bf16[4,64,384]{2,1,0:T(8,128)(2,1)S(1)}, u32[]{:S(2)}, u32[]{:S(2)}) %collective-permute-start.9) | collective-permute-done | bytes 196640 | tf_op jit(solution)/shard_map/ppermute | solution.py:26
  52.3 4.3 %shard_map.103 = (bf16[64,6144]{1,0:T(8,128)(2,1)S(1)}, f32[64,128]{1,0:T(8,128)S(1)}, f32[64,384]{1,0:T(8,128)}, bf16[64,384]{1,0:T(8,128)(2,1)S(1)}, bf16[64,3...) custom-call(s32[2]{0:T(128)S(1)} %pad_add_fusion.1.refs_0_, bf16[1,2,384,6144]{3,2,1,0:T(8,128)(2,1)S(1)} %copy-done.1, ...), custom_call_target="tpu_custom_call" | custom-call | flops 603979776 | bytes 4718592 | tf_op jit(solution)/shard_map/pallas_call | solution.py:220
  56.8 2.5 %collective-permute-start.13 = (bf16[4,200,128]{2,1,0:T(8,128)(2,1)S(1)}, bf16[4,200,128]{2,1,0:T(8,128)(2,1)S(1)}, u32[]{:S(2)}, u32[]{:S(2)}) collective-permute-start(bf16[4,200,128]{2,1,0:T(8,128)(2,1)S(1)} %get-tuple-element.53), channel_id=1, source_target_pairs={{0,3},{1,2},{2,1},{3,0},{4,7},{5,6},{6,5},{7,4},{8,11},{9,10},{10,... | collective-permute-start | bytes 614408 | tf_op jit(solution)/shard_map/ppermute | solution.py:26
  60.6 5.1 %collective-permute-done.13 = bf16[4,200,128]{2,1,0:T(8,128)(2,1)S(1)} collective-permute-done((bf16[4,200,128]{2,1,0:T(8,128)(2,1)S(1)}, bf16[4,200,128]{2,1,0:T(8,128)(2,1)S(1)}, u32[]{:S(2)}, u32[]{:S(2)}) %collective-permute-start.13) | collective-permute-done | bytes 204832 | tf_op jit(solution)/shard_map/ppermute | solution.py:26
  65.7 3.9 %collective-permute-done.15 = bf16[4,200,128]{2,1,0:T(8,128)(2,1)S(1)} collective-permute-done((bf16[4,200,128]{2,1,0:T(8,128)(2,1)S(1)}, bf16[4,200,128]{2,1,0:T(8,128)(2,1)S(1)}, u32[]{:S(2)}, u32[]{:S(2)}) %collective-permute-start.15) | collective-permute-done | bytes 204832 | tf_op jit(solution)/shard_map/ppermute | solution.py:26
  70.1 2.2 %collective-permute-start.17 = (bf16[1,200,128]{2,1,0:T(8,128)(2,1)S(1)}, bf16[1,200,128]{2,1,0:T(8,128)(2,1)S(1)}, u32[]{:S(2)}, u32[]{:S(2)}) collective-permute-start(bf16[1,200,128]{2,1,0:T(8,128)(2,1)S(1)} %get-tuple-element.57), channel_id=1, source_target_pairs={{0,4},{1,5},{2,6},{3,7},{4,0},{5,1},{6,2},{7,3},{8,12},{9,13},{10,... | collective-permute-start | bytes 153608 | tf_op jit(solution)/shard_map/ppermute | solution.py:26
  72.3 2.0 %collective-permute-start.16 = (bf16[1,200,128]{2,1,0:T(8,128)(2,1)S(1)}, bf16[1,200,128]{2,1,0:T(8,128)(2,1)S(1)}, u32[]{:S(2)}, u32[]{:S(2)}) collective-permute-start(bf16[1,200,128]{2,1,0:T(8,128)(2,1)S(1)} %get-tuple-element.58), channel_id=1, source_target_pairs={{0,12},{1,13},{2,14},{3,15},{4,8},{5,9},{6,10},{7,11},{8,4},{9,5},... | collective-permute-start | bytes 153608 | tf_op jit(solution)/shard_map/ppermute | solution.py:26
  74.3 1.4 %collective-permute-done.18 = bf16[1,200,128]{2,1,0:T(8,128)(2,1)S(1)} collective-permute-done((bf16[1,200,128]{2,1,0:T(8,128)(2,1)S(1)}, bf16[1,200,128]{2,1,0:T(8,128)(2,1)S(1)}, u32[]{:S(2)}, u32[]{:S(2)}) %collective-permute-start.18) | collective-permute-done | bytes 51232 | tf_op jit(solution)/shard_map/ppermute | solution.py:26
  76.2 2.0 %collective-permute-done.16 = bf16[1,200,128]{2,1,0:T(8,128)(2,1)S(1)} collective-permute-done((bf16[1,200,128]{2,1,0:T(8,128)(2,1)S(1)}, bf16[1,200,128]{2,1,0:T(8,128)(2,1)S(1)}, u32[]{:S(2)}, u32[]{:S(2)}) %collective-permute-start.16) | collective-permute-done | bytes 51232 | tf_op jit(solution)/shard_map/ppermute | solution.py:26
  78.2 1.6 %shard_map.104 = (bf16[64,384]{1,0:T(8,128)(2,1)S(1)}, f32[4,4,384]{2,1,0:T(4,128)S(1)}, f32[1,384]{1,0:T(1,128)S(1)}) custom-call(s32[2]{0:T(128)S(1)} %pad_add_fusion.scalars.refs_0_, bf16[1,2,384,6144]{3,2,1,0:T(8,128)(2,1)S(1)} %copy-done.1, bf16[16,72,384]{2,1,0:T(8,128)(2,1)S(1)} %constant_dynamic-update-slice_fusion.refs_2_, ...), custom_call_target="tpu_custom_call" | custom-call | flops 301989888 | bytes 4718592 | tf_op jit(solution)/shard_map/pallas_call | solution.py:301
  79.9 1.8 %collective-permute-start.23 = (f32[4,384]{1,0:T(4,128)S(1)}, f32[4,384]{1,0:T(4,128)S(1)}, u32[]{:S(2)}, u32[]{:S(2)}) collective-permute-start(f32[4,384]{1,0:T(4,128)S(1)} %get-tuple-element.61), channel_id=1, source_target_pairs={{0,3},{1,2},{2,1},{3,0},{4,7},{5,6},{6,5},{7,4},{8,11},{9,10},{10,... | collective-permute-start | bytes 18440 | tf_op jit(solution)/shard_map/ppermute | solution.py:26
  81.7 1.3 %collective-permute-start.25 = (f32[4,384]{1,0:T(4,128)S(1)}, f32[4,384]{1,0:T(4,128)S(1)}, u32[]{:S(2)}, u32[]{:S(2)}) collective-permute-start(f32[4,384]{1,0:T(4,128)S(1)} %get-tuple-element.62), channel_id=1, source_target_pairs={{0,2},{1,3},{2,0},{3,1},{4,6},{5,7},{6,4},{7,5},{8,10},{9,11},{10,... | collective-permute-start | bytes 18440 | tf_op jit(solution)/shard_map/ppermute | solution.py:26
  83.5 4.4 %shard_map.105 = (f32[384,3072]{1,0:T(8,128)}, f32[8,128]{1,0:T(8,128)S(1)}) custom-call(s32[2]{0:T(128)S(1)} %pad_add_fusion.scalars.refs_0_, bf16[64,384]{1,0:T(8,128)(2,1)S(1)} %get-tuple-element.35.refs_1_, bf16[64,384]{1,0:T(8,128)(2,1)S(1)} %collective-permute-done.19.refs_2_, bf16[64,384]{1,0:T(8,128)(2,1)S(1)} %get-tuple-element.36.refs_3_, ...), custom_call_target="tpu_custom_call" | custom-call | flops 301989888 | bytes 4718592 | tf_op jit(solution)/shard_map/pallas_call | solution.py:341
  89.1 2.1 %collective-permute-start.26 = (f32[1,384]{1,0:T(1,128)S(1)}, f32[1,384]{1,0:T(1,128)S(1)}, u32[]{:S(2)}, u32[]{:S(2)}) collective-permute-start(f32[1,384]{1,0:T(1,128)S(1)} %get-tuple-element.64), channel_id=1, source_target_pairs={{0,12},{1,13},{2,14},{3,15},{4,8},{5,9},{6,10},{7,11},{8,4},{9,5},... | collective-permute-start | bytes 4616 | tf_op jit(solution)/shard_map/ppermute | solution.py:26
  91.1 2.4 %collective-permute-start.27 = (f32[1,384]{1,0:T(1,128)S(1)}, f32[1,384]{1,0:T(1,128)S(1)}, u32[]{:S(2)}, u32[]{:S(2)}) collective-permute-start(f32[1,384]{1,0:T(1,128)S(1)} %get-tuple-element.66), channel_id=1, source_target_pairs={{0,4},{1,5},{2,6},{3,7},{4,0},{5,1},{6,2},{7,3},{8,12},{9,13},{10,... | collective-permute-start | bytes 4616 | tf_op jit(solution)/shard_map/ppermute | solution.py:26
  93.5 4.4 %shard_map.106 = (f32[384,3072]{1,0:T(8,128)}, f32[8,128]{1,0:T(8,128)S(1)}) custom-call(s32[2]{0:T(128)S(1)} %pad_add_fusion.scalars.refs_0_, bf16[64,384]{1,0:T(8,128)(2,1)S(1)} %get-tuple-element.35.refs_1_, bf16[64,384]{1,0:T(8,128)(2,1)S(1)} %collective-permute-done.19.refs_2_, bf16[64,384]{1,0:T(8,128)(2,1)S(1)} %get-tuple-element.36.refs_3_, ...), custom_call_target="tpu_custom_call" | custom-call | flops 301989888 | bytes 4718592 | tf_op jit(solution)/shard_map/pallas_call | solution.py:341
  (81 shorter events, 14.4 us)
Async XLA Ops:
  5.2 7.7 %collective-permute-start.2 = (bf16[1,72,384]{2,1,0:T(8,128)(2,1)S(1)}, bf16[1,72,384]{2,1,0:T(8,128)(2,1)S(1)}, u32[]{:S(2)}, u32[]{:S(2)}) collective-permute-start(bf16[1,72,384]{2,1,0:T(8,128)(2,1)S(1)} %bitcast.41), channel_id=1, source_target_pairs={{0,12},{1,13},{2,14},{3,15},{4,8},{5,9},{6,10},{7,11},{8,4},{9,5},... | collective-permute-start | bytes 165896 | tf_op jit(solution)/shard_map/ppermute | solution.py:26
  10.3 4.2 %collective-permute-start.1 = (bf16[1,72,384]{2,1,0:T(8,128)(2,1)S(1)}, bf16[1,72,384]{2,1,0:T(8,128)(2,1)S(1)}, u32[]{:S(2)}, u32[]{:S(2)}) collective-permute-start(bf16[1,72,384]{2,1,0:T(8,128)(2,1)S(1)} %bitcast.42), channel_id=1, source_target_pairs={{0,4},{1,5},{2,6},{3,7},{4,0},{5,1},{6,2},{7,3},{8,12},{9,13},{10,... | collective-permute-start | bytes 165896 | tf_op jit(solution)/shard_map/ppermute | solution.py:26
  10.3 5.4 %collective-permute-start = (bf16[1,72,384]{2,1,0:T(8,128)(2,1)S(1)}, bf16[1,72,384]{2,1,0:T(8,128)(2,1)S(1)}, u32[]{:S(2)}, u32[]{:S(2)}) collective-permute-start(bf16[1,72,384]{2,1,0:T(8,128)(2,1)S(1)} %bitcast.43), channel_id=1, source_target_pairs={{0,8},{1,9},{2,10},{3,11},{4,12},{5,13},{6,14},{7,15},{8,0},{9,1},... | collective-permute-start | bytes 165896 | tf_op jit(solution)/shard_map/ppermute | solution.py:26
  15.8 11.2 %collective-permute-start.5 = (bf16[4,72,384]{2,1,0:T(8,128)(2,1)S(1)}, bf16[4,72,384]{2,1,0:T(8,128)(2,1)S(1)}, u32[]{:S(2)}, u32[]{:S(2)}) collective-permute-start(bf16[4,72,384]{2,1,0:T(8,128)(2,1)S(1)} %pad_maximum_fusion), channel_id=1, source_target_pairs={{0,3},{1,2},{2,1},{3,0},{4,7},{5,6},{6,5},{7,4},{8,11},{9,10},{10,... | collective-permute-start | bytes 663560 | tf_op jit(solution)/shard_map/ppermute | solution.py:26
  18.3 8.7 %collective-permute-start.4 = (bf16[4,72,384]{2,1,0:T(8,128)(2,1)S(1)}, bf16[4,72,384]{2,1,0:T(8,128)(2,1)S(1)}, u32[]{:S(2)}, u32[]{:S(2)}) collective-permute-start(bf16[4,72,384]{2,1,0:T(8,128)(2,1)S(1)} %pad_maximum_fusion), channel_id=1, source_target_pairs={{0,1},{1,0},{2,3},{3,2},{4,5},{5,4},{6,7},{7,6},{8,9},{9,8},{10,11... | collective-permute-start | bytes 663560 | tf_op jit(solution)/shard_map/ppermute | solution.py:26
  18.8 8.0 %collective-permute-start.3 = (bf16[4,72,384]{2,1,0:T(8,128)(2,1)S(1)}, bf16[4,72,384]{2,1,0:T(8,128)(2,1)S(1)}, u32[]{:S(2)}, u32[]{:S(2)}) collective-permute-start(bf16[4,72,384]{2,1,0:T(8,128)(2,1)S(1)} %pad_maximum_fusion), channel_id=1, source_target_pairs={{0,2},{1,3},{2,0},{3,1},{4,6},{5,7},{6,4},{7,5},{8,10},{9,11},{10,... | collective-permute-start | bytes 663560 | tf_op jit(solution)/shard_map/ppermute | solution.py:26
  27.1 3.7 %copy-start = (bf16[1,2,384,6144]{3,2,1,0:T(8,128)(2,1)S(1)}, bf16[1,2,384,6144]{3,2,1,0:T(8,128)(2,1)}, u32[]{:S(2)}) copy-start(bf16[1,2,384,6144]{3,2,1,0:T(8,128)(2,1)} %refs_1_.5) | copy-start | bytes 28311556
  30.7 21.6 %copy-start.1 = (bf16[1,2,384,6144]{3,2,1,0:T(8,128)(2,1)S(1)}, bf16[1,2,384,6144]{3,2,1,0:T(8,128)(2,1)}, u32[]{:S(2)}) copy-start(bf16[1,2,384,6144]{3,2,1,0:T(8,128)(2,1)} %refs_1_.5) | copy-start | bytes 28311556
  33.4 6.5 %collective-permute-start.8 = (bf16[1,64,384]{2,1,0:T(8,128)(2,1)S(1)}, bf16[1,64,384]{2,1,0:T(8,128)(2,1)S(1)}, u32[]{:S(2)}, u32[]{:S(2)}) collective-permute-start(bf16[1,64,384]{2,1,0:T(8,128)(2,1)S(1)} %bitcast.37), channel_id=1, source_target_pairs={{0,12},{1,13},{2,14},{3,15},{4,8},{5,9},{6,10},{7,11},{8,4},{9,5},... | collective-permute-start | bytes 147464 | tf_op jit(solution)/shard_map/ppermute | solution.py:26
  35.6 4.6 %collective-permute-start.7 = (bf16[1,64,384]{2,1,0:T(8,128)(2,1)S(1)}, bf16[1,64,384]{2,1,0:T(8,128)(2,1)S(1)}, u32[]{:S(2)}, u32[]{:S(2)}) collective-permute-start(bf16[1,64,384]{2,1,0:T(8,128)(2,1)S(1)} %bitcast.38), channel_id=1, source_target_pairs={{0,4},{1,5},{2,6},{3,7},{4,0},{5,1},{6,2},{7,3},{8,12},{9,13},{10,... | collective-permute-start | bytes 147464 | tf_op jit(solution)/shard_map/ppermute | solution.py:26
  36.2 5.0 %collective-permute-start.6 = (bf16[1,64,384]{2,1,0:T(8,128)(2,1)S(1)}, bf16[1,64,384]{2,1,0:T(8,128)(2,1)S(1)}, u32[]{:S(2)}, u32[]{:S(2)}) collective-permute-start(bf16[1,64,384]{2,1,0:T(8,128)(2,1)S(1)} %bitcast.39), channel_id=1, source_target_pairs={{0,8},{1,9},{2,10},{3,11},{4,12},{5,13},{6,14},{7,15},{8,0},{9,1},... | collective-permute-start | bytes 147464 | tf_op jit(solution)/shard_map/ppermute | solution.py:26
  41.2 11.1 %collective-permute-start.11 = (bf16[4,64,384]{2,1,0:T(8,128)(2,1)S(1)}, bf16[4,64,384]{2,1,0:T(8,128)(2,1)S(1)}, u32[]{:S(2)}, u32[]{:S(2)}) collective-permute-start(bf16[4,64,384]{2,1,0:T(8,128)(2,1)S(1)} %pad_maximum_fusion.1), channel_id=1, source_target_pairs={{0,3},{1,2},{2,1},{3,0},{4,7},{5,6},{6,5},{7,4},{8,11},{9,10},{10,... | collective-permute-start | bytes 589832 | tf_op jit(solution)/shard_map/ppermute | solution.py:26
  43.7 8.6 %collective-permute-start.10 = (bf16[4,64,384]{2,1,0:T(8,128)(2,1)S(1)}, bf16[4,64,384]{2,1,0:T(8,128)(2,1)S(1)}, u32[]{:S(2)}, u32[]{:S(2)}) collective-permute-start(bf16[4,64,384]{2,1,0:T(8,128)(2,1)S(1)} %pad_maximum_fusion.1), channel_id=1, source_target_pairs={{0,1},{1,0},{2,3},{3,2},{4,5},{5,4},{6,7},{7,6},{8,9},{9,8},{10,11... | collective-permute-start | bytes 589832 | tf_op jit(solution)/shard_map/ppermute | solution.py:26
  44.2 7.7 %collective-permute-start.9 = (bf16[4,64,384]{2,1,0:T(8,128)(2,1)S(1)}, bf16[4,64,384]{2,1,0:T(8,128)(2,1)S(1)}, u32[]{:S(2)}, u32[]{:S(2)}) collective-permute-start(bf16[4,64,384]{2,1,0:T(8,128)(2,1)S(1)} %pad_maximum_fusion.1), channel_id=1, source_target_pairs={{0,2},{1,3},{2,0},{3,1},{4,6},{5,7},{6,4},{7,5},{8,10},{9,11},{10,... | collective-permute-start | bytes 589832 | tf_op jit(solution)/shard_map/ppermute | solution.py:26
  56.7 42.5 %collective-permute-start.12 = (bf16[64,384]{1,0:T(8,128)(2,1)S(1)}, bf16[64,384]{1,0:T(8,128)(2,1)S(1)}, u32[]{:S(2)}, u32[]{:S(2)}) collective-permute-start(bf16[64,384]{1,0:T(8,128)(2,1)S(1)} %get-tuple-element.30), channel_id=1, source_target_pairs={{0,16},{16,0},{1,17},{17,1},{2,18},{18,2},{3,19},{19,3},{4,20},{20... | collective-permute-start | bytes 147464 | tf_op jit(solution)/shard_map/ppermute | solution.py:31
  56.8 8.9 %collective-permute-start.13 = (bf16[4,200,128]{2,1,0:T(8,128)(2,1)S(1)}, bf16[4,200,128]{2,1,0:T(8,128)(2,1)S(1)}, u32[]{:S(2)}, u32[]{:S(2)}) collective-permute-start(bf16[4,200,128]{2,1,0:T(8,128)(2,1)S(1)} %get-tuple-element.53), channel_id=1, source_target_pairs={{0,3},{1,2},{2,1},{3,0},{4,7},{5,6},{6,5},{7,4},{8,11},{9,10},{10,... | collective-permute-start | bytes 614408 | tf_op jit(solution)/shard_map/ppermute | solution.py:26
  59.3 10.4 %collective-permute-start.15 = (bf16[4,200,128]{2,1,0:T(8,128)(2,1)S(1)}, bf16[4,200,128]{2,1,0:T(8,128)(2,1)S(1)}, u32[]{:S(2)}, u32[]{:S(2)}) collective-permute-start(bf16[4,200,128]{2,1,0:T(8,128)(2,1)S(1)} %get-tuple-element.54), channel_id=1, source_target_pairs={{0,2},{1,3},{2,0},{3,1},{4,6},{5,7},{6,4},{7,5},{8,10},{9,11},{10,... | collective-permute-start | bytes 614408 | tf_op jit(solution)/shard_map/ppermute | solution.py:26
  59.8 9.9 %collective-permute-start.14 = (bf16[4,200,128]{2,1,0:T(8,128)(2,1)S(1)}, bf16[4,200,128]{2,1,0:T(8,128)(2,1)S(1)}, u32[]{:S(2)}, u32[]{:S(2)}) collective-permute-start(bf16[4,200,128]{2,1,0:T(8,128)(2,1)S(1)} %get-tuple-element.55), channel_id=1, source_target_pairs={{0,1},{1,0},{2,3},{3,2},{4,5},{5,4},{6,7},{7,6},{8,9},{9,8},{10,11... | collective-permute-start | bytes 614408 | tf_op jit(solution)/shard_map/ppermute | solution.py:26
  60.5 22.5 %collective-permute-start.21 = (bf16[64,3072]{1,0:T(8,128)(2,1)S(1)}, bf16[64,3072]{1,0:T(8,128)(2,1)S(1)}, u32[]{:S(2)}, u32[]{:S(2)}) collective-permute-start(bf16[64,3072]{1,0:T(8,128)(2,1)S(1)} %get-tuple-element.50), channel_id=1, source_target_pairs={{0,16},{16,0},{1,17},{17,1},{2,18},{18,2},{3,19},{19,3},{4,20},{20... | collective-permute-start | bytes 1179656 | tf_op jit(solution)/shard_map/ppermute | solution.py:31
  69.8 5.9 %collective-permute-start.18 = (bf16[1,200,128]{2,1,0:T(8,128)(2,1)S(1)}, bf16[1,200,128]{2,1,0:T(8,128)(2,1)S(1)}, u32[]{:S(2)}, u32[]{:S(2)}) collective-permute-start(bf16[1,200,128]{2,1,0:T(8,128)(2,1)S(1)} %get-tuple-element.56), channel_id=1, source_target_pairs={{0,8},{1,9},{2,10},{3,11},{4,12},{5,13},{6,14},{7,15},{8,0},{9,1},... | collective-permute-start | bytes 153608 | tf_op jit(solution)/shard_map/ppermute | solution.py:26
  70.1 5.6 %collective-permute-start.17 = (bf16[1,200,128]{2,1,0:T(8,128)(2,1)S(1)}, bf16[1,200,128]{2,1,0:T(8,128)(2,1)S(1)}, u32[]{:S(2)}, u32[]{:S(2)}) collective-permute-start(bf16[1,200,128]{2,1,0:T(8,128)(2,1)S(1)} %get-tuple-element.57), channel_id=1, source_target_pairs={{0,4},{1,5},{2,6},{3,7},{4,0},{5,1},{6,2},{7,3},{8,12},{9,13},{10,... | collective-permute-start | bytes 153608 | tf_op jit(solution)/shard_map/ppermute | solution.py:26
  72.3 5.9 %collective-permute-start.16 = (bf16[1,200,128]{2,1,0:T(8,128)(2,1)S(1)}, bf16[1,200,128]{2,1,0:T(8,128)(2,1)S(1)}, u32[]{:S(2)}, u32[]{:S(2)}) collective-permute-start(bf16[1,200,128]{2,1,0:T(8,128)(2,1)S(1)} %get-tuple-element.58), channel_id=1, source_target_pairs={{0,12},{1,13},{2,14},{3,15},{4,8},{5,9},{6,10},{7,11},{8,4},{9,5},... | collective-permute-start | bytes 153608 | tf_op jit(solution)/shard_map/ppermute | solution.py:26
  75.7 4.2 %collective-permute-start.20 = (bf16[64,384]{1,0:T(8,128)(2,1)S(1)}, bf16[64,384]{1,0:T(8,128)(2,1)S(1)}, u32[]{:S(2)}, u32[]{:S(2)}) collective-permute-start(bf16[64,384]{1,0:T(8,128)(2,1)S(1)} %get-tuple-element.36.refs_3_), channel_id=1, source_target_pairs={{0,16},{16,0},{1,17},{17,1},{2,18},{18,2},{3,19},{19,3},{4,20},{20... | collective-permute-start | bytes 147464 | tf_op jit(solution)/shard_map/ppermute | solution.py:31
  75.7 17.8 %collective-permute-start.22 = (bf16[64,3072]{1,0:T(8,128)(2,1)S(1)}, bf16[64,3072]{1,0:T(8,128)(2,1)S(1)}, u32[]{:S(2)}, u32[]{:S(2)}) collective-permute-start(bf16[64,3072]{1,0:T(8,128)(2,1)S(1)} %get-tuple-element.49), channel_id=1, source_target_pairs={{0,16},{16,0},{1,17},{17,1},{2,18},{18,2},{3,19},{19,3},{4,20},{20... | collective-permute-start | bytes 1179656 | tf_op jit(solution)/shard_map/ppermute | solution.py:31
  79.8 1.9 %collective-permute-start.19 = (bf16[64,384]{1,0:T(8,128)(2,1)S(1)}, bf16[64,384]{1,0:T(8,128)(2,1)S(1)}, u32[]{:S(2)}, u32[]{:S(2)}) collective-permute-start(bf16[64,384]{1,0:T(8,128)(2,1)S(1)} %get-tuple-element.35.refs_1_), channel_id=1, source_target_pairs={{0,16},{16,0},{1,17},{17,1},{2,18},{18,2},{3,19},{19,3},{4,20},{20... | collective-permute-start | bytes 147464 | tf_op jit(solution)/shard_map/ppermute | solution.py:31
  79.9 8.4 %collective-permute-start.23 = (f32[4,384]{1,0:T(4,128)S(1)}, f32[4,384]{1,0:T(4,128)S(1)}, u32[]{:S(2)}, u32[]{:S(2)}) collective-permute-start(f32[4,384]{1,0:T(4,128)S(1)} %get-tuple-element.61), channel_id=1, source_target_pairs={{0,3},{1,2},{2,1},{3,0},{4,7},{5,6},{6,5},{7,4},{8,11},{9,10},{10,... | collective-permute-start | bytes 18440 | tf_op jit(solution)/shard_map/ppermute | solution.py:26
  81.7 6.7 %collective-permute-start.25 = (f32[4,384]{1,0:T(4,128)S(1)}, f32[4,384]{1,0:T(4,128)S(1)}, u32[]{:S(2)}, u32[]{:S(2)}) collective-permute-start(f32[4,384]{1,0:T(4,128)S(1)} %get-tuple-element.62), channel_id=1, source_target_pairs={{0,2},{1,3},{2,0},{3,1},{4,6},{5,7},{6,4},{7,5},{8,10},{9,11},{10,... | collective-permute-start | bytes 18440 | tf_op jit(solution)/shard_map/ppermute | solution.py:26
  83.0 5.4 %collective-permute-start.24 = (f32[4,384]{1,0:T(4,128)S(1)}, f32[4,384]{1,0:T(4,128)S(1)}, u32[]{:S(2)}, u32[]{:S(2)}) collective-permute-start(f32[4,384]{1,0:T(4,128)S(1)} %get-tuple-element.63), channel_id=1, source_target_pairs={{0,1},{1,0},{2,3},{3,2},{4,5},{5,4},{6,7},{7,6},{8,9},{9,8},{10,11... | collective-permute-start | bytes 18440 | tf_op jit(solution)/shard_map/ppermute | solution.py:26
  89.1 9.3 %collective-permute-start.26 = (f32[1,384]{1,0:T(1,128)S(1)}, f32[1,384]{1,0:T(1,128)S(1)}, u32[]{:S(2)}, u32[]{:S(2)}) collective-permute-start(f32[1,384]{1,0:T(1,128)S(1)} %get-tuple-element.64), channel_id=1, source_target_pairs={{0,12},{1,13},{2,14},{3,15},{4,8},{5,9},{6,10},{7,11},{8,4},{9,5},... | collective-permute-start | bytes 4616 | tf_op jit(solution)/shard_map/ppermute | solution.py:26
  91.1 7.3 %collective-permute-start.28 = (f32[1,384]{1,0:T(1,128)S(1)}, f32[1,384]{1,0:T(1,128)S(1)}, u32[]{:S(2)}, u32[]{:S(2)}) collective-permute-start(f32[1,384]{1,0:T(1,128)S(1)} %get-tuple-element.65), channel_id=1, source_target_pairs={{0,8},{1,9},{2,10},{3,11},{4,12},{5,13},{6,14},{7,15},{8,0},{9,1},... | collective-permute-start | bytes 4616 | tf_op jit(solution)/shard_map/ppermute | solution.py:26
  91.1 7.3 %collective-permute-start.27 = (f32[1,384]{1,0:T(1,128)S(1)}, f32[1,384]{1,0:T(1,128)S(1)}, u32[]{:S(2)}, u32[]{:S(2)}) collective-permute-start(f32[1,384]{1,0:T(1,128)S(1)} %get-tuple-element.66), channel_id=1, source_target_pairs={{0,4},{1,5},{2,6},{3,7},{4,0},{5,1},{6,2},{7,3},{8,12},{9,13},{10,... | collective-permute-start | bytes 4616 | tf_op jit(solution)/shard_map/ppermute | solution.py:26
  99.1 1.2 %collective-permute-start.29 = (f32[1,384]{1,0:T(1,128)S(1)}, f32[1,384]{1,0:T(1,128)S(1)}, u32[]{:S(2)}, u32[]{:S(2)}) collective-permute-start(f32[1,384]{1,0:T(1,128)S(1)} %get-tuple-element.45), channel_id=1, source_target_pairs={{0,16},{16,0},{1,17},{17,1},{2,18},{18,2},{3,19},{19,3},{4,20},{20... | collective-permute-start | bytes 4616 | tf_op jit(solution)/shard_map/ppermute | solution.py:31
  (5 other events, 3.9 us)

commit v3 on v2

--- a/solution.py
+++ b/solution.py
@@ -18,6 +18,7 @@
 VMEM_LIMIT = 32 * 1024 * 1024
 
 VMEM = pl.BlockSpec(memory_space=pltpu.VMEM)
+ANY = pl.BlockSpec(memory_space=pl.ANY)
 SMEM = pl.BlockSpec(memory_space=pltpu.SMEM)
 
 
@@ -49,9 +50,11 @@
 
 def gather_xor(block, groups):
     held = block[None]
-    for group in groups:
+    for n, group in enumerate(groups):
+        if n <= 1:
+            early = held
         held = jnp.concatenate([held] + [from_xor(held, d) for d in group], axis=0)
-    return held
+    return held, early
 
 
 def reduce_round(held, group):
@@ -238,7 +241,7 @@
 
 
 def last_kernel(offsets, places, dims, part_count, *refs):
-    tokens, wide, model_width = dims
+    tokens, wide, model_width, first_size = dims
     scalars, weights, pieces, stat, z_ref, dy_ref = refs[:6]
     refs = refs[6:]
     if part_count:
@@ -247,9 +250,8 @@
             refs[part_count : part_count + 3],
             refs[part_count + 3 :],
         )
-        dz_out, gain_out, next_gain_out = refs
-    else:
-        dz_out, gain_out = refs
+        next_gain_out = refs[-1]
+    dz_out, gain_out = refs[0], refs[1 : 1 + first_size]
     me, windex = scalars[0], scalars[1]
     held = weights.at[0, windex]
     dy = dy_ref[...]
@@ -279,7 +281,7 @@
         part = jnp.dot(dz, held[:, pl.ds(column, wide)], preferred_element_type=F32)
         hat = (pieces[e, 0:tokens, :].astype(F32) - mean) * scale
         a, b = places[e]
-        gain_out[a, b : b + 1, :] = jnp.sum(part * hat, axis=0, keepdims=True)
+        gain_out[a][b : b + 1, :] = jnp.sum(part * hat, axis=0, keepdims=True)
 
 
 def last_call(scalars, weights, pieces, stat, z, dy, finish, offsets, send_order, wide, first_size):
@@ -290,8 +292,7 @@
     operands = [scalars, weights, pieces, stat, z, dy]
     outs = [
         jax.ShapeDtypeStruct((tokens, rows), BF16),
-        jax.ShapeDtypeStruct((first_size, rest, wide), F32),
-    ]
+    ] + [jax.ShapeDtypeStruct((rest, wide), F32)] * first_size
     part_count = 0
     if finish is not None:
         parts, others = finish
@@ -300,7 +301,11 @@
         outs.append(jax.ShapeDtypeStruct((1, rows), F32))
     return pl.pallas_call(
         functools.partial(
-            last_kernel, offsets, places, (tokens, wide, model_width), part_count
+            last_kernel,
+            offsets,
+            places,
+            (tokens, wide, model_width, first_size),
+            part_count,
         ),
         out_shape=outs,
         in_specs=[SMEM] + [VMEM] * (len(operands) - 1),
@@ -314,40 +319,40 @@
     )(*operands)
 
 
-def weight_grad_kernel(take_early, tile, *refs):
+def weight_grad_kernel(take_early, *refs):
     scalars, early, early_other, late, late_other, u_own, u_other, _, out, order, depth = refs
     tokens = early.shape[0]
-    step = pl.program_id(0)
-
-    @pl.when(step == 0)
+
+    @pl.when(pl.program_id(0) == 0)
     def _():
         pick = scalars[1] == (0 if take_early else 1)
-        depth[0:tokens] = jnp.where(pick, early[...], late[...])
-        depth[tokens:] = jnp.where(pick, early_other[...], late_other[...])
+        mine = jnp.where(pick, early[...], late[...])
+        theirs = jnp.where(pick, early_other[...], late_other[...])
+        depth[...] = jnp.concatenate([mine, theirs], axis=0).T
         order[...] = jnp.zeros_like(order)
 
-    columns = pl.ds(pl.multiple_of(step * tile, LANES), tile)
-    both = jnp.concatenate([u_own[:, columns], u_other[:, columns]], axis=0)
-    out[...] = lax.dot_general(
-        depth[...], both, (((0,), (0,)), ((), ())), preferred_element_type=F32
-    )
+    both = jnp.concatenate([u_own[...], u_other[...]], axis=0)
+    out[...] = jnp.dot(depth[...], both, preferred_element_type=F32)
 
 
 def weight_grad_call(scalars, first, dz_a, dz_a_other, dz_b, dz_b_other, u_own, u_other, after):
     tokens, rows = dz_a.shape
     columns = u_own.shape[1]
-    steps = 6
+    steps = 4
     tile = columns // steps
+    whole = pl.BlockSpec((tokens, rows), lambda i: (0, 0))
+    narrow = pl.BlockSpec((tokens, tile), lambda i: (0, i))
+    small = pl.BlockSpec(after.shape, lambda i: (0,) * after.ndim)
     return pl.pallas_call(
-        functools.partial(weight_grad_kernel, first, tile),
+        functools.partial(weight_grad_kernel, first),
         grid=(steps,),
         out_shape=[
             jax.ShapeDtypeStruct((rows, columns), F32),
-            jax.ShapeDtypeStruct((8, LANES), F32),
+            jax.ShapeDtypeStruct(after.shape, F32),
         ],
-        in_specs=[SMEM] + [VMEM] * 7,
-        out_specs=[pl.BlockSpec((rows, tile), lambda i: (0, i)), VMEM],
-        scratch_shapes=[pltpu.VMEM((2 * tokens, rows), BF16)],
+        in_specs=[SMEM] + [whole] * 4 + [narrow] * 2 + [small],
+        out_specs=[pl.BlockSpec((rows, tile), lambda i: (0, i)), small],
+        scratch_shapes=[pltpu.VMEM((rows, 2 * tokens), BF16)],
         compiler_params=pltpu.CompilerParams(vmem_limit_bytes=VMEM_LIMIT),
         cost_estimate=pl.CostEstimate(
             flops=4 * tokens * rows * columns, bytes_accessed=4 * rows * columns, transcendentals=0
@@ -355,21 +360,60 @@
     )(scalars, dz_a, dz_a_other, dz_b, dz_b_other, u_own, u_other, after)
 
 
-def pack_kernel(scalars, down_input, up_input, down_cot, up_cot, gains, state, cot, payload):
-    lower = scalars[1] == 0
+def load_kernel(weights, _, held, sems):
+    copies = [
+        pltpu.make_async_copy(weights.at[0, n], held.at[0, n], sems.at[n]) for n in range(2)
+    ]
+    for copy in copies:
+        copy.start()
+    for copy in copies:
+        copy.wait()
+
+
+def load_call(weights, after):
+    return pl.pallas_call(
+        load_kernel,
+        out_shape=jax.ShapeDtypeStruct(weights.shape, weights.dtype),
+        in_specs=[ANY, ANY],
+        out_specs=VMEM,
+        scratch_shapes=[pltpu.SemaphoreType.DMA((2,))],
+        compiler_params=pltpu.CompilerParams(vmem_limit_bytes=VMEM_LIMIT),
+        cost_estimate=pl.CostEstimate(
+            flops=0, bytes_accessed=2 * weights.size, transcendentals=0
+        ),
+    )(weights, after)
+
+
+def pack_kernel(scalars, *refs):
+    sources, gains_source, (state, cot, payload), gains, sems = (
+        refs[:4],
+        refs[4],
+        refs[5:8],
+        refs[8],
+        refs[9],
+    )
     tokens = state.shape[0]
-    value = jnp.where(lower, down_input[...], up_input[...])
-    state[...] = value
-    payload[0:tokens] = value
-    cot[...] = jnp.where(lower, down_cot[...], up_cot[...])
-    row = lax.broadcasted_iota(jnp.int32, (PAD_ROWS, value.shape[1]), 0)
-    block = jnp.zeros((PAD_ROWS, value.shape[1]), F32)
+    gains_copy = pltpu.make_async_copy(gains_source, gains, sems.at[0])
+    gains_copy.start()
+    for n in range(2):
+
+        @pl.when(scalars[1] == n)
+        def _():
+            pltpu.make_async_copy(sources[n], state, sems.at[1]).start()
+            pltpu.make_async_copy(sources[2 + n], cot, sems.at[2]).start()
+
+    gains_copy.wait()
+    row = lax.broadcasted_iota(jnp.int32, (PAD_ROWS, state.shape[1]), 0)
+    block = jnp.zeros((PAD_ROWS, state.shape[1]), F32)
     n = 0
     for section in range(2):
         for term in three_terms(gains[section : section + 1, :]):
             block = jnp.where(row == n, term.astype(F32), block)
             n += 1
     payload[tokens:] = block.astype(BF16)
+    pltpu.make_async_copy(sources[0], state, sems.at[1]).wait()
+    payload[0:tokens] = state[...]
+    pltpu.make_async_copy(sources[2], cot, sems.at[2]).wait()
 
 
 def pack_call(scalars, down_input, up_input, down_cot, up_cot, gains):
@@ -381,8 +425,9 @@
             jax.ShapeDtypeStruct((tokens, block), BF16),
             jax.ShapeDtypeStruct((tokens + PAD_ROWS, block), BF16),
         ],
-        in_specs=[SMEM] + [VMEM] * 5,
+        in_specs=[SMEM] + [ANY] * 5,
         out_specs=[VMEM] * 3,
+        scratch_shapes=[pltpu.VMEM(gains.shape, F32), pltpu.SemaphoreType.DMA((3,))],
         compiler_params=pltpu.CompilerParams(vmem_limit_bytes=VMEM_LIMIT),
     )(scalars, down_input, up_input, down_cot, up_cot, gains)
 
@@ -492,10 +537,12 @@
     gains = None
     for step in range(sections):
         last = step == sections - 1
-        pieces = gathered(packed if step == 0 else state)
+        pieces, partly = gathered(packed if step == 0 else state)
+        if step == 0:
+            weights = load_call(section_weights, partly)
         result = section_call(
             scalars_at(step),
-            section_weights,
+            weights,
             pieces,
             state,
             gains,
@@ -533,7 +580,7 @@
         if step < sections - 1:
             dz, sent = section_call(
                 scalars_at(step),
-                section_weights,
+                weights,
                 None,
                 None,
                 gains,
@@ -575,7 +622,7 @@
     first_size = len(back_groups[0]) + 1
     result = last_call(
         scalars_at(0),
-        section_weights,
+        weights,
         pieces,
         stat,
         z,
@@ -586,15 +633,14 @@
         wide,
         first_size,
     )
-    dz, gain_parts = result[:2]
+    dz, gain_parts = result[0], result[1 : 1 + first_size]
     if finish is not None:
-        gain_b = result[2]
+        gain_b = result[-1]
     dz_a = keep_live(live_at(0), dz, dz_a)
     dz_a_other = swapped(dz_a)
     dz_b_other = swapped(dz_b)
     dz_all = (dz_a, dz_a_other, dz_b, dz_b_other)
     grads = []
-    token = jnp.zeros((8, LANES), F32)
     halves = [(True, u_first, other_first), (False, u_second, other_second)]
     for n, group in enumerate(back_groups):
         if n:
@@ -603,10 +649,10 @@
         if halves:
             first, mine, theirs = halves.pop(0)
             grad_half, token = weight_grad_call(
-                scalars_at(0), first, *dz_all, mine, theirs, token
+                scalars_at(0), first, *dz_all, mine, theirs, parts[0]
             )
             grads.append(grad_half)
-            parts.append(token[0, 0])
+            parts.append(token)
         gain_parts = functools.reduce(jnp.add, parts)
     for first, mine, theirs in halves:
         grads.append(weight_grad_call(scalars_at(0), first, *dz_all, mine, theirs, token)[0])

time: 101 us -> 89.3 us (0.88)
  waiting for transfers between devices: 35.3 us -> 25.8 us
  other arithmetic: 2.97 us -> 1.68 us
  local copies, waits for them, and re-layouts: 9.64 us -> 8.61 us
    ppermute x24, waiting for transfers between devices: 34.8 us -> 25.3 us  [from_xor(): return lax.ppermute(value, 'seq', [(i, i ^ distance) for i in range(size)])]
    slice x2 -> x0, local copies, waits for them, and re-layouts: 1.02 us -> none  [per_device(): parts.append(token[0, 0])]
    pallas_call x2 -> x3, Pallas kernels: 8.74 us -> 8.04 us  [the longest x2 7.4 us: weight_grad_call(): pl.pallas_call(functools.partial(weight_grad_kernel, first), grid=(steps,...]
    unnamed x26 -> x24, local copies, waits for them, and re-layouts: 7.78 us -> 7.78 us
  transfers between devices with their start and end apart: 30 -> 30, of which waited for: 15 -> 18; matrix products, arithmetic and copies ran while one was open for 4% -> 2% of each run, Pallas kernels for 10% -> 11%
where the time goes in v3:
time: 89.3 us; the launch traced here: 88.9 us
  starting transfers between devices  34.6 us (39%)
  waiting for transfers between devices  25.8 us (29%)
  Pallas kernels  17.4 us (19%)
  local copies, waits for them, and re-layouts  8.61 us (10%)
  other arithmetic  1.68 us (2%)
    ppermute x24, starting transfers between devices, from_xor(): return lax.ppermute(value, 'seq', [(i, i ^ distance) for i in range(size)])  33.3 us
    ppermute x24, waiting for transfers between devices, from_xor(): return lax.ppermute(value, 'seq', [(i, i ^ distance) for i in range(size)])  25.3 us
    unnamed x24, local copies, waits for them, and re-layouts  7.78 us
    pallas_call x2, Pallas kernels, weight_grad_call(): pl.pallas_call(functools.partial(weight_grad_kernel, first), grid=(steps,...  7.4 us
    pallas_call x2, Pallas kernels, section_call(): pl.pallas_call(functools.partial(section_kernel, offsets, (tokens, wide,...  7 us
  transfers between devices with their start and end apart: 30, of which 18 were waited for; matrix products, arithmetic and copies ran while one was open for 2% of the time, Pallas kernels for 11%

profile of v3, /device:TPU:0, one launch (start us, length us, event | category | flops | bytes accessed | tf_op | source)
XLA Modules:
  0.0 88.9 jit_solution(4218058799692817631)
XLA Ops:
  5.3 5.1 %collective-permute-start.2 = (bf16[1,72,384]{2,1,0:T(8,128)(2,1)S(1)}, bf16[1,72,384]{2,1,0:T(8,128)(2,1)S(1)}, u32[]{:S(2)}, u32[]{:S(2)}) collective-permute-start(bf16[1,72,384]{2,1,0:T(8,128)(2,1)S(1)} %bitcast.25), channel_id=1, source_target_pairs={{0,12},{1,13},{2,14},{3,15},{4,8},{5,9},{6,10},{7,11},{8,4},{9,5},... | collective-permute-start | bytes 165896 | tf_op jit(solution)/shard_map/ppermute | solution.py:27
  13.0 1.7 %collective-permute-done.1 = bf16[1,72,384]{2,1,0:T(8,128)(2,1)S(1)} collective-permute-done((bf16[1,72,384]{2,1,0:T(8,128)(2,1)S(1)}, bf16[1,72,384]{2,1,0:T(8,128)(2,1)S(1)}, u32[]{:S(2)}, u32[]{:S(2)}) %collective-permute-start.1) | collective-permute-done | bytes 55328 | tf_op jit(solution)/shard_map/ppermute | solution.py:27
  14.7 1.2 %collective-permute-done = bf16[1,72,384]{2,1,0:T(8,128)(2,1)S(1)} collective-permute-done((bf16[1,72,384]{2,1,0:T(8,128)(2,1)S(1)}, bf16[1,72,384]{2,1,0:T(8,128)(2,1)S(1)}, u32[]{:S(2)}, u32[]{:S(2)}) %collective-permute-start) | collective-permute-done | bytes 55328 | tf_op jit(solution)/shard_map/ppermute | solution.py:27
  15.9 1.6 %collective-permute-start.3 = (bf16[4,72,384]{2,1,0:T(8,128)(2,1)S(1)}, bf16[4,72,384]{2,1,0:T(8,128)(2,1)S(1)}, u32[]{:S(2)}, u32[]{:S(2)}) collective-permute-start(bf16[4,72,384]{2,1,0:T(8,128)(2,1)S(1)} %pad_maximum_fusion._), channel_id=1, source_target_pairs={{0,2},{1,3},{2,0},{3,1},{4,6},{5,7},{6,4},{7,5},{8,10},{9,11},{10,... | collective-permute-start | bytes 663560 | tf_op jit(solution)/shard_map/ppermute | solution.py:27
  17.5 1.5 %collective-permute-start.4 = (bf16[4,72,384]{2,1,0:T(8,128)(2,1)S(1)}, bf16[4,72,384]{2,1,0:T(8,128)(2,1)S(1)}, u32[]{:S(2)}, u32[]{:S(2)}) collective-permute-start(bf16[4,72,384]{2,1,0:T(8,128)(2,1)S(1)} %pad_maximum_fusion._), channel_id=1, source_target_pairs={{0,1},{1,0},{2,3},{3,2},{4,5},{5,4},{6,7},{7,6},{8,9},{9,8},{10,11... | collective-permute-start | bytes 663560 | tf_op jit(solution)/shard_map/ppermute | solution.py:27
  19.5 3.7 %copy-done = bf16[1,2,384,6144]{3,2,1,0:T(8,128)(2,1)S(1)} copy-done((bf16[1,2,384,6144]{3,2,1,0:T(8,128)(2,1)S(1)}, bf16[1,2,384,6144]{3,2,1,0:T(8,128)(2,1)}, u32[]{:S(2)}) %copy-start) | copy-done | bytes 9437208
  25.0 2.3 %collective-permute-done.5 = bf16[4,72,384]{2,1,0:T(8,128)(2,1)S(1)} collective-permute-done((bf16[4,72,384]{2,1,0:T(8,128)(2,1)S(1)}, bf16[4,72,384]{2,1,0:T(8,128)(2,1)S(1)}, u32[]{:S(2)}, u32[]{:S(2)}) %collective-permute-start.5) | collective-permute-done | bytes 221216 | tf_op jit(solution)/shard_map/ppermute | solution.py:27
  27.3 2.7 %shard_map.103 = (bf16[64,6144]{1,0:T(8,128)(2,1)S(1)}, f32[64,128]{1,0:T(8,128)S(1)}, f32[64,384]{1,0:T(8,128)S(1)}, bf16[64,384]{1,0:T(8,128)(2,1)S(1)}, f32[2,6144]{1,0:T(2,128)S(1)}) custom-call(s32[2]{0:T(128)S(1)} %pad_add_fusion.scalars.refs_0_, bf16[1,2,384,6144]{3,2,1,0:T(8,128)(2,1)S(1)} %shard_map.102.refs_1_, ...), custom_call_target="tpu_custom_call" | custom-call | flops 301989888 | bytes 4718592 | tf_op jit(solution)/shard_map/pallas_call | solution.py:223
  30.0 2.2 %collective-permute-start.6 = (bf16[1,64,384]{2,1,0:T(8,128)(2,1)S(1)}, bf16[1,64,384]{2,1,0:T(8,128)(2,1)S(1)}, u32[]{:S(2)}, u32[]{:S(2)}) collective-permute-start(bf16[1,64,384]{2,1,0:T(8,128)(2,1)S(1)} %bitcast.21), channel_id=1, source_target_pairs={{0,8},{1,9},{2,10},{3,11},{4,12},{5,13},{6,14},{7,15},{8,0},{9,1},... | collective-permute-start | bytes 147464 | tf_op jit(solution)/shard_map/ppermute | solution.py:27
  32.7 1.7 %collective-permute-start.8 = (bf16[1,64,384]{2,1,0:T(8,128)(2,1)S(1)}, bf16[1,64,384]{2,1,0:T(8,128)(2,1)S(1)}, u32[]{:S(2)}, u32[]{:S(2)}) collective-permute-start(bf16[1,64,384]{2,1,0:T(8,128)(2,1)S(1)} %bitcast.23), channel_id=1, source_target_pairs={{0,12},{1,13},{2,14},{3,15},{4,8},{5,9},{6,10},{7,11},{8,4},{9,5},... | collective-permute-start | bytes 147464 | tf_op jit(solution)/shard_map/ppermute | solution.py:27
  35.0 1.2 %collective-permute-done.7 = bf16[1,64,384]{2,1,0:T(8,128)(2,1)S(1)} collective-permute-done((bf16[1,64,384]{2,1,0:T(8,128)(2,1)S(1)}, bf16[1,64,384]{2,1,0:T(8,128)(2,1)S(1)}, u32[]{:S(2)}, u32[]{:S(2)}) %collective-permute-start.7) | collective-permute-done | bytes 49184 | tf_op jit(solution)/shard_map/ppermute | solution.py:27
  36.3 2.3 %collective-permute-done.8 = bf16[1,64,384]{2,1,0:T(8,128)(2,1)S(1)} collective-permute-done((bf16[1,64,384]{2,1,0:T(8,128)(2,1)S(1)}, bf16[1,64,384]{2,1,0:T(8,128)(2,1)S(1)}, u32[]{:S(2)}, u32[]{:S(2)}) %collective-permute-start.8) | collective-permute-done | bytes 49184 | tf_op jit(solution)/shard_map/ppermute | solution.py:27
  38.6 1.6 %collective-permute-start.9 = (bf16[4,64,384]{2,1,0:T(8,128)(2,1)S(1)}, bf16[4,64,384]{2,1,0:T(8,128)(2,1)S(1)}, u32[]{:S(2)}, u32[]{:S(2)}) collective-permute-start(bf16[4,64,384]{2,1,0:T(8,128)(2,1)S(1)} %pad_maximum_fusion.1), channel_id=1, source_target_pairs={{0,2},{1,3},{2,0},{3,1},{4,6},{5,7},{6,4},{7,5},{8,10},{9,11},{10,... | collective-permute-start | bytes 589832 | tf_op jit(solution)/shard_map/ppermute | solution.py:27
  40.3 1.5 %collective-permute-start.10 = (bf16[4,64,384]{2,1,0:T(8,128)(2,1)S(1)}, bf16[4,64,384]{2,1,0:T(8,128)(2,1)S(1)}, u32[]{:S(2)}, u32[]{:S(2)}) collective-permute-start(bf16[4,64,384]{2,1,0:T(8,128)(2,1)S(1)} %pad_maximum_fusion.1), channel_id=1, source_target_pairs={{0,1},{1,0},{2,3},{3,2},{4,5},{5,4},{6,7},{7,6},{8,9},{9,8},{10,11... | collective-permute-start | bytes 589832 | tf_op jit(solution)/shard_map/ppermute | solution.py:27
  42.2 2.1 %collective-permute-done.9 = bf16[4,64,384]{2,1,0:T(8,128)(2,1)S(1)} collective-permute-done((bf16[4,64,384]{2,1,0:T(8,128)(2,1)S(1)}, bf16[4,64,384]{2,1,0:T(8,128)(2,1)S(1)}, u32[]{:S(2)}, u32[]{:S(2)}) %collective-permute-start.9) | collective-permute-done | bytes 196640 | tf_op jit(solution)/shard_map/ppermute | solution.py:27
  44.4 1.5 %collective-permute-done.10 = bf16[4,64,384]{2,1,0:T(8,128)(2,1)S(1)} collective-permute-done((bf16[4,64,384]{2,1,0:T(8,128)(2,1)S(1)}, bf16[4,64,384]{2,1,0:T(8,128)(2,1)S(1)}, u32[]{:S(2)}, u32[]{:S(2)}) %collective-permute-start.10) | collective-permute-done | bytes 196640 | tf_op jit(solution)/shard_map/ppermute | solution.py:27
  46.0 2.4 %collective-permute-done.11 = bf16[4,64,384]{2,1,0:T(8,128)(2,1)S(1)} collective-permute-done((bf16[4,64,384]{2,1,0:T(8,128)(2,1)S(1)}, bf16[4,64,384]{2,1,0:T(8,128)(2,1)S(1)}, u32[]{:S(2)}, u32[]{:S(2)}) %collective-permute-start.11) | collective-permute-done | bytes 196640 | tf_op jit(solution)/shard_map/ppermute | solution.py:27
  48.4 4.3 %shard_map.104 = (bf16[64,6144]{1,0:T(8,128)(2,1)S(1)}, f32[64,128]{1,0:T(8,128)S(1)}, f32[64,384]{1,0:T(8,128)}, bf16[64,384]{1,0:T(8,128)(2,1)S(1)}, bf16[64,3...) custom-call(s32[2]{0:T(128)S(1)} %pad_add_fusion.1.refs_0_, bf16[1,2,384,6144]{3,2,1,0:T(8,128)(2,1)S(1)} %shard_map.102.refs_1_, ...), custom_call_target="tpu_custom_call" | custom-call | flops 603979776 | bytes 4718592 | tf_op jit(solution)/shard_map/pallas_call | solution.py:223
  52.8 1.2 %collective-permute-start.15 = (bf16[4,200,128]{2,1,0:T(8,128)(2,1)S(1)}, bf16[4,200,128]{2,1,0:T(8,128)(2,1)S(1)}, u32[]{:S(2)}, u32[]{:S(2)}) collective-permute-start(bf16[4,200,128]{2,1,0:T(8,128)(2,1)S(1)} %get-tuple-element.60), channel_id=1, source_target_pairs={{0,2},{1,3},{2,0},{3,1},{4,6},{5,7},{6,4},{7,5},{8,10},{9,11},{10,... | collective-permute-start | bytes 614408 | tf_op jit(solution)/shard_map/ppermute | solution.py:27
  54.0 1.5 %collective-permute-start.14 = (bf16[4,200,128]{2,1,0:T(8,128)(2,1)S(1)}, bf16[4,200,128]{2,1,0:T(8,128)(2,1)S(1)}, u32[]{:S(2)}, u32[]{:S(2)}) collective-permute-start(bf16[4,200,128]{2,1,0:T(8,128)(2,1)S(1)} %get-tuple-element.61), channel_id=1, source_target_pairs={{0,1},{1,0},{2,3},{3,2},{4,5},{5,4},{6,7},{7,6},{8,9},{9,8},{10,11... | collective-permute-start | bytes 614408 | tf_op jit(solution)/shard_map/ppermute | solution.py:27
  57.0 1.6 %collective-permute-done.15 = bf16[4,200,128]{2,1,0:T(8,128)(2,1)S(1)} collective-permute-done((bf16[4,200,128]{2,1,0:T(8,128)(2,1)S(1)}, bf16[4,200,128]{2,1,0:T(8,128)(2,1)S(1)}, u32[]{:S(2)}, u32[]{:S(2)}) %collective-permute-start.15) | collective-permute-done | bytes 204832 | tf_op jit(solution)/shard_map/ppermute | solution.py:27
  58.6 1.2 %collective-permute-done.14 = bf16[4,200,128]{2,1,0:T(8,128)(2,1)S(1)} collective-permute-done((bf16[4,200,128]{2,1,0:T(8,128)(2,1)S(1)}, bf16[4,200,128]{2,1,0:T(8,128)(2,1)S(1)}, u32[]{:S(2)}, u32[]{:S(2)}) %collective-permute-start.14) | collective-permute-done | bytes 204832 | tf_op jit(solution)/shard_map/ppermute | solution.py:27
  59.8 2.5 %collective-permute-done.13 = bf16[4,200,128]{2,1,0:T(8,128)(2,1)S(1)} collective-permute-done((bf16[4,200,128]{2,1,0:T(8,128)(2,1)S(1)}, bf16[4,200,128]{2,1,0:T(8,128)(2,1)S(1)}, u32[]{:S(2)}, u32[]{:S(2)}) %collective-permute-start.13) | collective-permute-done | bytes 204832 | tf_op jit(solution)/shard_map/ppermute | solution.py:27
  62.4 1.7 %collective-permute-start.16 = (bf16[1,200,128]{2,1,0:T(8,128)(2,1)S(1)}, bf16[1,200,128]{2,1,0:T(8,128)(2,1)S(1)}, u32[]{:S(2)}, u32[]{:S(2)}) collective-permute-start(bf16[1,200,128]{2,1,0:T(8,128)(2,1)S(1)} %get-tuple-element.64), channel_id=1, source_target_pairs={{0,12},{1,13},{2,14},{3,15},{4,8},{5,9},{6,10},{7,11},{8,4},{9,5},... | collective-permute-start | bytes 153608 | tf_op jit(solution)/shard_map/ppermute | solution.py:27
  64.2 2.7 %collective-permute-start.18 = (bf16[1,200,128]{2,1,0:T(8,128)(2,1)S(1)}, bf16[1,200,128]{2,1,0:T(8,128)(2,1)S(1)}, u32[]{:S(2)}, u32[]{:S(2)}) collective-permute-start(bf16[1,200,128]{2,1,0:T(8,128)(2,1)S(1)} %get-tuple-element.62), channel_id=1, source_target_pairs={{0,8},{1,9},{2,10},{3,11},{4,12},{5,13},{6,14},{7,15},{8,0},{9,1},... | collective-permute-start | bytes 153608 | tf_op jit(solution)/shard_map/ppermute | solution.py:27
  66.9 1.6 %collective-permute-done.16 = bf16[1,200,128]{2,1,0:T(8,128)(2,1)S(1)} collective-permute-done((bf16[1,200,128]{2,1,0:T(8,128)(2,1)S(1)}, bf16[1,200,128]{2,1,0:T(8,128)(2,1)S(1)}, u32[]{:S(2)}, u32[]{:S(2)}) %collective-permute-start.16) | collective-permute-done | bytes 51232 | tf_op jit(solution)/shard_map/ppermute | solution.py:27
  69.4 1.6 %shard_map.105 = (bf16[64,384]{1,0:T(8,128)(2,1)S(1)}, f32[4,384]{1,0:T(4,128)S(1)}, f32[4,384]{1,0:T(4,128)S(1)}, f32[4,384]{1,0:T(4,128)S(1)}, f32[4,384]{1,0:T(4,128)S(1)}, /*index=5*/f32[1,384]{1,0:T(1,128)S(1)}) custom-call(s32[2]{0:T(128)S(1)} %pad_add_fusion.scalars.refs_0_, bf16[1,2,384,6144]{3,2,1,0:T(8,128)(2,1)S(1)} %shard_map.102.refs_1_, ...), custom_call_target="tpu_custom_call" | custom-call | flops 301989888 | bytes 4718592 | tf_op jit(solution)/shard_map/pallas_call | solution.py:302
  72.8 1.5 %collective-permute-start.24 = (f32[4,384]{1,0:T(4,128)S(1)}, f32[4,384]{1,0:T(4,128)S(1)}, u32[]{:S(2)}, u32[]{:S(2)}) collective-permute-start(f32[4,384]{1,0:T(4,128)S(1)} %get-tuple-element.45), channel_id=1, source_target_pairs={{0,1},{1,0},{2,3},{3,2},{4,5},{5,4},{6,7},{7,6},{8,9},{9,8},{10,11... | collective-permute-start | bytes 18440 | tf_op jit(solution)/shard_map/ppermute | solution.py:27
  75.2 3.7 %shard_map.106 = (f32[384,3072]{1,0:T(8,128)}, f32[4,384]{1,0:T(4,128)S(1)}) custom-call(s32[2]{0:T(128)S(1)} %pad_add_fusion.scalars.refs_0_, bf16[64,384]{1,0:T(8,128)(2,1)S(1)} %get-tuple-element.38.refs_1_, bf16[64,384]{1,0:T(8,128)(2,1)S(1)} %collective-permute-done.19.refs_2_, bf16[64,384]{1,0:T(8,128)(2,1)S(1)} %get-tuple-element.39.refs_3_, ...), custom_call_target="tpu_custom_call" | custom-call | flops 301989888 | bytes 4718592 | tf_op jit(solution)/shard_map/pallas_call | solution.py:346
  78.9 2.6 %collective-permute-start.28 = (f32[1,384]{1,0:T(1,128)S(1)}, f32[1,384]{1,0:T(1,128)S(1)}, u32[]{:S(2)}, u32[]{:S(2)}) collective-permute-start(f32[1,384]{1,0:T(1,128)S(1)} %get-tuple-element.68), channel_id=1, source_target_pairs={{0,8},{1,9},{2,10},{3,11},{4,12},{5,13},{6,14},{7,15},{8,0},{9,1},... | collective-permute-start | bytes 4616 | tf_op jit(solution)/shard_map/ppermute | solution.py:27
  81.5 1.9 %collective-permute-start.26 = (f32[1,384]{1,0:T(1,128)S(1)}, f32[1,384]{1,0:T(1,128)S(1)}, u32[]{:S(2)}, u32[]{:S(2)}) collective-permute-start(f32[1,384]{1,0:T(1,128)S(1)} %get-tuple-element.67), channel_id=1, source_target_pairs={{0,12},{1,13},{2,14},{3,15},{4,8},{5,9},{6,10},{7,11},{8,4},{9,5},... | collective-permute-start | bytes 4616 | tf_op jit(solution)/shard_map/ppermute | solution.py:27
  83.3 3.7 %shard_map.107 = (f32[384,3072]{1,0:T(8,128)}, f32[1,384]{1,0:T(1,128)S(1)}) custom-call(s32[2]{0:T(128)S(1)} %pad_add_fusion.scalars.refs_0_, bf16[64,384]{1,0:T(8,128)(2,1)S(1)} %get-tuple-element.38.refs_1_, bf16[64,384]{1,0:T(8,128)(2,1)S(1)} %collective-permute-done.19.refs_2_, bf16[64,384]{1,0:T(8,128)(2,1)S(1)} %get-tuple-element.39.refs_3_, ...), custom_call_target="tpu_custom_call" | custom-call | flops 301989888 | bytes 4718592 | tf_op jit(solution)/shard_map/pallas_call | solution.py:346
  (76 shorter events, 18.4 us)
Async XLA Ops:
  0.7 0.8 copy-start.1
  5.3 7.7 %collective-permute-start.2 = (bf16[1,72,384]{2,1,0:T(8,128)(2,1)S(1)}, bf16[1,72,384]{2,1,0:T(8,128)(2,1)S(1)}, u32[]{:S(2)}, u32[]{:S(2)}) collective-permute-start(bf16[1,72,384]{2,1,0:T(8,128)(2,1)S(1)} %bitcast.25), channel_id=1, source_target_pairs={{0,12},{1,13},{2,14},{3,15},{4,8},{5,9},{6,10},{7,11},{8,4},{9,5},... | collective-permute-start | bytes 165896 | tf_op jit(solution)/shard_map/ppermute | solution.py:27
  10.5 4.2 %collective-permute-start.1 = (bf16[1,72,384]{2,1,0:T(8,128)(2,1)S(1)}, bf16[1,72,384]{2,1,0:T(8,128)(2,1)S(1)}, u32[]{:S(2)}, u32[]{:S(2)}) collective-permute-start(bf16[1,72,384]{2,1,0:T(8,128)(2,1)S(1)} %bitcast.26), channel_id=1, source_target_pairs={{0,4},{1,5},{2,6},{3,7},{4,0},{5,1},{6,2},{7,3},{8,12},{9,13},{10,... | collective-permute-start | bytes 165896 | tf_op jit(solution)/shard_map/ppermute | solution.py:27
  10.5 5.4 %collective-permute-start = (bf16[1,72,384]{2,1,0:T(8,128)(2,1)S(1)}, bf16[1,72,384]{2,1,0:T(8,128)(2,1)S(1)}, u32[]{:S(2)}, u32[]{:S(2)}) collective-permute-start(bf16[1,72,384]{2,1,0:T(8,128)(2,1)S(1)} %bitcast.27), channel_id=1, source_target_pairs={{0,8},{1,9},{2,10},{3,11},{4,12},{5,13},{6,14},{7,15},{8,0},{9,1},... | collective-permute-start | bytes 165896 | tf_op jit(solution)/shard_map/ppermute | solution.py:27
  15.9 8.4 %collective-permute-start.3 = (bf16[4,72,384]{2,1,0:T(8,128)(2,1)S(1)}, bf16[4,72,384]{2,1,0:T(8,128)(2,1)S(1)}, u32[]{:S(2)}, u32[]{:S(2)}) collective-permute-start(bf16[4,72,384]{2,1,0:T(8,128)(2,1)S(1)} %pad_maximum_fusion._), channel_id=1, source_target_pairs={{0,2},{1,3},{2,0},{3,1},{4,6},{5,7},{6,4},{7,5},{8,10},{9,11},{10,... | collective-permute-start | bytes 663560 | tf_op jit(solution)/shard_map/ppermute | solution.py:27
  17.5 7.5 %collective-permute-start.4 = (bf16[4,72,384]{2,1,0:T(8,128)(2,1)S(1)}, bf16[4,72,384]{2,1,0:T(8,128)(2,1)S(1)}, u32[]{:S(2)}, u32[]{:S(2)}) collective-permute-start(bf16[4,72,384]{2,1,0:T(8,128)(2,1)S(1)} %pad_maximum_fusion._), channel_id=1, source_target_pairs={{0,1},{1,0},{2,3},{3,2},{4,5},{5,4},{6,7},{7,6},{8,9},{9,8},{10,11... | collective-permute-start | bytes 663560 | tf_op jit(solution)/shard_map/ppermute | solution.py:27
  19.0 8.3 %collective-permute-start.5 = (bf16[4,72,384]{2,1,0:T(8,128)(2,1)S(1)}, bf16[4,72,384]{2,1,0:T(8,128)(2,1)S(1)}, u32[]{:S(2)}, u32[]{:S(2)}) collective-permute-start(bf16[4,72,384]{2,1,0:T(8,128)(2,1)S(1)} %pad_maximum_fusion._), channel_id=1, source_target_pairs={{0,3},{1,2},{2,1},{3,0},{4,7},{5,6},{6,5},{7,4},{8,11},{9,10},{10,... | collective-permute-start | bytes 663560 | tf_op jit(solution)/shard_map/ppermute | solution.py:27
  19.5 3.7 %copy-start = (bf16[1,2,384,6144]{3,2,1,0:T(8,128)(2,1)S(1)}, bf16[1,2,384,6144]{3,2,1,0:T(8,128)(2,1)}, u32[]{:S(2)}) copy-start(bf16[1,2,384,6144]{3,2,1,0:T(8,128)(2,1)} %weights.1) | copy-start | bytes 28311556
  30.0 5.1 %collective-permute-start.6 = (bf16[1,64,384]{2,1,0:T(8,128)(2,1)S(1)}, bf16[1,64,384]{2,1,0:T(8,128)(2,1)S(1)}, u32[]{:S(2)}, u32[]{:S(2)}) collective-permute-start(bf16[1,64,384]{2,1,0:T(8,128)(2,1)S(1)} %bitcast.21), channel_id=1, source_target_pairs={{0,8},{1,9},{2,10},{3,11},{4,12},{5,13},{6,14},{7,15},{8,0},{9,1},... | collective-permute-start | bytes 147464 | tf_op jit(solution)/shard_map/ppermute | solution.py:27
  32.2 4.1 %collective-permute-start.7 = (bf16[1,64,384]{2,1,0:T(8,128)(2,1)S(1)}, bf16[1,64,384]{2,1,0:T(8,128)(2,1)S(1)}, u32[]{:S(2)}, u32[]{:S(2)}) collective-permute-start(bf16[1,64,384]{2,1,0:T(8,128)(2,1)S(1)} %bitcast.22), channel_id=1, source_target_pairs={{0,4},{1,5},{2,6},{3,7},{4,0},{5,1},{6,2},{7,3},{8,12},{9,13},{10,... | collective-permute-start | bytes 147464 | tf_op jit(solution)/shard_map/ppermute | solution.py:27
  32.7 5.9 %collective-permute-start.8 = (bf16[1,64,384]{2,1,0:T(8,128)(2,1)S(1)}, bf16[1,64,384]{2,1,0:T(8,128)(2,1)S(1)}, u32[]{:S(2)}, u32[]{:S(2)}) collective-permute-start(bf16[1,64,384]{2,1,0:T(8,128)(2,1)S(1)} %bitcast.23), channel_id=1, source_target_pairs={{0,12},{1,13},{2,14},{3,15},{4,8},{5,9},{6,10},{7,11},{8,4},{9,5},... | collective-permute-start | bytes 147464 | tf_op jit(solution)/shard_map/ppermute | solution.py:27
  38.6 5.7 %collective-permute-start.9 = (bf16[4,64,384]{2,1,0:T(8,128)(2,1)S(1)}, bf16[4,64,384]{2,1,0:T(8,128)(2,1)S(1)}, u32[]{:S(2)}, u32[]{:S(2)}) collective-permute-start(bf16[4,64,384]{2,1,0:T(8,128)(2,1)S(1)} %pad_maximum_fusion.1), channel_id=1, source_target_pairs={{0,2},{1,3},{2,0},{3,1},{4,6},{5,7},{6,4},{7,5},{8,10},{9,11},{10,... | collective-permute-start | bytes 589832 | tf_op jit(solution)/shard_map/ppermute | solution.py:27
  40.3 5.7 %collective-permute-start.10 = (bf16[4,64,384]{2,1,0:T(8,128)(2,1)S(1)}, bf16[4,64,384]{2,1,0:T(8,128)(2,1)S(1)}, u32[]{:S(2)}, u32[]{:S(2)}) collective-permute-start(bf16[4,64,384]{2,1,0:T(8,128)(2,1)S(1)} %pad_maximum_fusion.1), channel_id=1, source_target_pairs={{0,1},{1,0},{2,3},{3,2},{4,5},{5,4},{6,7},{7,6},{8,9},{9,8},{10,11... | collective-permute-start | bytes 589832 | tf_op jit(solution)/shard_map/ppermute | solution.py:27
  41.8 6.6 %collective-permute-start.11 = (bf16[4,64,384]{2,1,0:T(8,128)(2,1)S(1)}, bf16[4,64,384]{2,1,0:T(8,128)(2,1)S(1)}, u32[]{:S(2)}, u32[]{:S(2)}) collective-permute-start(bf16[4,64,384]{2,1,0:T(8,128)(2,1)S(1)} %pad_maximum_fusion.1), channel_id=1, source_target_pairs={{0,3},{1,2},{2,1},{3,0},{4,7},{5,6},{6,5},{7,4},{8,11},{9,10},{10,... | collective-permute-start | bytes 589832 | tf_op jit(solution)/shard_map/ppermute | solution.py:27
  52.8 5.8 %collective-permute-start.15 = (bf16[4,200,128]{2,1,0:T(8,128)(2,1)S(1)}, bf16[4,200,128]{2,1,0:T(8,128)(2,1)S(1)}, u32[]{:S(2)}, u32[]{:S(2)}) collective-permute-start(bf16[4,200,128]{2,1,0:T(8,128)(2,1)S(1)} %get-tuple-element.60), channel_id=1, source_target_pairs={{0,2},{1,3},{2,0},{3,1},{4,6},{5,7},{6,4},{7,5},{8,10},{9,11},{10,... | collective-permute-start | bytes 614408 | tf_op jit(solution)/shard_map/ppermute | solution.py:27
  54.0 5.8 %collective-permute-start.14 = (bf16[4,200,128]{2,1,0:T(8,128)(2,1)S(1)}, bf16[4,200,128]{2,1,0:T(8,128)(2,1)S(1)}, u32[]{:S(2)}, u32[]{:S(2)}) collective-permute-start(bf16[4,200,128]{2,1,0:T(8,128)(2,1)S(1)} %get-tuple-element.61), channel_id=1, source_target_pairs={{0,1},{1,0},{2,3},{3,2},{4,5},{5,4},{6,7},{7,6},{8,9},{9,8},{10,11... | collective-permute-start | bytes 614408 | tf_op jit(solution)/shard_map/ppermute | solution.py:27
  55.5 6.8 %collective-permute-start.13 = (bf16[4,200,128]{2,1,0:T(8,128)(2,1)S(1)}, bf16[4,200,128]{2,1,0:T(8,128)(2,1)S(1)}, u32[]{:S(2)}, u32[]{:S(2)}) collective-permute-start(bf16[4,200,128]{2,1,0:T(8,128)(2,1)S(1)} %get-tuple-element.59), channel_id=1, source_target_pairs={{0,3},{1,2},{2,1},{3,0},{4,7},{5,6},{6,5},{7,4},{8,11},{9,10},{10,... | collective-permute-start | bytes 614408 | tf_op jit(solution)/shard_map/ppermute | solution.py:27
  56.3 15.3 %collective-permute-start.20 = (bf16[64,384]{1,0:T(8,128)(2,1)S(1)}, bf16[64,384]{1,0:T(8,128)(2,1)S(1)}, u32[]{:S(2)}, u32[]{:S(2)}) collective-permute-start(bf16[64,384]{1,0:T(8,128)(2,1)S(1)} %get-tuple-element.39.refs_3_), channel_id=1, source_target_pairs={{0,16},{16,0},{1,17},{17,1},{2,18},{18,2},{3,19},{19,3},{4,20},{20... | collective-permute-start | bytes 147464 | tf_op jit(solution)/shard_map/ppermute | solution.py:32
  56.5 17.9 %collective-permute-start.21 = (bf16[64,3072]{1,0:T(8,128)(2,1)S(1)}, bf16[64,3072]{1,0:T(8,128)(2,1)S(1)}, u32[]{:S(2)}, u32[]{:S(2)}) collective-permute-start(bf16[64,3072]{1,0:T(8,128)(2,1)S(1)} %get-tuple-element.56), channel_id=1, source_target_pairs={{0,16},{16,0},{1,17},{17,1},{2,18},{18,2},{3,19},{19,3},{4,20},{20... | collective-permute-start | bytes 1179656 | tf_op jit(solution)/shard_map/ppermute | solution.py:32
  62.4 6.1 %collective-permute-start.16 = (bf16[1,200,128]{2,1,0:T(8,128)(2,1)S(1)}, bf16[1,200,128]{2,1,0:T(8,128)(2,1)S(1)}, u32[]{:S(2)}, u32[]{:S(2)}) collective-permute-start(bf16[1,200,128]{2,1,0:T(8,128)(2,1)S(1)} %get-tuple-element.64), channel_id=1, source_target_pairs={{0,12},{1,13},{2,14},{3,15},{4,8},{5,9},{6,10},{7,11},{8,4},{9,5},... | collective-permute-start | bytes 153608 | tf_op jit(solution)/shard_map/ppermute | solution.py:27
  64.2 5.2 %collective-permute-start.17 = (bf16[1,200,128]{2,1,0:T(8,128)(2,1)S(1)}, bf16[1,200,128]{2,1,0:T(8,128)(2,1)S(1)}, u32[]{:S(2)}, u32[]{:S(2)}) collective-permute-start(bf16[1,200,128]{2,1,0:T(8,128)(2,1)S(1)} %get-tuple-element.63), channel_id=1, source_target_pairs={{0,4},{1,5},{2,6},{3,7},{4,0},{5,1},{6,2},{7,3},{8,12},{9,13},{10,... | collective-permute-start | bytes 153608 | tf_op jit(solution)/shard_map/ppermute | solution.py:27
  64.2 5.2 %collective-permute-start.18 = (bf16[1,200,128]{2,1,0:T(8,128)(2,1)S(1)}, bf16[1,200,128]{2,1,0:T(8,128)(2,1)S(1)}, u32[]{:S(2)}, u32[]{:S(2)}) collective-permute-start(bf16[1,200,128]{2,1,0:T(8,128)(2,1)S(1)} %get-tuple-element.62), channel_id=1, source_target_pairs={{0,8},{1,9},{2,10},{3,11},{4,12},{5,13},{6,14},{7,15},{8,0},{9,1},... | collective-permute-start | bytes 153608 | tf_op jit(solution)/shard_map/ppermute | solution.py:27
  71.0 1.8 %collective-permute-start.19 = (bf16[64,384]{1,0:T(8,128)(2,1)S(1)}, bf16[64,384]{1,0:T(8,128)(2,1)S(1)}, u32[]{:S(2)}, u32[]{:S(2)}) collective-permute-start(bf16[64,384]{1,0:T(8,128)(2,1)S(1)} %get-tuple-element.38.refs_1_), channel_id=1, source_target_pairs={{0,16},{16,0},{1,17},{17,1},{2,18},{18,2},{3,19},{19,3},{4,20},{20... | collective-permute-start | bytes 147464 | tf_op jit(solution)/shard_map/ppermute | solution.py:32
  71.1 16.1 %collective-permute-start.12 = (bf16[64,384]{1,0:T(8,128)(2,1)S(1)}, bf16[64,384]{1,0:T(8,128)(2,1)S(1)}, u32[]{:S(2)}, u32[]{:S(2)}) collective-permute-start(bf16[64,384]{1,0:T(8,128)(2,1)S(1)} %get-tuple-element.33), channel_id=1, source_target_pairs={{0,16},{16,0},{1,17},{17,1},{2,18},{18,2},{3,19},{19,3},{4,20},{20... | collective-permute-start | bytes 147464 | tf_op jit(solution)/shard_map/ppermute | solution.py:32
  71.6 11.8 %collective-permute-start.22 = (bf16[64,3072]{1,0:T(8,128)(2,1)S(1)}, bf16[64,3072]{1,0:T(8,128)(2,1)S(1)}, u32[]{:S(2)}, u32[]{:S(2)}) collective-permute-start(bf16[64,3072]{1,0:T(8,128)(2,1)S(1)} %get-tuple-element.55), channel_id=1, source_target_pairs={{0,16},{16,0},{1,17},{17,1},{2,18},{18,2},{3,19},{19,3},{4,20},{20... | collective-permute-start | bytes 1179656 | tf_op jit(solution)/shard_map/ppermute | solution.py:32
  71.7 7.2 %collective-permute-start.25 = (f32[4,384]{1,0:T(4,128)S(1)}, f32[4,384]{1,0:T(4,128)S(1)}, u32[]{:S(2)}, u32[]{:S(2)}) collective-permute-start(f32[4,384]{1,0:T(4,128)S(1)} %get-tuple-element.46), channel_id=1, source_target_pairs={{0,2},{1,3},{2,0},{3,1},{4,6},{5,7},{6,4},{7,5},{8,10},{9,11},{10,... | collective-permute-start | bytes 18440 | tf_op jit(solution)/shard_map/ppermute | solution.py:27
  72.8 6.0 %collective-permute-start.24 = (f32[4,384]{1,0:T(4,128)S(1)}, f32[4,384]{1,0:T(4,128)S(1)}, u32[]{:S(2)}, u32[]{:S(2)}) collective-permute-start(f32[4,384]{1,0:T(4,128)S(1)} %get-tuple-element.45), channel_id=1, source_target_pairs={{0,1},{1,0},{2,3},{3,2},{4,5},{5,4},{6,7},{7,6},{8,9},{9,8},{10,11... | collective-permute-start | bytes 18440 | tf_op jit(solution)/shard_map/ppermute | solution.py:27
  74.3 4.5 %collective-permute-start.23 = (f32[4,384]{1,0:T(4,128)S(1)}, f32[4,384]{1,0:T(4,128)S(1)}, u32[]{:S(2)}, u32[]{:S(2)}) collective-permute-start(f32[4,384]{1,0:T(4,128)S(1)} %get-tuple-element.44), channel_id=1, source_target_pairs={{0,3},{1,2},{2,1},{3,0},{4,7},{5,6},{6,5},{7,4},{8,11},{9,10},{10,... | collective-permute-start | bytes 18440 | tf_op jit(solution)/shard_map/ppermute | solution.py:27
  78.9 8.2 %collective-permute-start.28 = (f32[1,384]{1,0:T(1,128)S(1)}, f32[1,384]{1,0:T(1,128)S(1)}, u32[]{:S(2)}, u32[]{:S(2)}) collective-permute-start(f32[1,384]{1,0:T(1,128)S(1)} %get-tuple-element.68), channel_id=1, source_target_pairs={{0,8},{1,9},{2,10},{3,11},{4,12},{5,13},{6,14},{7,15},{8,0},{9,1},... | collective-permute-start | bytes 4616 | tf_op jit(solution)/shard_map/ppermute | solution.py:27
  81.5 5.6 %collective-permute-start.27 = (f32[1,384]{1,0:T(1,128)S(1)}, f32[1,384]{1,0:T(1,128)S(1)}, u32[]{:S(2)}, u32[]{:S(2)}) collective-permute-start(f32[1,384]{1,0:T(1,128)S(1)} %get-tuple-element.69), channel_id=1, source_target_pairs={{0,4},{1,5},{2,6},{3,7},{4,0},{5,1},{6,2},{7,3},{8,12},{9,13},{10,... | collective-permute-start | bytes 4616 | tf_op jit(solution)/shard_map/ppermute | solution.py:27
  81.5 5.6 %collective-permute-start.26 = (f32[1,384]{1,0:T(1,128)S(1)}, f32[1,384]{1,0:T(1,128)S(1)}, u32[]{:S(2)}, u32[]{:S(2)}) collective-permute-start(f32[1,384]{1,0:T(1,128)S(1)} %get-tuple-element.67), channel_id=1, source_target_pairs={{0,12},{1,13},{2,14},{3,15},{4,8},{5,9},{6,10},{7,11},{8,4},{9,5},... | collective-permute-start | bytes 4616 | tf_op jit(solution)/shard_map/ppermute | solution.py:27
  87.1 1.2 %collective-permute-start.29 = (f32[1,384]{1,0:T(1,128)S(1)}, f32[1,384]{1,0:T(1,128)S(1)}, u32[]{:S(2)}, u32[]{:S(2)}) collective-permute-start(f32[1,384]{1,0:T(1,128)S(1)} %get-tuple-element.51), channel_id=1, source_target_pairs={{0,16},{16,0},{1,17},{17,1},{2,18},{18,2},{3,19},{19,3},{4,20},{20... | collective-permute-start | bytes 4616 | tf_op jit(solution)/shard_map/ppermute | solution.py:32
  (4 other events, 3.1 us)

commit v4 on v3

--- a/solution.py
+++ b/solution.py
@@ -18,6 +18,7 @@
 VMEM_LIMIT = 32 * 1024 * 1024
 
 VMEM = pl.BlockSpec(memory_space=pltpu.VMEM)
+HBM = pl.BlockSpec(memory_space=pltpu.HBM)
 ANY = pl.BlockSpec(memory_space=pl.ANY)
 SMEM = pl.BlockSpec(memory_space=pltpu.SMEM)
 
@@ -38,6 +39,7 @@
     while bits:
         pair, bits = bits[:2], bits[2:]
         groups.append(tuple(pair) if len(pair) == 1 else (pair[0], pair[1], pair[0] ^ pair[1]))
+    groups[0] = groups[0][::-1]
     return groups
 
 
@@ -60,6 +62,10 @@
 def reduce_round(held, group):
     sent = [from_xor(held[n + 1], d) for n, d in enumerate(group)]
     return [held[0]] + sent
+
+
+def in_hbm(value):
+    return pltpu.with_memory_space_constraint(value, pltpu.HBM)
 
 
 def gelu_and_slope(z):
@@ -319,45 +325,54 @@
     )(*operands)
 
 
-def weight_grad_kernel(take_early, *refs):
-    scalars, early, early_other, late, late_other, u_own, u_other, _, out, order, depth = refs
-    tokens = early.shape[0]
-
-    @pl.when(pl.program_id(0) == 0)
-    def _():
-        pick = scalars[1] == (0 if take_early else 1)
-        mine = jnp.where(pick, early[...], late[...])
-        theirs = jnp.where(pick, early_other[...], late_other[...])
-        depth[...] = jnp.concatenate([mine, theirs], axis=0).T
-        order[...] = jnp.zeros_like(order)
-
-    both = jnp.concatenate([u_own[...], u_other[...]], axis=0)
-    out[...] = jnp.dot(depth[...], both, preferred_element_type=F32)
-
-
-def weight_grad_call(scalars, first, dz_a, dz_a_other, dz_b, dz_b_other, u_own, u_other, after):
-    tokens, rows = dz_a.shape
+def weight_grad_kernel(first_at, tiles, kept, *refs):
+    scalars, dz_own, dz_other, u_own, u_other, _ = refs[:6]
+    first, second, order, result, sems = refs[6 + kept :]
+    tile = u_own.shape[1] // tiles
+    depth = jnp.concatenate([dz_own[...], dz_other[...]], axis=0).T
+    order[...] = jnp.zeros_like(order)
+
+    def copy(n, target):
+        columns = pl.ds(n * tile, tile)
+        return pltpu.make_async_copy(result.at[:, columns], target.at[:, columns], sems.at[n])
+
+    for n in range(tiles):
+        columns = slice(n * tile, (n + 1) * tile)
+        both = jnp.concatenate([u_own[:, columns], u_other[:, columns]], axis=0)
+        result[:, columns] = jnp.dot(depth, both, preferred_element_type=F32)
+
+        @pl.when(scalars[1] == first_at)
+        def _():
+            copy(n, first).start()
+
+        @pl.when(scalars[1] != first_at)
+        def _():
+            copy(n, second).start()
+
+    for n in range(tiles):
+        copy(n, first).wait()
+
+
+def weight_grad_call(scalars, first_at, dz_own, dz_other, u_own, u_other, after, kept):
+    tokens, rows = dz_own.shape
     columns = u_own.shape[1]
-    steps = 4
-    tile = columns // steps
-    whole = pl.BlockSpec((tokens, rows), lambda i: (0, 0))
-    narrow = pl.BlockSpec((tokens, tile), lambda i: (0, i))
-    small = pl.BlockSpec(after.shape, lambda i: (0,) * after.ndim)
+    tiles = 4
     return pl.pallas_call(
-        functools.partial(weight_grad_kernel, first),
-        grid=(steps,),
+        functools.partial(weight_grad_kernel, first_at, tiles, len(kept)),
         out_shape=[
+            jax.ShapeDtypeStruct((rows, columns), F32),
             jax.ShapeDtypeStruct((rows, columns), F32),
             jax.ShapeDtypeStruct(after.shape, F32),
         ],
-        in_specs=[SMEM] + [whole] * 4 + [narrow] * 2 + [small],
-        out_specs=[pl.BlockSpec((rows, tile), lambda i: (0, i)), small],
-        scratch_shapes=[pltpu.VMEM((rows, 2 * tokens), BF16)],
+        in_specs=[SMEM] + [VMEM] * 5 + [HBM] * len(kept),
+        out_specs=[HBM, HBM, VMEM],
+        input_output_aliases={6 + n: n for n in range(len(kept))},
+        scratch_shapes=[pltpu.VMEM((rows, columns), F32), pltpu.SemaphoreType.DMA((tiles,))],
         compiler_params=pltpu.CompilerParams(vmem_limit_bytes=VMEM_LIMIT),
         cost_estimate=pl.CostEstimate(
             flops=4 * tokens * rows * columns, bytes_accessed=4 * rows * columns, transcendentals=0
         ),
-    )(scalars, dz_a, dz_a_other, dz_b, dz_b_other, u_own, u_other, after)
+    )(scalars, dz_own, dz_other, u_own, u_other, after, *kept)
 
 
 def load_kernel(weights, _, held, sems):
@@ -374,14 +389,14 @@
     return pl.pallas_call(
         load_kernel,
         out_shape=jax.ShapeDtypeStruct(weights.shape, weights.dtype),
-        in_specs=[ANY, ANY],
+        in_specs=[HBM, ANY],
         out_specs=VMEM,
         scratch_shapes=[pltpu.SemaphoreType.DMA((2,))],
         compiler_params=pltpu.CompilerParams(vmem_limit_bytes=VMEM_LIMIT),
         cost_estimate=pl.CostEstimate(
             flops=0, bytes_accessed=2 * weights.size, transcendentals=0
         ),
-    )(weights, after)
+    )(in_hbm(weights), after)
 
 
 def pack_kernel(scalars, *refs):
@@ -425,11 +440,11 @@
             jax.ShapeDtypeStruct((tokens, block), BF16),
             jax.ShapeDtypeStruct((tokens + PAD_ROWS, block), BF16),
         ],
-        in_specs=[SMEM] + [ANY] * 5,
+        in_specs=[SMEM] + [HBM] * 5,
         out_specs=[VMEM] * 3,
         scratch_shapes=[pltpu.VMEM(gains.shape, F32), pltpu.SemaphoreType.DMA((3,))],
         compiler_params=pltpu.CompilerParams(vmem_limit_bytes=VMEM_LIMIT),
-    )(scalars, down_input, up_input, down_cot, up_cot, gains)
+    )(scalars, *map(in_hbm, (down_input, up_input, down_cot, up_cot, gains)))
 
 
 def keep_live(live, record, previous):
@@ -454,7 +469,7 @@
     wide = block << merged
     bit_count = seq_size.bit_length() - 1
     groups = bit_groups(merged, bit_count)
-    back_groups = [group[::-1] for group in groups[::-1]]
+    back_groups = [group[::-1] for group in groups[:0:-1]] + groups[:1]
     offsets = [o >> merged for o in offsets_of(groups)]
     send_order = [o >> merged for o in offsets_of(back_groups[::-1])]
     me = (seq_index >> merged).astype(jnp.int32)
@@ -501,19 +516,21 @@
         route = [(low, new), (sections - 1 - low, sections - 1 - new)]
         return lax.ppermute(value, "section", route)
 
-    def reduced(sent):
-        parts = None
+    def reduced(sent, beside=None):
+        parts = grads = None
         for n, group in enumerate(back_groups):
             sent = sent.reshape((len(group) + 1, -1) + sent.shape[1:])
             parts = reduce_round(sent, group)
             if n + 1 < len(back_groups):
+                if n == 0 and beside is not None:
+                    parts, grads = lax.optimization_barrier((parts, beside()))
                 total = functools.reduce(jnp.add, [p.astype(F32) for p in parts])
                 sent = total.astype(BF16)
                 kept = total[0]
         parts = [kept if len(back_groups) > 1 else parts[0][0].astype(F32)] + [
             p[0] for p in parts[1:]
         ]
-        return parts
+        return parts, grads
 
     def finished(parts):
         total = functools.reduce(jnp.add, [p.astype(F32) for p in parts])
@@ -570,10 +587,10 @@
     y_other = swapped(y_b)
     down_out = jnp.where(lower, y_a, y_other)
     up_out = jnp.where(lower, y_other, y_a)
-    u_first = jnp.where(lower, u_a[:, :half], u_b[:, :half])
-    u_second = jnp.where(lower, u_b[:, half:], u_a[:, half:])
-    other_first = swapped(jnp.where(lower, u_b[:, :half], u_a[:, :half]))
-    other_second = swapped(jnp.where(lower, u_a[:, half:], u_b[:, half:]))
+    needed_a = jnp.where(lower, u_a[:, :half], u_a[:, half:])
+    needed_b = jnp.where(lower, u_b[:, half:], u_b[:, :half])
+    other_a = swapped(jnp.where(lower, u_a[:, half:], u_a[:, :half]))
+    other_b = swapped(jnp.where(lower, u_b[:, :half], u_b[:, half:]))
     dz_a = dz_b = gain_b = gain_a = None
     for step in reversed(range(1, sections)):
         source, _, _, stat, z, _ = second_record if step >= middle else first_record
@@ -591,12 +608,27 @@
                 wide,
                 False,
             )
-        parts = reduced(sent)
         gain_row = lax.dynamic_slice_in_dim(own_gains, index_at(step), 1, axis=0)
         if step >= middle:
             dz_b = keep_live(live_at(step), dz, dz_b)
         else:
             dz_a = keep_live(live_at(step), dz, dz_a)
+        beside = None
+        if step == middle:
+            beside = functools.partial(
+                weight_grad_call,
+                scalars_at(0),
+                1,
+                dz_b,
+                swapped(dz_b),
+                needed_b,
+                other_b,
+                jnp.zeros((8, LANES)),
+                (),
+            )
+        parts, grads = reduced(sent, beside)
+        if grads is not None:
+            early_grads = grads[:2]
         finish = None
         if sections == 2 and not merged:
             finish = (parts, (source, stat, gain_row))
@@ -638,25 +670,16 @@
         gain_b = result[-1]
     dz_a = keep_live(live_at(0), dz, dz_a)
     dz_a_other = swapped(dz_a)
-    dz_b_other = swapped(dz_b)
-    dz_all = (dz_a, dz_a_other, dz_b, dz_b_other)
-    grads = []
-    halves = [(True, u_first, other_first), (False, u_second, other_second)]
     for n, group in enumerate(back_groups):
         if n:
             gain_parts = gain_parts.reshape((len(group) + 1, -1) + gain_parts.shape[1:])
         parts = reduce_round(gain_parts, group)
-        if halves:
-            first, mine, theirs = halves.pop(0)
-            grad_half, token = weight_grad_call(
-                scalars_at(0), first, *dz_all, mine, theirs, parts[0]
+        if n == 0:
+            grad_first, grad_second, token = weight_grad_call(
+                scalars_at(0), 0, dz_a, dz_a_other, needed_a, other_a, parts[0], early_grads
             )
-            grads.append(grad_half)
             parts.append(token)
         gain_parts = functools.reduce(jnp.add, parts)
-    for first, mine, theirs in halves:
-        grads.append(weight_grad_call(scalars_at(0), first, *dz_all, mine, theirs, token)[0])
-    grad_first, grad_second = grads
     gain = gain_parts.reshape(1, wide)
     for bit in reversed(range(merged)):
         mine, theirs = own_part(gain, gain.shape[1] // 2, bit)

time: 89.3 us -> 87.4 us (0.979)
  local copies, waits for them, and re-layouts: 8.61 us -> 1.08 us
  Pallas kernels: 17.4 us -> 20.7 us
  waiting for transfers between devices: 25.8 us -> 28.7 us
    unnamed x24 -> x12, local copies, waits for them, and re-layouts: 7.78 us -> 0.23 us
    pallas_call x1, Pallas kernels: 0.65 us -> 3.79 us  [load_call(): pl.pallas_call(load_kernel, out_shape=jax.ShapeDtypeStruct(weights.shape,...]
    ppermute x24, waiting for transfers between devices: 25.3 us -> 28.2 us  [from_xor(): return lax.ppermute(value, 'seq', [(i, i ^ distance) for i in range(size)])]
  transfers between devices with their start and end apart: 30 -> 30, of which waited for: 18 -> 20; matrix products, arithmetic and copies ran while one was open for 2% -> 2% of each run, Pallas kernels for 11% -> 14%
where the time goes in v4:
time: 87.4 us; the launch traced here: 87.2 us
  starting transfers between devices  34 us (39%)
  waiting for transfers between devices  28.7 us (33%)
  Pallas kernels  20.7 us (24%)
  other arithmetic  1.68 us (2%)
  local copies, waits for them, and re-layouts  1.08 us (1%)
  between operations  0.92 us (1%)
    ppermute x24, starting transfers between devices, from_xor(): return lax.ppermute(value, 'seq', [(i, i ^ distance) for i in range(size)])  33.3 us
    ppermute x24, waiting for transfers between devices, from_xor(): return lax.ppermute(value, 'seq', [(i, i ^ distance) for i in range(size)])  28.2 us
    pallas_call x2, Pallas kernels, section_call(): pl.pallas_call(functools.partial(section_kernel, offsets, (tokens, wide,...  7.02 us
    pallas_call x2, Pallas kernels, weight_grad_call(): pl.pallas_call(functools.partial(weight_grad_kernel, first_at, tiles, len...  6.88 us
    pallas_call x1, Pallas kernels, load_call(): pl.pallas_call(load_kernel, out_shape=jax.ShapeDtypeStruct(weights.shape,...  3.79 us
  transfers between devices with their start and end apart: 30, of which 20 were waited for; matrix products, arithmetic and copies ran while one was open for 2% of the time, Pallas kernels for 14%

profile of v4, /device:TPU:0, one launch (start us, length us, event | category | flops | bytes accessed | tf_op | source)
XLA Modules:
  0.0 87.2 jit_solution(9847964397580228666)
XLA Ops:
  0.7 1.4 %shard_map.101 = (bf16[64,384]{1,0:T(8,128)(2,1)S(1)}, bf16[64,384]{1,0:T(8,128)(2,1)S(1)}, bf16[72,384]{1,0:T(8,128)(2,1)S(1)}) custom-call(s32[2]{0:T(128)S(1)} %pad_add_fusion.scalars.refs_0_, bf16[64,384]{1,0:T(8,128)(2,1)} %refs_0_.1, bf16[64,384]{1,0:T(8,128)(2,1)} %refs_1_.1, bf16[64,384]{1,0:T(8,128)(2,1)} %refs_2_.1, bf16[64,384]{1,0:T(8,128)(2,1)} %refs_3_.1, ...), custom_call_target="tpu_custom_call" | custom-call | tf_op jit(solution)/shard_map/pallas_call | solution.py:436
  2.1 5.1 %collective-permute-start = (bf16[1,72,384]{2,1,0:T(8,128)(2,1)S(1)}, bf16[1,72,384]{2,1,0:T(8,128)(2,1)S(1)}, u32[]{:S(2)}, u32[]{:S(2)}) collective-permute-start(bf16[1,72,384]{2,1,0:T(8,128)(2,1)S(1)} %bitcast.25), channel_id=1, source_target_pairs={{0,12},{1,13},{2,14},{3,15},{4,8},{5,9},{6,10},{7,11},{8,4},{9,5},... | collective-permute-start | bytes 165896 | tf_op jit(solution)/shard_map/ppermute | solution.py:28
  8.7 1.2 %collective-permute-done = bf16[1,72,384]{2,1,0:T(8,128)(2,1)S(1)} collective-permute-done((bf16[1,72,384]{2,1,0:T(8,128)(2,1)S(1)}, bf16[1,72,384]{2,1,0:T(8,128)(2,1)S(1)}, u32[]{:S(2)}, u32[]{:S(2)}) %collective-permute-start) | collective-permute-done | bytes 55328 | tf_op jit(solution)/shard_map/ppermute | solution.py:28
  9.8 1.7 %collective-permute-done.1 = bf16[1,72,384]{2,1,0:T(8,128)(2,1)S(1)} collective-permute-done((bf16[1,72,384]{2,1,0:T(8,128)(2,1)S(1)}, bf16[1,72,384]{2,1,0:T(8,128)(2,1)S(1)}, u32[]{:S(2)}, u32[]{:S(2)}) %collective-permute-start.1) | collective-permute-done | bytes 55328 | tf_op jit(solution)/shard_map/ppermute | solution.py:28
  11.5 1.2 %collective-permute-done.2 = bf16[1,72,384]{2,1,0:T(8,128)(2,1)S(1)} collective-permute-done((bf16[1,72,384]{2,1,0:T(8,128)(2,1)S(1)}, bf16[1,72,384]{2,1,0:T(8,128)(2,1)S(1)}, u32[]{:S(2)}, u32[]{:S(2)}) %collective-permute-start.2) | collective-permute-done | bytes 55328 | tf_op jit(solution)/shard_map/ppermute | solution.py:28
  12.7 1.6 %collective-permute-start.3 = (bf16[4,72,384]{2,1,0:T(8,128)(2,1)S(1)}, bf16[4,72,384]{2,1,0:T(8,128)(2,1)S(1)}, u32[]{:S(2)}, u32[]{:S(2)}) collective-permute-start(bf16[4,72,384]{2,1,0:T(8,128)(2,1)S(1)} %pad_maximum_fusion._), channel_id=1, source_target_pairs={{0,2},{1,3},{2,0},{3,1},{4,6},{5,7},{6,4},{7,5},{8,10},{9,11},{10,... | collective-permute-start | bytes 663560 | tf_op jit(solution)/shard_map/ppermute | solution.py:28
  14.3 1.5 %collective-permute-start.4 = (bf16[4,72,384]{2,1,0:T(8,128)(2,1)S(1)}, bf16[4,72,384]{2,1,0:T(8,128)(2,1)S(1)}, u32[]{:S(2)}, u32[]{:S(2)}) collective-permute-start(bf16[4,72,384]{2,1,0:T(8,128)(2,1)S(1)} %pad_maximum_fusion._), channel_id=1, source_target_pairs={{0,1},{1,0},{2,3},{3,2},{4,5},{5,4},{6,7},{7,6},{8,9},{9,8},{10,11... | collective-permute-start | bytes 663560 | tf_op jit(solution)/shard_map/ppermute | solution.py:28
  16.3 3.8 %shard_map.102.refs_1_ = bf16[1,2,384,6144]{3,2,1,0:T(8,128)(2,1)S(1)} custom-call(bf16[1,2,384,6144]{3,2,1,0:T(8,128)(2,1)} %weights.1, bf16[4,72,384]{2,1,0:T(8,128)(2,1)S(1)} %pad_maximum_fusion._), custom_call_target="tpu_custom_call" | custom-call | bytes 9437184 | tf_op jit(solution)/shard_map/pallas_call | solution.py:389
  21.8 2.3 %collective-permute-done.5 = bf16[4,72,384]{2,1,0:T(8,128)(2,1)S(1)} collective-permute-done((bf16[4,72,384]{2,1,0:T(8,128)(2,1)S(1)}, bf16[4,72,384]{2,1,0:T(8,128)(2,1)S(1)}, u32[]{:S(2)}, u32[]{:S(2)}) %collective-permute-start.5) | collective-permute-done | bytes 221216 | tf_op jit(solution)/shard_map/ppermute | solution.py:28
  24.1 2.7 %shard_map.103 = (bf16[64,6144]{1,0:T(8,128)(2,1)S(1)}, f32[64,128]{1,0:T(8,128)S(1)}, f32[64,384]{1,0:T(8,128)S(1)}, bf16[64,384]{1,0:T(8,128)(2,1)S(1)}, f32[2,6144]{1,0:T(2,128)S(1)}) custom-call(s32[2]{0:T(128)S(1)} %pad_add_fusion.scalars.refs_0_, bf16[1,2,384,6144]{3,2,1,0:T(8,128)(2,1)S(1)} %shard_map.102.refs_1_, ...), custom_call_target="tpu_custom_call" | custom-call | flops 301989888 | bytes 4718592 | tf_op jit(solution)/shard_map/pallas_call | solution.py:229
  26.8 2.2 %collective-permute-start.6 = (bf16[1,64,384]{2,1,0:T(8,128)(2,1)S(1)}, bf16[1,64,384]{2,1,0:T(8,128)(2,1)S(1)}, u32[]{:S(2)}, u32[]{:S(2)}) collective-permute-start(bf16[1,64,384]{2,1,0:T(8,128)(2,1)S(1)} %bitcast.21), channel_id=1, source_target_pairs={{0,12},{1,13},{2,14},{3,15},{4,8},{5,9},{6,10},{7,11},{8,4},{9,5},... | collective-permute-start | bytes 147464 | tf_op jit(solution)/shard_map/ppermute | solution.py:28
  29.5 1.7 %collective-permute-start.8 = (bf16[1,64,384]{2,1,0:T(8,128)(2,1)S(1)}, bf16[1,64,384]{2,1,0:T(8,128)(2,1)S(1)}, u32[]{:S(2)}, u32[]{:S(2)}) collective-permute-start(bf16[1,64,384]{2,1,0:T(8,128)(2,1)S(1)} %bitcast.23), channel_id=1, source_target_pairs={{0,8},{1,9},{2,10},{3,11},{4,12},{5,13},{6,14},{7,15},{8,0},{9,1},... | collective-permute-start | bytes 147464 | tf_op jit(solution)/shard_map/ppermute | solution.py:28
  31.2 1.5 %collective-permute-done.6 = bf16[1,64,384]{2,1,0:T(8,128)(2,1)S(1)} collective-permute-done((bf16[1,64,384]{2,1,0:T(8,128)(2,1)S(1)}, bf16[1,64,384]{2,1,0:T(8,128)(2,1)S(1)}, u32[]{:S(2)}, u32[]{:S(2)}) %collective-permute-start.6) | collective-permute-done | bytes 49184 | tf_op jit(solution)/shard_map/ppermute | solution.py:28
  33.3 1.3 %collective-permute-done.8 = bf16[1,64,384]{2,1,0:T(8,128)(2,1)S(1)} collective-permute-done((bf16[1,64,384]{2,1,0:T(8,128)(2,1)S(1)}, bf16[1,64,384]{2,1,0:T(8,128)(2,1)S(1)}, u32[]{:S(2)}, u32[]{:S(2)}) %collective-permute-start.8) | collective-permute-done | bytes 49184 | tf_op jit(solution)/shard_map/ppermute | solution.py:28
  34.6 1.6 %collective-permute-start.9 = (bf16[4,64,384]{2,1,0:T(8,128)(2,1)S(1)}, bf16[4,64,384]{2,1,0:T(8,128)(2,1)S(1)}, u32[]{:S(2)}, u32[]{:S(2)}) collective-permute-start(bf16[4,64,384]{2,1,0:T(8,128)(2,1)S(1)} %pad_maximum_fusion.1), channel_id=1, source_target_pairs={{0,2},{1,3},{2,0},{3,1},{4,6},{5,7},{6,4},{7,5},{8,10},{9,11},{10,... | collective-permute-start | bytes 589832 | tf_op jit(solution)/shard_map/ppermute | solution.py:28
  36.2 1.5 %collective-permute-start.10 = (bf16[4,64,384]{2,1,0:T(8,128)(2,1)S(1)}, bf16[4,64,384]{2,1,0:T(8,128)(2,1)S(1)}, u32[]{:S(2)}, u32[]{:S(2)}) collective-permute-start(bf16[4,64,384]{2,1,0:T(8,128)(2,1)S(1)} %pad_maximum_fusion.1), channel_id=1, source_target_pairs={{0,1},{1,0},{2,3},{3,2},{4,5},{5,4},{6,7},{7,6},{8,9},{9,8},{10,11... | collective-permute-start | bytes 589832 | tf_op jit(solution)/shard_map/ppermute | solution.py:28
  38.2 2.2 %collective-permute-done.9 = bf16[4,64,384]{2,1,0:T(8,128)(2,1)S(1)} collective-permute-done((bf16[4,64,384]{2,1,0:T(8,128)(2,1)S(1)}, bf16[4,64,384]{2,1,0:T(8,128)(2,1)S(1)}, u32[]{:S(2)}, u32[]{:S(2)}) %collective-permute-start.9) | collective-permute-done | bytes 196640 | tf_op jit(solution)/shard_map/ppermute | solution.py:28
  40.3 1.5 %collective-permute-done.10 = bf16[4,64,384]{2,1,0:T(8,128)(2,1)S(1)} collective-permute-done((bf16[4,64,384]{2,1,0:T(8,128)(2,1)S(1)}, bf16[4,64,384]{2,1,0:T(8,128)(2,1)S(1)}, u32[]{:S(2)}, u32[]{:S(2)}) %collective-permute-start.10) | collective-permute-done | bytes 196640 | tf_op jit(solution)/shard_map/ppermute | solution.py:28
  41.9 2.4 %collective-permute-done.11 = bf16[4,64,384]{2,1,0:T(8,128)(2,1)S(1)} collective-permute-done((bf16[4,64,384]{2,1,0:T(8,128)(2,1)S(1)}, bf16[4,64,384]{2,1,0:T(8,128)(2,1)S(1)}, u32[]{:S(2)}, u32[]{:S(2)}) %collective-permute-start.11) | collective-permute-done | bytes 196640 | tf_op jit(solution)/shard_map/ppermute | solution.py:28
  44.3 4.4 %shard_map.104 = (bf16[64,6144]{1,0:T(8,128)(2,1)S(1)}, f32[64,128]{1,0:T(8,128)S(1)}, f32[64,384]{1,0:T(8,128)}, bf16[64,384]{1,0:T(8,128)(2,1)S(1)}, bf16[64,3...) custom-call(s32[2]{0:T(128)S(1)} %pad_add_fusion.1.refs_0_, bf16[1,2,384,6144]{3,2,1,0:T(8,128)(2,1)S(1)} %shard_map.102.refs_1_, ...), custom_call_target="tpu_custom_call" | custom-call | flops 603979776 | bytes 4718592 | tf_op jit(solution)/shard_map/pallas_call | solution.py:229
  49.4 2.2 %collective-permute-start.13 = (bf16[4,200,128]{2,1,0:T(8,128)(2,1)S(1)}, bf16[4,200,128]{2,1,0:T(8,128)(2,1)S(1)}, u32[]{:S(2)}, u32[]{:S(2)}) collective-permute-start(bf16[4,200,128]{2,1,0:T(8,128)(2,1)S(1)} %get-tuple-element.71), channel_id=1, source_target_pairs={{0,3},{1,2},{2,1},{3,0},{4,7},{5,6},{6,5},{7,4},{8,11},{9,10},{10,... | collective-permute-start | bytes 614408 | tf_op jit(solution)/shard_map/ppermute | solution.py:28
  53.1 3.7 %shard_map.105 = (f32[384,3072]{1,0:T(8,128)}, f32[384,3072]{1,0:T(8,128)}, f32[8,128]{1,0:T(8,128)}) custom-call(s32[2]{0:T(128)S(1)} %pad_add_fusion.scalars.refs_0_, bf16[64,384]{1,0:T(8,128)(2,1)S(1)} %get-tuple-element.44.refs_1_, bf16[64,384]{1,0:T(8,128)(2,1)S(1)} %collective-permute-done.16.refs_2_, bf16[64,3072]{1,0:T(8,128)(2,1)S(1)} %get-tuple-element.76.refs_3_, ...), custom_call_target="tpu_custom_call" | custom-call | flops 301989888 | bytes 4718592 | tf_op jit(solution)/shard_map/pallas_call | solution.py:360
  56.8 1.5 %collective-permute-done.13 = bf16[4,200,128]{2,1,0:T(8,128)(2,1)S(1)} collective-permute-done((bf16[4,200,128]{2,1,0:T(8,128)(2,1)S(1)}, bf16[4,200,128]{2,1,0:T(8,128)(2,1)S(1)}, u32[]{:S(2)}, u32[]{:S(2)}) %collective-permute-start.13) | collective-permute-done | bytes 204832 | tf_op jit(solution)/shard_map/ppermute | solution.py:28
  58.3 3.2 %collective-permute-done.14 = bf16[4,200,128]{2,1,0:T(8,128)(2,1)S(1)} collective-permute-done((bf16[4,200,128]{2,1,0:T(8,128)(2,1)S(1)}, bf16[4,200,128]{2,1,0:T(8,128)(2,1)S(1)}, u32[]{:S(2)}, u32[]{:S(2)}) %collective-permute-start.14) | collective-permute-done | bytes 204832 | tf_op jit(solution)/shard_map/ppermute | solution.py:28
  61.9 1.5 %collective-permute-start.19 = (bf16[1,200,128]{2,1,0:T(8,128)(2,1)S(1)}, bf16[1,200,128]{2,1,0:T(8,128)(2,1)S(1)}, u32[]{:S(2)}, u32[]{:S(2)}) collective-permute-start(bf16[1,200,128]{2,1,0:T(8,128)(2,1)S(1)} %get-tuple-element.78), channel_id=1, source_target_pairs={{0,4},{1,5},{2,6},{3,7},{4,0},{5,1},{6,2},{7,3},{8,12},{9,13},{10,... | collective-permute-start | bytes 153608 | tf_op jit(solution)/shard_map/ppermute | solution.py:28
  64.5 1.8 %collective-permute-start.18 = (bf16[1,200,128]{2,1,0:T(8,128)(2,1)S(1)}, bf16[1,200,128]{2,1,0:T(8,128)(2,1)S(1)}, u32[]{:S(2)}, u32[]{:S(2)}) collective-permute-start(bf16[1,200,128]{2,1,0:T(8,128)(2,1)S(1)} %get-tuple-element.79), channel_id=1, source_target_pairs={{0,12},{1,13},{2,14},{3,15},{4,8},{5,9},{6,10},{7,11},{8,4},{9,5},... | collective-permute-start | bytes 153608 | tf_op jit(solution)/shard_map/ppermute | solution.py:28
  66.4 3.6 %collective-permute-done.20 = bf16[1,200,128]{2,1,0:T(8,128)(2,1)S(1)} collective-permute-done((bf16[1,200,128]{2,1,0:T(8,128)(2,1)S(1)}, bf16[1,200,128]{2,1,0:T(8,128)(2,1)S(1)}, u32[]{:S(2)}, u32[]{:S(2)}) %collective-permute-start.20) | collective-permute-done | bytes 51232 | tf_op jit(solution)/shard_map/ppermute | solution.py:28
  70.5 1.6 %shard_map.106 = (bf16[64,384]{1,0:T(8,128)(2,1)S(1)}, f32[4,384]{1,0:T(4,128)S(1)}, f32[4,384]{1,0:T(4,128)S(1)}, f32[4,384]{1,0:T(4,128)S(1)}, f32[4,384]{1,0:T(4,128)S(1)}, /*index=5*/f32[1,384]{1,0:T(1,128)S(1)}) custom-call(s32[2]{0:T(128)S(1)} %pad_add_fusion.scalars.refs_0_, bf16[1,2,384,6144]{3,2,1,0:T(8,128)(2,1)S(1)} %shard_map.102.refs_1_, ...), custom_call_target="tpu_custom_call" | custom-call | flops 301989888 | bytes 4718592 | tf_op jit(solution)/shard_map/pallas_call | solution.py:308
  72.2 2.2 %collective-permute-start.23 = (f32[4,384]{1,0:T(4,128)S(1)}, f32[4,384]{1,0:T(4,128)S(1)}, u32[]{:S(2)}, u32[]{:S(2)}) collective-permute-start(f32[4,384]{1,0:T(4,128)S(1)} %get-tuple-element.60), channel_id=1, source_target_pairs={{0,3},{1,2},{2,1},{3,0},{4,7},{5,6},{6,5},{7,4},{8,11},{9,10},{10,... | collective-permute-start | bytes 18440 | tf_op jit(solution)/shard_map/ppermute | solution.py:28
  75.8 3.1 %shard_map.107 = (f32[384,3072]{1,0:T(8,128)}, f32[384,3072]{1,0:T(8,128)}, f32[4,384]{1,0:T(4,128)S(1)}) custom-call(s32[2]{0:T(128)S(1)} %pad_add_fusion.scalars.refs_0_, bf16[64,384]{1,0:T(8,128)(2,1)S(1)} %get-tuple-element.53.refs_1_, bf16[64,384]{1,0:T(8,128)(2,1)S(1)} %collective-permute-done.21.refs_2_, ...), custom_call_target="tpu_custom_call", output_to_operand_aliasing={{0}: (6, {}), {1}: (7, {})} | custom-call | flops 301989888 | bytes 4718592 | tf_op jit(solution)/shard_map/pallas_call | solution.py:360
  79.0 1.9 %collective-permute-start.26 = (f32[1,384]{1,0:T(1,128)S(1)}, f32[1,384]{1,0:T(1,128)S(1)}, u32[]{:S(2)}, u32[]{:S(2)}) collective-permute-start(f32[1,384]{1,0:T(1,128)S(1)} %get-tuple-element.82), channel_id=1, source_target_pairs={{0,12},{1,13},{2,14},{3,15},{4,8},{5,9},{6,10},{7,11},{8,4},{9,5},... | collective-permute-start | bytes 4616 | tf_op jit(solution)/shard_map/ppermute | solution.py:28
  81.0 2.5 %collective-permute-start.28 = (f32[1,384]{1,0:T(1,128)S(1)}, f32[1,384]{1,0:T(1,128)S(1)}, u32[]{:S(2)}, u32[]{:S(2)}) collective-permute-start(f32[1,384]{1,0:T(1,128)S(1)} %get-tuple-element.83), channel_id=1, source_target_pairs={{0,8},{1,9},{2,10},{3,11},{4,12},{5,13},{6,14},{7,15},{8,0},{9,1},... | collective-permute-start | bytes 4616 | tf_op jit(solution)/shard_map/ppermute | solution.py:28
  (66 shorter events, 15.0 us)
Async XLA Ops:
  2.1 7.7 %collective-permute-start = (bf16[1,72,384]{2,1,0:T(8,128)(2,1)S(1)}, bf16[1,72,384]{2,1,0:T(8,128)(2,1)S(1)}, u32[]{:S(2)}, u32[]{:S(2)}) collective-permute-start(bf16[1,72,384]{2,1,0:T(8,128)(2,1)S(1)} %bitcast.25), channel_id=1, source_target_pairs={{0,12},{1,13},{2,14},{3,15},{4,8},{5,9},{6,10},{7,11},{8,4},{9,5},... | collective-permute-start | bytes 165896 | tf_op jit(solution)/shard_map/ppermute | solution.py:28
  7.2 4.2 %collective-permute-start.1 = (bf16[1,72,384]{2,1,0:T(8,128)(2,1)S(1)}, bf16[1,72,384]{2,1,0:T(8,128)(2,1)S(1)}, u32[]{:S(2)}, u32[]{:S(2)}) collective-permute-start(bf16[1,72,384]{2,1,0:T(8,128)(2,1)S(1)} %bitcast.26), channel_id=1, source_target_pairs={{0,4},{1,5},{2,6},{3,7},{4,0},{5,1},{6,2},{7,3},{8,12},{9,13},{10,... | collective-permute-start | bytes 165896 | tf_op jit(solution)/shard_map/ppermute | solution.py:28
  7.2 5.4 %collective-permute-start.2 = (bf16[1,72,384]{2,1,0:T(8,128)(2,1)S(1)}, bf16[1,72,384]{2,1,0:T(8,128)(2,1)S(1)}, u32[]{:S(2)}, u32[]{:S(2)}) collective-permute-start(bf16[1,72,384]{2,1,0:T(8,128)(2,1)S(1)} %bitcast.27), channel_id=1, source_target_pairs={{0,8},{1,9},{2,10},{3,11},{4,12},{5,13},{6,14},{7,15},{8,0},{9,1},... | collective-permute-start | bytes 165896 | tf_op jit(solution)/shard_map/ppermute | solution.py:28
  12.7 8.4 %collective-permute-start.3 = (bf16[4,72,384]{2,1,0:T(8,128)(2,1)S(1)}, bf16[4,72,384]{2,1,0:T(8,128)(2,1)S(1)}, u32[]{:S(2)}, u32[]{:S(2)}) collective-permute-start(bf16[4,72,384]{2,1,0:T(8,128)(2,1)S(1)} %pad_maximum_fusion._), channel_id=1, source_target_pairs={{0,2},{1,3},{2,0},{3,1},{4,6},{5,7},{6,4},{7,5},{8,10},{9,11},{10,... | collective-permute-start | bytes 663560 | tf_op jit(solution)/shard_map/ppermute | solution.py:28
  14.3 7.5 %collective-permute-start.4 = (bf16[4,72,384]{2,1,0:T(8,128)(2,1)S(1)}, bf16[4,72,384]{2,1,0:T(8,128)(2,1)S(1)}, u32[]{:S(2)}, u32[]{:S(2)}) collective-permute-start(bf16[4,72,384]{2,1,0:T(8,128)(2,1)S(1)} %pad_maximum_fusion._), channel_id=1, source_target_pairs={{0,1},{1,0},{2,3},{3,2},{4,5},{5,4},{6,7},{7,6},{8,9},{9,8},{10,11... | collective-permute-start | bytes 663560 | tf_op jit(solution)/shard_map/ppermute | solution.py:28
  15.8 8.3 %collective-permute-start.5 = (bf16[4,72,384]{2,1,0:T(8,128)(2,1)S(1)}, bf16[4,72,384]{2,1,0:T(8,128)(2,1)S(1)}, u32[]{:S(2)}, u32[]{:S(2)}) collective-permute-start(bf16[4,72,384]{2,1,0:T(8,128)(2,1)S(1)} %pad_maximum_fusion._), channel_id=1, source_target_pairs={{0,3},{1,2},{2,1},{3,0},{4,7},{5,6},{6,5},{7,4},{8,11},{9,10},{10,... | collective-permute-start | bytes 663560 | tf_op jit(solution)/shard_map/ppermute | solution.py:28
  26.8 6.0 %collective-permute-start.6 = (bf16[1,64,384]{2,1,0:T(8,128)(2,1)S(1)}, bf16[1,64,384]{2,1,0:T(8,128)(2,1)S(1)}, u32[]{:S(2)}, u32[]{:S(2)}) collective-permute-start(bf16[1,64,384]{2,1,0:T(8,128)(2,1)S(1)} %bitcast.21), channel_id=1, source_target_pairs={{0,12},{1,13},{2,14},{3,15},{4,8},{5,9},{6,10},{7,11},{8,4},{9,5},... | collective-permute-start | bytes 147464 | tf_op jit(solution)/shard_map/ppermute | solution.py:28
  28.9 4.3 %collective-permute-start.7 = (bf16[1,64,384]{2,1,0:T(8,128)(2,1)S(1)}, bf16[1,64,384]{2,1,0:T(8,128)(2,1)S(1)}, u32[]{:S(2)}, u32[]{:S(2)}) collective-permute-start(bf16[1,64,384]{2,1,0:T(8,128)(2,1)S(1)} %bitcast.22), channel_id=1, source_target_pairs={{0,4},{1,5},{2,6},{3,7},{4,0},{5,1},{6,2},{7,3},{8,12},{9,13},{10,... | collective-permute-start | bytes 147464 | tf_op jit(solution)/shard_map/ppermute | solution.py:28
  29.5 5.0 %collective-permute-start.8 = (bf16[1,64,384]{2,1,0:T(8,128)(2,1)S(1)}, bf16[1,64,384]{2,1,0:T(8,128)(2,1)S(1)}, u32[]{:S(2)}, u32[]{:S(2)}) collective-permute-start(bf16[1,64,384]{2,1,0:T(8,128)(2,1)S(1)} %bitcast.23), channel_id=1, source_target_pairs={{0,8},{1,9},{2,10},{3,11},{4,12},{5,13},{6,14},{7,15},{8,0},{9,1},... | collective-permute-start | bytes 147464 | tf_op jit(solution)/shard_map/ppermute | solution.py:28
  34.6 5.8 %collective-permute-start.9 = (bf16[4,64,384]{2,1,0:T(8,128)(2,1)S(1)}, bf16[4,64,384]{2,1,0:T(8,128)(2,1)S(1)}, u32[]{:S(2)}, u32[]{:S(2)}) collective-permute-start(bf16[4,64,384]{2,1,0:T(8,128)(2,1)S(1)} %pad_maximum_fusion.1), channel_id=1, source_target_pairs={{0,2},{1,3},{2,0},{3,1},{4,6},{5,7},{6,4},{7,5},{8,10},{9,11},{10,... | collective-permute-start | bytes 589832 | tf_op jit(solution)/shard_map/ppermute | solution.py:28
  36.2 5.7 %collective-permute-start.10 = (bf16[4,64,384]{2,1,0:T(8,128)(2,1)S(1)}, bf16[4,64,384]{2,1,0:T(8,128)(2,1)S(1)}, u32[]{:S(2)}, u32[]{:S(2)}) collective-permute-start(bf16[4,64,384]{2,1,0:T(8,128)(2,1)S(1)} %pad_maximum_fusion.1), channel_id=1, source_target_pairs={{0,1},{1,0},{2,3},{3,2},{4,5},{5,4},{6,7},{7,6},{8,9},{9,8},{10,11... | collective-permute-start | bytes 589832 | tf_op jit(solution)/shard_map/ppermute | solution.py:28
  37.7 6.6 %collective-permute-start.11 = (bf16[4,64,384]{2,1,0:T(8,128)(2,1)S(1)}, bf16[4,64,384]{2,1,0:T(8,128)(2,1)S(1)}, u32[]{:S(2)}, u32[]{:S(2)}) collective-permute-start(bf16[4,64,384]{2,1,0:T(8,128)(2,1)S(1)} %pad_maximum_fusion.1), channel_id=1, source_target_pairs={{0,3},{1,2},{2,1},{3,0},{4,7},{5,6},{6,5},{7,4},{8,11},{9,10},{10,... | collective-permute-start | bytes 589832 | tf_op jit(solution)/shard_map/ppermute | solution.py:28
  48.7 4.4 %collective-permute-start.17 = (bf16[64,3072]{1,0:T(8,128)(2,1)S(1)}, bf16[64,3072]{1,0:T(8,128)(2,1)S(1)}, u32[]{:S(2)}, u32[]{:S(2)}) collective-permute-start(bf16[64,3072]{1,0:T(8,128)(2,1)S(1)} %get-tuple-element.75), channel_id=1, source_target_pairs={{0,16},{16,0},{1,17},{17,1},{2,18},{18,2},{3,19},{19,3},{4,20},{20... | collective-permute-start | bytes 1179656 | tf_op jit(solution)/shard_map/ppermute | solution.py:33
  48.8 4.2 %collective-permute-start.16 = (bf16[64,384]{1,0:T(8,128)(2,1)S(1)}, bf16[64,384]{1,0:T(8,128)(2,1)S(1)}, u32[]{:S(2)}, u32[]{:S(2)}) collective-permute-start(bf16[64,384]{1,0:T(8,128)(2,1)S(1)} %get-tuple-element.44.refs_1_), channel_id=1, source_target_pairs={{0,16},{16,0},{1,17},{17,1},{2,18},{18,2},{3,19},{19,3},{4,20},{20... | collective-permute-start | bytes 147464 | tf_op jit(solution)/shard_map/ppermute | solution.py:33
  49.4 8.9 %collective-permute-start.13 = (bf16[4,200,128]{2,1,0:T(8,128)(2,1)S(1)}, bf16[4,200,128]{2,1,0:T(8,128)(2,1)S(1)}, u32[]{:S(2)}, u32[]{:S(2)}) collective-permute-start(bf16[4,200,128]{2,1,0:T(8,128)(2,1)S(1)} %get-tuple-element.71), channel_id=1, source_target_pairs={{0,3},{1,2},{2,1},{3,0},{4,7},{5,6},{6,5},{7,4},{8,11},{9,10},{10,... | collective-permute-start | bytes 614408 | tf_op jit(solution)/shard_map/ppermute | solution.py:28
  51.5 10.0 %collective-permute-start.14 = (bf16[4,200,128]{2,1,0:T(8,128)(2,1)S(1)}, bf16[4,200,128]{2,1,0:T(8,128)(2,1)S(1)}, u32[]{:S(2)}, u32[]{:S(2)}) collective-permute-start(bf16[4,200,128]{2,1,0:T(8,128)(2,1)S(1)} %get-tuple-element.70), channel_id=1, source_target_pairs={{0,1},{1,0},{2,3},{3,2},{4,5},{5,4},{6,7},{7,6},{8,9},{9,8},{10,11... | collective-permute-start | bytes 614408 | tf_op jit(solution)/shard_map/ppermute | solution.py:28
  52.0 9.7 %collective-permute-start.15 = (bf16[4,200,128]{2,1,0:T(8,128)(2,1)S(1)}, bf16[4,200,128]{2,1,0:T(8,128)(2,1)S(1)}, u32[]{:S(2)}, u32[]{:S(2)}) collective-permute-start(bf16[4,200,128]{2,1,0:T(8,128)(2,1)S(1)} %get-tuple-element.69), channel_id=1, source_target_pairs={{0,2},{1,3},{2,0},{3,1},{4,6},{5,7},{6,4},{7,5},{8,10},{9,11},{10,... | collective-permute-start | bytes 614408 | tf_op jit(solution)/shard_map/ppermute | solution.py:28
  53.0 22.8 %collective-permute-start.22 = (bf16[64,3072]{1,0:T(8,128)(2,1)S(1)}, bf16[64,3072]{1,0:T(8,128)(2,1)S(1)}, u32[]{:S(2)}, u32[]{:S(2)}) collective-permute-start(bf16[64,3072]{1,0:T(8,128)(2,1)S(1)} %get-tuple-element.73), channel_id=1, source_target_pairs={{0,16},{16,0},{1,17},{17,1},{2,18},{18,2},{3,19},{19,3},{4,20},{20... | collective-permute-start | bytes 1179656 | tf_op jit(solution)/shard_map/ppermute | solution.py:33
  61.9 4.5 %collective-permute-start.19 = (bf16[1,200,128]{2,1,0:T(8,128)(2,1)S(1)}, bf16[1,200,128]{2,1,0:T(8,128)(2,1)S(1)}, u32[]{:S(2)}, u32[]{:S(2)}) collective-permute-start(bf16[1,200,128]{2,1,0:T(8,128)(2,1)S(1)} %get-tuple-element.78), channel_id=1, source_target_pairs={{0,4},{1,5},{2,6},{3,7},{4,0},{5,1},{6,2},{7,3},{8,12},{9,13},{10,... | collective-permute-start | bytes 153608 | tf_op jit(solution)/shard_map/ppermute | solution.py:28
  63.4 6.5 %collective-permute-start.20 = (bf16[1,200,128]{2,1,0:T(8,128)(2,1)S(1)}, bf16[1,200,128]{2,1,0:T(8,128)(2,1)S(1)}, u32[]{:S(2)}, u32[]{:S(2)}) collective-permute-start(bf16[1,200,128]{2,1,0:T(8,128)(2,1)S(1)} %get-tuple-element.77), channel_id=1, source_target_pairs={{0,8},{1,9},{2,10},{3,11},{4,12},{5,13},{6,14},{7,15},{8,0},{9,1},... | collective-permute-start | bytes 153608 | tf_op jit(solution)/shard_map/ppermute | solution.py:28
  64.5 6.0 %collective-permute-start.18 = (bf16[1,200,128]{2,1,0:T(8,128)(2,1)S(1)}, bf16[1,200,128]{2,1,0:T(8,128)(2,1)S(1)}, u32[]{:S(2)}, u32[]{:S(2)}) collective-permute-start(bf16[1,200,128]{2,1,0:T(8,128)(2,1)S(1)} %get-tuple-element.79), channel_id=1, source_target_pairs={{0,12},{1,13},{2,14},{3,15},{4,8},{5,9},{6,10},{7,11},{8,4},{9,5},... | collective-permute-start | bytes 153608 | tf_op jit(solution)/shard_map/ppermute | solution.py:28
  72.2 3.6 %collective-permute-start.21 = (bf16[64,384]{1,0:T(8,128)(2,1)S(1)}, bf16[64,384]{1,0:T(8,128)(2,1)S(1)}, u32[]{:S(2)}, u32[]{:S(2)}) collective-permute-start(bf16[64,384]{1,0:T(8,128)(2,1)S(1)} %get-tuple-element.53.refs_1_), channel_id=1, source_target_pairs={{0,16},{16,0},{1,17},{17,1},{2,18},{18,2},{3,19},{19,3},{4,20},{20... | collective-permute-start | bytes 147464 | tf_op jit(solution)/shard_map/ppermute | solution.py:33
  72.2 6.7 %collective-permute-start.23 = (f32[4,384]{1,0:T(4,128)S(1)}, f32[4,384]{1,0:T(4,128)S(1)}, u32[]{:S(2)}, u32[]{:S(2)}) collective-permute-start(f32[4,384]{1,0:T(4,128)S(1)} %get-tuple-element.60), channel_id=1, source_target_pairs={{0,3},{1,2},{2,1},{3,0},{4,7},{5,6},{6,5},{7,4},{8,11},{9,10},{10,... | collective-permute-start | bytes 18440 | tf_op jit(solution)/shard_map/ppermute | solution.py:28
  74.4 4.6 %collective-permute-start.24 = (f32[4,384]{1,0:T(4,128)S(1)}, f32[4,384]{1,0:T(4,128)S(1)}, u32[]{:S(2)}, u32[]{:S(2)}) collective-permute-start(f32[4,384]{1,0:T(4,128)S(1)} %get-tuple-element.61), channel_id=1, source_target_pairs={{0,1},{1,0},{2,3},{3,2},{4,5},{5,4},{6,7},{7,6},{8,9},{9,8},{10,11... | collective-permute-start | bytes 18440 | tf_op jit(solution)/shard_map/ppermute | solution.py:28
  74.9 4.0 %collective-permute-start.25 = (f32[4,384]{1,0:T(4,128)S(1)}, f32[4,384]{1,0:T(4,128)S(1)}, u32[]{:S(2)}, u32[]{:S(2)}) collective-permute-start(f32[4,384]{1,0:T(4,128)S(1)} %get-tuple-element.62), channel_id=1, source_target_pairs={{0,2},{1,3},{2,0},{3,1},{4,6},{5,7},{6,4},{7,5},{8,10},{9,11},{10,... | collective-permute-start | bytes 18440 | tf_op jit(solution)/shard_map/ppermute | solution.py:28
  79.0 5.4 %collective-permute-start.26 = (f32[1,384]{1,0:T(1,128)S(1)}, f32[1,384]{1,0:T(1,128)S(1)}, u32[]{:S(2)}, u32[]{:S(2)}) collective-permute-start(f32[1,384]{1,0:T(1,128)S(1)} %get-tuple-element.82), channel_id=1, source_target_pairs={{0,12},{1,13},{2,14},{3,15},{4,8},{5,9},{6,10},{7,11},{8,4},{9,5},... | collective-permute-start | bytes 4616 | tf_op jit(solution)/shard_map/ppermute | solution.py:28
  80.9 3.6 %collective-permute-start.27 = (f32[1,384]{1,0:T(1,128)S(1)}, f32[1,384]{1,0:T(1,128)S(1)}, u32[]{:S(2)}, u32[]{:S(2)}) collective-permute-start(f32[1,384]{1,0:T(1,128)S(1)} %get-tuple-element.84), channel_id=1, source_target_pairs={{0,4},{1,5},{2,6},{3,7},{4,0},{5,1},{6,2},{7,3},{8,12},{9,13},{10,... | collective-permute-start | bytes 4616 | tf_op jit(solution)/shard_map/ppermute | solution.py:28
  81.0 4.5 %collective-permute-start.28 = (f32[1,384]{1,0:T(1,128)S(1)}, f32[1,384]{1,0:T(1,128)S(1)}, u32[]{:S(2)}, u32[]{:S(2)}) collective-permute-start(f32[1,384]{1,0:T(1,128)S(1)} %get-tuple-element.83), channel_id=1, source_target_pairs={{0,8},{1,9},{2,10},{3,11},{4,12},{5,13},{6,14},{7,15},{8,0},{9,1},... | collective-permute-start | bytes 4616 | tf_op jit(solution)/shard_map/ppermute | solution.py:28
  83.5 2.0 %collective-permute-start.12 = (bf16[64,384]{1,0:T(8,128)(2,1)S(1)}, bf16[64,384]{1,0:T(8,128)(2,1)S(1)}, u32[]{:S(2)}, u32[]{:S(2)}) collective-permute-start(bf16[64,384]{1,0:T(8,128)(2,1)S(1)} %get-tuple-element.40), channel_id=1, source_target_pairs={{0,16},{16,0},{1,17},{17,1},{2,18},{18,2},{3,19},{19,3},{4,20},{20... | collective-permute-start | bytes 147464 | tf_op jit(solution)/shard_map/ppermute | solution.py:33
  85.4 1.2 %collective-permute-start.29 = (f32[1,384]{1,0:T(1,128)S(1)}, f32[1,384]{1,0:T(1,128)S(1)}, u32[]{:S(2)}, u32[]{:S(2)}) collective-permute-start(f32[1,384]{1,0:T(1,128)S(1)} %get-tuple-element.65), channel_id=1, source_target_pairs={{0,16},{16,0},{1,17},{17,1},{2,18},{18,2},{3,19},{19,3},{4,20},{20... | collective-permute-start | bytes 4616 | tf_op jit(solution)/shard_map/ppermute | solution.py:33

commit v5 on v4

--- a/solution.py
+++ b/solution.py
@@ -469,7 +469,7 @@
     wide = block << merged
     bit_count = seq_size.bit_length() - 1
     groups = bit_groups(merged, bit_count)
-    back_groups = [group[::-1] for group in groups[:0:-1]] + groups[:1]
+    back_groups = groups[::-1]
     offsets = [o >> merged for o in offsets_of(groups)]
     send_order = [o >> merged for o in offsets_of(back_groups[::-1])]
     me = (seq_index >> merged).astype(jnp.int32)
@@ -584,13 +584,17 @@
             state = moved(y, step, step + 1)
     u_a, y_a = first_record[2], first_record[5]
     u_b, y_b = second_record[2], second_record[5]
-    y_other = swapped(y_b)
-    down_out = jnp.where(lower, y_a, y_other)
-    up_out = jnp.where(lower, y_other, y_a)
     needed_a = jnp.where(lower, u_a[:, :half], u_a[:, half:])
     needed_b = jnp.where(lower, u_b[:, half:], u_b[:, :half])
     other_a = swapped(jnp.where(lower, u_a[:, half:], u_a[:, :half]))
     other_b = swapped(jnp.where(lower, u_b[:, :half], u_b[:, half:]))
+    def early_results(dz):
+        y_other = swapped(y_b)
+        grads = weight_grad_call(
+            scalars_at(0), 1, dz, swapped(dz), needed_b, other_b, jnp.zeros((8, LANES), F32), ()
+        )
+        return grads, (jnp.where(lower, y_a, y_other), jnp.where(lower, y_other, y_a))
+
     dz_a = dz_b = gain_b = gain_a = None
     for step in reversed(range(1, sections)):
         source, _, _, stat, z, _ = second_record if step >= middle else first_record
@@ -615,20 +619,10 @@
             dz_a = keep_live(live_at(step), dz, dz_a)
         beside = None
         if step == middle:
-            beside = functools.partial(
-                weight_grad_call,
-                scalars_at(0),
-                1,
-                dz_b,
-                swapped(dz_b),
-                needed_b,
-                other_b,
-                jnp.zeros((8, LANES)),
-                (),
-            )
-        parts, grads = reduced(sent, beside)
-        if grads is not None:
-            early_grads = grads[:2]
+            beside = functools.partial(early_results, dz_b)
+        parts, done = reduced(sent, beside)
+        if beside is not None:
+            (early_first, early_second, _), (down_out, up_out) = beside() if done is None else done
         finish = None
         if sections == 2 and not merged:
             finish = (parts, (source, stat, gain_row))
@@ -670,13 +664,14 @@
         gain_b = result[-1]
     dz_a = keep_live(live_at(0), dz, dz_a)
     dz_a_other = swapped(dz_a)
+    early = (early_first, early_second)
     for n, group in enumerate(back_groups):
         if n:
             gain_parts = gain_parts.reshape((len(group) + 1, -1) + gain_parts.shape[1:])
         parts = reduce_round(gain_parts, group)
         if n == 0:
             grad_first, grad_second, token = weight_grad_call(
-                scalars_at(0), 0, dz_a, dz_a_other, needed_a, other_a, parts[0], early_grads
+                scalars_at(0), 0, dz_a, dz_a_other, needed_a, other_a, parts[0], early
             )
             parts.append(token)
         gain_parts = functools.reduce(jnp.add, parts)

time: 87.4 us -> 88.9 us (1.017)
  waiting for transfers between devices: 28.7 us -> 29.9 us
    ppermute x6, waiting for transfers between devices: 0.49 us -> 1.73 us  [swapped(): lax.ppermute(value, 'section', [(i, size - 1 - i) for i in range(size)])]
where the time goes in v5:
time: 88.9 us; the launch traced here: 88.7 us
  starting transfers between devices  34.1 us (38%)
  waiting for transfers between devices  29.9 us (34%)
  Pallas kernels  21.1 us (24%)
  other arithmetic  1.68 us (2%)
  local copies, waits for them, and re-layouts  1.09 us (1%)
    ppermute x24, starting transfers between devices, from_xor(): return lax.ppermute(value, 'seq', [(i, i ^ distance) for i in range(size)])  33.3 us
    ppermute x24, waiting for transfers between devices, from_xor(): return lax.ppermute(value, 'seq', [(i, i ^ distance) for i in range(size)])  28.2 us
    pallas_call x2, Pallas kernels, section_call(): pl.pallas_call(functools.partial(section_kernel, offsets, (tokens, wide,...  7.38 us
    pallas_call x2, Pallas kernels, weight_grad_call(): pl.pallas_call(functools.partial(weight_grad_kernel, first_at, tiles, len...  6.87 us
    pallas_call x1, Pallas kernels, load_call(): pl.pallas_call(load_kernel, out_shape=jax.ShapeDtypeStruct(weights.shape,...  3.79 us
  transfers between devices with their start and end apart: 30, of which 20 were waited for; matrix products, arithmetic and copies ran while one was open for 2% of the time, Pallas kernels for 14%

profile of v5, /device:TPU:0, one launch (start us, length us, event | category | flops | bytes accessed | tf_op | source)
XLA Modules:
  0.0 88.7 jit_solution(4857557471537641686)
XLA Ops:
  0.7 1.4 %shard_map.101 = (bf16[64,384]{1,0:T(8,128)(2,1)S(1)}, bf16[64,384]{1,0:T(8,128)(2,1)S(1)}, bf16[72,384]{1,0:T(8,128)(2,1)S(1)}) custom-call(s32[2]{0:T(128)S(1)} %pad_add_fusion.1.scalars.refs_0_, bf16[64,384]{1,0:T(8,128)(2,1)} %refs_0_.1, bf16[64,384]{1,0:T(8,128)(2,1)} %refs_1_.1, bf16[64,384]{1,0:T(8,128)(2,1)} %refs_2_.1, bf16[64,384]{1,0:T(8,128)(2,1)} %refs_3_.1, ...), custom_call_target="tpu_custom_call" | custom-call | tf_op jit(solution)/shard_map/pallas_call | solution.py:436
  2.1 4.1 %collective-permute-start.2 = (bf16[1,72,384]{2,1,0:T(8,128)(2,1)S(1)}, bf16[1,72,384]{2,1,0:T(8,128)(2,1)S(1)}, u32[]{:S(2)}, u32[]{:S(2)}) collective-permute-start(bf16[1,72,384]{2,1,0:T(8,128)(2,1)S(1)} %bitcast.23), channel_id=1, source_target_pairs={{0,8},{1,9},{2,10},{3,11},{4,12},{5,13},{6,14},{7,15},{8,0},{9,1},... | collective-permute-start | bytes 165896 | tf_op jit(solution)/shard_map/ppermute | solution.py:28
  6.2 1.6 %collective-permute-start.1 = (bf16[1,72,384]{2,1,0:T(8,128)(2,1)S(1)}, bf16[1,72,384]{2,1,0:T(8,128)(2,1)S(1)}, u32[]{:S(2)}, u32[]{:S(2)}) collective-permute-start(bf16[1,72,384]{2,1,0:T(8,128)(2,1)S(1)} %bitcast.24), channel_id=1, source_target_pairs={{0,4},{1,5},{2,6},{3,7},{4,0},{5,1},{6,2},{7,3},{8,12},{9,13},{10,... | collective-permute-start | bytes 165896 | tf_op jit(solution)/shard_map/ppermute | solution.py:28
  9.1 1.3 %collective-permute-done.1 = bf16[1,72,384]{2,1,0:T(8,128)(2,1)S(1)} collective-permute-done((bf16[1,72,384]{2,1,0:T(8,128)(2,1)S(1)}, bf16[1,72,384]{2,1,0:T(8,128)(2,1)S(1)}, u32[]{:S(2)}, u32[]{:S(2)}) %collective-permute-start.1) | collective-permute-done | bytes 55328 | tf_op jit(solution)/shard_map/ppermute | solution.py:28
  10.4 3.4 %collective-permute-done = bf16[1,72,384]{2,1,0:T(8,128)(2,1)S(1)} collective-permute-done((bf16[1,72,384]{2,1,0:T(8,128)(2,1)S(1)}, bf16[1,72,384]{2,1,0:T(8,128)(2,1)S(1)}, u32[]{:S(2)}, u32[]{:S(2)}) %collective-permute-start) | collective-permute-done | bytes 55328 | tf_op jit(solution)/shard_map/ppermute | solution.py:28
  13.8 1.6 %collective-permute-start.3 = (bf16[4,72,384]{2,1,0:T(8,128)(2,1)S(1)}, bf16[4,72,384]{2,1,0:T(8,128)(2,1)S(1)}, u32[]{:S(2)}, u32[]{:S(2)}) collective-permute-start(bf16[4,72,384]{2,1,0:T(8,128)(2,1)S(1)} %pad_maximum_fusion._), channel_id=1, source_target_pairs={{0,2},{1,3},{2,0},{3,1},{4,6},{5,7},{6,4},{7,5},{8,10},{9,11},{10,... | collective-permute-start | bytes 663560 | tf_op jit(solution)/shard_map/ppermute | solution.py:28
  15.4 1.5 %collective-permute-start.4 = (bf16[4,72,384]{2,1,0:T(8,128)(2,1)S(1)}, bf16[4,72,384]{2,1,0:T(8,128)(2,1)S(1)}, u32[]{:S(2)}, u32[]{:S(2)}) collective-permute-start(bf16[4,72,384]{2,1,0:T(8,128)(2,1)S(1)} %pad_maximum_fusion._), channel_id=1, source_target_pairs={{0,1},{1,0},{2,3},{3,2},{4,5},{5,4},{6,7},{7,6},{8,9},{9,8},{10,11... | collective-permute-start | bytes 663560 | tf_op jit(solution)/shard_map/ppermute | solution.py:28
  17.4 3.8 %shard_map.102.refs_1_ = bf16[1,2,384,6144]{3,2,1,0:T(8,128)(2,1)S(1)} custom-call(bf16[1,2,384,6144]{3,2,1,0:T(8,128)(2,1)} %weights.1, bf16[4,72,384]{2,1,0:T(8,128)(2,1)S(1)} %pad_maximum_fusion._), custom_call_target="tpu_custom_call" | custom-call | bytes 9437184 | tf_op jit(solution)/shard_map/pallas_call | solution.py:389
  23.1 2.3 %collective-permute-done.5 = bf16[4,72,384]{2,1,0:T(8,128)(2,1)S(1)} collective-permute-done((bf16[4,72,384]{2,1,0:T(8,128)(2,1)S(1)}, bf16[4,72,384]{2,1,0:T(8,128)(2,1)S(1)}, u32[]{:S(2)}, u32[]{:S(2)}) %collective-permute-start.5) | collective-permute-done | bytes 221216 | tf_op jit(solution)/shard_map/ppermute | solution.py:28
  25.4 2.7 %shard_map.103 = (bf16[64,6144]{1,0:T(8,128)(2,1)S(1)}, f32[64,128]{1,0:T(8,128)S(1)}, f32[64,384]{1,0:T(8,128)S(1)}, bf16[64,384]{1,0:T(8,128)(2,1)S(1)}, f32[2,6144]{1,0:T(2,128)S(1)}) custom-call(s32[2]{0:T(128)S(1)} %pad_add_fusion.1.scalars.refs_0_, bf16[1,2,384,6144]{3,2,1,0:T(8,128)(2,1)S(1)} %shard_map.102.refs_1_, ...), custom_call_target="tpu_custom_call" | custom-call | flops 301989888 | bytes 4718592 | tf_op jit(solution)/shard_map/pallas_call | solution.py:229
  28.1 1.4 %collective-permute-start.6 = (bf16[1,64,384]{2,1,0:T(8,128)(2,1)S(1)}, bf16[1,64,384]{2,1,0:T(8,128)(2,1)S(1)}, u32[]{:S(2)}, u32[]{:S(2)}) collective-permute-start(bf16[1,64,384]{2,1,0:T(8,128)(2,1)S(1)} %bitcast.19), channel_id=1, source_target_pairs={{0,12},{1,13},{2,14},{3,15},{4,8},{5,9},{6,10},{7,11},{8,4},{9,5},... | collective-permute-start | bytes 147464 | tf_op jit(solution)/shard_map/ppermute | solution.py:28
  29.6 3.0 %collective-permute-start.8 = (bf16[1,64,384]{2,1,0:T(8,128)(2,1)S(1)}, bf16[1,64,384]{2,1,0:T(8,128)(2,1)S(1)}, u32[]{:S(2)}, u32[]{:S(2)}) collective-permute-start(bf16[1,64,384]{2,1,0:T(8,128)(2,1)S(1)} %bitcast.21), channel_id=1, source_target_pairs={{0,8},{1,9},{2,10},{3,11},{4,12},{5,13},{6,14},{7,15},{8,0},{9,1},... | collective-permute-start | bytes 147464 | tf_op jit(solution)/shard_map/ppermute | solution.py:28
  32.6 1.5 %collective-permute-done.6 = bf16[1,64,384]{2,1,0:T(8,128)(2,1)S(1)} collective-permute-done((bf16[1,64,384]{2,1,0:T(8,128)(2,1)S(1)}, bf16[1,64,384]{2,1,0:T(8,128)(2,1)S(1)}, u32[]{:S(2)}, u32[]{:S(2)}) %collective-permute-start.6) | collective-permute-done | bytes 49184 | tf_op jit(solution)/shard_map/ppermute | solution.py:28
  34.6 1.6 %collective-permute-start.9 = (bf16[4,64,384]{2,1,0:T(8,128)(2,1)S(1)}, bf16[4,64,384]{2,1,0:T(8,128)(2,1)S(1)}, u32[]{:S(2)}, u32[]{:S(2)}) collective-permute-start(bf16[4,64,384]{2,1,0:T(8,128)(2,1)S(1)} %pad_maximum_fusion.1), channel_id=1, source_target_pairs={{0,2},{1,3},{2,0},{3,1},{4,6},{5,7},{6,4},{7,5},{8,10},{9,11},{10,... | collective-permute-start | bytes 589832 | tf_op jit(solution)/shard_map/ppermute | solution.py:28
  36.2 1.5 %collective-permute-start.10 = (bf16[4,64,384]{2,1,0:T(8,128)(2,1)S(1)}, bf16[4,64,384]{2,1,0:T(8,128)(2,1)S(1)}, u32[]{:S(2)}, u32[]{:S(2)}) collective-permute-start(bf16[4,64,384]{2,1,0:T(8,128)(2,1)S(1)} %pad_maximum_fusion.1), channel_id=1, source_target_pairs={{0,1},{1,0},{2,3},{3,2},{4,5},{5,4},{6,7},{7,6},{8,9},{9,8},{10,11... | collective-permute-start | bytes 589832 | tf_op jit(solution)/shard_map/ppermute | solution.py:28
  38.3 2.4 %collective-permute-done.9 = bf16[4,64,384]{2,1,0:T(8,128)(2,1)S(1)} collective-permute-done((bf16[4,64,384]{2,1,0:T(8,128)(2,1)S(1)}, bf16[4,64,384]{2,1,0:T(8,128)(2,1)S(1)}, u32[]{:S(2)}, u32[]{:S(2)}) %collective-permute-start.9) | collective-permute-done | bytes 196640 | tf_op jit(solution)/shard_map/ppermute | solution.py:28
  40.7 1.2 %collective-permute-done.10 = bf16[4,64,384]{2,1,0:T(8,128)(2,1)S(1)} collective-permute-done((bf16[4,64,384]{2,1,0:T(8,128)(2,1)S(1)}, bf16[4,64,384]{2,1,0:T(8,128)(2,1)S(1)}, u32[]{:S(2)}, u32[]{:S(2)}) %collective-permute-start.10) | collective-permute-done | bytes 196640 | tf_op jit(solution)/shard_map/ppermute | solution.py:28
  41.9 2.4 %collective-permute-done.11 = bf16[4,64,384]{2,1,0:T(8,128)(2,1)S(1)} collective-permute-done((bf16[4,64,384]{2,1,0:T(8,128)(2,1)S(1)}, bf16[4,64,384]{2,1,0:T(8,128)(2,1)S(1)}, u32[]{:S(2)}, u32[]{:S(2)}) %collective-permute-start.11) | collective-permute-done | bytes 196640 | tf_op jit(solution)/shard_map/ppermute | solution.py:28
  44.3 4.7 %shard_map.104 = (bf16[64,6144]{1,0:T(8,128)(2,1)S(1)}, f32[64,128]{1,0:T(8,128)S(1)}, f32[64,384]{1,0:T(8,128)}, bf16[64,384]{1,0:T(8,128)(2,1)S(1)}, bf16[64,3...) custom-call(s32[2]{0:T(128)S(1)} %pad_add_fusion.refs_0_, bf16[1,2,384,6144]{3,2,1,0:T(8,128)(2,1)S(1)} %shard_map.102.refs_1_, ...), custom_call_target="tpu_custom_call" | custom-call | flops 603979776 | bytes 4718592 | tf_op jit(solution)/shard_map/pallas_call | solution.py:229
  49.8 1.2 %collective-permute-start.12 = (bf16[4,200,128]{2,1,0:T(8,128)(2,1)S(1)}, bf16[4,200,128]{2,1,0:T(8,128)(2,1)S(1)}, u32[]{:S(2)}, u32[]{:S(2)}) collective-permute-start(bf16[4,200,128]{2,1,0:T(8,128)(2,1)S(1)} %get-tuple-element.75), channel_id=1, source_target_pairs={{0,2},{1,3},{2,0},{3,1},{4,6},{5,7},{6,4},{7,5},{8,10},{9,11},{10,... | collective-permute-start | bytes 614408 | tf_op jit(solution)/shard_map/ppermute | solution.py:28
  51.0 1.5 %collective-permute-start.13 = (bf16[4,200,128]{2,1,0:T(8,128)(2,1)S(1)}, bf16[4,200,128]{2,1,0:T(8,128)(2,1)S(1)}, u32[]{:S(2)}, u32[]{:S(2)}) collective-permute-start(bf16[4,200,128]{2,1,0:T(8,128)(2,1)S(1)} %get-tuple-element.74), channel_id=1, source_target_pairs={{0,1},{1,0},{2,3},{3,2},{4,5},{5,4},{6,7},{7,6},{8,9},{9,8},{10,11... | collective-permute-start | bytes 614408 | tf_op jit(solution)/shard_map/ppermute | solution.py:28
  54.7 3.7 %shard_map.105 = (f32[384,3072]{1,0:T(8,128)}, f32[384,3072]{1,0:T(8,128)}, f32[8,128]{1,0:T(8,128)}) custom-call(s32[2]{0:T(128)S(1)} %pad_add_fusion.1.scalars.refs_0_, bf16[64,384]{1,0:T(8,128)(2,1)S(1)} %get-tuple-element.43.refs_1_, bf16[64,384]{1,0:T(8,128)(2,1)S(1)} %collective-permute-done.15.refs_2_, ...), custom_call_target="tpu_custom_call" | custom-call | flops 301989888 | bytes 4718592 | tf_op jit(solution)/shard_map/pallas_call | solution.py:360
  59.0 3.5 %collective-permute-done.14 = bf16[4,200,128]{2,1,0:T(8,128)(2,1)S(1)} collective-permute-done((bf16[4,200,128]{2,1,0:T(8,128)(2,1)S(1)}, bf16[4,200,128]{2,1,0:T(8,128)(2,1)S(1)}, u32[]{:S(2)}, u32[]{:S(2)}) %collective-permute-start.14) | collective-permute-done | bytes 204832 | tf_op jit(solution)/shard_map/ppermute | solution.py:28
  62.6 2.4 %collective-permute-start.18 = (bf16[1,200,128]{2,1,0:T(8,128)(2,1)S(1)}, bf16[1,200,128]{2,1,0:T(8,128)(2,1)S(1)}, u32[]{:S(2)}, u32[]{:S(2)}) collective-permute-start(bf16[1,200,128]{2,1,0:T(8,128)(2,1)S(1)} %get-tuple-element.83), channel_id=1, source_target_pairs={{0,12},{1,13},{2,14},{3,15},{4,8},{5,9},{6,10},{7,11},{8,4},{9,5},... | collective-permute-start | bytes 153608 | tf_op jit(solution)/shard_map/ppermute | solution.py:28
  67.1 1.9 %collective-permute-done.18 = bf16[1,200,128]{2,1,0:T(8,128)(2,1)S(1)} collective-permute-done((bf16[1,200,128]{2,1,0:T(8,128)(2,1)S(1)}, bf16[1,200,128]{2,1,0:T(8,128)(2,1)S(1)}, u32[]{:S(2)}, u32[]{:S(2)}) %collective-permute-start.18) | collective-permute-done | bytes 51232 | tf_op jit(solution)/shard_map/ppermute | solution.py:28
  69.4 2.3 %collective-permute-done.20 = bf16[1,200,128]{2,1,0:T(8,128)(2,1)S(1)} collective-permute-done((bf16[1,200,128]{2,1,0:T(8,128)(2,1)S(1)}, bf16[1,200,128]{2,1,0:T(8,128)(2,1)S(1)}, u32[]{:S(2)}, u32[]{:S(2)}) %collective-permute-start.20) | collective-permute-done | bytes 51232 | tf_op jit(solution)/shard_map/ppermute | solution.py:28
  71.7 1.6 %shard_map.106 = (bf16[64,384]{1,0:T(8,128)(2,1)S(1)}, f32[4,384]{1,0:T(4,128)S(1)}, f32[4,384]{1,0:T(4,128)S(1)}, f32[4,384]{1,0:T(4,128)S(1)}, f32[4,384]{1,0:T(4,128)S(1)}, /*index=5*/f32[1,384]{1,0:T(1,128)S(1)}) custom-call(s32[2]{0:T(128)S(1)} %pad_add_fusion.1.scalars.refs_0_, bf16[1,2,384,6144]{3,2,1,0:T(8,128)(2,1)S(1)} %shard_map.102.refs_1_, ...), custom_call_target="tpu_custom_call" | custom-call | flops 301989888 | bytes 4718592 | tf_op jit(solution)/shard_map/pallas_call | solution.py:308
  73.4 2.2 %collective-permute-start.25 = (f32[4,384]{1,0:T(4,128)S(1)}, f32[4,384]{1,0:T(4,128)S(1)}, u32[]{:S(2)}, u32[]{:S(2)}) collective-permute-start(f32[4,384]{1,0:T(4,128)S(1)} %get-tuple-element.66), channel_id=1, source_target_pairs={{0,3},{1,2},{2,1},{3,0},{4,7},{5,6},{6,5},{7,4},{8,11},{9,10},{10,... | collective-permute-start | bytes 18440 | tf_op jit(solution)/shard_map/ppermute | solution.py:28
  77.0 3.1 %shard_map.107 = (f32[384,3072]{1,0:T(8,128)}, f32[384,3072]{1,0:T(8,128)}, f32[4,384]{1,0:T(4,128)S(1)}) custom-call(s32[2]{0:T(128)S(1)} %pad_add_fusion.1.scalars.refs_0_, bf16[64,384]{1,0:T(8,128)(2,1)S(1)} %get-tuple-element.57.refs_1_, bf16[64,384]{1,0:T(8,128)(2,1)S(1)} %collective-permute-done.21.refs_2_, ...), custom_call_target="tpu_custom_call", output_to_operand_aliasing={{0}: (6, {}), {1}: (7, {})} | custom-call | flops 301989888 | bytes 4718592 | tf_op jit(solution)/shard_map/pallas_call | solution.py:360
  81.6 3.0 %collective-permute-start.26 = (f32[1,384]{1,0:T(1,128)S(1)}, f32[1,384]{1,0:T(1,128)S(1)}, u32[]{:S(2)}, u32[]{:S(2)}) collective-permute-start(f32[1,384]{1,0:T(1,128)S(1)} %get-tuple-element.86), channel_id=1, source_target_pairs={{0,12},{1,13},{2,14},{3,15},{4,8},{5,9},{6,10},{7,11},{8,4},{9,5},... | collective-permute-start | bytes 4616 | tf_op jit(solution)/shard_map/ppermute | solution.py:28
  84.7 2.3 %collective-permute-done.26 = f32[1,384]{1,0:T(1,128)S(1)} collective-permute-done((f32[1,384]{1,0:T(1,128)S(1)}, f32[1,384]{1,0:T(1,128)S(1)}, u32[]{:S(2)}, u32[]{:S(2)}) %collective-permute-start.26) | collective-permute-done | bytes 1568 | tf_op jit(solution)/shard_map/ppermute | solution.py:28
  87.0 1.1 %collective-permute-done.29 = f32[1,384]{1,0:T(1,128)S(1)} collective-permute-done((f32[1,384]{1,0:T(1,128)S(1)}, f32[1,384]{1,0:T(1,128)S(1)}, u32[]{:S(2)}, u32[]{:S(2)}) %collective-permute-start.29) | collective-permute-done | bytes 1568 | tf_op jit(solution)/shard_map/ppermute | solution.py:33
  (66 shorter events, 14.7 us)
Async XLA Ops:
  2.1 6.9 %collective-permute-start.2 = (bf16[1,72,384]{2,1,0:T(8,128)(2,1)S(1)}, bf16[1,72,384]{2,1,0:T(8,128)(2,1)S(1)}, u32[]{:S(2)}, u32[]{:S(2)}) collective-permute-start(bf16[1,72,384]{2,1,0:T(8,128)(2,1)S(1)} %bitcast.23), channel_id=1, source_target_pairs={{0,8},{1,9},{2,10},{3,11},{4,12},{5,13},{6,14},{7,15},{8,0},{9,1},... | collective-permute-start | bytes 165896 | tf_op jit(solution)/shard_map/ppermute | solution.py:28
  6.2 4.2 %collective-permute-start.1 = (bf16[1,72,384]{2,1,0:T(8,128)(2,1)S(1)}, bf16[1,72,384]{2,1,0:T(8,128)(2,1)S(1)}, u32[]{:S(2)}, u32[]{:S(2)}) collective-permute-start(bf16[1,72,384]{2,1,0:T(8,128)(2,1)S(1)} %bitcast.24), channel_id=1, source_target_pairs={{0,4},{1,5},{2,6},{3,7},{4,0},{5,1},{6,2},{7,3},{8,12},{9,13},{10,... | collective-permute-start | bytes 165896 | tf_op jit(solution)/shard_map/ppermute | solution.py:28
  7.8 6.0 %collective-permute-start = (bf16[1,72,384]{2,1,0:T(8,128)(2,1)S(1)}, bf16[1,72,384]{2,1,0:T(8,128)(2,1)S(1)}, u32[]{:S(2)}, u32[]{:S(2)}) collective-permute-start(bf16[1,72,384]{2,1,0:T(8,128)(2,1)S(1)} %bitcast.25), channel_id=1, source_target_pairs={{0,12},{1,13},{2,14},{3,15},{4,8},{5,9},{6,10},{7,11},{8,4},{9,5},... | collective-permute-start | bytes 165896 | tf_op jit(solution)/shard_map/ppermute | solution.py:28
  13.8 8.3 %collective-permute-start.3 = (bf16[4,72,384]{2,1,0:T(8,128)(2,1)S(1)}, bf16[4,72,384]{2,1,0:T(8,128)(2,1)S(1)}, u32[]{:S(2)}, u32[]{:S(2)}) collective-permute-start(bf16[4,72,384]{2,1,0:T(8,128)(2,1)S(1)} %pad_maximum_fusion._), channel_id=1, source_target_pairs={{0,2},{1,3},{2,0},{3,1},{4,6},{5,7},{6,4},{7,5},{8,10},{9,11},{10,... | collective-permute-start | bytes 663560 | tf_op jit(solution)/shard_map/ppermute | solution.py:28
  15.4 7.7 %collective-permute-start.4 = (bf16[4,72,384]{2,1,0:T(8,128)(2,1)S(1)}, bf16[4,72,384]{2,1,0:T(8,128)(2,1)S(1)}, u32[]{:S(2)}, u32[]{:S(2)}) collective-permute-start(bf16[4,72,384]{2,1,0:T(8,128)(2,1)S(1)} %pad_maximum_fusion._), channel_id=1, source_target_pairs={{0,1},{1,0},{2,3},{3,2},{4,5},{5,4},{6,7},{7,6},{8,9},{9,8},{10,11... | collective-permute-start | bytes 663560 | tf_op jit(solution)/shard_map/ppermute | solution.py:28
  16.9 8.5 %collective-permute-start.5 = (bf16[4,72,384]{2,1,0:T(8,128)(2,1)S(1)}, bf16[4,72,384]{2,1,0:T(8,128)(2,1)S(1)}, u32[]{:S(2)}, u32[]{:S(2)}) collective-permute-start(bf16[4,72,384]{2,1,0:T(8,128)(2,1)S(1)} %pad_maximum_fusion._), channel_id=1, source_target_pairs={{0,3},{1,2},{2,1},{3,0},{4,7},{5,6},{6,5},{7,4},{8,11},{9,10},{10,... | collective-permute-start | bytes 663560 | tf_op jit(solution)/shard_map/ppermute | solution.py:28
  28.1 6.0 %collective-permute-start.6 = (bf16[1,64,384]{2,1,0:T(8,128)(2,1)S(1)}, bf16[1,64,384]{2,1,0:T(8,128)(2,1)S(1)}, u32[]{:S(2)}, u32[]{:S(2)}) collective-permute-start(bf16[1,64,384]{2,1,0:T(8,128)(2,1)S(1)} %bitcast.19), channel_id=1, source_target_pairs={{0,12},{1,13},{2,14},{3,15},{4,8},{5,9},{6,10},{7,11},{8,4},{9,5},... | collective-permute-start | bytes 147464 | tf_op jit(solution)/shard_map/ppermute | solution.py:28
  29.5 4.6 %collective-permute-start.7 = (bf16[1,64,384]{2,1,0:T(8,128)(2,1)S(1)}, bf16[1,64,384]{2,1,0:T(8,128)(2,1)S(1)}, u32[]{:S(2)}, u32[]{:S(2)}) collective-permute-start(bf16[1,64,384]{2,1,0:T(8,128)(2,1)S(1)} %bitcast.20), channel_id=1, source_target_pairs={{0,4},{1,5},{2,6},{3,7},{4,0},{5,1},{6,2},{7,3},{8,12},{9,13},{10,... | collective-permute-start | bytes 147464 | tf_op jit(solution)/shard_map/ppermute | solution.py:28
  29.6 5.0 %collective-permute-start.8 = (bf16[1,64,384]{2,1,0:T(8,128)(2,1)S(1)}, bf16[1,64,384]{2,1,0:T(8,128)(2,1)S(1)}, u32[]{:S(2)}, u32[]{:S(2)}) collective-permute-start(bf16[1,64,384]{2,1,0:T(8,128)(2,1)S(1)} %bitcast.21), channel_id=1, source_target_pairs={{0,8},{1,9},{2,10},{3,11},{4,12},{5,13},{6,14},{7,15},{8,0},{9,1},... | collective-permute-start | bytes 147464 | tf_op jit(solution)/shard_map/ppermute | solution.py:28
  34.6 6.0 %collective-permute-start.9 = (bf16[4,64,384]{2,1,0:T(8,128)(2,1)S(1)}, bf16[4,64,384]{2,1,0:T(8,128)(2,1)S(1)}, u32[]{:S(2)}, u32[]{:S(2)}) collective-permute-start(bf16[4,64,384]{2,1,0:T(8,128)(2,1)S(1)} %pad_maximum_fusion.1), channel_id=1, source_target_pairs={{0,2},{1,3},{2,0},{3,1},{4,6},{5,7},{6,4},{7,5},{8,10},{9,11},{10,... | collective-permute-start | bytes 589832 | tf_op jit(solution)/shard_map/ppermute | solution.py:28
  36.2 5.7 %collective-permute-start.10 = (bf16[4,64,384]{2,1,0:T(8,128)(2,1)S(1)}, bf16[4,64,384]{2,1,0:T(8,128)(2,1)S(1)}, u32[]{:S(2)}, u32[]{:S(2)}) collective-permute-start(bf16[4,64,384]{2,1,0:T(8,128)(2,1)S(1)} %pad_maximum_fusion.1), channel_id=1, source_target_pairs={{0,1},{1,0},{2,3},{3,2},{4,5},{5,4},{6,7},{7,6},{8,9},{9,8},{10,11... | collective-permute-start | bytes 589832 | tf_op jit(solution)/shard_map/ppermute | solution.py:28
  37.7 6.6 %collective-permute-start.11 = (bf16[4,64,384]{2,1,0:T(8,128)(2,1)S(1)}, bf16[4,64,384]{2,1,0:T(8,128)(2,1)S(1)}, u32[]{:S(2)}, u32[]{:S(2)}) collective-permute-start(bf16[4,64,384]{2,1,0:T(8,128)(2,1)S(1)} %pad_maximum_fusion.1), channel_id=1, source_target_pairs={{0,3},{1,2},{2,1},{3,0},{4,7},{5,6},{6,5},{7,4},{8,11},{9,10},{10,... | collective-permute-start | bytes 589832 | tf_op jit(solution)/shard_map/ppermute | solution.py:28
  49.1 5.6 %collective-permute-start.16 = (bf16[64,3072]{1,0:T(8,128)(2,1)S(1)}, bf16[64,3072]{1,0:T(8,128)(2,1)S(1)}, u32[]{:S(2)}, u32[]{:S(2)}) collective-permute-start(bf16[64,3072]{1,0:T(8,128)(2,1)S(1)} %get-tuple-element.79), channel_id=1, source_target_pairs={{0,16},{16,0},{1,17},{17,1},{2,18},{18,2},{3,19},{19,3},{4,20},{20... | collective-permute-start | bytes 1179656 | tf_op jit(solution)/shard_map/ppermute | solution.py:33
  49.2 4.1 %collective-permute-start.17 = (bf16[64,384]{1,0:T(8,128)(2,1)S(1)}, bf16[64,384]{1,0:T(8,128)(2,1)S(1)}, u32[]{:S(2)}, u32[]{:S(2)}) collective-permute-start(bf16[64,384]{1,0:T(8,128)(2,1)S(1)} %get-tuple-element.47), channel_id=1, source_target_pairs={{0,16},{16,0},{1,17},{17,1},{2,18},{18,2},{3,19},{19,3},{4,20},{20... | collective-permute-start | bytes 147464 | tf_op jit(solution)/shard_map/ppermute | solution.py:33
  49.8 8.7 %collective-permute-start.12 = (bf16[4,200,128]{2,1,0:T(8,128)(2,1)S(1)}, bf16[4,200,128]{2,1,0:T(8,128)(2,1)S(1)}, u32[]{:S(2)}, u32[]{:S(2)}) collective-permute-start(bf16[4,200,128]{2,1,0:T(8,128)(2,1)S(1)} %get-tuple-element.75), channel_id=1, source_target_pairs={{0,2},{1,3},{2,0},{3,1},{4,6},{5,7},{6,4},{7,5},{8,10},{9,11},{10,... | collective-permute-start | bytes 614408 | tf_op jit(solution)/shard_map/ppermute | solution.py:28
  51.0 8.0 %collective-permute-start.13 = (bf16[4,200,128]{2,1,0:T(8,128)(2,1)S(1)}, bf16[4,200,128]{2,1,0:T(8,128)(2,1)S(1)}, u32[]{:S(2)}, u32[]{:S(2)}) collective-permute-start(bf16[4,200,128]{2,1,0:T(8,128)(2,1)S(1)} %get-tuple-element.74), channel_id=1, source_target_pairs={{0,1},{1,0},{2,3},{3,2},{4,5},{5,4},{6,7},{7,6},{8,9},{9,8},{10,11... | collective-permute-start | bytes 614408 | tf_op jit(solution)/shard_map/ppermute | solution.py:28
  52.5 10.0 %collective-permute-start.14 = (bf16[4,200,128]{2,1,0:T(8,128)(2,1)S(1)}, bf16[4,200,128]{2,1,0:T(8,128)(2,1)S(1)}, u32[]{:S(2)}, u32[]{:S(2)}) collective-permute-start(bf16[4,200,128]{2,1,0:T(8,128)(2,1)S(1)} %get-tuple-element.73), channel_id=1, source_target_pairs={{0,3},{1,2},{2,1},{3,0},{4,7},{5,6},{6,5},{7,4},{8,11},{9,10},{10,... | collective-permute-start | bytes 614408 | tf_op jit(solution)/shard_map/ppermute | solution.py:28
  53.3 1.2 %collective-permute-start.15 = (bf16[64,384]{1,0:T(8,128)(2,1)S(1)}, bf16[64,384]{1,0:T(8,128)(2,1)S(1)}, u32[]{:S(2)}, u32[]{:S(2)}) collective-permute-start(bf16[64,384]{1,0:T(8,128)(2,1)S(1)} %get-tuple-element.43.refs_1_), channel_id=1, source_target_pairs={{0,16},{16,0},{1,17},{17,1},{2,18},{18,2},{3,19},{19,3},{4,20},{20... | collective-permute-start | bytes 147464 | tf_op jit(solution)/shard_map/ppermute | solution.py:33
  54.6 22.4 %collective-permute-start.22 = (bf16[64,3072]{1,0:T(8,128)(2,1)S(1)}, bf16[64,3072]{1,0:T(8,128)(2,1)S(1)}, u32[]{:S(2)}, u32[]{:S(2)}) collective-permute-start(bf16[64,3072]{1,0:T(8,128)(2,1)S(1)} %get-tuple-element.77), channel_id=1, source_target_pairs={{0,16},{16,0},{1,17},{17,1},{2,18},{18,2},{3,19},{19,3},{4,20},{20... | collective-permute-start | bytes 1179656 | tf_op jit(solution)/shard_map/ppermute | solution.py:33
  62.6 6.3 %collective-permute-start.18 = (bf16[1,200,128]{2,1,0:T(8,128)(2,1)S(1)}, bf16[1,200,128]{2,1,0:T(8,128)(2,1)S(1)}, u32[]{:S(2)}, u32[]{:S(2)}) collective-permute-start(bf16[1,200,128]{2,1,0:T(8,128)(2,1)S(1)} %get-tuple-element.83), channel_id=1, source_target_pairs={{0,12},{1,13},{2,14},{3,15},{4,8},{5,9},{6,10},{7,11},{8,4},{9,5},... | collective-permute-start | bytes 153608 | tf_op jit(solution)/shard_map/ppermute | solution.py:28
  65.0 4.4 %collective-permute-start.19 = (bf16[1,200,128]{2,1,0:T(8,128)(2,1)S(1)}, bf16[1,200,128]{2,1,0:T(8,128)(2,1)S(1)}, u32[]{:S(2)}, u32[]{:S(2)}) collective-permute-start(bf16[1,200,128]{2,1,0:T(8,128)(2,1)S(1)} %get-tuple-element.82), channel_id=1, source_target_pairs={{0,4},{1,5},{2,6},{3,7},{4,0},{5,1},{6,2},{7,3},{8,12},{9,13},{10,... | collective-permute-start | bytes 153608 | tf_op jit(solution)/shard_map/ppermute | solution.py:28
  66.1 5.6 %collective-permute-start.20 = (bf16[1,200,128]{2,1,0:T(8,128)(2,1)S(1)}, bf16[1,200,128]{2,1,0:T(8,128)(2,1)S(1)}, u32[]{:S(2)}, u32[]{:S(2)}) collective-permute-start(bf16[1,200,128]{2,1,0:T(8,128)(2,1)S(1)} %get-tuple-element.81), channel_id=1, source_target_pairs={{0,8},{1,9},{2,10},{3,11},{4,12},{5,13},{6,14},{7,15},{8,0},{9,1},... | collective-permute-start | bytes 153608 | tf_op jit(solution)/shard_map/ppermute | solution.py:28
  73.3 3.6 %collective-permute-start.21 = (bf16[64,384]{1,0:T(8,128)(2,1)S(1)}, bf16[64,384]{1,0:T(8,128)(2,1)S(1)}, u32[]{:S(2)}, u32[]{:S(2)}) collective-permute-start(bf16[64,384]{1,0:T(8,128)(2,1)S(1)} %get-tuple-element.57.refs_1_), channel_id=1, source_target_pairs={{0,16},{16,0},{1,17},{17,1},{2,18},{18,2},{3,19},{19,3},{4,20},{20... | collective-permute-start | bytes 147464 | tf_op jit(solution)/shard_map/ppermute | solution.py:33
  73.4 6.7 %collective-permute-start.25 = (f32[4,384]{1,0:T(4,128)S(1)}, f32[4,384]{1,0:T(4,128)S(1)}, u32[]{:S(2)}, u32[]{:S(2)}) collective-permute-start(f32[4,384]{1,0:T(4,128)S(1)} %get-tuple-element.66), channel_id=1, source_target_pairs={{0,3},{1,2},{2,1},{3,0},{4,7},{5,6},{6,5},{7,4},{8,11},{9,10},{10,... | collective-permute-start | bytes 18440 | tf_op jit(solution)/shard_map/ppermute | solution.py:28
  75.6 4.5 %collective-permute-start.24 = (f32[4,384]{1,0:T(4,128)S(1)}, f32[4,384]{1,0:T(4,128)S(1)}, u32[]{:S(2)}, u32[]{:S(2)}) collective-permute-start(f32[4,384]{1,0:T(4,128)S(1)} %get-tuple-element.65), channel_id=1, source_target_pairs={{0,1},{1,0},{2,3},{3,2},{4,5},{5,4},{6,7},{7,6},{8,9},{9,8},{10,11... | collective-permute-start | bytes 18440 | tf_op jit(solution)/shard_map/ppermute | solution.py:28
  76.1 4.0 %collective-permute-start.23 = (f32[4,384]{1,0:T(4,128)S(1)}, f32[4,384]{1,0:T(4,128)S(1)}, u32[]{:S(2)}, u32[]{:S(2)}) collective-permute-start(f32[4,384]{1,0:T(4,128)S(1)} %get-tuple-element.64), channel_id=1, source_target_pairs={{0,2},{1,3},{2,0},{3,1},{4,6},{5,7},{6,4},{7,5},{8,10},{9,11},{10,... | collective-permute-start | bytes 18440 | tf_op jit(solution)/shard_map/ppermute | solution.py:28
  80.2 4.5 %collective-permute-start.28 = (f32[1,384]{1,0:T(1,128)S(1)}, f32[1,384]{1,0:T(1,128)S(1)}, u32[]{:S(2)}, u32[]{:S(2)}) collective-permute-start(f32[1,384]{1,0:T(1,128)S(1)} %get-tuple-element.87), channel_id=1, source_target_pairs={{0,8},{1,9},{2,10},{3,11},{4,12},{5,13},{6,14},{7,15},{8,0},{9,1},... | collective-permute-start | bytes 4616 | tf_op jit(solution)/shard_map/ppermute | solution.py:28
  80.7 4.0 %collective-permute-start.27 = (f32[1,384]{1,0:T(1,128)S(1)}, f32[1,384]{1,0:T(1,128)S(1)}, u32[]{:S(2)}, u32[]{:S(2)}) collective-permute-start(f32[1,384]{1,0:T(1,128)S(1)} %get-tuple-element.88), channel_id=1, source_target_pairs={{0,4},{1,5},{2,6},{3,7},{4,0},{5,1},{6,2},{7,3},{8,12},{9,13},{10,... | collective-permute-start | bytes 4616 | tf_op jit(solution)/shard_map/ppermute | solution.py:28
  81.6 5.4 %collective-permute-start.26 = (f32[1,384]{1,0:T(1,128)S(1)}, f32[1,384]{1,0:T(1,128)S(1)}, u32[]{:S(2)}, u32[]{:S(2)}) collective-permute-start(f32[1,384]{1,0:T(1,128)S(1)} %get-tuple-element.86), channel_id=1, source_target_pairs={{0,12},{1,13},{2,14},{3,15},{4,8},{5,9},{6,10},{7,11},{8,4},{9,5},... | collective-permute-start | bytes 4616 | tf_op jit(solution)/shard_map/ppermute | solution.py:28
  87.0 1.2 %collective-permute-start.29 = (f32[1,384]{1,0:T(1,128)S(1)}, f32[1,384]{1,0:T(1,128)S(1)}, u32[]{:S(2)}, u32[]{:S(2)}) collective-permute-start(f32[1,384]{1,0:T(1,128)S(1)} %get-tuple-element.69), channel_id=1, source_target_pairs={{0,16},{16,0},{1,17},{17,1},{2,18},{18,2},{3,19},{19,3},{4,20},{20... | collective-permute-start | bytes 4616 | tf_op jit(solution)/shard_map/ppermute | solution.py:33

commit v6 on v3

--- a/solution.py
+++ b/solution.py
@@ -60,6 +60,10 @@
 def reduce_round(held, group):
     sent = [from_xor(held[n + 1], d) for n, d in enumerate(group)]
     return [held[0]] + sent
+
+
+def in_hbm(value):
+    return pltpu.with_memory_space_constraint(value, pltpu.HBM)
 
 
 def gelu_and_slope(z):
@@ -381,7 +385,7 @@
         cost_estimate=pl.CostEstimate(
             flops=0, bytes_accessed=2 * weights.size, transcendentals=0
         ),
-    )(weights, after)
+    )(in_hbm(weights), after)
 
 
 def pack_kernel(scalars, *refs):
@@ -429,7 +433,7 @@
         out_specs=[VMEM] * 3,
         scratch_shapes=[pltpu.VMEM(gains.shape, F32), pltpu.SemaphoreType.DMA((3,))],
         compiler_params=pltpu.CompilerParams(vmem_limit_bytes=VMEM_LIMIT),
-    )(scalars, down_input, up_input, down_cot, up_cot, gains)
+    )(scalars, *map(in_hbm, (down_input, up_input, down_cot, up_cot, gains)))
 
 
 def keep_live(live, record, previous):

time: 89.3 us -> 85.9 us (0.962)
  local copies, waits for them, and re-layouts: 8.61 us -> 1.06 us
  Pallas kernels: 17.4 us -> 21.2 us
    unnamed x24 -> x12, local copies, waits for them, and re-layouts: 7.78 us -> 0.23 us
    pallas_call x1, Pallas kernels: 0.65 us -> 3.79 us  [load_call(): pl.pallas_call(load_kernel, out_shape=jax.ShapeDtypeStruct(weights.shape,...]
  transfers between devices with their start and end apart: 30 -> 30, of which waited for: 18 -> 18; matrix products, arithmetic and copies ran while one was open for 2% -> 2% of each run, Pallas kernels for 11% -> 15%
where the time goes in v6:
time: 85.9 us; the launch traced here: 85.7 us
  starting transfers between devices  34.6 us (40%)
  waiting for transfers between devices  26.3 us (31%)
  Pallas kernels  21.2 us (25%)
  other arithmetic  1.68 us (2%)
  local copies, waits for them, and re-layouts  1.06 us (1%)
    ppermute x24, starting transfers between devices, from_xor(): return lax.ppermute(value, 'seq', [(i, i ^ distance) for i in range(size)])  33.3 us
    ppermute x24, waiting for transfers between devices, from_xor(): return lax.ppermute(value, 'seq', [(i, i ^ distance) for i in range(size)])  25.8 us
    pallas_call x2, Pallas kernels, weight_grad_call(): pl.pallas_call(functools.partial(weight_grad_kernel, first), grid=(steps,...  7.4 us
    pallas_call x2, Pallas kernels, section_call(): pl.pallas_call(functools.partial(section_kernel, offsets, (tokens, wide,...  7.01 us
    pallas_call x1, Pallas kernels, load_call(): pl.pallas_call(load_kernel, out_shape=jax.ShapeDtypeStruct(weights.shape,...  3.79 us
  transfers between devices with their start and end apart: 30, of which 18 were waited for; matrix products, arithmetic and copies ran while one was open for 2% of the time, Pallas kernels for 15%

profile of v6, /device:TPU:0, one launch (start us, length us, event | category | flops | bytes accessed | tf_op | source)
XLA Modules:
  0.0 85.7 jit_solution(3086497489849099041)
XLA Ops:
  0.7 1.4 %shard_map.101 = (bf16[64,384]{1,0:T(8,128)(2,1)S(1)}, bf16[64,384]{1,0:T(8,128)(2,1)S(1)}, bf16[72,384]{1,0:T(8,128)(2,1)S(1)}) custom-call(s32[2]{0:T(128)S(1)} %pad_add_fusion.scalars.refs_0_, bf16[64,384]{1,0:T(8,128)(2,1)} %refs_0_.1, bf16[64,384]{1,0:T(8,128)(2,1)} %refs_1_.1, bf16[64,384]{1,0:T(8,128)(2,1)} %refs_2_.1, bf16[64,384]{1,0:T(8,128)(2,1)} %refs_3_.1, ...), custom_call_target="tpu_custom_call" | custom-call | tf_op jit(solution)/shard_map/pallas_call | solution.py:425
  2.1 5.1 %collective-permute-start.2 = (bf16[1,72,384]{2,1,0:T(8,128)(2,1)S(1)}, bf16[1,72,384]{2,1,0:T(8,128)(2,1)S(1)}, u32[]{:S(2)}, u32[]{:S(2)}) collective-permute-start(bf16[1,72,384]{2,1,0:T(8,128)(2,1)S(1)} %bitcast.25), channel_id=1, source_target_pairs={{0,12},{1,13},{2,14},{3,15},{4,8},{5,9},{6,10},{7,11},{8,4},{9,5},... | collective-permute-start | bytes 165896 | tf_op jit(solution)/shard_map/ppermute | solution.py:27
  9.8 1.7 %collective-permute-done.1 = bf16[1,72,384]{2,1,0:T(8,128)(2,1)S(1)} collective-permute-done((bf16[1,72,384]{2,1,0:T(8,128)(2,1)S(1)}, bf16[1,72,384]{2,1,0:T(8,128)(2,1)S(1)}, u32[]{:S(2)}, u32[]{:S(2)}) %collective-permute-start.1) | collective-permute-done | bytes 55328 | tf_op jit(solution)/shard_map/ppermute | solution.py:27
  11.5 1.2 %collective-permute-done = bf16[1,72,384]{2,1,0:T(8,128)(2,1)S(1)} collective-permute-done((bf16[1,72,384]{2,1,0:T(8,128)(2,1)S(1)}, bf16[1,72,384]{2,1,0:T(8,128)(2,1)S(1)}, u32[]{:S(2)}, u32[]{:S(2)}) %collective-permute-start) | collective-permute-done | bytes 55328 | tf_op jit(solution)/shard_map/ppermute | solution.py:27
  12.7 1.6 %collective-permute-start.3 = (bf16[4,72,384]{2,1,0:T(8,128)(2,1)S(1)}, bf16[4,72,384]{2,1,0:T(8,128)(2,1)S(1)}, u32[]{:S(2)}, u32[]{:S(2)}) collective-permute-start(bf16[4,72,384]{2,1,0:T(8,128)(2,1)S(1)} %pad_maximum_fusion._), channel_id=1, source_target_pairs={{0,2},{1,3},{2,0},{3,1},{4,6},{5,7},{6,4},{7,5},{8,10},{9,11},{10,... | collective-permute-start | bytes 663560 | tf_op jit(solution)/shard_map/ppermute | solution.py:27
  14.3 1.5 %collective-permute-start.4 = (bf16[4,72,384]{2,1,0:T(8,128)(2,1)S(1)}, bf16[4,72,384]{2,1,0:T(8,128)(2,1)S(1)}, u32[]{:S(2)}, u32[]{:S(2)}) collective-permute-start(bf16[4,72,384]{2,1,0:T(8,128)(2,1)S(1)} %pad_maximum_fusion._), channel_id=1, source_target_pairs={{0,1},{1,0},{2,3},{3,2},{4,5},{5,4},{6,7},{7,6},{8,9},{9,8},{10,11... | collective-permute-start | bytes 663560 | tf_op jit(solution)/shard_map/ppermute | solution.py:27
  16.3 3.8 %shard_map.102.refs_1_ = bf16[1,2,384,6144]{3,2,1,0:T(8,128)(2,1)S(1)} custom-call(bf16[1,2,384,6144]{3,2,1,0:T(8,128)(2,1)} %weights.1, bf16[4,72,384]{2,1,0:T(8,128)(2,1)S(1)} %pad_maximum_fusion._), custom_call_target="tpu_custom_call" | custom-call | bytes 9437184 | tf_op jit(solution)/shard_map/pallas_call | solution.py:378
  21.8 2.3 %collective-permute-done.5 = bf16[4,72,384]{2,1,0:T(8,128)(2,1)S(1)} collective-permute-done((bf16[4,72,384]{2,1,0:T(8,128)(2,1)S(1)}, bf16[4,72,384]{2,1,0:T(8,128)(2,1)S(1)}, u32[]{:S(2)}, u32[]{:S(2)}) %collective-permute-start.5) | collective-permute-done | bytes 221216 | tf_op jit(solution)/shard_map/ppermute | solution.py:27
  24.1 2.7 %shard_map.103 = (bf16[64,6144]{1,0:T(8,128)(2,1)S(1)}, f32[64,128]{1,0:T(8,128)S(1)}, f32[64,384]{1,0:T(8,128)S(1)}, bf16[64,384]{1,0:T(8,128)(2,1)S(1)}, f32[2,6144]{1,0:T(2,128)S(1)}) custom-call(s32[2]{0:T(128)S(1)} %pad_add_fusion.scalars.refs_0_, bf16[1,2,384,6144]{3,2,1,0:T(8,128)(2,1)S(1)} %shard_map.102.refs_1_, ...), custom_call_target="tpu_custom_call" | custom-call | flops 301989888 | bytes 4718592 | tf_op jit(solution)/shard_map/pallas_call | solution.py:227
  26.8 2.2 %collective-permute-start.6 = (bf16[1,64,384]{2,1,0:T(8,128)(2,1)S(1)}, bf16[1,64,384]{2,1,0:T(8,128)(2,1)S(1)}, u32[]{:S(2)}, u32[]{:S(2)}) collective-permute-start(bf16[1,64,384]{2,1,0:T(8,128)(2,1)S(1)} %bitcast.21), channel_id=1, source_target_pairs={{0,8},{1,9},{2,10},{3,11},{4,12},{5,13},{6,14},{7,15},{8,0},{9,1},... | collective-permute-start | bytes 147464 | tf_op jit(solution)/shard_map/ppermute | solution.py:27
  29.5 1.7 %collective-permute-start.8 = (bf16[1,64,384]{2,1,0:T(8,128)(2,1)S(1)}, bf16[1,64,384]{2,1,0:T(8,128)(2,1)S(1)}, u32[]{:S(2)}, u32[]{:S(2)}) collective-permute-start(bf16[1,64,384]{2,1,0:T(8,128)(2,1)S(1)} %bitcast.23), channel_id=1, source_target_pairs={{0,12},{1,13},{2,14},{3,15},{4,8},{5,9},{6,10},{7,11},{8,4},{9,5},... | collective-permute-start | bytes 147464 | tf_op jit(solution)/shard_map/ppermute | solution.py:27
  31.8 1.2 %collective-permute-done.7 = bf16[1,64,384]{2,1,0:T(8,128)(2,1)S(1)} collective-permute-done((bf16[1,64,384]{2,1,0:T(8,128)(2,1)S(1)}, bf16[1,64,384]{2,1,0:T(8,128)(2,1)S(1)}, u32[]{:S(2)}, u32[]{:S(2)}) %collective-permute-start.7) | collective-permute-done | bytes 49184 | tf_op jit(solution)/shard_map/ppermute | solution.py:27
  33.1 2.3 %collective-permute-done.8 = bf16[1,64,384]{2,1,0:T(8,128)(2,1)S(1)} collective-permute-done((bf16[1,64,384]{2,1,0:T(8,128)(2,1)S(1)}, bf16[1,64,384]{2,1,0:T(8,128)(2,1)S(1)}, u32[]{:S(2)}, u32[]{:S(2)}) %collective-permute-start.8) | collective-permute-done | bytes 49184 | tf_op jit(solution)/shard_map/ppermute | solution.py:27
  35.4 1.6 %collective-permute-start.9 = (bf16[4,64,384]{2,1,0:T(8,128)(2,1)S(1)}, bf16[4,64,384]{2,1,0:T(8,128)(2,1)S(1)}, u32[]{:S(2)}, u32[]{:S(2)}) collective-permute-start(bf16[4,64,384]{2,1,0:T(8,128)(2,1)S(1)} %pad_maximum_fusion.1), channel_id=1, source_target_pairs={{0,2},{1,3},{2,0},{3,1},{4,6},{5,7},{6,4},{7,5},{8,10},{9,11},{10,... | collective-permute-start | bytes 589832 | tf_op jit(solution)/shard_map/ppermute | solution.py:27
  37.1 1.5 %collective-permute-start.10 = (bf16[4,64,384]{2,1,0:T(8,128)(2,1)S(1)}, bf16[4,64,384]{2,1,0:T(8,128)(2,1)S(1)}, u32[]{:S(2)}, u32[]{:S(2)}) collective-permute-start(bf16[4,64,384]{2,1,0:T(8,128)(2,1)S(1)} %pad_maximum_fusion.1), channel_id=1, source_target_pairs={{0,1},{1,0},{2,3},{3,2},{4,5},{5,4},{6,7},{7,6},{8,9},{9,8},{10,11... | collective-permute-start | bytes 589832 | tf_op jit(solution)/shard_map/ppermute | solution.py:27
  39.0 2.1 %collective-permute-done.9 = bf16[4,64,384]{2,1,0:T(8,128)(2,1)S(1)} collective-permute-done((bf16[4,64,384]{2,1,0:T(8,128)(2,1)S(1)}, bf16[4,64,384]{2,1,0:T(8,128)(2,1)S(1)}, u32[]{:S(2)}, u32[]{:S(2)}) %collective-permute-start.9) | collective-permute-done | bytes 196640 | tf_op jit(solution)/shard_map/ppermute | solution.py:27
  41.2 1.5 %collective-permute-done.10 = bf16[4,64,384]{2,1,0:T(8,128)(2,1)S(1)} collective-permute-done((bf16[4,64,384]{2,1,0:T(8,128)(2,1)S(1)}, bf16[4,64,384]{2,1,0:T(8,128)(2,1)S(1)}, u32[]{:S(2)}, u32[]{:S(2)}) %collective-permute-start.10) | collective-permute-done | bytes 196640 | tf_op jit(solution)/shard_map/ppermute | solution.py:27
  42.8 2.4 %collective-permute-done.11 = bf16[4,64,384]{2,1,0:T(8,128)(2,1)S(1)} collective-permute-done((bf16[4,64,384]{2,1,0:T(8,128)(2,1)S(1)}, bf16[4,64,384]{2,1,0:T(8,128)(2,1)S(1)}, u32[]{:S(2)}, u32[]{:S(2)}) %collective-permute-start.11) | collective-permute-done | bytes 196640 | tf_op jit(solution)/shard_map/ppermute | solution.py:27
  45.2 4.3 %shard_map.104 = (bf16[64,6144]{1,0:T(8,128)(2,1)S(1)}, f32[64,128]{1,0:T(8,128)S(1)}, f32[64,384]{1,0:T(8,128)}, bf16[64,384]{1,0:T(8,128)(2,1)S(1)}, bf16[64,3...) custom-call(s32[2]{0:T(128)S(1)} %pad_add_fusion.1.refs_0_, bf16[1,2,384,6144]{3,2,1,0:T(8,128)(2,1)S(1)} %shard_map.102.refs_1_, ...), custom_call_target="tpu_custom_call" | custom-call | flops 603979776 | bytes 4718592 | tf_op jit(solution)/shard_map/pallas_call | solution.py:227
  49.6 1.2 %collective-permute-start.15 = (bf16[4,200,128]{2,1,0:T(8,128)(2,1)S(1)}, bf16[4,200,128]{2,1,0:T(8,128)(2,1)S(1)}, u32[]{:S(2)}, u32[]{:S(2)}) collective-permute-start(bf16[4,200,128]{2,1,0:T(8,128)(2,1)S(1)} %get-tuple-element.60), channel_id=1, source_target_pairs={{0,2},{1,3},{2,0},{3,1},{4,6},{5,7},{6,4},{7,5},{8,10},{9,11},{10,... | collective-permute-start | bytes 614408 | tf_op jit(solution)/shard_map/ppermute | solution.py:27
  50.8 1.5 %collective-permute-start.14 = (bf16[4,200,128]{2,1,0:T(8,128)(2,1)S(1)}, bf16[4,200,128]{2,1,0:T(8,128)(2,1)S(1)}, u32[]{:S(2)}, u32[]{:S(2)}) collective-permute-start(bf16[4,200,128]{2,1,0:T(8,128)(2,1)S(1)} %get-tuple-element.61), channel_id=1, source_target_pairs={{0,1},{1,0},{2,3},{3,2},{4,5},{5,4},{6,7},{7,6},{8,9},{9,8},{10,11... | collective-permute-start | bytes 614408 | tf_op jit(solution)/shard_map/ppermute | solution.py:27
  53.8 1.6 %collective-permute-done.15 = bf16[4,200,128]{2,1,0:T(8,128)(2,1)S(1)} collective-permute-done((bf16[4,200,128]{2,1,0:T(8,128)(2,1)S(1)}, bf16[4,200,128]{2,1,0:T(8,128)(2,1)S(1)}, u32[]{:S(2)}, u32[]{:S(2)}) %collective-permute-start.15) | collective-permute-done | bytes 204832 | tf_op jit(solution)/shard_map/ppermute | solution.py:27
  56.6 2.5 %collective-permute-done.13 = bf16[4,200,128]{2,1,0:T(8,128)(2,1)S(1)} collective-permute-done((bf16[4,200,128]{2,1,0:T(8,128)(2,1)S(1)}, bf16[4,200,128]{2,1,0:T(8,128)(2,1)S(1)}, u32[]{:S(2)}, u32[]{:S(2)}) %collective-permute-start.13) | collective-permute-done | bytes 204832 | tf_op jit(solution)/shard_map/ppermute | solution.py:27
  59.2 1.8 %collective-permute-start.16 = (bf16[1,200,128]{2,1,0:T(8,128)(2,1)S(1)}, bf16[1,200,128]{2,1,0:T(8,128)(2,1)S(1)}, u32[]{:S(2)}, u32[]{:S(2)}) collective-permute-start(bf16[1,200,128]{2,1,0:T(8,128)(2,1)S(1)} %get-tuple-element.64), channel_id=1, source_target_pairs={{0,12},{1,13},{2,14},{3,15},{4,8},{5,9},{6,10},{7,11},{8,4},{9,5},... | collective-permute-start | bytes 153608 | tf_op jit(solution)/shard_map/ppermute | solution.py:27
  61.0 2.7 %collective-permute-start.18 = (bf16[1,200,128]{2,1,0:T(8,128)(2,1)S(1)}, bf16[1,200,128]{2,1,0:T(8,128)(2,1)S(1)}, u32[]{:S(2)}, u32[]{:S(2)}) collective-permute-start(bf16[1,200,128]{2,1,0:T(8,128)(2,1)S(1)} %get-tuple-element.62), channel_id=1, source_target_pairs={{0,8},{1,9},{2,10},{3,11},{4,12},{5,13},{6,14},{7,15},{8,0},{9,1},... | collective-permute-start | bytes 153608 | tf_op jit(solution)/shard_map/ppermute | solution.py:27
  63.7 1.6 %collective-permute-done.16 = bf16[1,200,128]{2,1,0:T(8,128)(2,1)S(1)} collective-permute-done((bf16[1,200,128]{2,1,0:T(8,128)(2,1)S(1)}, bf16[1,200,128]{2,1,0:T(8,128)(2,1)S(1)}, u32[]{:S(2)}, u32[]{:S(2)}) %collective-permute-start.16) | collective-permute-done | bytes 51232 | tf_op jit(solution)/shard_map/ppermute | solution.py:27
  66.2 1.6 %shard_map.105 = (bf16[64,384]{1,0:T(8,128)(2,1)S(1)}, f32[4,384]{1,0:T(4,128)S(1)}, f32[4,384]{1,0:T(4,128)S(1)}, f32[4,384]{1,0:T(4,128)S(1)}, f32[4,384]{1,0:T(4,128)S(1)}, /*index=5*/f32[1,384]{1,0:T(1,128)S(1)}) custom-call(s32[2]{0:T(128)S(1)} %pad_add_fusion.scalars.refs_0_, bf16[1,2,384,6144]{3,2,1,0:T(8,128)(2,1)S(1)} %shard_map.102.refs_1_, ...), custom_call_target="tpu_custom_call" | custom-call | flops 301989888 | bytes 4718592 | tf_op jit(solution)/shard_map/pallas_call | solution.py:306
  69.6 1.5 %collective-permute-start.24 = (f32[4,384]{1,0:T(4,128)S(1)}, f32[4,384]{1,0:T(4,128)S(1)}, u32[]{:S(2)}, u32[]{:S(2)}) collective-permute-start(f32[4,384]{1,0:T(4,128)S(1)} %get-tuple-element.45), channel_id=1, source_target_pairs={{0,1},{1,0},{2,3},{3,2},{4,5},{5,4},{6,7},{7,6},{8,9},{9,8},{10,11... | collective-permute-start | bytes 18440 | tf_op jit(solution)/shard_map/ppermute | solution.py:27
  72.0 3.7 %shard_map.106 = (f32[384,3072]{1,0:T(8,128)}, f32[4,384]{1,0:T(4,128)S(1)}) custom-call(s32[2]{0:T(128)S(1)} %pad_add_fusion.scalars.refs_0_, bf16[64,384]{1,0:T(8,128)(2,1)S(1)} %get-tuple-element.38.refs_1_, bf16[64,384]{1,0:T(8,128)(2,1)S(1)} %collective-permute-done.19.refs_2_, bf16[64,384]{1,0:T(8,128)(2,1)S(1)} %get-tuple-element.39.refs_3_, ...), custom_call_target="tpu_custom_call" | custom-call | flops 301989888 | bytes 4718592 | tf_op jit(solution)/shard_map/pallas_call | solution.py:350
  75.7 2.6 %collective-permute-start.28 = (f32[1,384]{1,0:T(1,128)S(1)}, f32[1,384]{1,0:T(1,128)S(1)}, u32[]{:S(2)}, u32[]{:S(2)}) collective-permute-start(f32[1,384]{1,0:T(1,128)S(1)} %get-tuple-element.68), channel_id=1, source_target_pairs={{0,8},{1,9},{2,10},{3,11},{4,12},{5,13},{6,14},{7,15},{8,0},{9,1},... | collective-permute-start | bytes 4616 | tf_op jit(solution)/shard_map/ppermute | solution.py:27
  78.3 1.9 %collective-permute-start.26 = (f32[1,384]{1,0:T(1,128)S(1)}, f32[1,384]{1,0:T(1,128)S(1)}, u32[]{:S(2)}, u32[]{:S(2)}) collective-permute-start(f32[1,384]{1,0:T(1,128)S(1)} %get-tuple-element.67), channel_id=1, source_target_pairs={{0,12},{1,13},{2,14},{3,15},{4,8},{5,9},{6,10},{7,11},{8,4},{9,5},... | collective-permute-start | bytes 4616 | tf_op jit(solution)/shard_map/ppermute | solution.py:27
  80.2 3.7 %shard_map.107 = (f32[384,3072]{1,0:T(8,128)}, f32[1,384]{1,0:T(1,128)S(1)}) custom-call(s32[2]{0:T(128)S(1)} %pad_add_fusion.scalars.refs_0_, bf16[64,384]{1,0:T(8,128)(2,1)S(1)} %get-tuple-element.38.refs_1_, bf16[64,384]{1,0:T(8,128)(2,1)S(1)} %collective-permute-done.19.refs_2_, bf16[64,384]{1,0:T(8,128)(2,1)S(1)} %get-tuple-element.39.refs_3_, ...), custom_call_target="tpu_custom_call" | custom-call | flops 301989888 | bytes 4718592 | tf_op jit(solution)/shard_map/pallas_call | solution.py:350
  (64 shorter events, 14.9 us)
Async XLA Ops:
  2.1 7.7 %collective-permute-start.2 = (bf16[1,72,384]{2,1,0:T(8,128)(2,1)S(1)}, bf16[1,72,384]{2,1,0:T(8,128)(2,1)S(1)}, u32[]{:S(2)}, u32[]{:S(2)}) collective-permute-start(bf16[1,72,384]{2,1,0:T(8,128)(2,1)S(1)} %bitcast.25), channel_id=1, source_target_pairs={{0,12},{1,13},{2,14},{3,15},{4,8},{5,9},{6,10},{7,11},{8,4},{9,5},... | collective-permute-start | bytes 165896 | tf_op jit(solution)/shard_map/ppermute | solution.py:27
  7.2 4.2 %collective-permute-start.1 = (bf16[1,72,384]{2,1,0:T(8,128)(2,1)S(1)}, bf16[1,72,384]{2,1,0:T(8,128)(2,1)S(1)}, u32[]{:S(2)}, u32[]{:S(2)}) collective-permute-start(bf16[1,72,384]{2,1,0:T(8,128)(2,1)S(1)} %bitcast.26), channel_id=1, source_target_pairs={{0,4},{1,5},{2,6},{3,7},{4,0},{5,1},{6,2},{7,3},{8,12},{9,13},{10,... | collective-permute-start | bytes 165896 | tf_op jit(solution)/shard_map/ppermute | solution.py:27
  7.2 5.4 %collective-permute-start = (bf16[1,72,384]{2,1,0:T(8,128)(2,1)S(1)}, bf16[1,72,384]{2,1,0:T(8,128)(2,1)S(1)}, u32[]{:S(2)}, u32[]{:S(2)}) collective-permute-start(bf16[1,72,384]{2,1,0:T(8,128)(2,1)S(1)} %bitcast.27), channel_id=1, source_target_pairs={{0,8},{1,9},{2,10},{3,11},{4,12},{5,13},{6,14},{7,15},{8,0},{9,1},... | collective-permute-start | bytes 165896 | tf_op jit(solution)/shard_map/ppermute | solution.py:27
  12.7 8.4 %collective-permute-start.3 = (bf16[4,72,384]{2,1,0:T(8,128)(2,1)S(1)}, bf16[4,72,384]{2,1,0:T(8,128)(2,1)S(1)}, u32[]{:S(2)}, u32[]{:S(2)}) collective-permute-start(bf16[4,72,384]{2,1,0:T(8,128)(2,1)S(1)} %pad_maximum_fusion._), channel_id=1, source_target_pairs={{0,2},{1,3},{2,0},{3,1},{4,6},{5,7},{6,4},{7,5},{8,10},{9,11},{10,... | collective-permute-start | bytes 663560 | tf_op jit(solution)/shard_map/ppermute | solution.py:27
  14.3 7.5 %collective-permute-start.4 = (bf16[4,72,384]{2,1,0:T(8,128)(2,1)S(1)}, bf16[4,72,384]{2,1,0:T(8,128)(2,1)S(1)}, u32[]{:S(2)}, u32[]{:S(2)}) collective-permute-start(bf16[4,72,384]{2,1,0:T(8,128)(2,1)S(1)} %pad_maximum_fusion._), channel_id=1, source_target_pairs={{0,1},{1,0},{2,3},{3,2},{4,5},{5,4},{6,7},{7,6},{8,9},{9,8},{10,11... | collective-permute-start | bytes 663560 | tf_op jit(solution)/shard_map/ppermute | solution.py:27
  15.8 8.3 %collective-permute-start.5 = (bf16[4,72,384]{2,1,0:T(8,128)(2,1)S(1)}, bf16[4,72,384]{2,1,0:T(8,128)(2,1)S(1)}, u32[]{:S(2)}, u32[]{:S(2)}) collective-permute-start(bf16[4,72,384]{2,1,0:T(8,128)(2,1)S(1)} %pad_maximum_fusion._), channel_id=1, source_target_pairs={{0,3},{1,2},{2,1},{3,0},{4,7},{5,6},{6,5},{7,4},{8,11},{9,10},{10,... | collective-permute-start | bytes 663560 | tf_op jit(solution)/shard_map/ppermute | solution.py:27
  26.8 5.1 %collective-permute-start.6 = (bf16[1,64,384]{2,1,0:T(8,128)(2,1)S(1)}, bf16[1,64,384]{2,1,0:T(8,128)(2,1)S(1)}, u32[]{:S(2)}, u32[]{:S(2)}) collective-permute-start(bf16[1,64,384]{2,1,0:T(8,128)(2,1)S(1)} %bitcast.21), channel_id=1, source_target_pairs={{0,8},{1,9},{2,10},{3,11},{4,12},{5,13},{6,14},{7,15},{8,0},{9,1},... | collective-permute-start | bytes 147464 | tf_op jit(solution)/shard_map/ppermute | solution.py:27
  29.0 4.1 %collective-permute-start.7 = (bf16[1,64,384]{2,1,0:T(8,128)(2,1)S(1)}, bf16[1,64,384]{2,1,0:T(8,128)(2,1)S(1)}, u32[]{:S(2)}, u32[]{:S(2)}) collective-permute-start(bf16[1,64,384]{2,1,0:T(8,128)(2,1)S(1)} %bitcast.22), channel_id=1, source_target_pairs={{0,4},{1,5},{2,6},{3,7},{4,0},{5,1},{6,2},{7,3},{8,12},{9,13},{10,... | collective-permute-start | bytes 147464 | tf_op jit(solution)/shard_map/ppermute | solution.py:27
  29.5 5.9 %collective-permute-start.8 = (bf16[1,64,384]{2,1,0:T(8,128)(2,1)S(1)}, bf16[1,64,384]{2,1,0:T(8,128)(2,1)S(1)}, u32[]{:S(2)}, u32[]{:S(2)}) collective-permute-start(bf16[1,64,384]{2,1,0:T(8,128)(2,1)S(1)} %bitcast.23), channel_id=1, source_target_pairs={{0,12},{1,13},{2,14},{3,15},{4,8},{5,9},{6,10},{7,11},{8,4},{9,5},... | collective-permute-start | bytes 147464 | tf_op jit(solution)/shard_map/ppermute | solution.py:27
  35.4 5.7 %collective-permute-start.9 = (bf16[4,64,384]{2,1,0:T(8,128)(2,1)S(1)}, bf16[4,64,384]{2,1,0:T(8,128)(2,1)S(1)}, u32[]{:S(2)}, u32[]{:S(2)}) collective-permute-start(bf16[4,64,384]{2,1,0:T(8,128)(2,1)S(1)} %pad_maximum_fusion.1), channel_id=1, source_target_pairs={{0,2},{1,3},{2,0},{3,1},{4,6},{5,7},{6,4},{7,5},{8,10},{9,11},{10,... | collective-permute-start | bytes 589832 | tf_op jit(solution)/shard_map/ppermute | solution.py:27
  37.1 5.7 %collective-permute-start.10 = (bf16[4,64,384]{2,1,0:T(8,128)(2,1)S(1)}, bf16[4,64,384]{2,1,0:T(8,128)(2,1)S(1)}, u32[]{:S(2)}, u32[]{:S(2)}) collective-permute-start(bf16[4,64,384]{2,1,0:T(8,128)(2,1)S(1)} %pad_maximum_fusion.1), channel_id=1, source_target_pairs={{0,1},{1,0},{2,3},{3,2},{4,5},{5,4},{6,7},{7,6},{8,9},{9,8},{10,11... | collective-permute-start | bytes 589832 | tf_op jit(solution)/shard_map/ppermute | solution.py:27
  38.6 6.6 %collective-permute-start.11 = (bf16[4,64,384]{2,1,0:T(8,128)(2,1)S(1)}, bf16[4,64,384]{2,1,0:T(8,128)(2,1)S(1)}, u32[]{:S(2)}, u32[]{:S(2)}) collective-permute-start(bf16[4,64,384]{2,1,0:T(8,128)(2,1)S(1)} %pad_maximum_fusion.1), channel_id=1, source_target_pairs={{0,3},{1,2},{2,1},{3,0},{4,7},{5,6},{6,5},{7,4},{8,11},{9,10},{10,... | collective-permute-start | bytes 589832 | tf_op jit(solution)/shard_map/ppermute | solution.py:27
  49.6 5.8 %collective-permute-start.15 = (bf16[4,200,128]{2,1,0:T(8,128)(2,1)S(1)}, bf16[4,200,128]{2,1,0:T(8,128)(2,1)S(1)}, u32[]{:S(2)}, u32[]{:S(2)}) collective-permute-start(bf16[4,200,128]{2,1,0:T(8,128)(2,1)S(1)} %get-tuple-element.60), channel_id=1, source_target_pairs={{0,2},{1,3},{2,0},{3,1},{4,6},{5,7},{6,4},{7,5},{8,10},{9,11},{10,... | collective-permute-start | bytes 614408 | tf_op jit(solution)/shard_map/ppermute | solution.py:27
  50.8 5.8 %collective-permute-start.14 = (bf16[4,200,128]{2,1,0:T(8,128)(2,1)S(1)}, bf16[4,200,128]{2,1,0:T(8,128)(2,1)S(1)}, u32[]{:S(2)}, u32[]{:S(2)}) collective-permute-start(bf16[4,200,128]{2,1,0:T(8,128)(2,1)S(1)} %get-tuple-element.61), channel_id=1, source_target_pairs={{0,1},{1,0},{2,3},{3,2},{4,5},{5,4},{6,7},{7,6},{8,9},{9,8},{10,11... | collective-permute-start | bytes 614408 | tf_op jit(solution)/shard_map/ppermute | solution.py:27
  52.3 6.8 %collective-permute-start.13 = (bf16[4,200,128]{2,1,0:T(8,128)(2,1)S(1)}, bf16[4,200,128]{2,1,0:T(8,128)(2,1)S(1)}, u32[]{:S(2)}, u32[]{:S(2)}) collective-permute-start(bf16[4,200,128]{2,1,0:T(8,128)(2,1)S(1)} %get-tuple-element.59), channel_id=1, source_target_pairs={{0,3},{1,2},{2,1},{3,0},{4,7},{5,6},{6,5},{7,4},{8,11},{9,10},{10,... | collective-permute-start | bytes 614408 | tf_op jit(solution)/shard_map/ppermute | solution.py:27
  53.1 15.3 %collective-permute-start.20 = (bf16[64,384]{1,0:T(8,128)(2,1)S(1)}, bf16[64,384]{1,0:T(8,128)(2,1)S(1)}, u32[]{:S(2)}, u32[]{:S(2)}) collective-permute-start(bf16[64,384]{1,0:T(8,128)(2,1)S(1)} %get-tuple-element.39.refs_3_), channel_id=1, source_target_pairs={{0,16},{16,0},{1,17},{17,1},{2,18},{18,2},{3,19},{19,3},{4,20},{20... | collective-permute-start | bytes 147464 | tf_op jit(solution)/shard_map/ppermute | solution.py:32
  53.2 17.9 %collective-permute-start.21 = (bf16[64,3072]{1,0:T(8,128)(2,1)S(1)}, bf16[64,3072]{1,0:T(8,128)(2,1)S(1)}, u32[]{:S(2)}, u32[]{:S(2)}) collective-permute-start(bf16[64,3072]{1,0:T(8,128)(2,1)S(1)} %get-tuple-element.56), channel_id=1, source_target_pairs={{0,16},{16,0},{1,17},{17,1},{2,18},{18,2},{3,19},{19,3},{4,20},{20... | collective-permute-start | bytes 1179656 | tf_op jit(solution)/shard_map/ppermute | solution.py:32
  59.2 6.1 %collective-permute-start.16 = (bf16[1,200,128]{2,1,0:T(8,128)(2,1)S(1)}, bf16[1,200,128]{2,1,0:T(8,128)(2,1)S(1)}, u32[]{:S(2)}, u32[]{:S(2)}) collective-permute-start(bf16[1,200,128]{2,1,0:T(8,128)(2,1)S(1)} %get-tuple-element.64), channel_id=1, source_target_pairs={{0,12},{1,13},{2,14},{3,15},{4,8},{5,9},{6,10},{7,11},{8,4},{9,5},... | collective-permute-start | bytes 153608 | tf_op jit(solution)/shard_map/ppermute | solution.py:27
  61.0 5.2 %collective-permute-start.17 = (bf16[1,200,128]{2,1,0:T(8,128)(2,1)S(1)}, bf16[1,200,128]{2,1,0:T(8,128)(2,1)S(1)}, u32[]{:S(2)}, u32[]{:S(2)}) collective-permute-start(bf16[1,200,128]{2,1,0:T(8,128)(2,1)S(1)} %get-tuple-element.63), channel_id=1, source_target_pairs={{0,4},{1,5},{2,6},{3,7},{4,0},{5,1},{6,2},{7,3},{8,12},{9,13},{10,... | collective-permute-start | bytes 153608 | tf_op jit(solution)/shard_map/ppermute | solution.py:27
  61.0 5.2 %collective-permute-start.18 = (bf16[1,200,128]{2,1,0:T(8,128)(2,1)S(1)}, bf16[1,200,128]{2,1,0:T(8,128)(2,1)S(1)}, u32[]{:S(2)}, u32[]{:S(2)}) collective-permute-start(bf16[1,200,128]{2,1,0:T(8,128)(2,1)S(1)} %get-tuple-element.62), channel_id=1, source_target_pairs={{0,8},{1,9},{2,10},{3,11},{4,12},{5,13},{6,14},{7,15},{8,0},{9,1},... | collective-permute-start | bytes 153608 | tf_op jit(solution)/shard_map/ppermute | solution.py:27
  67.8 1.8 %collective-permute-start.19 = (bf16[64,384]{1,0:T(8,128)(2,1)S(1)}, bf16[64,384]{1,0:T(8,128)(2,1)S(1)}, u32[]{:S(2)}, u32[]{:S(2)}) collective-permute-start(bf16[64,384]{1,0:T(8,128)(2,1)S(1)} %get-tuple-element.38.refs_1_), channel_id=1, source_target_pairs={{0,16},{16,0},{1,17},{17,1},{2,18},{18,2},{3,19},{19,3},{4,20},{20... | collective-permute-start | bytes 147464 | tf_op jit(solution)/shard_map/ppermute | solution.py:32
  67.9 16.1 %collective-permute-start.12 = (bf16[64,384]{1,0:T(8,128)(2,1)S(1)}, bf16[64,384]{1,0:T(8,128)(2,1)S(1)}, u32[]{:S(2)}, u32[]{:S(2)}) collective-permute-start(bf16[64,384]{1,0:T(8,128)(2,1)S(1)} %get-tuple-element.33), channel_id=1, source_target_pairs={{0,16},{16,0},{1,17},{17,1},{2,18},{18,2},{3,19},{19,3},{4,20},{20... | collective-permute-start | bytes 147464 | tf_op jit(solution)/shard_map/ppermute | solution.py:32
  68.4 11.8 %collective-permute-start.22 = (bf16[64,3072]{1,0:T(8,128)(2,1)S(1)}, bf16[64,3072]{1,0:T(8,128)(2,1)S(1)}, u32[]{:S(2)}, u32[]{:S(2)}) collective-permute-start(bf16[64,3072]{1,0:T(8,128)(2,1)S(1)} %get-tuple-element.55), channel_id=1, source_target_pairs={{0,16},{16,0},{1,17},{17,1},{2,18},{18,2},{3,19},{19,3},{4,20},{20... | collective-permute-start | bytes 1179656 | tf_op jit(solution)/shard_map/ppermute | solution.py:32
  68.5 7.2 %collective-permute-start.25 = (f32[4,384]{1,0:T(4,128)S(1)}, f32[4,384]{1,0:T(4,128)S(1)}, u32[]{:S(2)}, u32[]{:S(2)}) collective-permute-start(f32[4,384]{1,0:T(4,128)S(1)} %get-tuple-element.46), channel_id=1, source_target_pairs={{0,2},{1,3},{2,0},{3,1},{4,6},{5,7},{6,4},{7,5},{8,10},{9,11},{10,... | collective-permute-start | bytes 18440 | tf_op jit(solution)/shard_map/ppermute | solution.py:27
  69.6 6.0 %collective-permute-start.24 = (f32[4,384]{1,0:T(4,128)S(1)}, f32[4,384]{1,0:T(4,128)S(1)}, u32[]{:S(2)}, u32[]{:S(2)}) collective-permute-start(f32[4,384]{1,0:T(4,128)S(1)} %get-tuple-element.45), channel_id=1, source_target_pairs={{0,1},{1,0},{2,3},{3,2},{4,5},{5,4},{6,7},{7,6},{8,9},{9,8},{10,11... | collective-permute-start | bytes 18440 | tf_op jit(solution)/shard_map/ppermute | solution.py:27
  71.1 4.5 %collective-permute-start.23 = (f32[4,384]{1,0:T(4,128)S(1)}, f32[4,384]{1,0:T(4,128)S(1)}, u32[]{:S(2)}, u32[]{:S(2)}) collective-permute-start(f32[4,384]{1,0:T(4,128)S(1)} %get-tuple-element.44), channel_id=1, source_target_pairs={{0,3},{1,2},{2,1},{3,0},{4,7},{5,6},{6,5},{7,4},{8,11},{9,10},{10,... | collective-permute-start | bytes 18440 | tf_op jit(solution)/shard_map/ppermute | solution.py:27
  75.7 8.2 %collective-permute-start.28 = (f32[1,384]{1,0:T(1,128)S(1)}, f32[1,384]{1,0:T(1,128)S(1)}, u32[]{:S(2)}, u32[]{:S(2)}) collective-permute-start(f32[1,384]{1,0:T(1,128)S(1)} %get-tuple-element.68), channel_id=1, source_target_pairs={{0,8},{1,9},{2,10},{3,11},{4,12},{5,13},{6,14},{7,15},{8,0},{9,1},... | collective-permute-start | bytes 4616 | tf_op jit(solution)/shard_map/ppermute | solution.py:27
  78.3 5.6 %collective-permute-start.27 = (f32[1,384]{1,0:T(1,128)S(1)}, f32[1,384]{1,0:T(1,128)S(1)}, u32[]{:S(2)}, u32[]{:S(2)}) collective-permute-start(f32[1,384]{1,0:T(1,128)S(1)} %get-tuple-element.69), channel_id=1, source_target_pairs={{0,4},{1,5},{2,6},{3,7},{4,0},{5,1},{6,2},{7,3},{8,12},{9,13},{10,... | collective-permute-start | bytes 4616 | tf_op jit(solution)/shard_map/ppermute | solution.py:27
  78.3 5.6 %collective-permute-start.26 = (f32[1,384]{1,0:T(1,128)S(1)}, f32[1,384]{1,0:T(1,128)S(1)}, u32[]{:S(2)}, u32[]{:S(2)}) collective-permute-start(f32[1,384]{1,0:T(1,128)S(1)} %get-tuple-element.67), channel_id=1, source_target_pairs={{0,12},{1,13},{2,14},{3,15},{4,8},{5,9},{6,10},{7,11},{8,4},{9,5},... | collective-permute-start | bytes 4616 | tf_op jit(solution)/shard_map/ppermute | solution.py:27
  83.9 1.2 %collective-permute-start.29 = (f32[1,384]{1,0:T(1,128)S(1)}, f32[1,384]{1,0:T(1,128)S(1)}, u32[]{:S(2)}, u32[]{:S(2)}) collective-permute-start(f32[1,384]{1,0:T(1,128)S(1)} %get-tuple-element.51), channel_id=1, source_target_pairs={{0,16},{16,0},{1,17},{17,1},{2,18},{18,2},{3,19},{19,3},{4,20},{20... | collective-permute-start | bytes 4616 | tf_op jit(solution)/shard_map/ppermute | solution.py:32

commit v7 on v6

--- a/solution.py
+++ b/solution.py
@@ -18,6 +18,7 @@
 VMEM_LIMIT = 32 * 1024 * 1024
 
 VMEM = pl.BlockSpec(memory_space=pltpu.VMEM)
+HBM = pl.BlockSpec(memory_space=pltpu.HBM)
 ANY = pl.BlockSpec(memory_space=pl.ANY)
 SMEM = pl.BlockSpec(memory_space=pltpu.SMEM)
 
@@ -168,9 +169,11 @@
             gain = gains[pl.ds(windex, 1), pl.ds(column, wide)]
             hat = (pieces[e, 0:tokens, :].astype(F32) - mean) * scale
             u_out[:, pl.ds(column, wide)] = (hat * gain).astype(BF16)
-        z = lax.dot_general(
-            u_out[...], held[...], (((1,), (1,)), ((), ())), preferred_element_type=F32
-        )
+        contract = (((1,), (1,)), ((), ()))
+        if backward:
+            z = lax.dot_general(u_out[...], held[...], contract, preferred_element_type=F32)
+        else:
+            z = lax.dot_general(held[...], u_out[...], contract, preferred_element_type=F32).T
         gelu, slope = gelu_and_slope(z)
         z_out[...] = z
         y_out[...] = (own[...].astype(F32) + gelu).astype(BF16)
@@ -323,40 +326,40 @@
     )(*operands)
 
 
-def weight_grad_kernel(take_early, *refs):
-    scalars, early, early_other, late, late_other, u_own, u_other, _, out, order, depth = refs
-    tokens = early.shape[0]
-
-    @pl.when(pl.program_id(0) == 0)
-    def _():
-        pick = scalars[1] == (0 if take_early else 1)
-        mine = jnp.where(pick, early[...], late[...])
-        theirs = jnp.where(pick, early_other[...], late_other[...])
-        depth[...] = jnp.concatenate([mine, theirs], axis=0).T
-        order[...] = jnp.zeros_like(order)
-
-    both = jnp.concatenate([u_own[...], u_other[...]], axis=0)
-    out[...] = jnp.dot(depth[...], both, preferred_element_type=F32)
+def weight_grad_kernel(take_early, tiles, *refs):
+    scalars, early, early_other, late, late_other, u_own, u_other, _ = refs[:8]
+    out, order, result, sems = refs[8:]
+    pick = scalars[1] == (0 if take_early else 1)
+    mine = jnp.where(pick, early[...], late[...])
+    theirs = jnp.where(pick, early_other[...], late_other[...])
+    depth = jnp.concatenate([mine, theirs], axis=0).T
+    order[...] = jnp.zeros_like(order)
+    tile = u_own.shape[1] // tiles
+    copies = []
+    for n in range(tiles):
+        columns = slice(n * tile, (n + 1) * tile)
+        both = jnp.concatenate([u_own[:, columns], u_other[:, columns]], axis=0)
+        result[:, columns] = jnp.dot(depth, both, preferred_element_type=F32)
+        where = pl.ds(n * tile, tile)
+        copies.append(pltpu.make_async_copy(result.at[:, where], out.at[:, where], sems.at[n]))
+        copies[n].start()
+    for copy in copies:
+        copy.wait()
 
 
 def weight_grad_call(scalars, first, dz_a, dz_a_other, dz_b, dz_b_other, u_own, u_other, after):
     tokens, rows = dz_a.shape
     columns = u_own.shape[1]
-    steps = 4
-    tile = columns // steps
-    whole = pl.BlockSpec((tokens, rows), lambda i: (0, 0))
-    narrow = pl.BlockSpec((tokens, tile), lambda i: (0, i))
-    small = pl.BlockSpec(after.shape, lambda i: (0,) * after.ndim)
+    tiles = 6
     return pl.pallas_call(
-        functools.partial(weight_grad_kernel, first),
-        grid=(steps,),
+        functools.partial(weight_grad_kernel, first, tiles),
         out_shape=[
             jax.ShapeDtypeStruct((rows, columns), F32),
             jax.ShapeDtypeStruct(after.shape, F32),
         ],
-        in_specs=[SMEM] + [whole] * 4 + [narrow] * 2 + [small],
-        out_specs=[pl.BlockSpec((rows, tile), lambda i: (0, i)), small],
-        scratch_shapes=[pltpu.VMEM((rows, 2 * tokens), BF16)],
+        in_specs=[SMEM] + [VMEM] * 7,
+        out_specs=[HBM, VMEM],
+        scratch_shapes=[pltpu.VMEM((rows, columns), F32), pltpu.SemaphoreType.DMA((tiles,))],
         compiler_params=pltpu.CompilerParams(vmem_limit_bytes=VMEM_LIMIT),
         cost_estimate=pl.CostEstimate(
             flops=4 * tokens * rows * columns, bytes_accessed=4 * rows * columns, transcendentals=0
@@ -459,7 +462,9 @@
     bit_count = seq_size.bit_length() - 1
     groups = bit_groups(merged, bit_count)
     back_groups = [group[::-1] for group in groups[::-1]]
+    later_groups = groups if sections > 2 else [groups[0][::-1]] + groups[1:]
     offsets = [o >> merged for o in offsets_of(groups)]
+    later_offsets = [o >> merged for o in offsets_of(later_groups)]
     send_order = [o >> merged for o in offsets_of(back_groups[::-1])]
     me = (seq_index >> merged).astype(jnp.int32)
     first_index = jnp.where(lower, 0, 1).astype(jnp.int32)
@@ -494,8 +499,8 @@
             lax.dynamic_slice_in_dim(value, width - start, width, axis=1),
         )
 
-    def gathered(value):
-        return gather_xor(joined_halves(value, 1), groups)
+    def gathered(value, step):
+        return gather_xor(joined_halves(value, 1), groups if step == 0 else later_groups)
 
     def moved(value, step, later):
         low = min(step, sections - 1 - step)
@@ -541,7 +546,7 @@
     gains = None
     for step in range(sections):
         last = step == sections - 1
-        pieces, partly = gathered(packed if step == 0 else state)
+        pieces, partly = gathered(packed if step == 0 else state, step)
         if step == 0:
             weights = load_call(section_weights, partly)
         result = section_call(
@@ -552,7 +557,7 @@
             gains,
             grad if last else None,
             None,
-            offsets,
+            offsets if step == 0 else later_offsets,
             send_order,
             wide,
             step == 0,

time: 85.9 us -> 85.2 us (level)
  Pallas kernels: 21.2 us -> 19.9 us
    pallas_call x2, Pallas kernels: 7.4 us -> 6.12 us  [weight_grad_call(): pl.pallas_call(functools.partial(weight_grad_kernel, first, tiles), out_s...]
  transfers between devices with their start and end apart: 30 -> 30, of which waited for: 18 -> 21; matrix products, arithmetic and copies ran while one was open for 2% -> 2% of each run, Pallas kernels for 15% -> 14%
where the time goes in v7:
time: 85.2 us; the launch traced here: 85 us
  starting transfers between devices  34.6 us (41%)
  waiting for transfers between devices  27 us (32%)
  Pallas kernels  19.9 us (23%)
  other arithmetic  1.68 us (2%)
  local copies, waits for them, and re-layouts  1.06 us (1%)
  between operations  0.86 us (1%)
    ppermute x24, starting transfers between devices, from_xor(): return lax.ppermute(value, 'seq', [(i, i ^ distance) for i in range(size)])  33.3 us
    ppermute x24, waiting for transfers between devices, from_xor(): return lax.ppermute(value, 'seq', [(i, i ^ distance) for i in range(size)])  26.5 us
    pallas_call x2, Pallas kernels, section_call(): pl.pallas_call(functools.partial(section_kernel, offsets, (tokens, wide,...  6.92 us
    pallas_call x2, Pallas kernels, weight_grad_call(): pl.pallas_call(functools.partial(weight_grad_kernel, first, tiles), out_s...  6.12 us
    pallas_call x1, Pallas kernels, load_call(): pl.pallas_call(load_kernel, out_shape=jax.ShapeDtypeStruct(weights.shape,...  3.79 us
  transfers between devices with their start and end apart: 30, of which 21 were waited for; matrix products, arithmetic and copies ran while one was open for 2% of the time, Pallas kernels for 14%

profile of v7, /device:TPU:0, one launch (start us, length us, event | category | flops | bytes accessed | tf_op | source)
XLA Modules:
  0.0 85.0 jit_solution(2584989107070503369)
XLA Ops:
  0.7 1.4 %shard_map.101 = (bf16[64,384]{1,0:T(8,128)(2,1)S(1)}, bf16[64,384]{1,0:T(8,128)(2,1)S(1)}, bf16[72,384]{1,0:T(8,128)(2,1)S(1)}) custom-call(s32[2]{0:T(128)S(1)} %pad_add_fusion.scalars.refs_0_, bf16[64,384]{1,0:T(8,128)(2,1)} %refs_0_.1, bf16[64,384]{1,0:T(8,128)(2,1)} %refs_1_.1, bf16[64,384]{1,0:T(8,128)(2,1)} %refs_2_.1, bf16[64,384]{1,0:T(8,128)(2,1)} %refs_3_.1, ...), custom_call_target="tpu_custom_call" | custom-call | tf_op jit(solution)/shard_map/pallas_call | solution.py:428
  2.1 5.1 %collective-permute-start.2 = (bf16[1,72,384]{2,1,0:T(8,128)(2,1)S(1)}, bf16[1,72,384]{2,1,0:T(8,128)(2,1)S(1)}, u32[]{:S(2)}, u32[]{:S(2)}) collective-permute-start(bf16[1,72,384]{2,1,0:T(8,128)(2,1)S(1)} %bitcast.25), channel_id=1, source_target_pairs={{0,12},{1,13},{2,14},{3,15},{4,8},{5,9},{6,10},{7,11},{8,4},{9,5},... | collective-permute-start | bytes 165896 | tf_op jit(solution)/shard_map/ppermute | solution.py:28
  9.8 1.7 %collective-permute-done.1 = bf16[1,72,384]{2,1,0:T(8,128)(2,1)S(1)} collective-permute-done((bf16[1,72,384]{2,1,0:T(8,128)(2,1)S(1)}, bf16[1,72,384]{2,1,0:T(8,128)(2,1)S(1)}, u32[]{:S(2)}, u32[]{:S(2)}) %collective-permute-start.1) | collective-permute-done | bytes 55328 | tf_op jit(solution)/shard_map/ppermute | solution.py:28
  12.7 1.6 %collective-permute-start.3 = (bf16[4,72,384]{2,1,0:T(8,128)(2,1)S(1)}, bf16[4,72,384]{2,1,0:T(8,128)(2,1)S(1)}, u32[]{:S(2)}, u32[]{:S(2)}) collective-permute-start(bf16[4,72,384]{2,1,0:T(8,128)(2,1)S(1)} %pad_maximum_fusion._), channel_id=1, source_target_pairs={{0,2},{1,3},{2,0},{3,1},{4,6},{5,7},{6,4},{7,5},{8,10},{9,11},{10,... | collective-permute-start | bytes 663560 | tf_op jit(solution)/shard_map/ppermute | solution.py:28
  14.3 1.5 %collective-permute-start.4 = (bf16[4,72,384]{2,1,0:T(8,128)(2,1)S(1)}, bf16[4,72,384]{2,1,0:T(8,128)(2,1)S(1)}, u32[]{:S(2)}, u32[]{:S(2)}) collective-permute-start(bf16[4,72,384]{2,1,0:T(8,128)(2,1)S(1)} %pad_maximum_fusion._), channel_id=1, source_target_pairs={{0,1},{1,0},{2,3},{3,2},{4,5},{5,4},{6,7},{7,6},{8,9},{9,8},{10,11... | collective-permute-start | bytes 663560 | tf_op jit(solution)/shard_map/ppermute | solution.py:28
  16.3 3.8 %shard_map.102.refs_1_ = bf16[1,2,384,6144]{3,2,1,0:T(8,128)(2,1)S(1)} custom-call(bf16[1,2,384,6144]{3,2,1,0:T(8,128)(2,1)} %weights.1, bf16[4,72,384]{2,1,0:T(8,128)(2,1)S(1)} %pad_maximum_fusion._), custom_call_target="tpu_custom_call" | custom-call | bytes 9437184 | tf_op jit(solution)/shard_map/pallas_call | solution.py:381
  21.8 2.3 %collective-permute-done.5 = bf16[4,72,384]{2,1,0:T(8,128)(2,1)S(1)} collective-permute-done((bf16[4,72,384]{2,1,0:T(8,128)(2,1)S(1)}, bf16[4,72,384]{2,1,0:T(8,128)(2,1)S(1)}, u32[]{:S(2)}, u32[]{:S(2)}) %collective-permute-start.5) | collective-permute-done | bytes 221216 | tf_op jit(solution)/shard_map/ppermute | solution.py:28
  24.1 2.6 %shard_map.103 = (bf16[64,6144]{1,0:T(8,128)(2,1)S(1)}, f32[64,128]{1,0:T(8,128)S(1)}, f32[64,384]{1,0:T(8,128)S(1)}, bf16[64,384]{1,0:T(8,128)(2,1)S(1)}, f32[2,6144]{1,0:T(2,128)S(1)}) custom-call(s32[2]{0:T(128)S(1)} %pad_add_fusion.scalars.refs_0_, bf16[1,2,384,6144]{3,2,1,0:T(8,128)(2,1)S(1)} %shard_map.102.refs_1_, ...), custom_call_target="tpu_custom_call" | custom-call | flops 301989888 | bytes 4718592 | tf_op jit(solution)/shard_map/pallas_call | solution.py:230
  26.7 2.2 %collective-permute-start.6 = (bf16[1,64,384]{2,1,0:T(8,128)(2,1)S(1)}, bf16[1,64,384]{2,1,0:T(8,128)(2,1)S(1)}, u32[]{:S(2)}, u32[]{:S(2)}) collective-permute-start(bf16[1,64,384]{2,1,0:T(8,128)(2,1)S(1)} %bitcast.21), channel_id=1, source_target_pairs={{0,12},{1,13},{2,14},{3,15},{4,8},{5,9},{6,10},{7,11},{8,4},{9,5},... | collective-permute-start | bytes 147464 | tf_op jit(solution)/shard_map/ppermute | solution.py:28
  29.4 1.7 %collective-permute-start.8 = (bf16[1,64,384]{2,1,0:T(8,128)(2,1)S(1)}, bf16[1,64,384]{2,1,0:T(8,128)(2,1)S(1)}, u32[]{:S(2)}, u32[]{:S(2)}) collective-permute-start(bf16[1,64,384]{2,1,0:T(8,128)(2,1)S(1)} %bitcast.23), channel_id=1, source_target_pairs={{0,8},{1,9},{2,10},{3,11},{4,12},{5,13},{6,14},{7,15},{8,0},{9,1},... | collective-permute-start | bytes 147464 | tf_op jit(solution)/shard_map/ppermute | solution.py:28
  31.1 1.5 %collective-permute-done.6 = bf16[1,64,384]{2,1,0:T(8,128)(2,1)S(1)} collective-permute-done((bf16[1,64,384]{2,1,0:T(8,128)(2,1)S(1)}, bf16[1,64,384]{2,1,0:T(8,128)(2,1)S(1)}, u32[]{:S(2)}, u32[]{:S(2)}) %collective-permute-start.6) | collective-permute-done | bytes 49184 | tf_op jit(solution)/shard_map/ppermute | solution.py:28
  33.2 1.3 %collective-permute-done.8 = bf16[1,64,384]{2,1,0:T(8,128)(2,1)S(1)} collective-permute-done((bf16[1,64,384]{2,1,0:T(8,128)(2,1)S(1)}, bf16[1,64,384]{2,1,0:T(8,128)(2,1)S(1)}, u32[]{:S(2)}, u32[]{:S(2)}) %collective-permute-start.8) | collective-permute-done | bytes 49184 | tf_op jit(solution)/shard_map/ppermute | solution.py:28
  34.5 1.6 %collective-permute-start.9 = (bf16[4,64,384]{2,1,0:T(8,128)(2,1)S(1)}, bf16[4,64,384]{2,1,0:T(8,128)(2,1)S(1)}, u32[]{:S(2)}, u32[]{:S(2)}) collective-permute-start(bf16[4,64,384]{2,1,0:T(8,128)(2,1)S(1)} %pad_maximum_fusion.1), channel_id=1, source_target_pairs={{0,2},{1,3},{2,0},{3,1},{4,6},{5,7},{6,4},{7,5},{8,10},{9,11},{10,... | collective-permute-start | bytes 589832 | tf_op jit(solution)/shard_map/ppermute | solution.py:28
  36.1 1.5 %collective-permute-start.10 = (bf16[4,64,384]{2,1,0:T(8,128)(2,1)S(1)}, bf16[4,64,384]{2,1,0:T(8,128)(2,1)S(1)}, u32[]{:S(2)}, u32[]{:S(2)}) collective-permute-start(bf16[4,64,384]{2,1,0:T(8,128)(2,1)S(1)} %pad_maximum_fusion.1), channel_id=1, source_target_pairs={{0,1},{1,0},{2,3},{3,2},{4,5},{5,4},{6,7},{7,6},{8,9},{9,8},{10,11... | collective-permute-start | bytes 589832 | tf_op jit(solution)/shard_map/ppermute | solution.py:28
  38.1 2.2 %collective-permute-done.9 = bf16[4,64,384]{2,1,0:T(8,128)(2,1)S(1)} collective-permute-done((bf16[4,64,384]{2,1,0:T(8,128)(2,1)S(1)}, bf16[4,64,384]{2,1,0:T(8,128)(2,1)S(1)}, u32[]{:S(2)}, u32[]{:S(2)}) %collective-permute-start.9) | collective-permute-done | bytes 196640 | tf_op jit(solution)/shard_map/ppermute | solution.py:28
  40.2 1.5 %collective-permute-done.10 = bf16[4,64,384]{2,1,0:T(8,128)(2,1)S(1)} collective-permute-done((bf16[4,64,384]{2,1,0:T(8,128)(2,1)S(1)}, bf16[4,64,384]{2,1,0:T(8,128)(2,1)S(1)}, u32[]{:S(2)}, u32[]{:S(2)}) %collective-permute-start.10) | collective-permute-done | bytes 196640 | tf_op jit(solution)/shard_map/ppermute | solution.py:28
  41.8 2.4 %collective-permute-done.11 = bf16[4,64,384]{2,1,0:T(8,128)(2,1)S(1)} collective-permute-done((bf16[4,64,384]{2,1,0:T(8,128)(2,1)S(1)}, bf16[4,64,384]{2,1,0:T(8,128)(2,1)S(1)}, u32[]{:S(2)}, u32[]{:S(2)}) %collective-permute-start.11) | collective-permute-done | bytes 196640 | tf_op jit(solution)/shard_map/ppermute | solution.py:28
  44.2 4.4 %shard_map.104 = (bf16[64,6144]{1,0:T(8,128)(2,1)S(1)}, f32[64,128]{1,0:T(8,128)S(1)}, f32[64,384]{1,0:T(8,128)}, bf16[64,384]{1,0:T(8,128)(2,1)S(1)}, bf16[64,3...) custom-call(s32[2]{0:T(128)S(1)} %pad_add_fusion.1.refs_0_, bf16[1,2,384,6144]{3,2,1,0:T(8,128)(2,1)S(1)} %shard_map.102.refs_1_, ...), custom_call_target="tpu_custom_call" | custom-call | flops 603979776 | bytes 4718592 | tf_op jit(solution)/shard_map/pallas_call | solution.py:230
  48.6 1.2 %collective-permute-start.15 = (bf16[4,200,128]{2,1,0:T(8,128)(2,1)S(1)}, bf16[4,200,128]{2,1,0:T(8,128)(2,1)S(1)}, u32[]{:S(2)}, u32[]{:S(2)}) collective-permute-start(bf16[4,200,128]{2,1,0:T(8,128)(2,1)S(1)} %get-tuple-element.60), channel_id=1, source_target_pairs={{0,2},{1,3},{2,0},{3,1},{4,6},{5,7},{6,4},{7,5},{8,10},{9,11},{10,... | collective-permute-start | bytes 614408 | tf_op jit(solution)/shard_map/ppermute | solution.py:28
  49.8 1.5 %collective-permute-start.14 = (bf16[4,200,128]{2,1,0:T(8,128)(2,1)S(1)}, bf16[4,200,128]{2,1,0:T(8,128)(2,1)S(1)}, u32[]{:S(2)}, u32[]{:S(2)}) collective-permute-start(bf16[4,200,128]{2,1,0:T(8,128)(2,1)S(1)} %get-tuple-element.61), channel_id=1, source_target_pairs={{0,1},{1,0},{2,3},{3,2},{4,5},{5,4},{6,7},{7,6},{8,9},{9,8},{10,11... | collective-permute-start | bytes 614408 | tf_op jit(solution)/shard_map/ppermute | solution.py:28
  52.8 1.6 %collective-permute-done.15 = bf16[4,200,128]{2,1,0:T(8,128)(2,1)S(1)} collective-permute-done((bf16[4,200,128]{2,1,0:T(8,128)(2,1)S(1)}, bf16[4,200,128]{2,1,0:T(8,128)(2,1)S(1)}, u32[]{:S(2)}, u32[]{:S(2)}) %collective-permute-start.15) | collective-permute-done | bytes 204832 | tf_op jit(solution)/shard_map/ppermute | solution.py:28
  55.6 2.5 %collective-permute-done.13 = bf16[4,200,128]{2,1,0:T(8,128)(2,1)S(1)} collective-permute-done((bf16[4,200,128]{2,1,0:T(8,128)(2,1)S(1)}, bf16[4,200,128]{2,1,0:T(8,128)(2,1)S(1)}, u32[]{:S(2)}, u32[]{:S(2)}) %collective-permute-start.13) | collective-permute-done | bytes 204832 | tf_op jit(solution)/shard_map/ppermute | solution.py:28
  58.2 2.0 %collective-permute-start.16 = (bf16[1,200,128]{2,1,0:T(8,128)(2,1)S(1)}, bf16[1,200,128]{2,1,0:T(8,128)(2,1)S(1)}, u32[]{:S(2)}, u32[]{:S(2)}) collective-permute-start(bf16[1,200,128]{2,1,0:T(8,128)(2,1)S(1)} %get-tuple-element.64), channel_id=1, source_target_pairs={{0,12},{1,13},{2,14},{3,15},{4,8},{5,9},{6,10},{7,11},{8,4},{9,5},... | collective-permute-start | bytes 153608 | tf_op jit(solution)/shard_map/ppermute | solution.py:28
  60.5 2.2 %collective-permute-start.18 = (bf16[1,200,128]{2,1,0:T(8,128)(2,1)S(1)}, bf16[1,200,128]{2,1,0:T(8,128)(2,1)S(1)}, u32[]{:S(2)}, u32[]{:S(2)}) collective-permute-start(bf16[1,200,128]{2,1,0:T(8,128)(2,1)S(1)} %get-tuple-element.62), channel_id=1, source_target_pairs={{0,8},{1,9},{2,10},{3,11},{4,12},{5,13},{6,14},{7,15},{8,0},{9,1},... | collective-permute-start | bytes 153608 | tf_op jit(solution)/shard_map/ppermute | solution.py:28
  62.7 1.5 %collective-permute-done.16 = bf16[1,200,128]{2,1,0:T(8,128)(2,1)S(1)} collective-permute-done((bf16[1,200,128]{2,1,0:T(8,128)(2,1)S(1)}, bf16[1,200,128]{2,1,0:T(8,128)(2,1)S(1)}, u32[]{:S(2)}, u32[]{:S(2)}) %collective-permute-start.16) | collective-permute-done | bytes 51232 | tf_op jit(solution)/shard_map/ppermute | solution.py:28
  65.5 1.6 %shard_map.105 = (bf16[64,384]{1,0:T(8,128)(2,1)S(1)}, f32[4,384]{1,0:T(4,128)S(1)}, f32[4,384]{1,0:T(4,128)S(1)}, f32[4,384]{1,0:T(4,128)S(1)}, f32[4,384]{1,0:T(4,128)S(1)}, /*index=5*/f32[1,384]{1,0:T(1,128)S(1)}) custom-call(s32[2]{0:T(128)S(1)} %pad_add_fusion.scalars.refs_0_, bf16[1,2,384,6144]{3,2,1,0:T(8,128)(2,1)S(1)} %shard_map.102.refs_1_, ...), custom_call_target="tpu_custom_call" | custom-call | flops 301989888 | bytes 4718592 | tf_op jit(solution)/shard_map/pallas_call | solution.py:309
  67.8 1.2 %collective-permute-start.25 = (f32[4,384]{1,0:T(4,128)S(1)}, f32[4,384]{1,0:T(4,128)S(1)}, u32[]{:S(2)}, u32[]{:S(2)}) collective-permute-start(f32[4,384]{1,0:T(4,128)S(1)} %get-tuple-element.46), channel_id=1, source_target_pairs={{0,2},{1,3},{2,0},{3,1},{4,6},{5,7},{6,4},{7,5},{8,10},{9,11},{10,... | collective-permute-start | bytes 18440 | tf_op jit(solution)/shard_map/ppermute | solution.py:28
  69.0 1.5 %collective-permute-start.24 = (f32[4,384]{1,0:T(4,128)S(1)}, f32[4,384]{1,0:T(4,128)S(1)}, u32[]{:S(2)}, u32[]{:S(2)}) collective-permute-start(f32[4,384]{1,0:T(4,128)S(1)} %get-tuple-element.45), channel_id=1, source_target_pairs={{0,1},{1,0},{2,3},{3,2},{4,5},{5,4},{6,7},{7,6},{8,9},{9,8},{10,11... | collective-permute-start | bytes 18440 | tf_op jit(solution)/shard_map/ppermute | solution.py:28
  71.3 3.1 %shard_map.106 = (f32[384,3072]{1,0:T(8,128)}, f32[4,384]{1,0:T(4,128)S(1)}) custom-call(s32[2]{0:T(128)S(1)} %pad_add_fusion.scalars.refs_0_, bf16[64,384]{1,0:T(8,128)(2,1)S(1)} %get-tuple-element.38.refs_1_, bf16[64,384]{1,0:T(8,128)(2,1)S(1)} %collective-permute-done.19.refs_2_, bf16[64,384]{1,0:T(8,128)(2,1)S(1)} %get-tuple-element.39.refs_3_, ...), custom_call_target="tpu_custom_call" | custom-call | flops 301989888 | bytes 4718592 | tf_op jit(solution)/shard_map/pallas_call | solution.py:354
  75.0 2.2 %collective-permute-start.28 = (f32[1,384]{1,0:T(1,128)S(1)}, f32[1,384]{1,0:T(1,128)S(1)}, u32[]{:S(2)}, u32[]{:S(2)}) collective-permute-start(f32[1,384]{1,0:T(1,128)S(1)} %get-tuple-element.68), channel_id=1, source_target_pairs={{0,8},{1,9},{2,10},{3,11},{4,12},{5,13},{6,14},{7,15},{8,0},{9,1},... | collective-permute-start | bytes 4616 | tf_op jit(solution)/shard_map/ppermute | solution.py:28
  77.8 1.7 %collective-permute-start.26 = (f32[1,384]{1,0:T(1,128)S(1)}, f32[1,384]{1,0:T(1,128)S(1)}, u32[]{:S(2)}, u32[]{:S(2)}) collective-permute-start(f32[1,384]{1,0:T(1,128)S(1)} %get-tuple-element.67), channel_id=1, source_target_pairs={{0,12},{1,13},{2,14},{3,15},{4,8},{5,9},{6,10},{7,11},{8,4},{9,5},... | collective-permute-start | bytes 4616 | tf_op jit(solution)/shard_map/ppermute | solution.py:28
  79.5 3.1 %shard_map.107 = (f32[384,3072]{1,0:T(8,128)}, f32[1,384]{1,0:T(1,128)S(1)}) custom-call(s32[2]{0:T(128)S(1)} %pad_add_fusion.scalars.refs_0_, bf16[64,384]{1,0:T(8,128)(2,1)S(1)} %get-tuple-element.38.refs_1_, bf16[64,384]{1,0:T(8,128)(2,1)S(1)} %collective-permute-done.19.refs_2_, bf16[64,384]{1,0:T(8,128)(2,1)S(1)} %get-tuple-element.39.refs_3_, ...), custom_call_target="tpu_custom_call" | custom-call | flops 301989888 | bytes 4718592 | tf_op jit(solution)/shard_map/pallas_call | solution.py:354
  (64 shorter events, 17.3 us)
Async XLA Ops:
  2.1 7.7 %collective-permute-start.2 = (bf16[1,72,384]{2,1,0:T(8,128)(2,1)S(1)}, bf16[1,72,384]{2,1,0:T(8,128)(2,1)S(1)}, u32[]{:S(2)}, u32[]{:S(2)}) collective-permute-start(bf16[1,72,384]{2,1,0:T(8,128)(2,1)S(1)} %bitcast.25), channel_id=1, source_target_pairs={{0,12},{1,13},{2,14},{3,15},{4,8},{5,9},{6,10},{7,11},{8,4},{9,5},... | collective-permute-start | bytes 165896 | tf_op jit(solution)/shard_map/ppermute | solution.py:28
  7.2 4.2 %collective-permute-start.1 = (bf16[1,72,384]{2,1,0:T(8,128)(2,1)S(1)}, bf16[1,72,384]{2,1,0:T(8,128)(2,1)S(1)}, u32[]{:S(2)}, u32[]{:S(2)}) collective-permute-start(bf16[1,72,384]{2,1,0:T(8,128)(2,1)S(1)} %bitcast.26), channel_id=1, source_target_pairs={{0,4},{1,5},{2,6},{3,7},{4,0},{5,1},{6,2},{7,3},{8,12},{9,13},{10,... | collective-permute-start | bytes 165896 | tf_op jit(solution)/shard_map/ppermute | solution.py:28
  7.2 5.4 %collective-permute-start = (bf16[1,72,384]{2,1,0:T(8,128)(2,1)S(1)}, bf16[1,72,384]{2,1,0:T(8,128)(2,1)S(1)}, u32[]{:S(2)}, u32[]{:S(2)}) collective-permute-start(bf16[1,72,384]{2,1,0:T(8,128)(2,1)S(1)} %bitcast.27), channel_id=1, source_target_pairs={{0,8},{1,9},{2,10},{3,11},{4,12},{5,13},{6,14},{7,15},{8,0},{9,1},... | collective-permute-start | bytes 165896 | tf_op jit(solution)/shard_map/ppermute | solution.py:28
  12.7 8.4 %collective-permute-start.3 = (bf16[4,72,384]{2,1,0:T(8,128)(2,1)S(1)}, bf16[4,72,384]{2,1,0:T(8,128)(2,1)S(1)}, u32[]{:S(2)}, u32[]{:S(2)}) collective-permute-start(bf16[4,72,384]{2,1,0:T(8,128)(2,1)S(1)} %pad_maximum_fusion._), channel_id=1, source_target_pairs={{0,2},{1,3},{2,0},{3,1},{4,6},{5,7},{6,4},{7,5},{8,10},{9,11},{10,... | collective-permute-start | bytes 663560 | tf_op jit(solution)/shard_map/ppermute | solution.py:28
  14.3 7.5 %collective-permute-start.4 = (bf16[4,72,384]{2,1,0:T(8,128)(2,1)S(1)}, bf16[4,72,384]{2,1,0:T(8,128)(2,1)S(1)}, u32[]{:S(2)}, u32[]{:S(2)}) collective-permute-start(bf16[4,72,384]{2,1,0:T(8,128)(2,1)S(1)} %pad_maximum_fusion._), channel_id=1, source_target_pairs={{0,1},{1,0},{2,3},{3,2},{4,5},{5,4},{6,7},{7,6},{8,9},{9,8},{10,11... | collective-permute-start | bytes 663560 | tf_op jit(solution)/shard_map/ppermute | solution.py:28
  15.8 8.3 %collective-permute-start.5 = (bf16[4,72,384]{2,1,0:T(8,128)(2,1)S(1)}, bf16[4,72,384]{2,1,0:T(8,128)(2,1)S(1)}, u32[]{:S(2)}, u32[]{:S(2)}) collective-permute-start(bf16[4,72,384]{2,1,0:T(8,128)(2,1)S(1)} %pad_maximum_fusion._), channel_id=1, source_target_pairs={{0,3},{1,2},{2,1},{3,0},{4,7},{5,6},{6,5},{7,4},{8,11},{9,10},{10,... | collective-permute-start | bytes 663560 | tf_op jit(solution)/shard_map/ppermute | solution.py:28
  26.7 6.0 %collective-permute-start.6 = (bf16[1,64,384]{2,1,0:T(8,128)(2,1)S(1)}, bf16[1,64,384]{2,1,0:T(8,128)(2,1)S(1)}, u32[]{:S(2)}, u32[]{:S(2)}) collective-permute-start(bf16[1,64,384]{2,1,0:T(8,128)(2,1)S(1)} %bitcast.21), channel_id=1, source_target_pairs={{0,12},{1,13},{2,14},{3,15},{4,8},{5,9},{6,10},{7,11},{8,4},{9,5},... | collective-permute-start | bytes 147464 | tf_op jit(solution)/shard_map/ppermute | solution.py:28
  28.8 4.3 %collective-permute-start.7 = (bf16[1,64,384]{2,1,0:T(8,128)(2,1)S(1)}, bf16[1,64,384]{2,1,0:T(8,128)(2,1)S(1)}, u32[]{:S(2)}, u32[]{:S(2)}) collective-permute-start(bf16[1,64,384]{2,1,0:T(8,128)(2,1)S(1)} %bitcast.22), channel_id=1, source_target_pairs={{0,4},{1,5},{2,6},{3,7},{4,0},{5,1},{6,2},{7,3},{8,12},{9,13},{10,... | collective-permute-start | bytes 147464 | tf_op jit(solution)/shard_map/ppermute | solution.py:28
  29.4 5.0 %collective-permute-start.8 = (bf16[1,64,384]{2,1,0:T(8,128)(2,1)S(1)}, bf16[1,64,384]{2,1,0:T(8,128)(2,1)S(1)}, u32[]{:S(2)}, u32[]{:S(2)}) collective-permute-start(bf16[1,64,384]{2,1,0:T(8,128)(2,1)S(1)} %bitcast.23), channel_id=1, source_target_pairs={{0,8},{1,9},{2,10},{3,11},{4,12},{5,13},{6,14},{7,15},{8,0},{9,1},... | collective-permute-start | bytes 147464 | tf_op jit(solution)/shard_map/ppermute | solution.py:28
  34.5 5.8 %collective-permute-start.9 = (bf16[4,64,384]{2,1,0:T(8,128)(2,1)S(1)}, bf16[4,64,384]{2,1,0:T(8,128)(2,1)S(1)}, u32[]{:S(2)}, u32[]{:S(2)}) collective-permute-start(bf16[4,64,384]{2,1,0:T(8,128)(2,1)S(1)} %pad_maximum_fusion.1), channel_id=1, source_target_pairs={{0,2},{1,3},{2,0},{3,1},{4,6},{5,7},{6,4},{7,5},{8,10},{9,11},{10,... | collective-permute-start | bytes 589832 | tf_op jit(solution)/shard_map/ppermute | solution.py:28
  36.1 5.7 %collective-permute-start.10 = (bf16[4,64,384]{2,1,0:T(8,128)(2,1)S(1)}, bf16[4,64,384]{2,1,0:T(8,128)(2,1)S(1)}, u32[]{:S(2)}, u32[]{:S(2)}) collective-permute-start(bf16[4,64,384]{2,1,0:T(8,128)(2,1)S(1)} %pad_maximum_fusion.1), channel_id=1, source_target_pairs={{0,1},{1,0},{2,3},{3,2},{4,5},{5,4},{6,7},{7,6},{8,9},{9,8},{10,11... | collective-permute-start | bytes 589832 | tf_op jit(solution)/shard_map/ppermute | solution.py:28
  37.6 6.6 %collective-permute-start.11 = (bf16[4,64,384]{2,1,0:T(8,128)(2,1)S(1)}, bf16[4,64,384]{2,1,0:T(8,128)(2,1)S(1)}, u32[]{:S(2)}, u32[]{:S(2)}) collective-permute-start(bf16[4,64,384]{2,1,0:T(8,128)(2,1)S(1)} %pad_maximum_fusion.1), channel_id=1, source_target_pairs={{0,3},{1,2},{2,1},{3,0},{4,7},{5,6},{6,5},{7,4},{8,11},{9,10},{10,... | collective-permute-start | bytes 589832 | tf_op jit(solution)/shard_map/ppermute | solution.py:28
  48.6 5.8 %collective-permute-start.15 = (bf16[4,200,128]{2,1,0:T(8,128)(2,1)S(1)}, bf16[4,200,128]{2,1,0:T(8,128)(2,1)S(1)}, u32[]{:S(2)}, u32[]{:S(2)}) collective-permute-start(bf16[4,200,128]{2,1,0:T(8,128)(2,1)S(1)} %get-tuple-element.60), channel_id=1, source_target_pairs={{0,2},{1,3},{2,0},{3,1},{4,6},{5,7},{6,4},{7,5},{8,10},{9,11},{10,... | collective-permute-start | bytes 614408 | tf_op jit(solution)/shard_map/ppermute | solution.py:28
  49.8 5.8 %collective-permute-start.14 = (bf16[4,200,128]{2,1,0:T(8,128)(2,1)S(1)}, bf16[4,200,128]{2,1,0:T(8,128)(2,1)S(1)}, u32[]{:S(2)}, u32[]{:S(2)}) collective-permute-start(bf16[4,200,128]{2,1,0:T(8,128)(2,1)S(1)} %get-tuple-element.61), channel_id=1, source_target_pairs={{0,1},{1,0},{2,3},{3,2},{4,5},{5,4},{6,7},{7,6},{8,9},{9,8},{10,11... | collective-permute-start | bytes 614408 | tf_op jit(solution)/shard_map/ppermute | solution.py:28
  51.3 6.8 %collective-permute-start.13 = (bf16[4,200,128]{2,1,0:T(8,128)(2,1)S(1)}, bf16[4,200,128]{2,1,0:T(8,128)(2,1)S(1)}, u32[]{:S(2)}, u32[]{:S(2)}) collective-permute-start(bf16[4,200,128]{2,1,0:T(8,128)(2,1)S(1)} %get-tuple-element.59), channel_id=1, source_target_pairs={{0,3},{1,2},{2,1},{3,0},{4,7},{5,6},{6,5},{7,4},{8,11},{9,10},{10,... | collective-permute-start | bytes 614408 | tf_op jit(solution)/shard_map/ppermute | solution.py:28
  52.1 15.7 %collective-permute-start.20 = (bf16[64,384]{1,0:T(8,128)(2,1)S(1)}, bf16[64,384]{1,0:T(8,128)(2,1)S(1)}, u32[]{:S(2)}, u32[]{:S(2)}) collective-permute-start(bf16[64,384]{1,0:T(8,128)(2,1)S(1)} %get-tuple-element.39.refs_3_), channel_id=1, source_target_pairs={{0,16},{16,0},{1,17},{17,1},{2,18},{18,2},{3,19},{19,3},{4,20},{20... | collective-permute-start | bytes 147464 | tf_op jit(solution)/shard_map/ppermute | solution.py:33
  52.3 18.2 %collective-permute-start.21 = (bf16[64,3072]{1,0:T(8,128)(2,1)S(1)}, bf16[64,3072]{1,0:T(8,128)(2,1)S(1)}, u32[]{:S(2)}, u32[]{:S(2)}) collective-permute-start(bf16[64,3072]{1,0:T(8,128)(2,1)S(1)} %get-tuple-element.56), channel_id=1, source_target_pairs={{0,16},{16,0},{1,17},{17,1},{2,18},{18,2},{3,19},{19,3},{4,20},{20... | collective-permute-start | bytes 1179656 | tf_op jit(solution)/shard_map/ppermute | solution.py:33
  58.2 6.0 %collective-permute-start.16 = (bf16[1,200,128]{2,1,0:T(8,128)(2,1)S(1)}, bf16[1,200,128]{2,1,0:T(8,128)(2,1)S(1)}, u32[]{:S(2)}, u32[]{:S(2)}) collective-permute-start(bf16[1,200,128]{2,1,0:T(8,128)(2,1)S(1)} %get-tuple-element.64), channel_id=1, source_target_pairs={{0,12},{1,13},{2,14},{3,15},{4,8},{5,9},{6,10},{7,11},{8,4},{9,5},... | collective-permute-start | bytes 153608 | tf_op jit(solution)/shard_map/ppermute | solution.py:28
  60.3 4.5 %collective-permute-start.17 = (bf16[1,200,128]{2,1,0:T(8,128)(2,1)S(1)}, bf16[1,200,128]{2,1,0:T(8,128)(2,1)S(1)}, u32[]{:S(2)}, u32[]{:S(2)}) collective-permute-start(bf16[1,200,128]{2,1,0:T(8,128)(2,1)S(1)} %get-tuple-element.63), channel_id=1, source_target_pairs={{0,4},{1,5},{2,6},{3,7},{4,0},{5,1},{6,2},{7,3},{8,12},{9,13},{10,... | collective-permute-start | bytes 153608 | tf_op jit(solution)/shard_map/ppermute | solution.py:28
  60.5 5.0 %collective-permute-start.18 = (bf16[1,200,128]{2,1,0:T(8,128)(2,1)S(1)}, bf16[1,200,128]{2,1,0:T(8,128)(2,1)S(1)}, u32[]{:S(2)}, u32[]{:S(2)}) collective-permute-start(bf16[1,200,128]{2,1,0:T(8,128)(2,1)S(1)} %get-tuple-element.62), channel_id=1, source_target_pairs={{0,8},{1,9},{2,10},{3,11},{4,12},{5,13},{6,14},{7,15},{8,0},{9,1},... | collective-permute-start | bytes 153608 | tf_op jit(solution)/shard_map/ppermute | solution.py:28
  67.1 1.8 %collective-permute-start.19 = (bf16[64,384]{1,0:T(8,128)(2,1)S(1)}, bf16[64,384]{1,0:T(8,128)(2,1)S(1)}, u32[]{:S(2)}, u32[]{:S(2)}) collective-permute-start(bf16[64,384]{1,0:T(8,128)(2,1)S(1)} %get-tuple-element.38.refs_1_), channel_id=1, source_target_pairs={{0,16},{16,0},{1,17},{17,1},{2,18},{18,2},{3,19},{19,3},{4,20},{20... | collective-permute-start | bytes 147464 | tf_op jit(solution)/shard_map/ppermute | solution.py:33
  67.2 16.0 %collective-permute-start.12 = (bf16[64,384]{1,0:T(8,128)(2,1)S(1)}, bf16[64,384]{1,0:T(8,128)(2,1)S(1)}, u32[]{:S(2)}, u32[]{:S(2)}) collective-permute-start(bf16[64,384]{1,0:T(8,128)(2,1)S(1)} %get-tuple-element.33), channel_id=1, source_target_pairs={{0,16},{16,0},{1,17},{17,1},{2,18},{18,2},{3,19},{19,3},{4,20},{20... | collective-permute-start | bytes 147464 | tf_op jit(solution)/shard_map/ppermute | solution.py:33
  67.7 11.8 %collective-permute-start.22 = (bf16[64,3072]{1,0:T(8,128)(2,1)S(1)}, bf16[64,3072]{1,0:T(8,128)(2,1)S(1)}, u32[]{:S(2)}, u32[]{:S(2)}) collective-permute-start(bf16[64,3072]{1,0:T(8,128)(2,1)S(1)} %get-tuple-element.55), channel_id=1, source_target_pairs={{0,16},{16,0},{1,17},{17,1},{2,18},{18,2},{3,19},{19,3},{4,20},{20... | collective-permute-start | bytes 1179656 | tf_op jit(solution)/shard_map/ppermute | solution.py:33
  67.8 6.6 %collective-permute-start.25 = (f32[4,384]{1,0:T(4,128)S(1)}, f32[4,384]{1,0:T(4,128)S(1)}, u32[]{:S(2)}, u32[]{:S(2)}) collective-permute-start(f32[4,384]{1,0:T(4,128)S(1)} %get-tuple-element.46), channel_id=1, source_target_pairs={{0,2},{1,3},{2,0},{3,1},{4,6},{5,7},{6,4},{7,5},{8,10},{9,11},{10,... | collective-permute-start | bytes 18440 | tf_op jit(solution)/shard_map/ppermute | solution.py:28
  69.0 5.4 %collective-permute-start.24 = (f32[4,384]{1,0:T(4,128)S(1)}, f32[4,384]{1,0:T(4,128)S(1)}, u32[]{:S(2)}, u32[]{:S(2)}) collective-permute-start(f32[4,384]{1,0:T(4,128)S(1)} %get-tuple-element.45), channel_id=1, source_target_pairs={{0,1},{1,0},{2,3},{3,2},{4,5},{5,4},{6,7},{7,6},{8,9},{9,8},{10,11... | collective-permute-start | bytes 18440 | tf_op jit(solution)/shard_map/ppermute | solution.py:28
  70.5 4.5 %collective-permute-start.23 = (f32[4,384]{1,0:T(4,128)S(1)}, f32[4,384]{1,0:T(4,128)S(1)}, u32[]{:S(2)}, u32[]{:S(2)}) collective-permute-start(f32[4,384]{1,0:T(4,128)S(1)} %get-tuple-element.44), channel_id=1, source_target_pairs={{0,3},{1,2},{2,1},{3,0},{4,7},{5,6},{6,5},{7,4},{8,11},{9,10},{10,... | collective-permute-start | bytes 18440 | tf_op jit(solution)/shard_map/ppermute | solution.py:28
  75.0 7.5 %collective-permute-start.28 = (f32[1,384]{1,0:T(1,128)S(1)}, f32[1,384]{1,0:T(1,128)S(1)}, u32[]{:S(2)}, u32[]{:S(2)}) collective-permute-start(f32[1,384]{1,0:T(1,128)S(1)} %get-tuple-element.68), channel_id=1, source_target_pairs={{0,8},{1,9},{2,10},{3,11},{4,12},{5,13},{6,14},{7,15},{8,0},{9,1},... | collective-permute-start | bytes 4616 | tf_op jit(solution)/shard_map/ppermute | solution.py:28
  77.2 5.3 %collective-permute-start.27 = (f32[1,384]{1,0:T(1,128)S(1)}, f32[1,384]{1,0:T(1,128)S(1)}, u32[]{:S(2)}, u32[]{:S(2)}) collective-permute-start(f32[1,384]{1,0:T(1,128)S(1)} %get-tuple-element.69), channel_id=1, source_target_pairs={{0,4},{1,5},{2,6},{3,7},{4,0},{5,1},{6,2},{7,3},{8,12},{9,13},{10,... | collective-permute-start | bytes 4616 | tf_op jit(solution)/shard_map/ppermute | solution.py:28
  77.8 5.4 %collective-permute-start.26 = (f32[1,384]{1,0:T(1,128)S(1)}, f32[1,384]{1,0:T(1,128)S(1)}, u32[]{:S(2)}, u32[]{:S(2)}) collective-permute-start(f32[1,384]{1,0:T(1,128)S(1)} %get-tuple-element.67), channel_id=1, source_target_pairs={{0,12},{1,13},{2,14},{3,15},{4,8},{5,9},{6,10},{7,11},{8,4},{9,5},... | collective-permute-start | bytes 4616 | tf_op jit(solution)/shard_map/ppermute | solution.py:28
  83.2 1.2 %collective-permute-start.29 = (f32[1,384]{1,0:T(1,128)S(1)}, f32[1,384]{1,0:T(1,128)S(1)}, u32[]{:S(2)}, u32[]{:S(2)}) collective-permute-start(f32[1,384]{1,0:T(1,128)S(1)} %get-tuple-element.51), channel_id=1, source_target_pairs={{0,16},{16,0},{1,17},{17,1},{2,18},{18,2},{3,19},{19,3},{4,20},{20... | collective-permute-start | bytes 4616 | tf_op jit(solution)/shard_map/ppermute | solution.py:33

commit v8 on v5

--- a/solution.py
+++ b/solution.py
@@ -39,7 +39,6 @@
     while bits:
         pair, bits = bits[:2], bits[2:]
         groups.append(tuple(pair) if len(pair) == 1 else (pair[0], pair[1], pair[0] ^ pair[1]))
-    groups[0] = groups[0][::-1]
     return groups
 
 
@@ -170,9 +169,11 @@
             gain = gains[pl.ds(windex, 1), pl.ds(column, wide)]
             hat = (pieces[e, 0:tokens, :].astype(F32) - mean) * scale
             u_out[:, pl.ds(column, wide)] = (hat * gain).astype(BF16)
-        z = lax.dot_general(
-            u_out[...], held[...], (((1,), (1,)), ((), ())), preferred_element_type=F32
-        )
+        contract = (((1,), (1,)), ((), ()))
+        if backward:
+            z = lax.dot_general(u_out[...], held[...], contract, preferred_element_type=F32)
+        else:
+            z = lax.dot_general(held[...], u_out[...], contract, preferred_element_type=F32).T
         gelu, slope = gelu_and_slope(z)
         z_out[...] = z
         y_out[...] = (own[...].astype(F32) + gelu).astype(BF16)
@@ -249,7 +250,7 @@
 def last_kernel(offsets, places, dims, part_count, *refs):
     tokens, wide, model_width, first_size = dims
     scalars, weights, pieces, stat, z_ref, dy_ref = refs[:6]
-    refs = refs[6:]
+    refs = refs[7:]
     if part_count:
         parts, (block_ref, next_stat, next_gain), refs = (
             refs[:part_count],
@@ -290,12 +291,12 @@
         gain_out[a][b : b + 1, :] = jnp.sum(part * hat, axis=0, keepdims=True)
 
 
-def last_call(scalars, weights, pieces, stat, z, dy, finish, offsets, send_order, wide, first_size):
+def last_call(scalars, weights, pieces, stat, z, dy, after, finish, offsets, send_order, wide, first_size):
     rows, model_width = weights.shape[2:]
     tokens = dy.shape[0]
     rest = len(offsets) // first_size
     places = [divmod(send_order.index(o), rest) for o in offsets]
-    operands = [scalars, weights, pieces, stat, z, dy]
+    operands = [scalars, weights, pieces, stat, z, dy, after]
     outs = [
         jax.ShapeDtypeStruct((tokens, rows), BF16),
     ] + [jax.ShapeDtypeStruct((rest, wide), F32)] * first_size
@@ -389,7 +390,7 @@
     return pl.pallas_call(
         load_kernel,
         out_shape=jax.ShapeDtypeStruct(weights.shape, weights.dtype),
-        in_specs=[HBM, ANY],
+        in_specs=[ANY, ANY],
         out_specs=VMEM,
         scratch_shapes=[pltpu.SemaphoreType.DMA((2,))],
         compiler_params=pltpu.CompilerParams(vmem_limit_bytes=VMEM_LIMIT),
@@ -440,7 +441,7 @@
             jax.ShapeDtypeStruct((tokens, block), BF16),
             jax.ShapeDtypeStruct((tokens + PAD_ROWS, block), BF16),
         ],
-        in_specs=[SMEM] + [HBM] * 5,
+        in_specs=[SMEM] + [ANY] * 5,
         out_specs=[VMEM] * 3,
         scratch_shapes=[pltpu.VMEM(gains.shape, F32), pltpu.SemaphoreType.DMA((3,))],
         compiler_params=pltpu.CompilerParams(vmem_limit_bytes=VMEM_LIMIT),
@@ -469,8 +470,10 @@
     wide = block << merged
     bit_count = seq_size.bit_length() - 1
     groups = bit_groups(merged, bit_count)
-    back_groups = groups[::-1]
+    back_groups = [group[::-1] for group in groups[::-1]]
+    later_groups = groups if sections > 2 else [groups[0][::-1]] + groups[1:]
     offsets = [o >> merged for o in offsets_of(groups)]
+    later_offsets = [o >> merged for o in offsets_of(later_groups)]
     send_order = [o >> merged for o in offsets_of(back_groups[::-1])]
     me = (seq_index >> merged).astype(jnp.int32)
     first_index = jnp.where(lower, 0, 1).astype(jnp.int32)
@@ -505,8 +508,8 @@
             lax.dynamic_slice_in_dim(value, width - start, width, axis=1),
         )
 
-    def gathered(value):
-        return gather_xor(joined_halves(value, 1), groups)
+    def gathered(value, step):
+        return gather_xor(joined_halves(value, 1), groups if step == 0 else later_groups)
 
     def moved(value, step, later):
         low = min(step, sections - 1 - step)
@@ -516,21 +519,19 @@
         route = [(low, new), (sections - 1 - low, sections - 1 - new)]
         return lax.ppermute(value, "section", route)
 
-    def reduced(sent, beside=None):
-        parts = grads = None
+    def reduced(sent):
+        parts = None
         for n, group in enumerate(back_groups):
             sent = sent.reshape((len(group) + 1, -1) + sent.shape[1:])
             parts = reduce_round(sent, group)
             if n + 1 < len(back_groups):
-                if n == 0 and beside is not None:
-                    parts, grads = lax.optimization_barrier((parts, beside()))
                 total = functools.reduce(jnp.add, [p.astype(F32) for p in parts])
                 sent = total.astype(BF16)
                 kept = total[0]
         parts = [kept if len(back_groups) > 1 else parts[0][0].astype(F32)] + [
             p[0] for p in parts[1:]
         ]
-        return parts, grads
+        return parts
 
     def finished(parts):
         total = functools.reduce(jnp.add, [p.astype(F32) for p in parts])
@@ -554,7 +555,7 @@
     gains = None
     for step in range(sections):
         last = step == sections - 1
-        pieces, partly = gathered(packed if step == 0 else state)
+        pieces, partly = gathered(packed if step == 0 else state, step)
         if step == 0:
             weights = load_call(section_weights, partly)
         result = section_call(
@@ -565,7 +566,7 @@
             gains,
             grad if last else None,
             None,
-            offsets,
+            offsets if step == 0 else later_offsets,
             send_order,
             wide,
             step == 0,
@@ -584,16 +585,13 @@
             state = moved(y, step, step + 1)
     u_a, y_a = first_record[2], first_record[5]
     u_b, y_b = second_record[2], second_record[5]
+    y_other = swapped(y_b)
+    down_out = jnp.where(lower, y_a, y_other)
+    up_out = jnp.where(lower, y_other, y_a)
     needed_a = jnp.where(lower, u_a[:, :half], u_a[:, half:])
     needed_b = jnp.where(lower, u_b[:, half:], u_b[:, :half])
-    other_a = swapped(jnp.where(lower, u_a[:, half:], u_a[:, :half]))
+    sent_a = jnp.where(lower, u_a[:, half:], u_a[:, :half])
     other_b = swapped(jnp.where(lower, u_b[:, :half], u_b[:, half:]))
-    def early_results(dz):
-        y_other = swapped(y_b)
-        grads = weight_grad_call(
-            scalars_at(0), 1, dz, swapped(dz), needed_b, other_b, jnp.zeros((8, LANES), F32), ()
-        )
-        return grads, (jnp.where(lower, y_a, y_other), jnp.where(lower, y_other, y_a))
 
     dz_a = dz_b = gain_b = gain_a = None
     for step in reversed(range(1, sections)):
@@ -612,17 +610,12 @@
                 wide,
                 False,
             )
+        parts = reduced(sent)
         gain_row = lax.dynamic_slice_in_dim(own_gains, index_at(step), 1, axis=0)
         if step >= middle:
             dz_b = keep_live(live_at(step), dz, dz_b)
         else:
             dz_a = keep_live(live_at(step), dz, dz_a)
-        beside = None
-        if step == middle:
-            beside = functools.partial(early_results, dz_b)
-        parts, done = reduced(sent, beside)
-        if beside is not None:
-            (early_first, early_second, _), (down_out, up_out) = beside() if done is None else done
         finish = None
         if sections == 2 and not merged:
             finish = (parts, (source, stat, gain_row))
@@ -644,6 +637,9 @@
             else:
                 gain_a = keep_live(live_at(step), gain_grad, gain_a)
             grad = moved(new_grad, step, step - 1)
+    *early, token = weight_grad_call(
+        scalars_at(0), 1, dz_b, swapped(dz_b), needed_b, other_b, jnp.zeros((8, LANES), F32), ()
+    )
     _, pieces, _, stat, z, _ = first_record
     first_size = len(back_groups[0]) + 1
     result = last_call(
@@ -653,6 +649,7 @@
         stat,
         z,
         grad,
+        token,
         finish,
         offsets,
         send_order,
@@ -663,8 +660,9 @@
     if finish is not None:
         gain_b = result[-1]
     dz_a = keep_live(live_at(0), dz, dz_a)
+    sent_a, dz_a = lax.optimization_barrier((sent_a, dz_a))
+    other_a = swapped(sent_a)
     dz_a_other = swapped(dz_a)
-    early = (early_first, early_second)
     for n, group in enumerate(back_groups):
         if n:
             gain_parts = gain_parts.reshape((len(group) + 1, -1) + gain_parts.shape[1:])

time: 88.9 us -> 83.6 us (0.940)
  waiting for transfers between devices: 29.9 us -> 25.4 us
  Pallas kernels: 21.1 us -> 20 us
    ppermute x24, waiting for transfers between devices: 28.2 us -> 24.9 us  [from_xor(): return lax.ppermute(value, 'seq', [(i, i ^ distance) for i in range(size)])]
    ppermute x6, waiting for transfers between devices: 1.73 us -> 0.49 us  [swapped(): lax.ppermute(value, 'section', [(i, size - 1 - i) for i in range(size)])]
  transfers between devices with their start and end apart: 30 -> 30, of which waited for: 20 -> 18; matrix products, arithmetic and copies ran while one was open for 2% -> 2% of each run, Pallas kernels for 14% -> 12%
where the time goes in v8:
time: 83.6 us; the launch traced here: 83.4 us
  starting transfers between devices  34.3 us (41%)
  waiting for transfers between devices  25.4 us (30%)
  Pallas kernels  20 us (24%)
  other arithmetic  1.68 us (2%)
  local copies, waits for them, and re-layouts  1.06 us (1%)
  between operations  0.92 us (1%)
    ppermute x24, starting transfers between devices, from_xor(): return lax.ppermute(value, 'seq', [(i, i ^ distance) for i in range(size)])  33.2 us
    ppermute x24, waiting for transfers between devices, from_xor(): return lax.ppermute(value, 'seq', [(i, i ^ distance) for i in range(size)])  24.9 us
    pallas_call x2, Pallas kernels, section_call(): pl.pallas_call(functools.partial(section_kernel, offsets, (tokens, wide,...  6.91 us
    pallas_call x2, Pallas kernels, weight_grad_call(): pl.pallas_call(functools.partial(weight_grad_kernel, first_at, tiles, len...  6.29 us
    pallas_call x1, Pallas kernels, load_call(): pl.pallas_call(load_kernel, out_shape=jax.ShapeDtypeStruct(weights.shape,...  3.79 us
  transfers between devices with their start and end apart: 30, of which 18 were waited for; matrix products, arithmetic and copies ran while one was open for 2% of the time, Pallas kernels for 12%

profile of v8, /device:TPU:0, one launch (start us, length us, event | category | flops | bytes accessed | tf_op | source)
XLA Modules:
  0.0 83.4 jit_solution(4620344631819363490)
XLA Ops:
  0.7 1.4 %shard_map.101 = (bf16[64,384]{1,0:T(8,128)(2,1)S(1)}, bf16[64,384]{1,0:T(8,128)(2,1)S(1)}, bf16[72,384]{1,0:T(8,128)(2,1)S(1)}) custom-call(s32[2]{0:T(128)S(1)} %pad_add_fusion.scalars.refs_0_, bf16[64,384]{1,0:T(8,128)(2,1)} %refs_0_.1, bf16[64,384]{1,0:T(8,128)(2,1)} %refs_1_.1, bf16[64,384]{1,0:T(8,128)(2,1)} %refs_2_.1, bf16[64,384]{1,0:T(8,128)(2,1)} %refs_3_.1, ...), custom_call_target="tpu_custom_call" | custom-call | tf_op jit(solution)/shard_map/pallas_call | solution.py:437
  2.1 4.1 %collective-permute-start = (bf16[1,72,384]{2,1,0:T(8,128)(2,1)S(1)}, bf16[1,72,384]{2,1,0:T(8,128)(2,1)S(1)}, u32[]{:S(2)}, u32[]{:S(2)}) collective-permute-start(bf16[1,72,384]{2,1,0:T(8,128)(2,1)S(1)} %bitcast.25), channel_id=1, source_target_pairs={{0,8},{1,9},{2,10},{3,11},{4,12},{5,13},{6,14},{7,15},{8,0},{9,1},... | collective-permute-start | bytes 165896 | tf_op jit(solution)/shard_map/ppermute | solution.py:28
  6.2 1.6 %collective-permute-start.1 = (bf16[1,72,384]{2,1,0:T(8,128)(2,1)S(1)}, bf16[1,72,384]{2,1,0:T(8,128)(2,1)S(1)}, u32[]{:S(2)}, u32[]{:S(2)}) collective-permute-start(bf16[1,72,384]{2,1,0:T(8,128)(2,1)S(1)} %bitcast.26), channel_id=1, source_target_pairs={{0,4},{1,5},{2,6},{3,7},{4,0},{5,1},{6,2},{7,3},{8,12},{9,13},{10,... | collective-permute-start | bytes 165896 | tf_op jit(solution)/shard_map/ppermute | solution.py:28
  9.1 1.3 %collective-permute-done.1 = bf16[1,72,384]{2,1,0:T(8,128)(2,1)S(1)} collective-permute-done((bf16[1,72,384]{2,1,0:T(8,128)(2,1)S(1)}, bf16[1,72,384]{2,1,0:T(8,128)(2,1)S(1)}, u32[]{:S(2)}, u32[]{:S(2)}) %collective-permute-start.1) | collective-permute-done | bytes 55328 | tf_op jit(solution)/shard_map/ppermute | solution.py:28
  10.4 3.4 %collective-permute-done.2 = bf16[1,72,384]{2,1,0:T(8,128)(2,1)S(1)} collective-permute-done((bf16[1,72,384]{2,1,0:T(8,128)(2,1)S(1)}, bf16[1,72,384]{2,1,0:T(8,128)(2,1)S(1)}, u32[]{:S(2)}, u32[]{:S(2)}) %collective-permute-start.2) | collective-permute-done | bytes 55328 | tf_op jit(solution)/shard_map/ppermute | solution.py:28
  13.8 1.6 %collective-permute-start.3 = (bf16[4,72,384]{2,1,0:T(8,128)(2,1)S(1)}, bf16[4,72,384]{2,1,0:T(8,128)(2,1)S(1)}, u32[]{:S(2)}, u32[]{:S(2)}) collective-permute-start(bf16[4,72,384]{2,1,0:T(8,128)(2,1)S(1)} %pad_maximum_fusion._), channel_id=1, source_target_pairs={{0,2},{1,3},{2,0},{3,1},{4,6},{5,7},{6,4},{7,5},{8,10},{9,11},{10,... | collective-permute-start | bytes 663560 | tf_op jit(solution)/shard_map/ppermute | solution.py:28
  15.4 1.5 %collective-permute-start.4 = (bf16[4,72,384]{2,1,0:T(8,128)(2,1)S(1)}, bf16[4,72,384]{2,1,0:T(8,128)(2,1)S(1)}, u32[]{:S(2)}, u32[]{:S(2)}) collective-permute-start(bf16[4,72,384]{2,1,0:T(8,128)(2,1)S(1)} %pad_maximum_fusion._), channel_id=1, source_target_pairs={{0,1},{1,0},{2,3},{3,2},{4,5},{5,4},{6,7},{7,6},{8,9},{9,8},{10,11... | collective-permute-start | bytes 663560 | tf_op jit(solution)/shard_map/ppermute | solution.py:28
  17.4 3.8 %shard_map.102.refs_1_ = bf16[1,2,384,6144]{3,2,1,0:T(8,128)(2,1)S(1)} custom-call(bf16[1,2,384,6144]{3,2,1,0:T(8,128)(2,1)} %weights.1, bf16[4,72,384]{2,1,0:T(8,128)(2,1)S(1)} %pad_maximum_fusion._), custom_call_target="tpu_custom_call" | custom-call | bytes 9437184 | tf_op jit(solution)/shard_map/pallas_call | solution.py:390
  23.1 2.3 %collective-permute-done.5 = bf16[4,72,384]{2,1,0:T(8,128)(2,1)S(1)} collective-permute-done((bf16[4,72,384]{2,1,0:T(8,128)(2,1)S(1)}, bf16[4,72,384]{2,1,0:T(8,128)(2,1)S(1)}, u32[]{:S(2)}, u32[]{:S(2)}) %collective-permute-start.5) | collective-permute-done | bytes 221216 | tf_op jit(solution)/shard_map/ppermute | solution.py:28
  25.4 2.6 %shard_map.103 = (bf16[64,6144]{1,0:T(8,128)(2,1)S(1)}, f32[64,128]{1,0:T(8,128)S(1)}, f32[64,384]{1,0:T(8,128)S(1)}, bf16[64,384]{1,0:T(8,128)(2,1)S(1)}, f32[2,6144]{1,0:T(2,128)S(1)}) custom-call(s32[2]{0:T(128)S(1)} %pad_add_fusion.scalars.refs_0_, bf16[1,2,384,6144]{3,2,1,0:T(8,128)(2,1)S(1)} %shard_map.102.refs_1_, ...), custom_call_target="tpu_custom_call" | custom-call | flops 301989888 | bytes 4718592 | tf_op jit(solution)/shard_map/pallas_call | solution.py:230
  28.0 1.4 %collective-permute-start.6 = (bf16[1,64,384]{2,1,0:T(8,128)(2,1)S(1)}, bf16[1,64,384]{2,1,0:T(8,128)(2,1)S(1)}, u32[]{:S(2)}, u32[]{:S(2)}) collective-permute-start(bf16[1,64,384]{2,1,0:T(8,128)(2,1)S(1)} %bitcast.21), channel_id=1, source_target_pairs={{0,12},{1,13},{2,14},{3,15},{4,8},{5,9},{6,10},{7,11},{8,4},{9,5},... | collective-permute-start | bytes 147464 | tf_op jit(solution)/shard_map/ppermute | solution.py:28
  29.5 3.0 %collective-permute-start.8 = (bf16[1,64,384]{2,1,0:T(8,128)(2,1)S(1)}, bf16[1,64,384]{2,1,0:T(8,128)(2,1)S(1)}, u32[]{:S(2)}, u32[]{:S(2)}) collective-permute-start(bf16[1,64,384]{2,1,0:T(8,128)(2,1)S(1)} %bitcast.23), channel_id=1, source_target_pairs={{0,8},{1,9},{2,10},{3,11},{4,12},{5,13},{6,14},{7,15},{8,0},{9,1},... | collective-permute-start | bytes 147464 | tf_op jit(solution)/shard_map/ppermute | solution.py:28
  32.5 1.5 %collective-permute-done.6 = bf16[1,64,384]{2,1,0:T(8,128)(2,1)S(1)} collective-permute-done((bf16[1,64,384]{2,1,0:T(8,128)(2,1)S(1)}, bf16[1,64,384]{2,1,0:T(8,128)(2,1)S(1)}, u32[]{:S(2)}, u32[]{:S(2)}) %collective-permute-start.6) | collective-permute-done | bytes 49184 | tf_op jit(solution)/shard_map/ppermute | solution.py:28
  34.5 1.6 %collective-permute-start.9 = (bf16[4,64,384]{2,1,0:T(8,128)(2,1)S(1)}, bf16[4,64,384]{2,1,0:T(8,128)(2,1)S(1)}, u32[]{:S(2)}, u32[]{:S(2)}) collective-permute-start(bf16[4,64,384]{2,1,0:T(8,128)(2,1)S(1)} %pad_maximum_fusion.1), channel_id=1, source_target_pairs={{0,2},{1,3},{2,0},{3,1},{4,6},{5,7},{6,4},{7,5},{8,10},{9,11},{10,... | collective-permute-start | bytes 589832 | tf_op jit(solution)/shard_map/ppermute | solution.py:28
  36.1 1.5 %collective-permute-start.10 = (bf16[4,64,384]{2,1,0:T(8,128)(2,1)S(1)}, bf16[4,64,384]{2,1,0:T(8,128)(2,1)S(1)}, u32[]{:S(2)}, u32[]{:S(2)}) collective-permute-start(bf16[4,64,384]{2,1,0:T(8,128)(2,1)S(1)} %pad_maximum_fusion.1), channel_id=1, source_target_pairs={{0,1},{1,0},{2,3},{3,2},{4,5},{5,4},{6,7},{7,6},{8,9},{9,8},{10,11... | collective-permute-start | bytes 589832 | tf_op jit(solution)/shard_map/ppermute | solution.py:28
  38.1 2.4 %collective-permute-done.9 = bf16[4,64,384]{2,1,0:T(8,128)(2,1)S(1)} collective-permute-done((bf16[4,64,384]{2,1,0:T(8,128)(2,1)S(1)}, bf16[4,64,384]{2,1,0:T(8,128)(2,1)S(1)}, u32[]{:S(2)}, u32[]{:S(2)}) %collective-permute-start.9) | collective-permute-done | bytes 196640 | tf_op jit(solution)/shard_map/ppermute | solution.py:28
  40.6 1.2 %collective-permute-done.10 = bf16[4,64,384]{2,1,0:T(8,128)(2,1)S(1)} collective-permute-done((bf16[4,64,384]{2,1,0:T(8,128)(2,1)S(1)}, bf16[4,64,384]{2,1,0:T(8,128)(2,1)S(1)}, u32[]{:S(2)}, u32[]{:S(2)}) %collective-permute-start.10) | collective-permute-done | bytes 196640 | tf_op jit(solution)/shard_map/ppermute | solution.py:28
  41.8 2.4 %collective-permute-done.11 = bf16[4,64,384]{2,1,0:T(8,128)(2,1)S(1)} collective-permute-done((bf16[4,64,384]{2,1,0:T(8,128)(2,1)S(1)}, bf16[4,64,384]{2,1,0:T(8,128)(2,1)S(1)}, u32[]{:S(2)}, u32[]{:S(2)}) %collective-permute-start.11) | collective-permute-done | bytes 196640 | tf_op jit(solution)/shard_map/ppermute | solution.py:28
  44.2 4.4 %shard_map.104 = (bf16[64,6144]{1,0:T(8,128)(2,1)S(1)}, f32[64,128]{1,0:T(8,128)S(1)}, f32[64,384]{1,0:T(8,128)}, bf16[64,384]{1,0:T(8,128)(2,1)S(1)}, bf16[64,3...) custom-call(s32[2]{0:T(128)S(1)} %pad_add_fusion.1.refs_0_, bf16[1,2,384,6144]{3,2,1,0:T(8,128)(2,1)S(1)} %shard_map.102.refs_1_, ...), custom_call_target="tpu_custom_call" | custom-call | flops 603979776 | bytes 4718592 | tf_op jit(solution)/shard_map/pallas_call | solution.py:230
  48.6 2.2 %collective-permute-start.15 = (bf16[4,200,128]{2,1,0:T(8,128)(2,1)S(1)}, bf16[4,200,128]{2,1,0:T(8,128)(2,1)S(1)}, u32[]{:S(2)}, u32[]{:S(2)}) collective-permute-start(bf16[4,200,128]{2,1,0:T(8,128)(2,1)S(1)} %get-tuple-element.63), channel_id=1, source_target_pairs={{0,3},{1,2},{2,1},{3,0},{4,7},{5,6},{6,5},{7,4},{8,11},{9,10},{10,... | collective-permute-start | bytes 614408 | tf_op jit(solution)/shard_map/ppermute | solution.py:28
  52.8 2.6 %collective-permute-done.15 = bf16[4,200,128]{2,1,0:T(8,128)(2,1)S(1)} collective-permute-done((bf16[4,200,128]{2,1,0:T(8,128)(2,1)S(1)}, bf16[4,200,128]{2,1,0:T(8,128)(2,1)S(1)}, u32[]{:S(2)}, u32[]{:S(2)}) %collective-permute-start.15) | collective-permute-done | bytes 204832 | tf_op jit(solution)/shard_map/ppermute | solution.py:28
  55.4 1.8 %collective-permute-done.16 = bf16[4,200,128]{2,1,0:T(8,128)(2,1)S(1)} collective-permute-done((bf16[4,200,128]{2,1,0:T(8,128)(2,1)S(1)}, bf16[4,200,128]{2,1,0:T(8,128)(2,1)S(1)}, u32[]{:S(2)}, u32[]{:S(2)}) %collective-permute-start.16) | collective-permute-done | bytes 204832 | tf_op jit(solution)/shard_map/ppermute | solution.py:28
  57.7 1.9 %collective-permute-start.19 = (bf16[1,200,128]{2,1,0:T(8,128)(2,1)S(1)}, bf16[1,200,128]{2,1,0:T(8,128)(2,1)S(1)}, u32[]{:S(2)}, u32[]{:S(2)}) collective-permute-start(bf16[1,200,128]{2,1,0:T(8,128)(2,1)S(1)} %get-tuple-element.71), channel_id=1, source_target_pairs={{0,4},{1,5},{2,6},{3,7},{4,0},{5,1},{6,2},{7,3},{8,12},{9,13},{10,... | collective-permute-start | bytes 153608 | tf_op jit(solution)/shard_map/ppermute | solution.py:28
  59.6 1.1 %collective-permute-start.20 = (bf16[1,200,128]{2,1,0:T(8,128)(2,1)S(1)}, bf16[1,200,128]{2,1,0:T(8,128)(2,1)S(1)}, u32[]{:S(2)}, u32[]{:S(2)}) collective-permute-start(bf16[1,200,128]{2,1,0:T(8,128)(2,1)S(1)} %get-tuple-element.70), channel_id=1, source_target_pairs={{0,8},{1,9},{2,10},{3,11},{4,12},{5,13},{6,14},{7,15},{8,0},{9,1},... | collective-permute-start | bytes 153608 | tf_op jit(solution)/shard_map/ppermute | solution.py:28
  60.7 1.4 %collective-permute-start.18 = (bf16[1,200,128]{2,1,0:T(8,128)(2,1)S(1)}, bf16[1,200,128]{2,1,0:T(8,128)(2,1)S(1)}, u32[]{:S(2)}, u32[]{:S(2)}) collective-permute-start(bf16[1,200,128]{2,1,0:T(8,128)(2,1)S(1)} %get-tuple-element.72), channel_id=1, source_target_pairs={{0,12},{1,13},{2,14},{3,15},{4,8},{5,9},{6,10},{7,11},{8,4},{9,5},... | collective-permute-start | bytes 153608 | tf_op jit(solution)/shard_map/ppermute | solution.py:28
  62.2 3.1 %shard_map.105 = (f32[384,3072]{1,0:T(8,128)}, f32[384,3072]{1,0:T(8,128)}, f32[8,128]{1,0:T(8,128)S(1)}) custom-call(s32[2]{0:T(128)S(1)} %pad_add_fusion.scalars.refs_0_, bf16[64,384]{1,0:T(8,128)(2,1)S(1)} %get-tuple-element.41.refs_1_, bf16[64,384]{1,0:T(8,128)(2,1)S(1)} %collective-permute-done.13.refs_2_, ...), custom_call_target="tpu_custom_call" | custom-call | flops 301989888 | bytes 4718592 | tf_op jit(solution)/shard_map/pallas_call | solution.py:361
  65.4 1.4 %collective-permute-done.18 = bf16[1,200,128]{2,1,0:T(8,128)(2,1)S(1)} collective-permute-done((bf16[1,200,128]{2,1,0:T(8,128)(2,1)S(1)}, bf16[1,200,128]{2,1,0:T(8,128)(2,1)S(1)}, u32[]{:S(2)}, u32[]{:S(2)}) %collective-permute-start.18) | collective-permute-done | bytes 51232 | tf_op jit(solution)/shard_map/ppermute | solution.py:28
  66.7 1.6 %shard_map.106 = (bf16[64,384]{1,0:T(8,128)(2,1)S(1)}, f32[4,384]{1,0:T(4,128)S(1)}, f32[4,384]{1,0:T(4,128)S(1)}, f32[4,384]{1,0:T(4,128)S(1)}, f32[4,384]{1,0:T(4,128)S(1)}, /*index=5*/f32[1,384]{1,0:T(1,128)S(1)}) custom-call(s32[2]{0:T(128)S(1)} %pad_add_fusion.scalars.refs_0_, bf16[1,2,384,6144]{3,2,1,0:T(8,128)(2,1)S(1)} %shard_map.102.refs_1_, ...), custom_call_target="tpu_custom_call" | custom-call | flops 301989888 | bytes 4718592 | tf_op jit(solution)/shard_map/pallas_call | solution.py:309
  69.0 2.1 %collective-permute-start.23 = (f32[4,384]{1,0:T(4,128)S(1)}, f32[4,384]{1,0:T(4,128)S(1)}, u32[]{:S(2)}, u32[]{:S(2)}) collective-permute-start(f32[4,384]{1,0:T(4,128)S(1)} %get-tuple-element.54), channel_id=1, source_target_pairs={{0,3},{1,2},{2,1},{3,0},{4,7},{5,6},{6,5},{7,4},{8,11},{9,10},{10,... | collective-permute-start | bytes 18440 | tf_op jit(solution)/shard_map/ppermute | solution.py:28
  72.5 3.1 %shard_map.107 = (f32[384,3072]{1,0:T(8,128)}, f32[384,3072]{1,0:T(8,128)}, f32[4,384]{1,0:T(4,128)S(1)}) custom-call(s32[2]{0:T(128)S(1)} %pad_add_fusion.scalars.refs_0_, bf16[64,384]{1,0:T(8,128)(2,1)S(1)} %get-tuple-element.47.refs_1_, bf16[64,384]{1,0:T(8,128)(2,1)S(1)} %collective-permute-done.21.refs_2_, ...), custom_call_target="tpu_custom_call", output_to_operand_aliasing={{0}: (6, {}), {1}: (7, {})} | custom-call | flops 301989888 | bytes 4718592 | tf_op jit(solution)/shard_map/pallas_call | solution.py:361
  75.7 1.5 %collective-permute-start.26 = (f32[1,384]{1,0:T(1,128)S(1)}, f32[1,384]{1,0:T(1,128)S(1)}, u32[]{:S(2)}, u32[]{:S(2)}) collective-permute-start(f32[1,384]{1,0:T(1,128)S(1)} %get-tuple-element.75), channel_id=1, source_target_pairs={{0,12},{1,13},{2,14},{3,15},{4,8},{5,9},{6,10},{7,11},{8,4},{9,5},... | collective-permute-start | bytes 4616 | tf_op jit(solution)/shard_map/ppermute | solution.py:28
  77.2 3.0 %collective-permute-start.28 = (f32[1,384]{1,0:T(1,128)S(1)}, f32[1,384]{1,0:T(1,128)S(1)}, u32[]{:S(2)}, u32[]{:S(2)}) collective-permute-start(f32[1,384]{1,0:T(1,128)S(1)} %get-tuple-element.76), channel_id=1, source_target_pairs={{0,8},{1,9},{2,10},{3,11},{4,12},{5,13},{6,14},{7,15},{8,0},{9,1},... | collective-permute-start | bytes 4616 | tf_op jit(solution)/shard_map/ppermute | solution.py:28
  (66 shorter events, 12.9 us)
Async XLA Ops:
  2.1 6.9 %collective-permute-start = (bf16[1,72,384]{2,1,0:T(8,128)(2,1)S(1)}, bf16[1,72,384]{2,1,0:T(8,128)(2,1)S(1)}, u32[]{:S(2)}, u32[]{:S(2)}) collective-permute-start(bf16[1,72,384]{2,1,0:T(8,128)(2,1)S(1)} %bitcast.25), channel_id=1, source_target_pairs={{0,8},{1,9},{2,10},{3,11},{4,12},{5,13},{6,14},{7,15},{8,0},{9,1},... | collective-permute-start | bytes 165896 | tf_op jit(solution)/shard_map/ppermute | solution.py:28
  6.2 4.2 %collective-permute-start.1 = (bf16[1,72,384]{2,1,0:T(8,128)(2,1)S(1)}, bf16[1,72,384]{2,1,0:T(8,128)(2,1)S(1)}, u32[]{:S(2)}, u32[]{:S(2)}) collective-permute-start(bf16[1,72,384]{2,1,0:T(8,128)(2,1)S(1)} %bitcast.26), channel_id=1, source_target_pairs={{0,4},{1,5},{2,6},{3,7},{4,0},{5,1},{6,2},{7,3},{8,12},{9,13},{10,... | collective-permute-start | bytes 165896 | tf_op jit(solution)/shard_map/ppermute | solution.py:28
  7.8 6.0 %collective-permute-start.2 = (bf16[1,72,384]{2,1,0:T(8,128)(2,1)S(1)}, bf16[1,72,384]{2,1,0:T(8,128)(2,1)S(1)}, u32[]{:S(2)}, u32[]{:S(2)}) collective-permute-start(bf16[1,72,384]{2,1,0:T(8,128)(2,1)S(1)} %bitcast.27), channel_id=1, source_target_pairs={{0,12},{1,13},{2,14},{3,15},{4,8},{5,9},{6,10},{7,11},{8,4},{9,5},... | collective-permute-start | bytes 165896 | tf_op jit(solution)/shard_map/ppermute | solution.py:28
  13.8 8.3 %collective-permute-start.3 = (bf16[4,72,384]{2,1,0:T(8,128)(2,1)S(1)}, bf16[4,72,384]{2,1,0:T(8,128)(2,1)S(1)}, u32[]{:S(2)}, u32[]{:S(2)}) collective-permute-start(bf16[4,72,384]{2,1,0:T(8,128)(2,1)S(1)} %pad_maximum_fusion._), channel_id=1, source_target_pairs={{0,2},{1,3},{2,0},{3,1},{4,6},{5,7},{6,4},{7,5},{8,10},{9,11},{10,... | collective-permute-start | bytes 663560 | tf_op jit(solution)/shard_map/ppermute | solution.py:28
  15.4 7.7 %collective-permute-start.4 = (bf16[4,72,384]{2,1,0:T(8,128)(2,1)S(1)}, bf16[4,72,384]{2,1,0:T(8,128)(2,1)S(1)}, u32[]{:S(2)}, u32[]{:S(2)}) collective-permute-start(bf16[4,72,384]{2,1,0:T(8,128)(2,1)S(1)} %pad_maximum_fusion._), channel_id=1, source_target_pairs={{0,1},{1,0},{2,3},{3,2},{4,5},{5,4},{6,7},{7,6},{8,9},{9,8},{10,11... | collective-permute-start | bytes 663560 | tf_op jit(solution)/shard_map/ppermute | solution.py:28
  16.9 8.5 %collective-permute-start.5 = (bf16[4,72,384]{2,1,0:T(8,128)(2,1)S(1)}, bf16[4,72,384]{2,1,0:T(8,128)(2,1)S(1)}, u32[]{:S(2)}, u32[]{:S(2)}) collective-permute-start(bf16[4,72,384]{2,1,0:T(8,128)(2,1)S(1)} %pad_maximum_fusion._), channel_id=1, source_target_pairs={{0,3},{1,2},{2,1},{3,0},{4,7},{5,6},{6,5},{7,4},{8,11},{9,10},{10,... | collective-permute-start | bytes 663560 | tf_op jit(solution)/shard_map/ppermute | solution.py:28
  28.0 6.0 %collective-permute-start.6 = (bf16[1,64,384]{2,1,0:T(8,128)(2,1)S(1)}, bf16[1,64,384]{2,1,0:T(8,128)(2,1)S(1)}, u32[]{:S(2)}, u32[]{:S(2)}) collective-permute-start(bf16[1,64,384]{2,1,0:T(8,128)(2,1)S(1)} %bitcast.21), channel_id=1, source_target_pairs={{0,12},{1,13},{2,14},{3,15},{4,8},{5,9},{6,10},{7,11},{8,4},{9,5},... | collective-permute-start | bytes 147464 | tf_op jit(solution)/shard_map/ppermute | solution.py:28
  29.4 4.6 %collective-permute-start.7 = (bf16[1,64,384]{2,1,0:T(8,128)(2,1)S(1)}, bf16[1,64,384]{2,1,0:T(8,128)(2,1)S(1)}, u32[]{:S(2)}, u32[]{:S(2)}) collective-permute-start(bf16[1,64,384]{2,1,0:T(8,128)(2,1)S(1)} %bitcast.22), channel_id=1, source_target_pairs={{0,4},{1,5},{2,6},{3,7},{4,0},{5,1},{6,2},{7,3},{8,12},{9,13},{10,... | collective-permute-start | bytes 147464 | tf_op jit(solution)/shard_map/ppermute | solution.py:28
  29.5 5.0 %collective-permute-start.8 = (bf16[1,64,384]{2,1,0:T(8,128)(2,1)S(1)}, bf16[1,64,384]{2,1,0:T(8,128)(2,1)S(1)}, u32[]{:S(2)}, u32[]{:S(2)}) collective-permute-start(bf16[1,64,384]{2,1,0:T(8,128)(2,1)S(1)} %bitcast.23), channel_id=1, source_target_pairs={{0,8},{1,9},{2,10},{3,11},{4,12},{5,13},{6,14},{7,15},{8,0},{9,1},... | collective-permute-start | bytes 147464 | tf_op jit(solution)/shard_map/ppermute | solution.py:28
  34.5 6.0 %collective-permute-start.9 = (bf16[4,64,384]{2,1,0:T(8,128)(2,1)S(1)}, bf16[4,64,384]{2,1,0:T(8,128)(2,1)S(1)}, u32[]{:S(2)}, u32[]{:S(2)}) collective-permute-start(bf16[4,64,384]{2,1,0:T(8,128)(2,1)S(1)} %pad_maximum_fusion.1), channel_id=1, source_target_pairs={{0,2},{1,3},{2,0},{3,1},{4,6},{5,7},{6,4},{7,5},{8,10},{9,11},{10,... | collective-permute-start | bytes 589832 | tf_op jit(solution)/shard_map/ppermute | solution.py:28
  36.1 5.7 %collective-permute-start.10 = (bf16[4,64,384]{2,1,0:T(8,128)(2,1)S(1)}, bf16[4,64,384]{2,1,0:T(8,128)(2,1)S(1)}, u32[]{:S(2)}, u32[]{:S(2)}) collective-permute-start(bf16[4,64,384]{2,1,0:T(8,128)(2,1)S(1)} %pad_maximum_fusion.1), channel_id=1, source_target_pairs={{0,1},{1,0},{2,3},{3,2},{4,5},{5,4},{6,7},{7,6},{8,9},{9,8},{10,11... | collective-permute-start | bytes 589832 | tf_op jit(solution)/shard_map/ppermute | solution.py:28
  37.6 6.6 %collective-permute-start.11 = (bf16[4,64,384]{2,1,0:T(8,128)(2,1)S(1)}, bf16[4,64,384]{2,1,0:T(8,128)(2,1)S(1)}, u32[]{:S(2)}, u32[]{:S(2)}) collective-permute-start(bf16[4,64,384]{2,1,0:T(8,128)(2,1)S(1)} %pad_maximum_fusion.1), channel_id=1, source_target_pairs={{0,3},{1,2},{2,1},{3,0},{4,7},{5,6},{6,5},{7,4},{8,11},{9,10},{10,... | collective-permute-start | bytes 589832 | tf_op jit(solution)/shard_map/ppermute | solution.py:28
  48.6 6.8 %collective-permute-start.15 = (bf16[4,200,128]{2,1,0:T(8,128)(2,1)S(1)}, bf16[4,200,128]{2,1,0:T(8,128)(2,1)S(1)}, u32[]{:S(2)}, u32[]{:S(2)}) collective-permute-start(bf16[4,200,128]{2,1,0:T(8,128)(2,1)S(1)} %get-tuple-element.63), channel_id=1, source_target_pairs={{0,3},{1,2},{2,1},{3,0},{4,7},{5,6},{6,5},{7,4},{8,11},{9,10},{10,... | collective-permute-start | bytes 614408 | tf_op jit(solution)/shard_map/ppermute | solution.py:28
  50.8 6.5 %collective-permute-start.16 = (bf16[4,200,128]{2,1,0:T(8,128)(2,1)S(1)}, bf16[4,200,128]{2,1,0:T(8,128)(2,1)S(1)}, u32[]{:S(2)}, u32[]{:S(2)}) collective-permute-start(bf16[4,200,128]{2,1,0:T(8,128)(2,1)S(1)} %get-tuple-element.65), channel_id=1, source_target_pairs={{0,1},{1,0},{2,3},{3,2},{4,5},{5,4},{6,7},{7,6},{8,9},{9,8},{10,11... | collective-permute-start | bytes 614408 | tf_op jit(solution)/shard_map/ppermute | solution.py:28
  51.3 6.2 %collective-permute-start.17 = (bf16[4,200,128]{2,1,0:T(8,128)(2,1)S(1)}, bf16[4,200,128]{2,1,0:T(8,128)(2,1)S(1)}, u32[]{:S(2)}, u32[]{:S(2)}) collective-permute-start(bf16[4,200,128]{2,1,0:T(8,128)(2,1)S(1)} %get-tuple-element.64), channel_id=1, source_target_pairs={{0,2},{1,3},{2,0},{3,1},{4,6},{5,7},{6,4},{7,5},{8,10},{9,11},{10,... | collective-permute-start | bytes 614408 | tf_op jit(solution)/shard_map/ppermute | solution.py:28
  52.3 9.9 %collective-permute-start.14 = (bf16[64,3072]{1,0:T(8,128)(2,1)S(1)}, bf16[64,3072]{1,0:T(8,128)(2,1)S(1)}, u32[]{:S(2)}, u32[]{:S(2)}) collective-permute-start(bf16[64,3072]{1,0:T(8,128)(2,1)S(1)} %get-tuple-element.68), channel_id=1, source_target_pairs={{0,16},{16,0},{1,17},{17,1},{2,18},{18,2},{3,19},{19,3},{4,20},{20... | collective-permute-start | bytes 1179656 | tf_op jit(solution)/shard_map/ppermute | solution.py:33
  52.3 9.8 %collective-permute-start.13 = (bf16[64,384]{1,0:T(8,128)(2,1)S(1)}, bf16[64,384]{1,0:T(8,128)(2,1)S(1)}, u32[]{:S(2)}, u32[]{:S(2)}) collective-permute-start(bf16[64,384]{1,0:T(8,128)(2,1)S(1)} %get-tuple-element.41.refs_1_), channel_id=1, source_target_pairs={{0,16},{16,0},{1,17},{17,1},{2,18},{18,2},{3,19},{19,3},{4,20},{20... | collective-permute-start | bytes 147464 | tf_op jit(solution)/shard_map/ppermute | solution.py:33
  57.7 7.7 %collective-permute-start.19 = (bf16[1,200,128]{2,1,0:T(8,128)(2,1)S(1)}, bf16[1,200,128]{2,1,0:T(8,128)(2,1)S(1)}, u32[]{:S(2)}, u32[]{:S(2)}) collective-permute-start(bf16[1,200,128]{2,1,0:T(8,128)(2,1)S(1)} %get-tuple-element.71), channel_id=1, source_target_pairs={{0,4},{1,5},{2,6},{3,7},{4,0},{5,1},{6,2},{7,3},{8,12},{9,13},{10,... | collective-permute-start | bytes 153608 | tf_op jit(solution)/shard_map/ppermute | solution.py:28
  59.6 5.7 %collective-permute-start.20 = (bf16[1,200,128]{2,1,0:T(8,128)(2,1)S(1)}, bf16[1,200,128]{2,1,0:T(8,128)(2,1)S(1)}, u32[]{:S(2)}, u32[]{:S(2)}) collective-permute-start(bf16[1,200,128]{2,1,0:T(8,128)(2,1)S(1)} %get-tuple-element.70), channel_id=1, source_target_pairs={{0,8},{1,9},{2,10},{3,11},{4,12},{5,13},{6,14},{7,15},{8,0},{9,1},... | collective-permute-start | bytes 153608 | tf_op jit(solution)/shard_map/ppermute | solution.py:28
  60.7 6.0 %collective-permute-start.18 = (bf16[1,200,128]{2,1,0:T(8,128)(2,1)S(1)}, bf16[1,200,128]{2,1,0:T(8,128)(2,1)S(1)}, u32[]{:S(2)}, u32[]{:S(2)}) collective-permute-start(bf16[1,200,128]{2,1,0:T(8,128)(2,1)S(1)} %get-tuple-element.72), channel_id=1, source_target_pairs={{0,12},{1,13},{2,14},{3,15},{4,8},{5,9},{6,10},{7,11},{8,4},{9,5},... | collective-permute-start | bytes 153608 | tf_op jit(solution)/shard_map/ppermute | solution.py:28
  68.4 4.1 %collective-permute-start.22 = (bf16[64,3072]{1,0:T(8,128)(2,1)S(1)}, bf16[64,3072]{1,0:T(8,128)(2,1)S(1)}, u32[]{:S(2)}, u32[]{:S(2)}) collective-permute-start(bf16[64,3072]{1,0:T(8,128)(2,1)S(1)} %get-tuple-element.48), channel_id=1, source_target_pairs={{0,16},{16,0},{1,17},{17,1},{2,18},{18,2},{3,19},{19,3},{4,20},{20... | collective-permute-start | bytes 1179656 | tf_op jit(solution)/shard_map/ppermute | solution.py:33
  68.5 4.0 %collective-permute-start.21 = (bf16[64,384]{1,0:T(8,128)(2,1)S(1)}, bf16[64,384]{1,0:T(8,128)(2,1)S(1)}, u32[]{:S(2)}, u32[]{:S(2)}) collective-permute-start(bf16[64,384]{1,0:T(8,128)(2,1)S(1)} %get-tuple-element.47.refs_1_), channel_id=1, source_target_pairs={{0,16},{16,0},{1,17},{17,1},{2,18},{18,2},{3,19},{19,3},{4,20},{20... | collective-permute-start | bytes 147464 | tf_op jit(solution)/shard_map/ppermute | solution.py:33
  69.0 6.6 %collective-permute-start.23 = (f32[4,384]{1,0:T(4,128)S(1)}, f32[4,384]{1,0:T(4,128)S(1)}, u32[]{:S(2)}, u32[]{:S(2)}) collective-permute-start(f32[4,384]{1,0:T(4,128)S(1)} %get-tuple-element.54), channel_id=1, source_target_pairs={{0,3},{1,2},{2,1},{3,0},{4,7},{5,6},{6,5},{7,4},{8,11},{9,10},{10,... | collective-permute-start | bytes 18440 | tf_op jit(solution)/shard_map/ppermute | solution.py:28
  71.1 4.6 %collective-permute-start.24 = (f32[4,384]{1,0:T(4,128)S(1)}, f32[4,384]{1,0:T(4,128)S(1)}, u32[]{:S(2)}, u32[]{:S(2)}) collective-permute-start(f32[4,384]{1,0:T(4,128)S(1)} %get-tuple-element.55), channel_id=1, source_target_pairs={{0,1},{1,0},{2,3},{3,2},{4,5},{5,4},{6,7},{7,6},{8,9},{9,8},{10,11... | collective-permute-start | bytes 18440 | tf_op jit(solution)/shard_map/ppermute | solution.py:28
  71.6 4.0 %collective-permute-start.25 = (f32[4,384]{1,0:T(4,128)S(1)}, f32[4,384]{1,0:T(4,128)S(1)}, u32[]{:S(2)}, u32[]{:S(2)}) collective-permute-start(f32[4,384]{1,0:T(4,128)S(1)} %get-tuple-element.56), channel_id=1, source_target_pairs={{0,2},{1,3},{2,0},{3,1},{4,6},{5,7},{6,4},{7,5},{8,10},{9,11},{10,... | collective-permute-start | bytes 18440 | tf_op jit(solution)/shard_map/ppermute | solution.py:28
  75.7 5.4 %collective-permute-start.26 = (f32[1,384]{1,0:T(1,128)S(1)}, f32[1,384]{1,0:T(1,128)S(1)}, u32[]{:S(2)}, u32[]{:S(2)}) collective-permute-start(f32[1,384]{1,0:T(1,128)S(1)} %get-tuple-element.75), channel_id=1, source_target_pairs={{0,12},{1,13},{2,14},{3,15},{4,8},{5,9},{6,10},{7,11},{8,4},{9,5},... | collective-permute-start | bytes 4616 | tf_op jit(solution)/shard_map/ppermute | solution.py:28
  77.1 4.0 %collective-permute-start.27 = (f32[1,384]{1,0:T(1,128)S(1)}, f32[1,384]{1,0:T(1,128)S(1)}, u32[]{:S(2)}, u32[]{:S(2)}) collective-permute-start(f32[1,384]{1,0:T(1,128)S(1)} %get-tuple-element.77), channel_id=1, source_target_pairs={{0,4},{1,5},{2,6},{3,7},{4,0},{5,1},{6,2},{7,3},{8,12},{9,13},{10,... | collective-permute-start | bytes 4616 | tf_op jit(solution)/shard_map/ppermute | solution.py:28
  77.2 4.5 %collective-permute-start.28 = (f32[1,384]{1,0:T(1,128)S(1)}, f32[1,384]{1,0:T(1,128)S(1)}, u32[]{:S(2)}, u32[]{:S(2)}) collective-permute-start(f32[1,384]{1,0:T(1,128)S(1)} %get-tuple-element.76), channel_id=1, source_target_pairs={{0,8},{1,9},{2,10},{3,11},{4,12},{5,13},{6,14},{7,15},{8,0},{9,1},... | collective-permute-start | bytes 4616 | tf_op jit(solution)/shard_map/ppermute | solution.py:28
  80.1 1.6 %collective-permute-start.12 = (bf16[64,384]{1,0:T(8,128)(2,1)S(1)}, bf16[64,384]{1,0:T(8,128)(2,1)S(1)}, u32[]{:S(2)}, u32[]{:S(2)}) collective-permute-start(bf16[64,384]{1,0:T(8,128)(2,1)S(1)} %get-tuple-element.37), channel_id=1, source_target_pairs={{0,16},{16,0},{1,17},{17,1},{2,18},{18,2},{3,19},{19,3},{4,20},{20... | collective-permute-start | bytes 147464 | tf_op jit(solution)/shard_map/ppermute | solution.py:33
  81.7 1.2 %collective-permute-start.29 = (f32[1,384]{1,0:T(1,128)S(1)}, f32[1,384]{1,0:T(1,128)S(1)}, u32[]{:S(2)}, u32[]{:S(2)}) collective-permute-start(f32[1,384]{1,0:T(1,128)S(1)} %get-tuple-element.59), channel_id=1, source_target_pairs={{0,16},{16,0},{1,17},{17,1},{2,18},{18,2},{3,19},{19,3},{4,20},{20... | collective-permute-start | bytes 4616 | tf_op jit(solution)/shard_map/ppermute | solution.py:33

commit v9 on v8

--- a/solution.py
+++ b/solution.py
@@ -357,7 +357,7 @@
 def weight_grad_call(scalars, first_at, dz_own, dz_other, u_own, u_other, after, kept):
     tokens, rows = dz_own.shape
     columns = u_own.shape[1]
-    tiles = 4
+    tiles = 6
     return pl.pallas_call(
         functools.partial(weight_grad_kernel, first_at, tiles, len(kept)),
         out_shape=[
@@ -471,8 +471,9 @@
     bit_count = seq_size.bit_length() - 1
     groups = bit_groups(merged, bit_count)
     back_groups = [group[::-1] for group in groups[::-1]]
+    first_groups = groups if sections > 2 else [groups[0][::-1]] + groups[1:]
     later_groups = groups if sections > 2 else [groups[0][::-1]] + groups[1:]
-    offsets = [o >> merged for o in offsets_of(groups)]
+    offsets = [o >> merged for o in offsets_of(first_groups)]
     later_offsets = [o >> merged for o in offsets_of(later_groups)]
     send_order = [o >> merged for o in offsets_of(back_groups[::-1])]
     me = (seq_index >> merged).astype(jnp.int32)
@@ -509,7 +510,7 @@
         )
 
     def gathered(value, step):
-        return gather_xor(joined_halves(value, 1), groups if step == 0 else later_groups)
+        return gather_xor(joined_halves(value, 1), first_groups if step == 0 else later_groups)
 
     def moved(value, step, later):
         low = min(step, sections - 1 - step)
@@ -640,6 +641,7 @@
     *early, token = weight_grad_call(
         scalars_at(0), 1, dz_b, swapped(dz_b), needed_b, other_b, jnp.zeros((8, LANES), F32), ()
     )
+    token, down_out, up_out = lax.optimization_barrier((token, down_out, up_out))
     _, pieces, _, stat, z, _ = first_record
     first_size = len(back_groups[0]) + 1
     result = last_call(

time: 83.6 us -> 83.3 us (level)
    ppermute x24, waiting for transfers between devices: 24.9 us -> 23.3 us  [from_xor(): return lax.ppermute(value, 'seq', [(i, i ^ distance) for i in range(size)])]
    ppermute x6, waiting for transfers between devices: 0.49 us -> 1.75 us  [swapped(): lax.ppermute(value, 'section', [(i, size - 1 - i) for i in range(size)])]
  transfers between devices with their start and end apart: 30 -> 30, of which waited for: 18 -> 20; matrix products, arithmetic and copies ran while one was open for 2% -> 2% of each run, Pallas kernels for 12% -> 12%
where the time goes in v9:
time: 83.3 us; the launch traced here: 83.1 us
  starting transfers between devices  34.6 us (42%)
  waiting for transfers between devices  25.1 us (30%)
  Pallas kernels  19.8 us (24%)
  other arithmetic  1.68 us (2%)
  local copies, waits for them, and re-layouts  1.06 us (1%)
  between operations  0.9 us (1%)
    ppermute x24, starting transfers between devices, from_xor(): return lax.ppermute(value, 'seq', [(i, i ^ distance) for i in range(size)])  33.3 us
    ppermute x24, waiting for transfers between devices, from_xor(): return lax.ppermute(value, 'seq', [(i, i ^ distance) for i in range(size)])  23.3 us
    pallas_call x2, Pallas kernels, section_call(): pl.pallas_call(functools.partial(section_kernel, offsets, (tokens, wide,...  6.91 us
    pallas_call x2, Pallas kernels, weight_grad_call(): pl.pallas_call(functools.partial(weight_grad_kernel, first_at, tiles, len...  6.11 us
    pallas_call x1, Pallas kernels, load_call(): pl.pallas_call(load_kernel, out_shape=jax.ShapeDtypeStruct(weights.shape,...  3.79 us
    ppermute x6, waiting for transfers between devices, swapped(): lax.ppermute(value, 'section', [(i, size - 1 - i) for i in range(size)])  1.75 us
  transfers between devices with their start and end apart: 30, of which 20 were waited for; matrix products, arithmetic and copies ran while one was open for 2% of the time, Pallas kernels for 12%

profile of v9, /device:TPU:0, one launch (start us, length us, event | category | flops | bytes accessed | tf_op | source)
XLA Modules:
  0.0 83.1 jit_solution(14499211298519345653)
XLA Ops:
  0.7 1.4 %shard_map.101 = (bf16[64,384]{1,0:T(8,128)(2,1)S(1)}, bf16[64,384]{1,0:T(8,128)(2,1)S(1)}, bf16[72,384]{1,0:T(8,128)(2,1)S(1)}) custom-call(s32[2]{0:T(128)S(1)} %pad_add_fusion.scalars.refs_0_, bf16[64,384]{1,0:T(8,128)(2,1)} %refs_0_.1, bf16[64,384]{1,0:T(8,128)(2,1)} %refs_1_.1, bf16[64,384]{1,0:T(8,128)(2,1)} %refs_2_.1, bf16[64,384]{1,0:T(8,128)(2,1)} %refs_3_.1, ...), custom_call_target="tpu_custom_call" | custom-call | tf_op jit(solution)/shard_map/pallas_call | solution.py:437
  2.1 5.1 %collective-permute-start = (bf16[1,72,384]{2,1,0:T(8,128)(2,1)S(1)}, bf16[1,72,384]{2,1,0:T(8,128)(2,1)S(1)}, u32[]{:S(2)}, u32[]{:S(2)}) collective-permute-start(bf16[1,72,384]{2,1,0:T(8,128)(2,1)S(1)} %bitcast.23), channel_id=1, source_target_pairs={{0,12},{1,13},{2,14},{3,15},{4,8},{5,9},{6,10},{7,11},{8,4},{9,5},... | collective-permute-start | bytes 165896 | tf_op jit(solution)/shard_map/ppermute | solution.py:28
  8.7 1.2 %collective-permute-done = bf16[1,72,384]{2,1,0:T(8,128)(2,1)S(1)} collective-permute-done((bf16[1,72,384]{2,1,0:T(8,128)(2,1)S(1)}, bf16[1,72,384]{2,1,0:T(8,128)(2,1)S(1)}, u32[]{:S(2)}, u32[]{:S(2)}) %collective-permute-start) | collective-permute-done | bytes 55328 | tf_op jit(solution)/shard_map/ppermute | solution.py:28
  9.8 1.7 %collective-permute-done.1 = bf16[1,72,384]{2,1,0:T(8,128)(2,1)S(1)} collective-permute-done((bf16[1,72,384]{2,1,0:T(8,128)(2,1)S(1)}, bf16[1,72,384]{2,1,0:T(8,128)(2,1)S(1)}, u32[]{:S(2)}, u32[]{:S(2)}) %collective-permute-start.1) | collective-permute-done | bytes 55328 | tf_op jit(solution)/shard_map/ppermute | solution.py:28
  11.5 1.2 %collective-permute-done.2 = bf16[1,72,384]{2,1,0:T(8,128)(2,1)S(1)} collective-permute-done((bf16[1,72,384]{2,1,0:T(8,128)(2,1)S(1)}, bf16[1,72,384]{2,1,0:T(8,128)(2,1)S(1)}, u32[]{:S(2)}, u32[]{:S(2)}) %collective-permute-start.2) | collective-permute-done | bytes 55328 | tf_op jit(solution)/shard_map/ppermute | solution.py:28
  12.7 1.6 %collective-permute-start.3 = (bf16[4,72,384]{2,1,0:T(8,128)(2,1)S(1)}, bf16[4,72,384]{2,1,0:T(8,128)(2,1)S(1)}, u32[]{:S(2)}, u32[]{:S(2)}) collective-permute-start(bf16[4,72,384]{2,1,0:T(8,128)(2,1)S(1)} %pad_maximum_fusion._), channel_id=1, source_target_pairs={{0,2},{1,3},{2,0},{3,1},{4,6},{5,7},{6,4},{7,5},{8,10},{9,11},{10,... | collective-permute-start | bytes 663560 | tf_op jit(solution)/shard_map/ppermute | solution.py:28
  14.3 1.5 %collective-permute-start.4 = (bf16[4,72,384]{2,1,0:T(8,128)(2,1)S(1)}, bf16[4,72,384]{2,1,0:T(8,128)(2,1)S(1)}, u32[]{:S(2)}, u32[]{:S(2)}) collective-permute-start(bf16[4,72,384]{2,1,0:T(8,128)(2,1)S(1)} %pad_maximum_fusion._), channel_id=1, source_target_pairs={{0,1},{1,0},{2,3},{3,2},{4,5},{5,4},{6,7},{7,6},{8,9},{9,8},{10,11... | collective-permute-start | bytes 663560 | tf_op jit(solution)/shard_map/ppermute | solution.py:28
  16.3 3.8 %shard_map.102.refs_1_ = bf16[1,2,384,6144]{3,2,1,0:T(8,128)(2,1)S(1)} custom-call(bf16[1,2,384,6144]{3,2,1,0:T(8,128)(2,1)} %weights.1, bf16[4,72,384]{2,1,0:T(8,128)(2,1)S(1)} %pad_maximum_fusion._), custom_call_target="tpu_custom_call" | custom-call | bytes 9437184 | tf_op jit(solution)/shard_map/pallas_call | solution.py:390
  21.8 2.3 %collective-permute-done.5 = bf16[4,72,384]{2,1,0:T(8,128)(2,1)S(1)} collective-permute-done((bf16[4,72,384]{2,1,0:T(8,128)(2,1)S(1)}, bf16[4,72,384]{2,1,0:T(8,128)(2,1)S(1)}, u32[]{:S(2)}, u32[]{:S(2)}) %collective-permute-start.5) | collective-permute-done | bytes 221216 | tf_op jit(solution)/shard_map/ppermute | solution.py:28
  24.1 2.6 %shard_map.103 = (bf16[64,6144]{1,0:T(8,128)(2,1)S(1)}, f32[64,128]{1,0:T(8,128)S(1)}, f32[64,384]{1,0:T(8,128)S(1)}, bf16[64,384]{1,0:T(8,128)(2,1)S(1)}, f32[2,6144]{1,0:T(2,128)S(1)}) custom-call(s32[2]{0:T(128)S(1)} %pad_add_fusion.scalars.refs_0_, bf16[1,2,384,6144]{3,2,1,0:T(8,128)(2,1)S(1)} %shard_map.102.refs_1_, ...), custom_call_target="tpu_custom_call" | custom-call | flops 301989888 | bytes 4718592 | tf_op jit(solution)/shard_map/pallas_call | solution.py:230
  26.7 2.2 %collective-permute-start.6 = (bf16[1,64,384]{2,1,0:T(8,128)(2,1)S(1)}, bf16[1,64,384]{2,1,0:T(8,128)(2,1)S(1)}, u32[]{:S(2)}, u32[]{:S(2)}) collective-permute-start(bf16[1,64,384]{2,1,0:T(8,128)(2,1)S(1)} %bitcast.19), channel_id=1, source_target_pairs={{0,12},{1,13},{2,14},{3,15},{4,8},{5,9},{6,10},{7,11},{8,4},{9,5},... | collective-permute-start | bytes 147464 | tf_op jit(solution)/shard_map/ppermute | solution.py:28
  29.4 1.7 %collective-permute-start.8 = (bf16[1,64,384]{2,1,0:T(8,128)(2,1)S(1)}, bf16[1,64,384]{2,1,0:T(8,128)(2,1)S(1)}, u32[]{:S(2)}, u32[]{:S(2)}) collective-permute-start(bf16[1,64,384]{2,1,0:T(8,128)(2,1)S(1)} %bitcast.21), channel_id=1, source_target_pairs={{0,8},{1,9},{2,10},{3,11},{4,12},{5,13},{6,14},{7,15},{8,0},{9,1},... | collective-permute-start | bytes 147464 | tf_op jit(solution)/shard_map/ppermute | solution.py:28
  31.2 1.4 %collective-permute-done.6 = bf16[1,64,384]{2,1,0:T(8,128)(2,1)S(1)} collective-permute-done((bf16[1,64,384]{2,1,0:T(8,128)(2,1)S(1)}, bf16[1,64,384]{2,1,0:T(8,128)(2,1)S(1)}, u32[]{:S(2)}, u32[]{:S(2)}) %collective-permute-start.6) | collective-permute-done | bytes 49184 | tf_op jit(solution)/shard_map/ppermute | solution.py:28
  33.2 1.3 %collective-permute-done.8 = bf16[1,64,384]{2,1,0:T(8,128)(2,1)S(1)} collective-permute-done((bf16[1,64,384]{2,1,0:T(8,128)(2,1)S(1)}, bf16[1,64,384]{2,1,0:T(8,128)(2,1)S(1)}, u32[]{:S(2)}, u32[]{:S(2)}) %collective-permute-start.8) | collective-permute-done | bytes 49184 | tf_op jit(solution)/shard_map/ppermute | solution.py:28
  34.5 1.6 %collective-permute-start.9 = (bf16[4,64,384]{2,1,0:T(8,128)(2,1)S(1)}, bf16[4,64,384]{2,1,0:T(8,128)(2,1)S(1)}, u32[]{:S(2)}, u32[]{:S(2)}) collective-permute-start(bf16[4,64,384]{2,1,0:T(8,128)(2,1)S(1)} %pad_maximum_fusion.1), channel_id=1, source_target_pairs={{0,2},{1,3},{2,0},{3,1},{4,6},{5,7},{6,4},{7,5},{8,10},{9,11},{10,... | collective-permute-start | bytes 589832 | tf_op jit(solution)/shard_map/ppermute | solution.py:28
  36.1 1.5 %collective-permute-start.10 = (bf16[4,64,384]{2,1,0:T(8,128)(2,1)S(1)}, bf16[4,64,384]{2,1,0:T(8,128)(2,1)S(1)}, u32[]{:S(2)}, u32[]{:S(2)}) collective-permute-start(bf16[4,64,384]{2,1,0:T(8,128)(2,1)S(1)} %pad_maximum_fusion.1), channel_id=1, source_target_pairs={{0,1},{1,0},{2,3},{3,2},{4,5},{5,4},{6,7},{7,6},{8,9},{9,8},{10,11... | collective-permute-start | bytes 589832 | tf_op jit(solution)/shard_map/ppermute | solution.py:28
  38.1 2.2 %collective-permute-done.9 = bf16[4,64,384]{2,1,0:T(8,128)(2,1)S(1)} collective-permute-done((bf16[4,64,384]{2,1,0:T(8,128)(2,1)S(1)}, bf16[4,64,384]{2,1,0:T(8,128)(2,1)S(1)}, u32[]{:S(2)}, u32[]{:S(2)}) %collective-permute-start.9) | collective-permute-done | bytes 196640 | tf_op jit(solution)/shard_map/ppermute | solution.py:28
  40.2 1.5 %collective-permute-done.10 = bf16[4,64,384]{2,1,0:T(8,128)(2,1)S(1)} collective-permute-done((bf16[4,64,384]{2,1,0:T(8,128)(2,1)S(1)}, bf16[4,64,384]{2,1,0:T(8,128)(2,1)S(1)}, u32[]{:S(2)}, u32[]{:S(2)}) %collective-permute-start.10) | collective-permute-done | bytes 196640 | tf_op jit(solution)/shard_map/ppermute | solution.py:28
  41.8 2.4 %collective-permute-done.11 = bf16[4,64,384]{2,1,0:T(8,128)(2,1)S(1)} collective-permute-done((bf16[4,64,384]{2,1,0:T(8,128)(2,1)S(1)}, bf16[4,64,384]{2,1,0:T(8,128)(2,1)S(1)}, u32[]{:S(2)}, u32[]{:S(2)}) %collective-permute-start.11) | collective-permute-done | bytes 196640 | tf_op jit(solution)/shard_map/ppermute | solution.py:28
  44.2 4.4 %shard_map.104 = (bf16[64,6144]{1,0:T(8,128)(2,1)S(1)}, f32[64,128]{1,0:T(8,128)S(1)}, f32[64,384]{1,0:T(8,128)}, bf16[64,384]{1,0:T(8,128)(2,1)S(1)}, bf16[64,3...) custom-call(s32[2]{0:T(128)S(1)} %pad_add_fusion.1.refs_0_, bf16[1,2,384,6144]{3,2,1,0:T(8,128)(2,1)S(1)} %shard_map.102.refs_1_, ...), custom_call_target="tpu_custom_call" | custom-call | flops 603979776 | bytes 4718592 | tf_op jit(solution)/shard_map/pallas_call | solution.py:230
  48.6 2.2 %collective-permute-start.15 = (bf16[4,200,128]{2,1,0:T(8,128)(2,1)S(1)}, bf16[4,200,128]{2,1,0:T(8,128)(2,1)S(1)}, u32[]{:S(2)}, u32[]{:S(2)}) collective-permute-start(bf16[4,200,128]{2,1,0:T(8,128)(2,1)S(1)} %get-tuple-element.69), channel_id=1, source_target_pairs={{0,3},{1,2},{2,1},{3,0},{4,7},{5,6},{6,5},{7,4},{8,11},{9,10},{10,... | collective-permute-start | bytes 614408 | tf_op jit(solution)/shard_map/ppermute | solution.py:28
  54.2 1.2 %collective-permute-done.15 = bf16[4,200,128]{2,1,0:T(8,128)(2,1)S(1)} collective-permute-done((bf16[4,200,128]{2,1,0:T(8,128)(2,1)S(1)}, bf16[4,200,128]{2,1,0:T(8,128)(2,1)S(1)}, u32[]{:S(2)}, u32[]{:S(2)}) %collective-permute-start.15) | collective-permute-done | bytes 204832 | tf_op jit(solution)/shard_map/ppermute | solution.py:28
  55.4 1.8 %collective-permute-done.16 = bf16[4,200,128]{2,1,0:T(8,128)(2,1)S(1)} collective-permute-done((bf16[4,200,128]{2,1,0:T(8,128)(2,1)S(1)}, bf16[4,200,128]{2,1,0:T(8,128)(2,1)S(1)}, u32[]{:S(2)}, u32[]{:S(2)}) %collective-permute-start.16) | collective-permute-done | bytes 204832 | tf_op jit(solution)/shard_map/ppermute | solution.py:28
  57.6 1.5 %collective-permute-start.19 = (bf16[1,200,128]{2,1,0:T(8,128)(2,1)S(1)}, bf16[1,200,128]{2,1,0:T(8,128)(2,1)S(1)}, u32[]{:S(2)}, u32[]{:S(2)}) collective-permute-start(bf16[1,200,128]{2,1,0:T(8,128)(2,1)S(1)} %get-tuple-element.77), channel_id=1, source_target_pairs={{0,4},{1,5},{2,6},{3,7},{4,0},{5,1},{6,2},{7,3},{8,12},{9,13},{10,... | collective-permute-start | bytes 153608 | tf_op jit(solution)/shard_map/ppermute | solution.py:28
  60.3 1.8 %collective-permute-start.18 = (bf16[1,200,128]{2,1,0:T(8,128)(2,1)S(1)}, bf16[1,200,128]{2,1,0:T(8,128)(2,1)S(1)}, u32[]{:S(2)}, u32[]{:S(2)}) collective-permute-start(bf16[1,200,128]{2,1,0:T(8,128)(2,1)S(1)} %get-tuple-element.78), channel_id=1, source_target_pairs={{0,12},{1,13},{2,14},{3,15},{4,8},{5,9},{6,10},{7,11},{8,4},{9,5},... | collective-permute-start | bytes 153608 | tf_op jit(solution)/shard_map/ppermute | solution.py:28
  62.1 3.1 %shard_map.105 = (f32[384,3072]{1,0:T(8,128)}, f32[384,3072]{1,0:T(8,128)}, f32[8,128]{1,0:T(8,128)S(1)}) custom-call(s32[2]{0:T(128)S(1)} %pad_add_fusion.scalars.refs_0_, bf16[64,384]{1,0:T(8,128)(2,1)S(1)} %get-tuple-element.40.refs_1_, bf16[64,384]{1,0:T(8,128)(2,1)S(1)} %collective-permute-done.12.refs_2_, ...), custom_call_target="tpu_custom_call" | custom-call | flops 301989888 | bytes 4718592 | tf_op jit(solution)/shard_map/pallas_call | solution.py:361
  66.2 1.6 %shard_map.106 = (bf16[64,384]{1,0:T(8,128)(2,1)S(1)}, f32[4,384]{1,0:T(4,128)S(1)}, f32[4,384]{1,0:T(4,128)S(1)}, f32[4,384]{1,0:T(4,128)S(1)}, f32[4,384]{1,0:T(4,128)S(1)}, /*index=5*/f32[1,384]{1,0:T(1,128)S(1)}) custom-call(s32[2]{0:T(128)S(1)} %pad_add_fusion.scalars.refs_0_, bf16[1,2,384,6144]{3,2,1,0:T(8,128)(2,1)S(1)} %shard_map.102.refs_1_, ...), custom_call_target="tpu_custom_call" | custom-call | flops 301989888 | bytes 4718592 | tf_op jit(solution)/shard_map/pallas_call | solution.py:309
  68.4 2.1 %collective-permute-start.23 = (f32[4,384]{1,0:T(4,128)S(1)}, f32[4,384]{1,0:T(4,128)S(1)}, u32[]{:S(2)}, u32[]{:S(2)}) collective-permute-start(f32[4,384]{1,0:T(4,128)S(1)} %get-tuple-element.60), channel_id=1, source_target_pairs={{0,3},{1,2},{2,1},{3,0},{4,7},{5,6},{6,5},{7,4},{8,11},{9,10},{10,... | collective-permute-start | bytes 18440 | tf_op jit(solution)/shard_map/ppermute | solution.py:28
  71.9 3.0 %shard_map.107 = (f32[384,3072]{1,0:T(8,128)}, f32[384,3072]{1,0:T(8,128)}, f32[4,384]{1,0:T(4,128)S(1)}) custom-call(s32[2]{0:T(128)S(1)} %pad_add_fusion.scalars.refs_0_, bf16[64,384]{1,0:T(8,128)(2,1)S(1)} %get-tuple-element.53.refs_1_, bf16[64,384]{1,0:T(8,128)(2,1)S(1)} %collective-permute-done.21.refs_2_, ...), custom_call_target="tpu_custom_call", output_to_operand_aliasing={{0}: (6, {}), {1}: (7, {})} | custom-call | flops 301989888 | bytes 4718592 | tf_op jit(solution)/shard_map/pallas_call | solution.py:361
  75.0 1.9 %collective-permute-start.26 = (f32[1,384]{1,0:T(1,128)S(1)}, f32[1,384]{1,0:T(1,128)S(1)}, u32[]{:S(2)}, u32[]{:S(2)}) collective-permute-start(f32[1,384]{1,0:T(1,128)S(1)} %get-tuple-element.81), channel_id=1, source_target_pairs={{0,12},{1,13},{2,14},{3,15},{4,8},{5,9},{6,10},{7,11},{8,4},{9,5},... | collective-permute-start | bytes 4616 | tf_op jit(solution)/shard_map/ppermute | solution.py:28
  76.9 2.5 %collective-permute-start.28 = (f32[1,384]{1,0:T(1,128)S(1)}, f32[1,384]{1,0:T(1,128)S(1)}, u32[]{:S(2)}, u32[]{:S(2)}) collective-permute-start(f32[1,384]{1,0:T(1,128)S(1)} %get-tuple-element.82), channel_id=1, source_target_pairs={{0,8},{1,9},{2,10},{3,11},{4,12},{5,13},{6,14},{7,15},{8,0},{9,1},... | collective-permute-start | bytes 4616 | tf_op jit(solution)/shard_map/ppermute | solution.py:28
  81.4 1.1 %collective-permute-done.29 = f32[1,384]{1,0:T(1,128)S(1)} collective-permute-done((f32[1,384]{1,0:T(1,128)S(1)}, f32[1,384]{1,0:T(1,128)S(1)}, u32[]{:S(2)}, u32[]{:S(2)}) %collective-permute-start.29) | collective-permute-done | bytes 1568 | tf_op jit(solution)/shard_map/ppermute | solution.py:33
  (66 shorter events, 16.0 us)
Async XLA Ops:
  2.1 7.7 %collective-permute-start = (bf16[1,72,384]{2,1,0:T(8,128)(2,1)S(1)}, bf16[1,72,384]{2,1,0:T(8,128)(2,1)S(1)}, u32[]{:S(2)}, u32[]{:S(2)}) collective-permute-start(bf16[1,72,384]{2,1,0:T(8,128)(2,1)S(1)} %bitcast.23), channel_id=1, source_target_pairs={{0,12},{1,13},{2,14},{3,15},{4,8},{5,9},{6,10},{7,11},{8,4},{9,5},... | collective-permute-start | bytes 165896 | tf_op jit(solution)/shard_map/ppermute | solution.py:28
  7.2 4.2 %collective-permute-start.1 = (bf16[1,72,384]{2,1,0:T(8,128)(2,1)S(1)}, bf16[1,72,384]{2,1,0:T(8,128)(2,1)S(1)}, u32[]{:S(2)}, u32[]{:S(2)}) collective-permute-start(bf16[1,72,384]{2,1,0:T(8,128)(2,1)S(1)} %bitcast.24), channel_id=1, source_target_pairs={{0,4},{1,5},{2,6},{3,7},{4,0},{5,1},{6,2},{7,3},{8,12},{9,13},{10,... | collective-permute-start | bytes 165896 | tf_op jit(solution)/shard_map/ppermute | solution.py:28
  7.2 5.4 %collective-permute-start.2 = (bf16[1,72,384]{2,1,0:T(8,128)(2,1)S(1)}, bf16[1,72,384]{2,1,0:T(8,128)(2,1)S(1)}, u32[]{:S(2)}, u32[]{:S(2)}) collective-permute-start(bf16[1,72,384]{2,1,0:T(8,128)(2,1)S(1)} %bitcast.25), channel_id=1, source_target_pairs={{0,8},{1,9},{2,10},{3,11},{4,12},{5,13},{6,14},{7,15},{8,0},{9,1},... | collective-permute-start | bytes 165896 | tf_op jit(solution)/shard_map/ppermute | solution.py:28
  12.7 8.4 %collective-permute-start.3 = (bf16[4,72,384]{2,1,0:T(8,128)(2,1)S(1)}, bf16[4,72,384]{2,1,0:T(8,128)(2,1)S(1)}, u32[]{:S(2)}, u32[]{:S(2)}) collective-permute-start(bf16[4,72,384]{2,1,0:T(8,128)(2,1)S(1)} %pad_maximum_fusion._), channel_id=1, source_target_pairs={{0,2},{1,3},{2,0},{3,1},{4,6},{5,7},{6,4},{7,5},{8,10},{9,11},{10,... | collective-permute-start | bytes 663560 | tf_op jit(solution)/shard_map/ppermute | solution.py:28
  14.3 7.5 %collective-permute-start.4 = (bf16[4,72,384]{2,1,0:T(8,128)(2,1)S(1)}, bf16[4,72,384]{2,1,0:T(8,128)(2,1)S(1)}, u32[]{:S(2)}, u32[]{:S(2)}) collective-permute-start(bf16[4,72,384]{2,1,0:T(8,128)(2,1)S(1)} %pad_maximum_fusion._), channel_id=1, source_target_pairs={{0,1},{1,0},{2,3},{3,2},{4,5},{5,4},{6,7},{7,6},{8,9},{9,8},{10,11... | collective-permute-start | bytes 663560 | tf_op jit(solution)/shard_map/ppermute | solution.py:28
  15.8 8.3 %collective-permute-start.5 = (bf16[4,72,384]{2,1,0:T(8,128)(2,1)S(1)}, bf16[4,72,384]{2,1,0:T(8,128)(2,1)S(1)}, u32[]{:S(2)}, u32[]{:S(2)}) collective-permute-start(bf16[4,72,384]{2,1,0:T(8,128)(2,1)S(1)} %pad_maximum_fusion._), channel_id=1, source_target_pairs={{0,3},{1,2},{2,1},{3,0},{4,7},{5,6},{6,5},{7,4},{8,11},{9,10},{10,... | collective-permute-start | bytes 663560 | tf_op jit(solution)/shard_map/ppermute | solution.py:28
  26.7 6.0 %collective-permute-start.6 = (bf16[1,64,384]{2,1,0:T(8,128)(2,1)S(1)}, bf16[1,64,384]{2,1,0:T(8,128)(2,1)S(1)}, u32[]{:S(2)}, u32[]{:S(2)}) collective-permute-start(bf16[1,64,384]{2,1,0:T(8,128)(2,1)S(1)} %bitcast.19), channel_id=1, source_target_pairs={{0,12},{1,13},{2,14},{3,15},{4,8},{5,9},{6,10},{7,11},{8,4},{9,5},... | collective-permute-start | bytes 147464 | tf_op jit(solution)/shard_map/ppermute | solution.py:28
  28.8 4.3 %collective-permute-start.7 = (bf16[1,64,384]{2,1,0:T(8,128)(2,1)S(1)}, bf16[1,64,384]{2,1,0:T(8,128)(2,1)S(1)}, u32[]{:S(2)}, u32[]{:S(2)}) collective-permute-start(bf16[1,64,384]{2,1,0:T(8,128)(2,1)S(1)} %bitcast.20), channel_id=1, source_target_pairs={{0,4},{1,5},{2,6},{3,7},{4,0},{5,1},{6,2},{7,3},{8,12},{9,13},{10,... | collective-permute-start | bytes 147464 | tf_op jit(solution)/shard_map/ppermute | solution.py:28
  29.4 5.0 %collective-permute-start.8 = (bf16[1,64,384]{2,1,0:T(8,128)(2,1)S(1)}, bf16[1,64,384]{2,1,0:T(8,128)(2,1)S(1)}, u32[]{:S(2)}, u32[]{:S(2)}) collective-permute-start(bf16[1,64,384]{2,1,0:T(8,128)(2,1)S(1)} %bitcast.21), channel_id=1, source_target_pairs={{0,8},{1,9},{2,10},{3,11},{4,12},{5,13},{6,14},{7,15},{8,0},{9,1},... | collective-permute-start | bytes 147464 | tf_op jit(solution)/shard_map/ppermute | solution.py:28
  34.5 5.8 %collective-permute-start.9 = (bf16[4,64,384]{2,1,0:T(8,128)(2,1)S(1)}, bf16[4,64,384]{2,1,0:T(8,128)(2,1)S(1)}, u32[]{:S(2)}, u32[]{:S(2)}) collective-permute-start(bf16[4,64,384]{2,1,0:T(8,128)(2,1)S(1)} %pad_maximum_fusion.1), channel_id=1, source_target_pairs={{0,2},{1,3},{2,0},{3,1},{4,6},{5,7},{6,4},{7,5},{8,10},{9,11},{10,... | collective-permute-start | bytes 589832 | tf_op jit(solution)/shard_map/ppermute | solution.py:28
  36.1 5.7 %collective-permute-start.10 = (bf16[4,64,384]{2,1,0:T(8,128)(2,1)S(1)}, bf16[4,64,384]{2,1,0:T(8,128)(2,1)S(1)}, u32[]{:S(2)}, u32[]{:S(2)}) collective-permute-start(bf16[4,64,384]{2,1,0:T(8,128)(2,1)S(1)} %pad_maximum_fusion.1), channel_id=1, source_target_pairs={{0,1},{1,0},{2,3},{3,2},{4,5},{5,4},{6,7},{7,6},{8,9},{9,8},{10,11... | collective-permute-start | bytes 589832 | tf_op jit(solution)/shard_map/ppermute | solution.py:28
  37.6 6.6 %collective-permute-start.11 = (bf16[4,64,384]{2,1,0:T(8,128)(2,1)S(1)}, bf16[4,64,384]{2,1,0:T(8,128)(2,1)S(1)}, u32[]{:S(2)}, u32[]{:S(2)}) collective-permute-start(bf16[4,64,384]{2,1,0:T(8,128)(2,1)S(1)} %pad_maximum_fusion.1), channel_id=1, source_target_pairs={{0,3},{1,2},{2,1},{3,0},{4,7},{5,6},{6,5},{7,4},{8,11},{9,10},{10,... | collective-permute-start | bytes 589832 | tf_op jit(solution)/shard_map/ppermute | solution.py:28
  48.6 6.8 %collective-permute-start.15 = (bf16[4,200,128]{2,1,0:T(8,128)(2,1)S(1)}, bf16[4,200,128]{2,1,0:T(8,128)(2,1)S(1)}, u32[]{:S(2)}, u32[]{:S(2)}) collective-permute-start(bf16[4,200,128]{2,1,0:T(8,128)(2,1)S(1)} %get-tuple-element.69), channel_id=1, source_target_pairs={{0,3},{1,2},{2,1},{3,0},{4,7},{5,6},{6,5},{7,4},{8,11},{9,10},{10,... | collective-permute-start | bytes 614408 | tf_op jit(solution)/shard_map/ppermute | solution.py:28
  50.7 6.5 %collective-permute-start.16 = (bf16[4,200,128]{2,1,0:T(8,128)(2,1)S(1)}, bf16[4,200,128]{2,1,0:T(8,128)(2,1)S(1)}, u32[]{:S(2)}, u32[]{:S(2)}) collective-permute-start(bf16[4,200,128]{2,1,0:T(8,128)(2,1)S(1)} %get-tuple-element.71), channel_id=1, source_target_pairs={{0,1},{1,0},{2,3},{3,2},{4,5},{5,4},{6,7},{7,6},{8,9},{9,8},{10,11... | collective-permute-start | bytes 614408 | tf_op jit(solution)/shard_map/ppermute | solution.py:28
  51.3 6.2 %collective-permute-start.17 = (bf16[4,200,128]{2,1,0:T(8,128)(2,1)S(1)}, bf16[4,200,128]{2,1,0:T(8,128)(2,1)S(1)}, u32[]{:S(2)}, u32[]{:S(2)}) collective-permute-start(bf16[4,200,128]{2,1,0:T(8,128)(2,1)S(1)} %get-tuple-element.70), channel_id=1, source_target_pairs={{0,2},{1,3},{2,0},{3,1},{4,6},{5,7},{6,4},{7,5},{8,10},{9,11},{10,... | collective-permute-start | bytes 614408 | tf_op jit(solution)/shard_map/ppermute | solution.py:28
  52.1 1.2 %collective-permute-start.14 = (bf16[64,384]{1,0:T(8,128)(2,1)S(1)}, bf16[64,384]{1,0:T(8,128)(2,1)S(1)}, u32[]{:S(2)}, u32[]{:S(2)}) collective-permute-start(bf16[64,384]{1,0:T(8,128)(2,1)S(1)} %get-tuple-element.43), channel_id=1, source_target_pairs={{0,16},{16,0},{1,17},{17,1},{2,18},{18,2},{3,19},{19,3},{4,20},{20... | collective-permute-start | bytes 147464 | tf_op jit(solution)/shard_map/ppermute | solution.py:33
  52.2 9.9 %collective-permute-start.13 = (bf16[64,3072]{1,0:T(8,128)(2,1)S(1)}, bf16[64,3072]{1,0:T(8,128)(2,1)S(1)}, u32[]{:S(2)}, u32[]{:S(2)}) collective-permute-start(bf16[64,3072]{1,0:T(8,128)(2,1)S(1)} %get-tuple-element.74), channel_id=1, source_target_pairs={{0,16},{16,0},{1,17},{17,1},{2,18},{18,2},{3,19},{19,3},{4,20},{20... | collective-permute-start | bytes 1179656 | tf_op jit(solution)/shard_map/ppermute | solution.py:33
  53.4 8.7 %collective-permute-start.12 = (bf16[64,384]{1,0:T(8,128)(2,1)S(1)}, bf16[64,384]{1,0:T(8,128)(2,1)S(1)}, u32[]{:S(2)}, u32[]{:S(2)}) collective-permute-start(bf16[64,384]{1,0:T(8,128)(2,1)S(1)} %get-tuple-element.40.refs_1_), channel_id=1, source_target_pairs={{0,16},{16,0},{1,17},{17,1},{2,18},{18,2},{3,19},{19,3},{4,20},{20... | collective-permute-start | bytes 147464 | tf_op jit(solution)/shard_map/ppermute | solution.py:33
  57.6 7.6 %collective-permute-start.19 = (bf16[1,200,128]{2,1,0:T(8,128)(2,1)S(1)}, bf16[1,200,128]{2,1,0:T(8,128)(2,1)S(1)}, u32[]{:S(2)}, u32[]{:S(2)}) collective-permute-start(bf16[1,200,128]{2,1,0:T(8,128)(2,1)S(1)} %get-tuple-element.77), channel_id=1, source_target_pairs={{0,4},{1,5},{2,6},{3,7},{4,0},{5,1},{6,2},{7,3},{8,12},{9,13},{10,... | collective-permute-start | bytes 153608 | tf_op jit(solution)/shard_map/ppermute | solution.py:28
  59.2 6.0 %collective-permute-start.20 = (bf16[1,200,128]{2,1,0:T(8,128)(2,1)S(1)}, bf16[1,200,128]{2,1,0:T(8,128)(2,1)S(1)}, u32[]{:S(2)}, u32[]{:S(2)}) collective-permute-start(bf16[1,200,128]{2,1,0:T(8,128)(2,1)S(1)} %get-tuple-element.76), channel_id=1, source_target_pairs={{0,8},{1,9},{2,10},{3,11},{4,12},{5,13},{6,14},{7,15},{8,0},{9,1},... | collective-permute-start | bytes 153608 | tf_op jit(solution)/shard_map/ppermute | solution.py:28
  60.3 5.9 %collective-permute-start.18 = (bf16[1,200,128]{2,1,0:T(8,128)(2,1)S(1)}, bf16[1,200,128]{2,1,0:T(8,128)(2,1)S(1)}, u32[]{:S(2)}, u32[]{:S(2)}) collective-permute-start(bf16[1,200,128]{2,1,0:T(8,128)(2,1)S(1)} %get-tuple-element.78), channel_id=1, source_target_pairs={{0,12},{1,13},{2,14},{3,15},{4,8},{5,9},{6,10},{7,11},{8,4},{9,5},... | collective-permute-start | bytes 153608 | tf_op jit(solution)/shard_map/ppermute | solution.py:28
  67.8 4.1 %collective-permute-start.22 = (bf16[64,3072]{1,0:T(8,128)(2,1)S(1)}, bf16[64,3072]{1,0:T(8,128)(2,1)S(1)}, u32[]{:S(2)}, u32[]{:S(2)}) collective-permute-start(bf16[64,3072]{1,0:T(8,128)(2,1)S(1)} %get-tuple-element.54), channel_id=1, source_target_pairs={{0,16},{16,0},{1,17},{17,1},{2,18},{18,2},{3,19},{19,3},{4,20},{20... | collective-permute-start | bytes 1179656 | tf_op jit(solution)/shard_map/ppermute | solution.py:33
  67.9 4.0 %collective-permute-start.21 = (bf16[64,384]{1,0:T(8,128)(2,1)S(1)}, bf16[64,384]{1,0:T(8,128)(2,1)S(1)}, u32[]{:S(2)}, u32[]{:S(2)}) collective-permute-start(bf16[64,384]{1,0:T(8,128)(2,1)S(1)} %get-tuple-element.53.refs_1_), channel_id=1, source_target_pairs={{0,16},{16,0},{1,17},{17,1},{2,18},{18,2},{3,19},{19,3},{4,20},{20... | collective-permute-start | bytes 147464 | tf_op jit(solution)/shard_map/ppermute | solution.py:33
  68.4 6.6 %collective-permute-start.23 = (f32[4,384]{1,0:T(4,128)S(1)}, f32[4,384]{1,0:T(4,128)S(1)}, u32[]{:S(2)}, u32[]{:S(2)}) collective-permute-start(f32[4,384]{1,0:T(4,128)S(1)} %get-tuple-element.60), channel_id=1, source_target_pairs={{0,3},{1,2},{2,1},{3,0},{4,7},{5,6},{6,5},{7,4},{8,11},{9,10},{10,... | collective-permute-start | bytes 18440 | tf_op jit(solution)/shard_map/ppermute | solution.py:28
  70.5 4.5 %collective-permute-start.24 = (f32[4,384]{1,0:T(4,128)S(1)}, f32[4,384]{1,0:T(4,128)S(1)}, u32[]{:S(2)}, u32[]{:S(2)}) collective-permute-start(f32[4,384]{1,0:T(4,128)S(1)} %get-tuple-element.61), channel_id=1, source_target_pairs={{0,1},{1,0},{2,3},{3,2},{4,5},{5,4},{6,7},{7,6},{8,9},{9,8},{10,11... | collective-permute-start | bytes 18440 | tf_op jit(solution)/shard_map/ppermute | solution.py:28
  71.0 4.0 %collective-permute-start.25 = (f32[4,384]{1,0:T(4,128)S(1)}, f32[4,384]{1,0:T(4,128)S(1)}, u32[]{:S(2)}, u32[]{:S(2)}) collective-permute-start(f32[4,384]{1,0:T(4,128)S(1)} %get-tuple-element.62), channel_id=1, source_target_pairs={{0,2},{1,3},{2,0},{3,1},{4,6},{5,7},{6,4},{7,5},{8,10},{9,11},{10,... | collective-permute-start | bytes 18440 | tf_op jit(solution)/shard_map/ppermute | solution.py:28
  75.0 5.4 %collective-permute-start.26 = (f32[1,384]{1,0:T(1,128)S(1)}, f32[1,384]{1,0:T(1,128)S(1)}, u32[]{:S(2)}, u32[]{:S(2)}) collective-permute-start(f32[1,384]{1,0:T(1,128)S(1)} %get-tuple-element.81), channel_id=1, source_target_pairs={{0,12},{1,13},{2,14},{3,15},{4,8},{5,9},{6,10},{7,11},{8,4},{9,5},... | collective-permute-start | bytes 4616 | tf_op jit(solution)/shard_map/ppermute | solution.py:28
  76.9 3.6 %collective-permute-start.27 = (f32[1,384]{1,0:T(1,128)S(1)}, f32[1,384]{1,0:T(1,128)S(1)}, u32[]{:S(2)}, u32[]{:S(2)}) collective-permute-start(f32[1,384]{1,0:T(1,128)S(1)} %get-tuple-element.83), channel_id=1, source_target_pairs={{0,4},{1,5},{2,6},{3,7},{4,0},{5,1},{6,2},{7,3},{8,12},{9,13},{10,... | collective-permute-start | bytes 4616 | tf_op jit(solution)/shard_map/ppermute | solution.py:28
  76.9 4.5 %collective-permute-start.28 = (f32[1,384]{1,0:T(1,128)S(1)}, f32[1,384]{1,0:T(1,128)S(1)}, u32[]{:S(2)}, u32[]{:S(2)}) collective-permute-start(f32[1,384]{1,0:T(1,128)S(1)} %get-tuple-element.82), channel_id=1, source_target_pairs={{0,8},{1,9},{2,10},{3,11},{4,12},{5,13},{6,14},{7,15},{8,0},{9,1},... | collective-permute-start | bytes 4616 | tf_op jit(solution)/shard_map/ppermute | solution.py:28
  81.4 1.2 %collective-permute-start.29 = (f32[1,384]{1,0:T(1,128)S(1)}, f32[1,384]{1,0:T(1,128)S(1)}, u32[]{:S(2)}, u32[]{:S(2)}) collective-permute-start(f32[1,384]{1,0:T(1,128)S(1)} %get-tuple-element.65), channel_id=1, source_target_pairs={{0,16},{16,0},{1,17},{17,1},{2,18},{18,2},{3,19},{19,3},{4,20},{20... | collective-permute-start | bytes 4616 | tf_op jit(solution)/shard_map/ppermute | solution.py:33

commit v10 on v9

--- a/solution.py
+++ b/solution.py
@@ -357,7 +357,7 @@
 def weight_grad_call(scalars, first_at, dz_own, dz_other, u_own, u_other, after, kept):
     tokens, rows = dz_own.shape
     columns = u_own.shape[1]
-    tiles = 6
+    tiles = 4
     return pl.pallas_call(
         functools.partial(weight_grad_kernel, first_at, tiles, len(kept)),
         out_shape=[

time: 83.3 us -> 83.4 us (level)
  no operation moved by 1% of the time
where the time goes in v10:
time: 83.4 us; the launch traced here: 83.2 us
  starting transfers between devices  34.6 us (41%)
  waiting for transfers between devices  25 us (30%)
  Pallas kernels  20 us (24%)
  other arithmetic  1.68 us (2%)
  local copies, waits for them, and re-layouts  1.06 us (1%)
  between operations  0.9 us (1%)
    ppermute x24, starting transfers between devices, from_xor(): return lax.ppermute(value, 'seq', [(i, i ^ distance) for i in range(size)])  33.3 us
    ppermute x24, waiting for transfers between devices, from_xor(): return lax.ppermute(value, 'seq', [(i, i ^ distance) for i in range(size)])  23.2 us
    pallas_call x2, Pallas kernels, section_call(): pl.pallas_call(functools.partial(section_kernel, offsets, (tokens, wide,...  6.91 us
    pallas_call x2, Pallas kernels, weight_grad_call(): pl.pallas_call(functools.partial(weight_grad_kernel, first_at, tiles, len...  6.29 us
    pallas_call x1, Pallas kernels, load_call(): pl.pallas_call(load_kernel, out_shape=jax.ShapeDtypeStruct(weights.shape,...  3.79 us
    ppermute x6, waiting for transfers between devices, swapped(): lax.ppermute(value, 'section', [(i, size - 1 - i) for i in range(size)])  1.75 us
  transfers between devices with their start and end apart: 30, of which 20 were waited for; matrix products, arithmetic and copies ran while one was open for 2% of the time, Pallas kernels for 12%

profile of v10, /device:TPU:0, one launch (start us, length us, event | category | flops | bytes accessed | tf_op | source)
XLA Modules:
  0.0 83.2 jit_solution(5366757558107505101)
XLA Ops:
  0.7 1.4 %shard_map.101 = (bf16[64,384]{1,0:T(8,128)(2,1)S(1)}, bf16[64,384]{1,0:T(8,128)(2,1)S(1)}, bf16[72,384]{1,0:T(8,128)(2,1)S(1)}) custom-call(s32[2]{0:T(128)S(1)} %pad_add_fusion.scalars.refs_0_, bf16[64,384]{1,0:T(8,128)(2,1)} %refs_0_.1, bf16[64,384]{1,0:T(8,128)(2,1)} %refs_1_.1, bf16[64,384]{1,0:T(8,128)(2,1)} %refs_2_.1, bf16[64,384]{1,0:T(8,128)(2,1)} %refs_3_.1, ...), custom_call_target="tpu_custom_call" | custom-call | tf_op jit(solution)/shard_map/pallas_call | solution.py:437
  2.1 5.1 %collective-permute-start = (bf16[1,72,384]{2,1,0:T(8,128)(2,1)S(1)}, bf16[1,72,384]{2,1,0:T(8,128)(2,1)S(1)}, u32[]{:S(2)}, u32[]{:S(2)}) collective-permute-start(bf16[1,72,384]{2,1,0:T(8,128)(2,1)S(1)} %bitcast.23), channel_id=1, source_target_pairs={{0,12},{1,13},{2,14},{3,15},{4,8},{5,9},{6,10},{7,11},{8,4},{9,5},... | collective-permute-start | bytes 165896 | tf_op jit(solution)/shard_map/ppermute | solution.py:28
  8.7 1.2 %collective-permute-done = bf16[1,72,384]{2,1,0:T(8,128)(2,1)S(1)} collective-permute-done((bf16[1,72,384]{2,1,0:T(8,128)(2,1)S(1)}, bf16[1,72,384]{2,1,0:T(8,128)(2,1)S(1)}, u32[]{:S(2)}, u32[]{:S(2)}) %collective-permute-start) | collective-permute-done | bytes 55328 | tf_op jit(solution)/shard_map/ppermute | solution.py:28
  9.8 1.7 %collective-permute-done.1 = bf16[1,72,384]{2,1,0:T(8,128)(2,1)S(1)} collective-permute-done((bf16[1,72,384]{2,1,0:T(8,128)(2,1)S(1)}, bf16[1,72,384]{2,1,0:T(8,128)(2,1)S(1)}, u32[]{:S(2)}, u32[]{:S(2)}) %collective-permute-start.1) | collective-permute-done | bytes 55328 | tf_op jit(solution)/shard_map/ppermute | solution.py:28
  11.5 1.2 %collective-permute-done.2 = bf16[1,72,384]{2,1,0:T(8,128)(2,1)S(1)} collective-permute-done((bf16[1,72,384]{2,1,0:T(8,128)(2,1)S(1)}, bf16[1,72,384]{2,1,0:T(8,128)(2,1)S(1)}, u32[]{:S(2)}, u32[]{:S(2)}) %collective-permute-start.2) | collective-permute-done | bytes 55328 | tf_op jit(solution)/shard_map/ppermute | solution.py:28
  12.7 1.6 %collective-permute-start.3 = (bf16[4,72,384]{2,1,0:T(8,128)(2,1)S(1)}, bf16[4,72,384]{2,1,0:T(8,128)(2,1)S(1)}, u32[]{:S(2)}, u32[]{:S(2)}) collective-permute-start(bf16[4,72,384]{2,1,0:T(8,128)(2,1)S(1)} %pad_maximum_fusion._), channel_id=1, source_target_pairs={{0,2},{1,3},{2,0},{3,1},{4,6},{5,7},{6,4},{7,5},{8,10},{9,11},{10,... | collective-permute-start | bytes 663560 | tf_op jit(solution)/shard_map/ppermute | solution.py:28
  14.3 1.5 %collective-permute-start.4 = (bf16[4,72,384]{2,1,0:T(8,128)(2,1)S(1)}, bf16[4,72,384]{2,1,0:T(8,128)(2,1)S(1)}, u32[]{:S(2)}, u32[]{:S(2)}) collective-permute-start(bf16[4,72,384]{2,1,0:T(8,128)(2,1)S(1)} %pad_maximum_fusion._), channel_id=1, source_target_pairs={{0,1},{1,0},{2,3},{3,2},{4,5},{5,4},{6,7},{7,6},{8,9},{9,8},{10,11... | collective-permute-start | bytes 663560 | tf_op jit(solution)/shard_map/ppermute | solution.py:28
  16.3 3.8 %shard_map.102.refs_1_ = bf16[1,2,384,6144]{3,2,1,0:T(8,128)(2,1)S(1)} custom-call(bf16[1,2,384,6144]{3,2,1,0:T(8,128)(2,1)} %weights.1, bf16[4,72,384]{2,1,0:T(8,128)(2,1)S(1)} %pad_maximum_fusion._), custom_call_target="tpu_custom_call" | custom-call | bytes 9437184 | tf_op jit(solution)/shard_map/pallas_call | solution.py:390
  21.8 2.3 %collective-permute-done.5 = bf16[4,72,384]{2,1,0:T(8,128)(2,1)S(1)} collective-permute-done((bf16[4,72,384]{2,1,0:T(8,128)(2,1)S(1)}, bf16[4,72,384]{2,1,0:T(8,128)(2,1)S(1)}, u32[]{:S(2)}, u32[]{:S(2)}) %collective-permute-start.5) | collective-permute-done | bytes 221216 | tf_op jit(solution)/shard_map/ppermute | solution.py:28
  24.1 2.6 %shard_map.103 = (bf16[64,6144]{1,0:T(8,128)(2,1)S(1)}, f32[64,128]{1,0:T(8,128)S(1)}, f32[64,384]{1,0:T(8,128)S(1)}, bf16[64,384]{1,0:T(8,128)(2,1)S(1)}, f32[2,6144]{1,0:T(2,128)S(1)}) custom-call(s32[2]{0:T(128)S(1)} %pad_add_fusion.scalars.refs_0_, bf16[1,2,384,6144]{3,2,1,0:T(8,128)(2,1)S(1)} %shard_map.102.refs_1_, ...), custom_call_target="tpu_custom_call" | custom-call | flops 301989888 | bytes 4718592 | tf_op jit(solution)/shard_map/pallas_call | solution.py:230
  26.7 2.2 %collective-permute-start.6 = (bf16[1,64,384]{2,1,0:T(8,128)(2,1)S(1)}, bf16[1,64,384]{2,1,0:T(8,128)(2,1)S(1)}, u32[]{:S(2)}, u32[]{:S(2)}) collective-permute-start(bf16[1,64,384]{2,1,0:T(8,128)(2,1)S(1)} %bitcast.19), channel_id=1, source_target_pairs={{0,12},{1,13},{2,14},{3,15},{4,8},{5,9},{6,10},{7,11},{8,4},{9,5},... | collective-permute-start | bytes 147464 | tf_op jit(solution)/shard_map/ppermute | solution.py:28
  29.4 1.7 %collective-permute-start.8 = (bf16[1,64,384]{2,1,0:T(8,128)(2,1)S(1)}, bf16[1,64,384]{2,1,0:T(8,128)(2,1)S(1)}, u32[]{:S(2)}, u32[]{:S(2)}) collective-permute-start(bf16[1,64,384]{2,1,0:T(8,128)(2,1)S(1)} %bitcast.21), channel_id=1, source_target_pairs={{0,8},{1,9},{2,10},{3,11},{4,12},{5,13},{6,14},{7,15},{8,0},{9,1},... | collective-permute-start | bytes 147464 | tf_op jit(solution)/shard_map/ppermute | solution.py:28
  31.2 1.4 %collective-permute-done.6 = bf16[1,64,384]{2,1,0:T(8,128)(2,1)S(1)} collective-permute-done((bf16[1,64,384]{2,1,0:T(8,128)(2,1)S(1)}, bf16[1,64,384]{2,1,0:T(8,128)(2,1)S(1)}, u32[]{:S(2)}, u32[]{:S(2)}) %collective-permute-start.6) | collective-permute-done | bytes 49184 | tf_op jit(solution)/shard_map/ppermute | solution.py:28
  33.2 1.3 %collective-permute-done.8 = bf16[1,64,384]{2,1,0:T(8,128)(2,1)S(1)} collective-permute-done((bf16[1,64,384]{2,1,0:T(8,128)(2,1)S(1)}, bf16[1,64,384]{2,1,0:T(8,128)(2,1)S(1)}, u32[]{:S(2)}, u32[]{:S(2)}) %collective-permute-start.8) | collective-permute-done | bytes 49184 | tf_op jit(solution)/shard_map/ppermute | solution.py:28
  34.5 1.6 %collective-permute-start.9 = (bf16[4,64,384]{2,1,0:T(8,128)(2,1)S(1)}, bf16[4,64,384]{2,1,0:T(8,128)(2,1)S(1)}, u32[]{:S(2)}, u32[]{:S(2)}) collective-permute-start(bf16[4,64,384]{2,1,0:T(8,128)(2,1)S(1)} %pad_maximum_fusion.1), channel_id=1, source_target_pairs={{0,2},{1,3},{2,0},{3,1},{4,6},{5,7},{6,4},{7,5},{8,10},{9,11},{10,... | collective-permute-start | bytes 589832 | tf_op jit(solution)/shard_map/ppermute | solution.py:28
  36.1 1.5 %collective-permute-start.10 = (bf16[4,64,384]{2,1,0:T(8,128)(2,1)S(1)}, bf16[4,64,384]{2,1,0:T(8,128)(2,1)S(1)}, u32[]{:S(2)}, u32[]{:S(2)}) collective-permute-start(bf16[4,64,384]{2,1,0:T(8,128)(2,1)S(1)} %pad_maximum_fusion.1), channel_id=1, source_target_pairs={{0,1},{1,0},{2,3},{3,2},{4,5},{5,4},{6,7},{7,6},{8,9},{9,8},{10,11... | collective-permute-start | bytes 589832 | tf_op jit(solution)/shard_map/ppermute | solution.py:28
  38.1 2.2 %collective-permute-done.9 = bf16[4,64,384]{2,1,0:T(8,128)(2,1)S(1)} collective-permute-done((bf16[4,64,384]{2,1,0:T(8,128)(2,1)S(1)}, bf16[4,64,384]{2,1,0:T(8,128)(2,1)S(1)}, u32[]{:S(2)}, u32[]{:S(2)}) %collective-permute-start.9) | collective-permute-done | bytes 196640 | tf_op jit(solution)/shard_map/ppermute | solution.py:28
  40.2 1.5 %collective-permute-done.10 = bf16[4,64,384]{2,1,0:T(8,128)(2,1)S(1)} collective-permute-done((bf16[4,64,384]{2,1,0:T(8,128)(2,1)S(1)}, bf16[4,64,384]{2,1,0:T(8,128)(2,1)S(1)}, u32[]{:S(2)}, u32[]{:S(2)}) %collective-permute-start.10) | collective-permute-done | bytes 196640 | tf_op jit(solution)/shard_map/ppermute | solution.py:28
  41.8 2.4 %collective-permute-done.11 = bf16[4,64,384]{2,1,0:T(8,128)(2,1)S(1)} collective-permute-done((bf16[4,64,384]{2,1,0:T(8,128)(2,1)S(1)}, bf16[4,64,384]{2,1,0:T(8,128)(2,1)S(1)}, u32[]{:S(2)}, u32[]{:S(2)}) %collective-permute-start.11) | collective-permute-done | bytes 196640 | tf_op jit(solution)/shard_map/ppermute | solution.py:28
  44.2 4.4 %shard_map.104 = (bf16[64,6144]{1,0:T(8,128)(2,1)S(1)}, f32[64,128]{1,0:T(8,128)S(1)}, f32[64,384]{1,0:T(8,128)}, bf16[64,384]{1,0:T(8,128)(2,1)S(1)}, bf16[64,3...) custom-call(s32[2]{0:T(128)S(1)} %pad_add_fusion.1.refs_0_, bf16[1,2,384,6144]{3,2,1,0:T(8,128)(2,1)S(1)} %shard_map.102.refs_1_, ...), custom_call_target="tpu_custom_call" | custom-call | flops 603979776 | bytes 4718592 | tf_op jit(solution)/shard_map/pallas_call | solution.py:230
  48.6 2.2 %collective-permute-start.15 = (bf16[4,200,128]{2,1,0:T(8,128)(2,1)S(1)}, bf16[4,200,128]{2,1,0:T(8,128)(2,1)S(1)}, u32[]{:S(2)}, u32[]{:S(2)}) collective-permute-start(bf16[4,200,128]{2,1,0:T(8,128)(2,1)S(1)} %get-tuple-element.69), channel_id=1, source_target_pairs={{0,3},{1,2},{2,1},{3,0},{4,7},{5,6},{6,5},{7,4},{8,11},{9,10},{10,... | collective-permute-start | bytes 614408 | tf_op jit(solution)/shard_map/ppermute | solution.py:28
  54.2 1.2 %collective-permute-done.15 = bf16[4,200,128]{2,1,0:T(8,128)(2,1)S(1)} collective-permute-done((bf16[4,200,128]{2,1,0:T(8,128)(2,1)S(1)}, bf16[4,200,128]{2,1,0:T(8,128)(2,1)S(1)}, u32[]{:S(2)}, u32[]{:S(2)}) %collective-permute-start.15) | collective-permute-done | bytes 204832 | tf_op jit(solution)/shard_map/ppermute | solution.py:28
  55.4 1.8 %collective-permute-done.16 = bf16[4,200,128]{2,1,0:T(8,128)(2,1)S(1)} collective-permute-done((bf16[4,200,128]{2,1,0:T(8,128)(2,1)S(1)}, bf16[4,200,128]{2,1,0:T(8,128)(2,1)S(1)}, u32[]{:S(2)}, u32[]{:S(2)}) %collective-permute-start.16) | collective-permute-done | bytes 204832 | tf_op jit(solution)/shard_map/ppermute | solution.py:28
  57.6 1.5 %collective-permute-start.19 = (bf16[1,200,128]{2,1,0:T(8,128)(2,1)S(1)}, bf16[1,200,128]{2,1,0:T(8,128)(2,1)S(1)}, u32[]{:S(2)}, u32[]{:S(2)}) collective-permute-start(bf16[1,200,128]{2,1,0:T(8,128)(2,1)S(1)} %get-tuple-element.77), channel_id=1, source_target_pairs={{0,4},{1,5},{2,6},{3,7},{4,0},{5,1},{6,2},{7,3},{8,12},{9,13},{10,... | collective-permute-start | bytes 153608 | tf_op jit(solution)/shard_map/ppermute | solution.py:28
  60.3 1.8 %collective-permute-start.18 = (bf16[1,200,128]{2,1,0:T(8,128)(2,1)S(1)}, bf16[1,200,128]{2,1,0:T(8,128)(2,1)S(1)}, u32[]{:S(2)}, u32[]{:S(2)}) collective-permute-start(bf16[1,200,128]{2,1,0:T(8,128)(2,1)S(1)} %get-tuple-element.78), channel_id=1, source_target_pairs={{0,12},{1,13},{2,14},{3,15},{4,8},{5,9},{6,10},{7,11},{8,4},{9,5},... | collective-permute-start | bytes 153608 | tf_op jit(solution)/shard_map/ppermute | solution.py:28
  62.1 3.1 %shard_map.105 = (f32[384,3072]{1,0:T(8,128)}, f32[384,3072]{1,0:T(8,128)}, f32[8,128]{1,0:T(8,128)S(1)}) custom-call(s32[2]{0:T(128)S(1)} %pad_add_fusion.scalars.refs_0_, bf16[64,384]{1,0:T(8,128)(2,1)S(1)} %get-tuple-element.40.refs_1_, bf16[64,384]{1,0:T(8,128)(2,1)S(1)} %collective-permute-done.12.refs_2_, ...), custom_call_target="tpu_custom_call" | custom-call | flops 301989888 | bytes 4718592 | tf_op jit(solution)/shard_map/pallas_call | solution.py:361
  66.2 1.6 %shard_map.106 = (bf16[64,384]{1,0:T(8,128)(2,1)S(1)}, f32[4,384]{1,0:T(4,128)S(1)}, f32[4,384]{1,0:T(4,128)S(1)}, f32[4,384]{1,0:T(4,128)S(1)}, f32[4,384]{1,0:T(4,128)S(1)}, /*index=5*/f32[1,384]{1,0:T(1,128)S(1)}) custom-call(s32[2]{0:T(128)S(1)} %pad_add_fusion.scalars.refs_0_, bf16[1,2,384,6144]{3,2,1,0:T(8,128)(2,1)S(1)} %shard_map.102.refs_1_, ...), custom_call_target="tpu_custom_call" | custom-call | flops 301989888 | bytes 4718592 | tf_op jit(solution)/shard_map/pallas_call | solution.py:309
  68.4 2.1 %collective-permute-start.23 = (f32[4,384]{1,0:T(4,128)S(1)}, f32[4,384]{1,0:T(4,128)S(1)}, u32[]{:S(2)}, u32[]{:S(2)}) collective-permute-start(f32[4,384]{1,0:T(4,128)S(1)} %get-tuple-element.60), channel_id=1, source_target_pairs={{0,3},{1,2},{2,1},{3,0},{4,7},{5,6},{6,5},{7,4},{8,11},{9,10},{10,... | collective-permute-start | bytes 18440 | tf_op jit(solution)/shard_map/ppermute | solution.py:28
  71.9 3.1 %shard_map.107 = (f32[384,3072]{1,0:T(8,128)}, f32[384,3072]{1,0:T(8,128)}, f32[4,384]{1,0:T(4,128)S(1)}) custom-call(s32[2]{0:T(128)S(1)} %pad_add_fusion.scalars.refs_0_, bf16[64,384]{1,0:T(8,128)(2,1)S(1)} %get-tuple-element.53.refs_1_, bf16[64,384]{1,0:T(8,128)(2,1)S(1)} %collective-permute-done.21.refs_2_, ...), custom_call_target="tpu_custom_call", output_to_operand_aliasing={{0}: (6, {}), {1}: (7, {})} | custom-call | flops 301989888 | bytes 4718592 | tf_op jit(solution)/shard_map/pallas_call | solution.py:361
  75.1 1.9 %collective-permute-start.26 = (f32[1,384]{1,0:T(1,128)S(1)}, f32[1,384]{1,0:T(1,128)S(1)}, u32[]{:S(2)}, u32[]{:S(2)}) collective-permute-start(f32[1,384]{1,0:T(1,128)S(1)} %get-tuple-element.81), channel_id=1, source_target_pairs={{0,12},{1,13},{2,14},{3,15},{4,8},{5,9},{6,10},{7,11},{8,4},{9,5},... | collective-permute-start | bytes 4616 | tf_op jit(solution)/shard_map/ppermute | solution.py:28
  77.0 2.5 %collective-permute-start.28 = (f32[1,384]{1,0:T(1,128)S(1)}, f32[1,384]{1,0:T(1,128)S(1)}, u32[]{:S(2)}, u32[]{:S(2)}) collective-permute-start(f32[1,384]{1,0:T(1,128)S(1)} %get-tuple-element.82), channel_id=1, source_target_pairs={{0,8},{1,9},{2,10},{3,11},{4,12},{5,13},{6,14},{7,15},{8,0},{9,1},... | collective-permute-start | bytes 4616 | tf_op jit(solution)/shard_map/ppermute | solution.py:28
  81.5 1.1 %collective-permute-done.29 = f32[1,384]{1,0:T(1,128)S(1)} collective-permute-done((f32[1,384]{1,0:T(1,128)S(1)}, f32[1,384]{1,0:T(1,128)S(1)}, u32[]{:S(2)}, u32[]{:S(2)}) %collective-permute-start.29) | collective-permute-done | bytes 1568 | tf_op jit(solution)/shard_map/ppermute | solution.py:33
  (66 shorter events, 15.9 us)
Async XLA Ops:
  2.1 7.7 %collective-permute-start = (bf16[1,72,384]{2,1,0:T(8,128)(2,1)S(1)}, bf16[1,72,384]{2,1,0:T(8,128)(2,1)S(1)}, u32[]{:S(2)}, u32[]{:S(2)}) collective-permute-start(bf16[1,72,384]{2,1,0:T(8,128)(2,1)S(1)} %bitcast.23), channel_id=1, source_target_pairs={{0,12},{1,13},{2,14},{3,15},{4,8},{5,9},{6,10},{7,11},{8,4},{9,5},... | collective-permute-start | bytes 165896 | tf_op jit(solution)/shard_map/ppermute | solution.py:28
  7.2 4.2 %collective-permute-start.1 = (bf16[1,72,384]{2,1,0:T(8,128)(2,1)S(1)}, bf16[1,72,384]{2,1,0:T(8,128)(2,1)S(1)}, u32[]{:S(2)}, u32[]{:S(2)}) collective-permute-start(bf16[1,72,384]{2,1,0:T(8,128)(2,1)S(1)} %bitcast.24), channel_id=1, source_target_pairs={{0,4},{1,5},{2,6},{3,7},{4,0},{5,1},{6,2},{7,3},{8,12},{9,13},{10,... | collective-permute-start | bytes 165896 | tf_op jit(solution)/shard_map/ppermute | solution.py:28
  7.2 5.4 %collective-permute-start.2 = (bf16[1,72,384]{2,1,0:T(8,128)(2,1)S(1)}, bf16[1,72,384]{2,1,0:T(8,128)(2,1)S(1)}, u32[]{:S(2)}, u32[]{:S(2)}) collective-permute-start(bf16[1,72,384]{2,1,0:T(8,128)(2,1)S(1)} %bitcast.25), channel_id=1, source_target_pairs={{0,8},{1,9},{2,10},{3,11},{4,12},{5,13},{6,14},{7,15},{8,0},{9,1},... | collective-permute-start | bytes 165896 | tf_op jit(solution)/shard_map/ppermute | solution.py:28
  12.7 8.4 %collective-permute-start.3 = (bf16[4,72,384]{2,1,0:T(8,128)(2,1)S(1)}, bf16[4,72,384]{2,1,0:T(8,128)(2,1)S(1)}, u32[]{:S(2)}, u32[]{:S(2)}) collective-permute-start(bf16[4,72,384]{2,1,0:T(8,128)(2,1)S(1)} %pad_maximum_fusion._), channel_id=1, source_target_pairs={{0,2},{1,3},{2,0},{3,1},{4,6},{5,7},{6,4},{7,5},{8,10},{9,11},{10,... | collective-permute-start | bytes 663560 | tf_op jit(solution)/shard_map/ppermute | solution.py:28
  14.3 7.5 %collective-permute-start.4 = (bf16[4,72,384]{2,1,0:T(8,128)(2,1)S(1)}, bf16[4,72,384]{2,1,0:T(8,128)(2,1)S(1)}, u32[]{:S(2)}, u32[]{:S(2)}) collective-permute-start(bf16[4,72,384]{2,1,0:T(8,128)(2,1)S(1)} %pad_maximum_fusion._), channel_id=1, source_target_pairs={{0,1},{1,0},{2,3},{3,2},{4,5},{5,4},{6,7},{7,6},{8,9},{9,8},{10,11... | collective-permute-start | bytes 663560 | tf_op jit(solution)/shard_map/ppermute | solution.py:28
  15.8 8.3 %collective-permute-start.5 = (bf16[4,72,384]{2,1,0:T(8,128)(2,1)S(1)}, bf16[4,72,384]{2,1,0:T(8,128)(2,1)S(1)}, u32[]{:S(2)}, u32[]{:S(2)}) collective-permute-start(bf16[4,72,384]{2,1,0:T(8,128)(2,1)S(1)} %pad_maximum_fusion._), channel_id=1, source_target_pairs={{0,3},{1,2},{2,1},{3,0},{4,7},{5,6},{6,5},{7,4},{8,11},{9,10},{10,... | collective-permute-start | bytes 663560 | tf_op jit(solution)/shard_map/ppermute | solution.py:28
  26.7 6.0 %collective-permute-start.6 = (bf16[1,64,384]{2,1,0:T(8,128)(2,1)S(1)}, bf16[1,64,384]{2,1,0:T(8,128)(2,1)S(1)}, u32[]{:S(2)}, u32[]{:S(2)}) collective-permute-start(bf16[1,64,384]{2,1,0:T(8,128)(2,1)S(1)} %bitcast.19), channel_id=1, source_target_pairs={{0,12},{1,13},{2,14},{3,15},{4,8},{5,9},{6,10},{7,11},{8,4},{9,5},... | collective-permute-start | bytes 147464 | tf_op jit(solution)/shard_map/ppermute | solution.py:28
  28.8 4.3 %collective-permute-start.7 = (bf16[1,64,384]{2,1,0:T(8,128)(2,1)S(1)}, bf16[1,64,384]{2,1,0:T(8,128)(2,1)S(1)}, u32[]{:S(2)}, u32[]{:S(2)}) collective-permute-start(bf16[1,64,384]{2,1,0:T(8,128)(2,1)S(1)} %bitcast.20), channel_id=1, source_target_pairs={{0,4},{1,5},{2,6},{3,7},{4,0},{5,1},{6,2},{7,3},{8,12},{9,13},{10,... | collective-permute-start | bytes 147464 | tf_op jit(solution)/shard_map/ppermute | solution.py:28
  29.4 5.0 %collective-permute-start.8 = (bf16[1,64,384]{2,1,0:T(8,128)(2,1)S(1)}, bf16[1,64,384]{2,1,0:T(8,128)(2,1)S(1)}, u32[]{:S(2)}, u32[]{:S(2)}) collective-permute-start(bf16[1,64,384]{2,1,0:T(8,128)(2,1)S(1)} %bitcast.21), channel_id=1, source_target_pairs={{0,8},{1,9},{2,10},{3,11},{4,12},{5,13},{6,14},{7,15},{8,0},{9,1},... | collective-permute-start | bytes 147464 | tf_op jit(solution)/shard_map/ppermute | solution.py:28
  34.5 5.8 %collective-permute-start.9 = (bf16[4,64,384]{2,1,0:T(8,128)(2,1)S(1)}, bf16[4,64,384]{2,1,0:T(8,128)(2,1)S(1)}, u32[]{:S(2)}, u32[]{:S(2)}) collective-permute-start(bf16[4,64,384]{2,1,0:T(8,128)(2,1)S(1)} %pad_maximum_fusion.1), channel_id=1, source_target_pairs={{0,2},{1,3},{2,0},{3,1},{4,6},{5,7},{6,4},{7,5},{8,10},{9,11},{10,... | collective-permute-start | bytes 589832 | tf_op jit(solution)/shard_map/ppermute | solution.py:28
  36.1 5.7 %collective-permute-start.10 = (bf16[4,64,384]{2,1,0:T(8,128)(2,1)S(1)}, bf16[4,64,384]{2,1,0:T(8,128)(2,1)S(1)}, u32[]{:S(2)}, u32[]{:S(2)}) collective-permute-start(bf16[4,64,384]{2,1,0:T(8,128)(2,1)S(1)} %pad_maximum_fusion.1), channel_id=1, source_target_pairs={{0,1},{1,0},{2,3},{3,2},{4,5},{5,4},{6,7},{7,6},{8,9},{9,8},{10,11... | collective-permute-start | bytes 589832 | tf_op jit(solution)/shard_map/ppermute | solution.py:28
  37.6 6.6 %collective-permute-start.11 = (bf16[4,64,384]{2,1,0:T(8,128)(2,1)S(1)}, bf16[4,64,384]{2,1,0:T(8,128)(2,1)S(1)}, u32[]{:S(2)}, u32[]{:S(2)}) collective-permute-start(bf16[4,64,384]{2,1,0:T(8,128)(2,1)S(1)} %pad_maximum_fusion.1), channel_id=1, source_target_pairs={{0,3},{1,2},{2,1},{3,0},{4,7},{5,6},{6,5},{7,4},{8,11},{9,10},{10,... | collective-permute-start | bytes 589832 | tf_op jit(solution)/shard_map/ppermute | solution.py:28
  48.6 6.8 %collective-permute-start.15 = (bf16[4,200,128]{2,1,0:T(8,128)(2,1)S(1)}, bf16[4,200,128]{2,1,0:T(8,128)(2,1)S(1)}, u32[]{:S(2)}, u32[]{:S(2)}) collective-permute-start(bf16[4,200,128]{2,1,0:T(8,128)(2,1)S(1)} %get-tuple-element.69), channel_id=1, source_target_pairs={{0,3},{1,2},{2,1},{3,0},{4,7},{5,6},{6,5},{7,4},{8,11},{9,10},{10,... | collective-permute-start | bytes 614408 | tf_op jit(solution)/shard_map/ppermute | solution.py:28
  50.7 6.5 %collective-permute-start.16 = (bf16[4,200,128]{2,1,0:T(8,128)(2,1)S(1)}, bf16[4,200,128]{2,1,0:T(8,128)(2,1)S(1)}, u32[]{:S(2)}, u32[]{:S(2)}) collective-permute-start(bf16[4,200,128]{2,1,0:T(8,128)(2,1)S(1)} %get-tuple-element.71), channel_id=1, source_target_pairs={{0,1},{1,0},{2,3},{3,2},{4,5},{5,4},{6,7},{7,6},{8,9},{9,8},{10,11... | collective-permute-start | bytes 614408 | tf_op jit(solution)/shard_map/ppermute | solution.py:28
  51.3 6.2 %collective-permute-start.17 = (bf16[4,200,128]{2,1,0:T(8,128)(2,1)S(1)}, bf16[4,200,128]{2,1,0:T(8,128)(2,1)S(1)}, u32[]{:S(2)}, u32[]{:S(2)}) collective-permute-start(bf16[4,200,128]{2,1,0:T(8,128)(2,1)S(1)} %get-tuple-element.70), channel_id=1, source_target_pairs={{0,2},{1,3},{2,0},{3,1},{4,6},{5,7},{6,4},{7,5},{8,10},{9,11},{10,... | collective-permute-start | bytes 614408 | tf_op jit(solution)/shard_map/ppermute | solution.py:28
  52.1 1.2 %collective-permute-start.14 = (bf16[64,384]{1,0:T(8,128)(2,1)S(1)}, bf16[64,384]{1,0:T(8,128)(2,1)S(1)}, u32[]{:S(2)}, u32[]{:S(2)}) collective-permute-start(bf16[64,384]{1,0:T(8,128)(2,1)S(1)} %get-tuple-element.43), channel_id=1, source_target_pairs={{0,16},{16,0},{1,17},{17,1},{2,18},{18,2},{3,19},{19,3},{4,20},{20... | collective-permute-start | bytes 147464 | tf_op jit(solution)/shard_map/ppermute | solution.py:33
  52.2 9.9 %collective-permute-start.13 = (bf16[64,3072]{1,0:T(8,128)(2,1)S(1)}, bf16[64,3072]{1,0:T(8,128)(2,1)S(1)}, u32[]{:S(2)}, u32[]{:S(2)}) collective-permute-start(bf16[64,3072]{1,0:T(8,128)(2,1)S(1)} %get-tuple-element.74), channel_id=1, source_target_pairs={{0,16},{16,0},{1,17},{17,1},{2,18},{18,2},{3,19},{19,3},{4,20},{20... | collective-permute-start | bytes 1179656 | tf_op jit(solution)/shard_map/ppermute | solution.py:33
  53.4 8.7 %collective-permute-start.12 = (bf16[64,384]{1,0:T(8,128)(2,1)S(1)}, bf16[64,384]{1,0:T(8,128)(2,1)S(1)}, u32[]{:S(2)}, u32[]{:S(2)}) collective-permute-start(bf16[64,384]{1,0:T(8,128)(2,1)S(1)} %get-tuple-element.40.refs_1_), channel_id=1, source_target_pairs={{0,16},{16,0},{1,17},{17,1},{2,18},{18,2},{3,19},{19,3},{4,20},{20... | collective-permute-start | bytes 147464 | tf_op jit(solution)/shard_map/ppermute | solution.py:33
  57.6 7.7 %collective-permute-start.19 = (bf16[1,200,128]{2,1,0:T(8,128)(2,1)S(1)}, bf16[1,200,128]{2,1,0:T(8,128)(2,1)S(1)}, u32[]{:S(2)}, u32[]{:S(2)}) collective-permute-start(bf16[1,200,128]{2,1,0:T(8,128)(2,1)S(1)} %get-tuple-element.77), channel_id=1, source_target_pairs={{0,4},{1,5},{2,6},{3,7},{4,0},{5,1},{6,2},{7,3},{8,12},{9,13},{10,... | collective-permute-start | bytes 153608 | tf_op jit(solution)/shard_map/ppermute | solution.py:28
  59.2 6.1 %collective-permute-start.20 = (bf16[1,200,128]{2,1,0:T(8,128)(2,1)S(1)}, bf16[1,200,128]{2,1,0:T(8,128)(2,1)S(1)}, u32[]{:S(2)}, u32[]{:S(2)}) collective-permute-start(bf16[1,200,128]{2,1,0:T(8,128)(2,1)S(1)} %get-tuple-element.76), channel_id=1, source_target_pairs={{0,8},{1,9},{2,10},{3,11},{4,12},{5,13},{6,14},{7,15},{8,0},{9,1},... | collective-permute-start | bytes 153608 | tf_op jit(solution)/shard_map/ppermute | solution.py:28
  60.3 5.9 %collective-permute-start.18 = (bf16[1,200,128]{2,1,0:T(8,128)(2,1)S(1)}, bf16[1,200,128]{2,1,0:T(8,128)(2,1)S(1)}, u32[]{:S(2)}, u32[]{:S(2)}) collective-permute-start(bf16[1,200,128]{2,1,0:T(8,128)(2,1)S(1)} %get-tuple-element.78), channel_id=1, source_target_pairs={{0,12},{1,13},{2,14},{3,15},{4,8},{5,9},{6,10},{7,11},{8,4},{9,5},... | collective-permute-start | bytes 153608 | tf_op jit(solution)/shard_map/ppermute | solution.py:28
  67.8 4.1 %collective-permute-start.22 = (bf16[64,3072]{1,0:T(8,128)(2,1)S(1)}, bf16[64,3072]{1,0:T(8,128)(2,1)S(1)}, u32[]{:S(2)}, u32[]{:S(2)}) collective-permute-start(bf16[64,3072]{1,0:T(8,128)(2,1)S(1)} %get-tuple-element.54), channel_id=1, source_target_pairs={{0,16},{16,0},{1,17},{17,1},{2,18},{18,2},{3,19},{19,3},{4,20},{20... | collective-permute-start | bytes 1179656 | tf_op jit(solution)/shard_map/ppermute | solution.py:33
  67.9 4.0 %collective-permute-start.21 = (bf16[64,384]{1,0:T(8,128)(2,1)S(1)}, bf16[64,384]{1,0:T(8,128)(2,1)S(1)}, u32[]{:S(2)}, u32[]{:S(2)}) collective-permute-start(bf16[64,384]{1,0:T(8,128)(2,1)S(1)} %get-tuple-element.53.refs_1_), channel_id=1, source_target_pairs={{0,16},{16,0},{1,17},{17,1},{2,18},{18,2},{3,19},{19,3},{4,20},{20... | collective-permute-start | bytes 147464 | tf_op jit(solution)/shard_map/ppermute | solution.py:33
  68.4 6.6 %collective-permute-start.23 = (f32[4,384]{1,0:T(4,128)S(1)}, f32[4,384]{1,0:T(4,128)S(1)}, u32[]{:S(2)}, u32[]{:S(2)}) collective-permute-start(f32[4,384]{1,0:T(4,128)S(1)} %get-tuple-element.60), channel_id=1, source_target_pairs={{0,3},{1,2},{2,1},{3,0},{4,7},{5,6},{6,5},{7,4},{8,11},{9,10},{10,... | collective-permute-start | bytes 18440 | tf_op jit(solution)/shard_map/ppermute | solution.py:28
  70.5 4.6 %collective-permute-start.24 = (f32[4,384]{1,0:T(4,128)S(1)}, f32[4,384]{1,0:T(4,128)S(1)}, u32[]{:S(2)}, u32[]{:S(2)}) collective-permute-start(f32[4,384]{1,0:T(4,128)S(1)} %get-tuple-element.61), channel_id=1, source_target_pairs={{0,1},{1,0},{2,3},{3,2},{4,5},{5,4},{6,7},{7,6},{8,9},{9,8},{10,11... | collective-permute-start | bytes 18440 | tf_op jit(solution)/shard_map/ppermute | solution.py:28
  71.0 4.0 %collective-permute-start.25 = (f32[4,384]{1,0:T(4,128)S(1)}, f32[4,384]{1,0:T(4,128)S(1)}, u32[]{:S(2)}, u32[]{:S(2)}) collective-permute-start(f32[4,384]{1,0:T(4,128)S(1)} %get-tuple-element.62), channel_id=1, source_target_pairs={{0,2},{1,3},{2,0},{3,1},{4,6},{5,7},{6,4},{7,5},{8,10},{9,11},{10,... | collective-permute-start | bytes 18440 | tf_op jit(solution)/shard_map/ppermute | solution.py:28
  75.1 5.4 %collective-permute-start.26 = (f32[1,384]{1,0:T(1,128)S(1)}, f32[1,384]{1,0:T(1,128)S(1)}, u32[]{:S(2)}, u32[]{:S(2)}) collective-permute-start(f32[1,384]{1,0:T(1,128)S(1)} %get-tuple-element.81), channel_id=1, source_target_pairs={{0,12},{1,13},{2,14},{3,15},{4,8},{5,9},{6,10},{7,11},{8,4},{9,5},... | collective-permute-start | bytes 4616 | tf_op jit(solution)/shard_map/ppermute | solution.py:28
  77.0 3.6 %collective-permute-start.27 = (f32[1,384]{1,0:T(1,128)S(1)}, f32[1,384]{1,0:T(1,128)S(1)}, u32[]{:S(2)}, u32[]{:S(2)}) collective-permute-start(f32[1,384]{1,0:T(1,128)S(1)} %get-tuple-element.83), channel_id=1, source_target_pairs={{0,4},{1,5},{2,6},{3,7},{4,0},{5,1},{6,2},{7,3},{8,12},{9,13},{10,... | collective-permute-start | bytes 4616 | tf_op jit(solution)/shard_map/ppermute | solution.py:28
  77.0 4.5 %collective-permute-start.28 = (f32[1,384]{1,0:T(1,128)S(1)}, f32[1,384]{1,0:T(1,128)S(1)}, u32[]{:S(2)}, u32[]{:S(2)}) collective-permute-start(f32[1,384]{1,0:T(1,128)S(1)} %get-tuple-element.82), channel_id=1, source_target_pairs={{0,8},{1,9},{2,10},{3,11},{4,12},{5,13},{6,14},{7,15},{8,0},{9,1},... | collective-permute-start | bytes 4616 | tf_op jit(solution)/shard_map/ppermute | solution.py:28
  81.5 1.2 %collective-permute-start.29 = (f32[1,384]{1,0:T(1,128)S(1)}, f32[1,384]{1,0:T(1,128)S(1)}, u32[]{:S(2)}, u32[]{:S(2)}) collective-permute-start(f32[1,384]{1,0:T(1,128)S(1)} %get-tuple-element.65), channel_id=1, source_target_pairs={{0,16},{16,0},{1,17},{17,1},{2,18},{18,2},{3,19},{19,3},{4,20},{20... | collective-permute-start | bytes 4616 | tf_op jit(solution)/shard_map/ppermute | solution.py:33
